TPU v7x, 32 devices: a whole 2x2x4 slice. The times are simulated.
32 devices in a mesh: dp: 8 (over z, x), row: 2 (over y), col: 2 (over core).
Axes of the slice: x: 2, y: 2, z: 4, core: 2. Of those that a mesh axis runs over, the one named last changes fastest.
Arguments:
- hidden: bfloat16 [2048, 1024], P('dp', ('row', 'col')), may hold values from -6 to 6
- segment_ids: int32 [8, 256], P('dp'), may hold values from 0 to 3, never falling along the last dimension, each value on 1 to 128 neighbouring positions
- norm1_gain: bfloat16 [1024], P('row'), may hold values from 0.5 to 1.5
- w_gate: bfloat16 [1024, 1536], P('row', 'col'), may hold values from -0.1875 to 0.1875
- w_xin: bfloat16 [1024, 1536], P('row', 'col'), may hold values from -0.1875 to 0.1875
- w_dt: bfloat16 [1024, 24], P('row', 'col'), may hold values from -0.1875 to 0.1875
- w_bc: bfloat16 [1024, 256], P('row'), may hold values from -0.1875 to 0.1875
- w_query: bfloat16 [1024, 512], P('row', 'col'), may hold values from -0.1875 to 0.1875
- w_kv: bfloat16 [1024, 2, 128], P('row', 'col'), may hold values from -0.1875 to 0.1875
- convx_weight: bfloat16 [1536, 4], P(('col', 'row')), may hold values from -3 to 3
- convx_bias: bfloat16 [1536], P(('col', 'row')), may hold values from -3 to 3
- convbc_weight: bfloat16 [256, 4], replicated, may hold values from -3 to 3
- convbc_bias: bfloat16 [256], replicated, may hold values from -3 to 3
- dt_bias: bfloat16 [24], P(('col', 'row')), may hold values from -3 to 0.5
- a_log: bfloat16 [24], P(('col', 'row')), may hold values from -4.5 to 0
- d_skip: bfloat16 [24], P(('col', 'row')), may hold values from 0.5 to 1.5
- w_mixout: bfloat16 [1536, 1024], P('col', 'row'), may hold values from -0.009765625 to 0.009765625
- w_attnout: bfloat16 [512, 1024], P('col', 'row'), may hold values from -2 to 2
- norm2_gain: bfloat16 [1024], P('row'), may hold values from 0.5 to 1.5
- w_gateup: bfloat16 [1024, 2, 2048], P('row', None, 'col'), may hold values from -0.1875 to 0.1875
- w_down: bfloat16 [2048, 1024], P('col', 'row'), may hold values from -0.125 to 0.125
- cotangent: bfloat16 [2048, 1024], P('dp', ('row', 'col')), may hold values from -6 to 6
Outputs:
- output: bfloat16 [2048, 1024], P('dp', ('row', 'col'))
- grad_hidden: float32 [2048, 1024], P('dp', ('row', 'col'))
- grad_norm1_gain: float32 [1024], P('row')
- grad_w_gate: float32 [1024, 1536], P(('row', 'dp'), 'col')
- grad_w_xin: float32 [1024, 1536], P(('row', 'dp'), 'col')
- grad_w_dt: float32 [1024, 24], P(('row', 'dp'), 'col')
- grad_w_bc: float32 [1024, 256], P(('row', 'dp'))
- grad_w_query: float32 [1024, 512], P(('row', 'dp'), 'col')
- grad_w_kv: float32 [1024, 2, 128], P(('row', 'dp'), 'col')
- grad_convx_weight: float32 [1536, 4], P(('col', 'row'))
- grad_convx_bias: float32 [1536], P(('col', 'row'))
- grad_convbc_weight: float32 [256, 4], replicated
- grad_convbc_bias: float32 [256], replicated
- grad_dt_bias: float32 [24], P(('col', 'row'))
- grad_a_log: float32 [24], P(('col', 'row'))
- grad_d_skip: float32 [24], P(('col', 'row'))
- grad_w_mixout: float32 [1536, 1024], P(('col', 'dp'), 'row')
- grad_w_attnout: float32 [512, 1024], P(('col', 'dp'), 'row')
- grad_norm2_gain: float32 [1024], P('row')
- grad_w_gateup: float32 [1024, 2, 2048], P(('row', 'dp'), None, 'col')
- grad_w_down: float32 [2048, 1024], P(('col', 'dp'), 'row')
Inputs may be any that keep to these rules, and one draw needn't show every extreme that they name: `segment_ids`: segment ids never fall along a sequence.
All inputs are finite; a program needn't handle non-finite values.
Results may differ from a plain program's by a relative error of at most 0.0093.
Values may be sent and summed in bfloat16 or wider, within the bound.
No kernel may reach another device: no remote copies, remote signals or barrier semaphores. Data moves between devices by JAX's collectives and lax.ppermute only.
A program may use at most 128 MiB of HBM per device.

v0:
```python
import jax
import jax.numpy as jnp
import numpy as np
from jax import lax
from jax.experimental import pallas as pl
from jax.experimental.pallas import tpu as pltpu
from jax.sharding import PartitionSpec as P

NORM_EPS = 1e-05
F32 = jnp.float32
BF16 = jnp.bfloat16
HEAD = 64
LANES = 128
TAPS = 4
FAR = -1e30


def swap(values, axis, step=1):
    count = lax.axis_size(axis)
    return lax.ppermute(values, axis, [(i, i ^ step) for i in range(count)])


def dot(left, right):
    return jnp.dot(left, right, preferred_element_type=F32)


def dot_bt(left, right):
    return lax.dot_general(left, right, (((1,), (1,)), ((), ())), preferred_element_type=F32)


def dot_at(left, right):
    return lax.dot_general(left, right, (((0,), (0,)), ((), ())), preferred_element_type=F32)


def fine(left, right, dims=((1,), (0,))):
    return lax.dot_general(
        left, right, (dims, ((), ())), precision=lax.Precision.HIGHEST, preferred_element_type=F32
    )


def call(kernel, outs, *args, scratch=(), smem=()):
    specs = [
        pl.BlockSpec(memory_space=pltpu.SMEM if i in smem else pltpu.VMEM)
        for i in range(len(args))
    ]
    return pl.pallas_call(
        kernel,
        out_shape=[jax.ShapeDtypeStruct(s, d) for s, d in outs],
        in_specs=specs,
        out_specs=[pl.BlockSpec(memory_space=pltpu.VMEM)] * len(outs),
        scratch_shapes=[pltpu.VMEM(s, d) for s, d in scratch],
        compiler_params=pltpu.CompilerParams(vmem_limit_bytes=56 << 20),
    )(*args)


def iota(shape, dim):
    return lax.broadcasted_iota(jnp.int32, shape, dim)


def column(row_vector):
    ones = jnp.full((row_vector.shape[0], LANES), 1.0 / row_vector.shape[0], F32)
    return fine(row_vector, ones, ((0,), (0,)))


def token_sums(values):
    return fine(jnp.ones((8, values.shape[1]), F32), values, ((1,), (1,)))


def open_kernel(place, mine, came, own_out, sums_out):
    tokens = mine.shape[0] // 2
    width = mine.shape[1]
    first = place[0] == 0
    a = mine[...]
    b = came[...]
    own_out[:, :width] = jnp.where(first, a, b)
    own_out[:, width:] = jnp.where(first, b, a)
    ha = a[:tokens].astype(F32)
    hb = b[:tokens].astype(F32)
    sums_out[...] = token_sums(ha * ha + hb * hb)


def project_kernel(full_width, own, sums, sums_far, gain, wx, wb, wd, wg, wq, wk, n1_out, p_out, low_out):
    tokens = n1_out.shape[0]
    mean = column(sums[...] + sums_far[...])[:, :1] / full_width
    factor = lax.rsqrt(mean + NORM_EPS)
    n1 = (own[:tokens].astype(F32) * factor * gain[...]).astype(BF16)
    n1_out[...] = n1
    at = 0
    for w in (wx, wb, wd, wg, wq, wk):
        size = w.shape[1]
        part = dot(n1, w[...])
        p_out[:, at : at + size] = part
        low_out[:, at : at + size] = part.astype(BF16)
        at += size


def masks(seg_row, seg_col, turned):
    tokens = seg_row.shape[1]
    i = iota((tokens, tokens), 1 if turned else 0)
    j = iota((tokens, tokens), 0 if turned else 1)
    same = seg_col[:, :1] == seg_row[...]
    return jnp.where((i >= j) & same, 0.0, FAR)


def valids(seg_col):
    seg = seg_col[...]
    t = iota(seg.shape, 0)
    return [
        jnp.where((t >= k) & (pltpu.roll(seg, k, 0) == seg), 1.0, 0.0) for k in range(1, TAPS)
    ]


def conv(block, taps, bias, valid):
    total = block * taps[TAPS - 1 : TAPS] + bias
    for k in range(1, TAPS):
        total = total + (pltpu.roll(block, k, 0) * valid[k - 1]) * taps[TAPS - 1 - k : TAPS - k]
    return total


def conv_turn(grad, block, taps, valid):
    tokens = grad.shape[0]
    back = grad * taps[TAPS - 1 : TAPS]
    rows = [None] * TAPS
    rows[TAPS - 1] = jnp.sum(grad * block, axis=0, keepdims=True)
    for k in range(1, TAPS):
        kept = grad * valid[k - 1]
        back = back + pltpu.roll(kept, tokens - k, 0) * taps[TAPS - 1 - k : TAPS - k]
        rows[TAPS - 1 - k] = jnp.sum(kept * pltpu.roll(block, k, 0), axis=0, keepdims=True)
    rows.append(jnp.sum(grad, axis=0, keepdims=True))
    rows.append(jnp.zeros((8 - len(rows), grad.shape[1]), F32))
    return back, jnp.concatenate(rows, 0)


def silu_turn(value):
    sig = jax.nn.sigmoid(value)
    return value * sig, sig * (1.0 + value * (1.0 - sig))


def steps(dt_raw, head_par):
    shifted = dt_raw + head_par[0:1]
    return jnp.maximum(shifted, 0.0) + jnp.log1p(jnp.exp(-jnp.abs(shifted)))


def mix_kernel(
    ch, nq, seg_row, seg_col, own, came, x_par, bc_par, head_par,
    mixed_out, sums_out, pre_out, y_out,
):
    tokens = own.shape[0]
    nbc = bc_par.shape[1]
    state = nbc // 2
    sums_out[...] = own[...] + came[...].astype(F32)
    lane = iota((tokens, LANES), 1)
    low = lane < HEAD
    mask = masks(seg_row, seg_col, False)
    valid = valids(seg_col)
    for b in range(nbc // LANES):
        at = ch + b * LANES
        part = slice(b * LANES, (b + 1) * LANES)
        pre_out[:, at : at + LANES] = conv(
            sums_out[:, at : at + LANES], bc_par[0:TAPS, part], bc_par[TAPS : TAPS + 1, part], valid
        )
    bcc = pre_out[:, ch : ch + nbc]
    bcc = bcc * jax.nn.sigmoid(bcc)
    inner = fine(bcc[:, state:], bcc[:, :state], ((1,), (1,)))
    dt = steps(sums_out[:, ch + nbc : ch + nbc + LANES], head_par)
    tri = jnp.where(iota((tokens, tokens), 0) >= iota((tokens, tokens), 1), 1.0, 0.0)
    cum = fine(tri, dt * -jnp.exp(head_par[1:2]))
    cum_row = cum.T
    base = ch + nbc + LANES
    for p in range(ch // LANES):
        part = slice(p * LANES, (p + 1) * LANES)
        pre = conv(sums_out[:, part], x_par[0:TAPS, part], x_par[TAPS : TAPS + 1, part], valid)
        pre_out[:, part] = pre
        xc = pre * jax.nn.sigmoid(pre)
        h = 2 * p
        xdt = (xc * jnp.where(low, dt[:, h : h + 1], dt[:, h + 1 : h + 2])).astype(BF16)
        ys = []
        for e in (h, h + 1):
            decay = jnp.exp((cum[:, e : e + 1] - cum_row[e : e + 1]) + mask)
            ys.append(dot((inner * decay).astype(BF16), xdt))
        y = jnp.where(low, ys[0], ys[1])
        y_out[:, part] = y
        y = y + x_par[TAPS + 1 : TAPS + 2, part] * xc
        z = sums_out[:, base + p * LANES : base + (p + 1) * LANES]
        mixed_out[:, part] = (y * (z * jax.nn.sigmoid(z))).astype(BF16)
    at = base + ch
    kv = sums_out[:, at + nq : at + nq + LANES].astype(BF16)
    kv_turn = pltpu.roll(sums_out[:, at + nq : at + nq + LANES], HEAD, 1).astype(BF16)
    keys = jnp.where(low, kv, kv_turn)
    vals = jnp.where(low, kv_turn, kv)
    for p in range(nq // LANES):
        query = sums_out[:, at + p * LANES : at + (p + 1) * LANES] * (HEAD ** -0.5)
        outs = []
        for side in (low, ~low):
            score = dot_bt(jnp.where(side, query, 0.0).astype(BF16), keys) + mask
            score = jnp.exp(score - jnp.max(score, axis=1, keepdims=True))
            total = jnp.sum(score, axis=1, keepdims=True)
            outs.append(dot(score.astype(BF16), vals) / total)
        mixed_out[:, ch + p * LANES : ch + (p + 1) * LANES] = jnp.where(
            low, outs[0], outs[1]
        ).astype(BF16)


def unmix_kernel(
    ch, nq, seg_row, seg_col, sums, pre, ys, dym, x_par, bc_par, head_par,
    gx_out, gtwo_out, gdt_out, gbc_out, small_out, prod_a, prod_b, turned,
):
    tokens = sums.shape[0]
    nbc = bc_par.shape[1]
    state = nbc // 2
    lane = iota((tokens, LANES), 1)
    low = lane < HEAD
    mask = masks(seg_row, seg_col, True)
    valid = valids(seg_col)
    bc_pre = pre[:, ch : ch + nbc]
    bcc, bcc_turn = silu_turn(bc_pre)
    b_in = bcc[:, :state]
    c_in = bcc[:, state:]
    inner = fine(b_in, c_in, ((1,), (1,)))
    dt_raw = sums[:, ch + nbc : ch + nbc + LANES]
    dt = steps(dt_raw, head_par)
    rate = jnp.exp(head_par[1:2])
    tri = jnp.where(iota((tokens, tokens), 0) >= iota((tokens, tokens), 1), 1.0, 0.0)
    cum = fine(tri, dt * -rate)
    cum_row = cum.T
    base = ch + nbc + LANES
    small_out[...] = jnp.zeros_like(small_out)
    turned[...] = jnp.zeros_like(turned)
    for p in range(ch // LANES):
        part = slice(p * LANES, (p + 1) * LANES)
        xc, xc_turn = silu_turn(pre[:, part])
        skip = x_par[TAPS + 1 : TAPS + 2, part]
        z = sums[:, base + p * LANES : base + (p + 1) * LANES]
        gate, gate_turn = silu_turn(z)
        dy_in = dym[:, part]
        y = ys[:, part]
        gtwo_out[:, part] = (dy_in * (y + skip * xc) * gate_turn).astype(BF16)
        dy = dy_in * gate
        h = 2 * p
        dt_pair = jnp.where(low, dt[:, h : h + 1], dt[:, h + 1 : h + 2])
        xdt = xc * dt_pair
        dy_low = dy.astype(BF16)
        x_low = xdt.astype(BF16)
        sides = []
        for e, side in ((h, low), (h + 1, ~low)):
            decay = jnp.exp((cum_row[e : e + 1] - cum[:, e : e + 1]) + mask)
            turned[...] += dot_bt(jnp.where(side, xdt, 0.0).astype(BF16), dy_low) * decay
            sides.append(dot((inner * decay).astype(BF16), dy_low))
        dxdt = jnp.where(low, sides[0], sides[1])
        prod_a[:, part] = dy_low.astype(F32) * y - x_low.astype(F32) * dxdt
        prod_b[:, part] = dxdt * xc
        small_out[8 + TAPS + 1 : 8 + TAPS + 2, part] = jnp.sum(dy * xc, axis=0, keepdims=True)
        dpre = (skip * dy + dxdt * dt_pair) * xc_turn
        back, rows = conv_turn(dpre, sums[:, part], x_par[0:TAPS, part], valid)
        gx_out[:, part] = back.astype(BF16)
        small_out[0:8, part] = rows
    pick = jnp.where(iota((ch, LANES), 0) // HEAD == iota((ch, LANES), 1), 1.0, 0.0)
    dcum = fine(prod_a[...], pick)
    ddt = fine(prod_b[...], pick)
    after = fine(tri, dcum, ((0,), (0,)))
    ddt = ddt - rate * after
    ddt = ddt * jax.nn.sigmoid(dt_raw + head_par[0:1])
    gdt_out[...] = ddt.astype(BF16)
    small_out[8 + TAPS : 8 + TAPS + 1, 0:LANES] = jnp.sum(ddt, axis=0, keepdims=True)
    small_out[8 + TAPS : 8 + TAPS + 1, LANES : 2 * LANES] = jnp.sum(
        after * (-dt * rate), axis=0, keepdims=True
    )
    skip_sum = jnp.broadcast_to(small_out[8 + TAPS + 1 : 8 + TAPS + 2, :], (8, ch))
    small_out[8 + TAPS : 8 + TAPS + 1, 2 * LANES : 3 * LANES] = fine(skip_sum, pick)[0:1]
    dinner = turned[...]
    d_b = fine(dinner, c_in) * bcc_turn[:, :state]
    d_c = fine(dinner, b_in, ((0,), (0,))) * bcc_turn[:, state:]
    for b, grad in enumerate((d_b, d_c)):
        at = ch + b * LANES
        part = slice(b * LANES, (b + 1) * LANES)
        back, rows = conv_turn(grad, sums[:, at : at + LANES], bc_par[0:TAPS, part], valid)
        gbc_out[0:tokens, part] = back
        gbc_out[tokens : tokens + 8, part] = rows
    at = base + ch
    kv = sums[:, at + nq : at + nq + LANES]
    kv_turn = pltpu.roll(kv, HEAD, 1)
    keys = jnp.where(low, kv, kv_turn).astype(BF16)
    vals = jnp.where(low, kv_turn, kv).astype(BF16)
    dk = jnp.zeros((tokens, LANES), F32)
    dv = jnp.zeros((tokens, LANES), F32)
    for p in range(nq // LANES):
        query = sums[:, at + p * LANES : at + (p + 1) * LANES] * (HEAD ** -0.5)
        grad = dym[:, ch + p * LANES : ch + (p + 1) * LANES]
        dqs = []
        for side in (low, ~low):
            q_low = jnp.where(side, query, 0.0).astype(BF16)
            g_low = jnp.where(side, grad, 0.0).astype(BF16)
            score = dot_bt(keys, q_low) + mask
            score = jnp.exp(score - jnp.max(score, axis=0, keepdims=True))
            prob = score * (1.0 / jnp.sum(score, axis=0, keepdims=True))
            dprob = dot_bt(vals, g_low)
            dv = dv + dot(prob.astype(BF16), g_low)
            inner_sum = jnp.sum(prob * dprob, axis=0, keepdims=True)
            dscore = (prob * (dprob - inner_sum)).astype(BF16)
            dk = dk + dot(dscore, q_low)
            dqs.append(dot_at(dscore, keys))
        gtwo_out[:, ch + p * LANES : ch + (p + 1) * LANES] = (
            jnp.where(low, dqs[0], dqs[1]) * (HEAD ** -0.5)
        ).astype(BF16)
    dk = dk + pltpu.roll(dk, HEAD, 1)
    dv = dv + pltpu.roll(dv, HEAD, 1)
    gtwo_out[:, ch + nq : ch + nq + LANES] = jnp.where(low, dk, dv).astype(BF16)


def tall_far(first, second, pair, start, size):
    return jnp.concatenate(
        [r[start : start + size] for r in (first, second, pair)], axis=1
    )


def out_kernel(mixed, tall, first, second, pair, part_out):
    inner = mixed.shape[1]
    half = tall.shape[1]
    value = mixed[...]
    part_out[:, :half] = dot(value, tall[0:inner])
    part_out[:, half:] = dot(value, tall_far(first, second, pair, 0, inner))


def norm_factor(value):
    return lax.rsqrt(jnp.mean(value * value, axis=1, keepdims=True) + NORM_EPS)


def feed_kernel(
    inner, place, own, far, part, came, gain, gu, gu_first, gu_second, gu_pair,
    tall, first, second, pair,
    h2_out, n2_out, act_out, ggu_out, n2p_out, down_out, far_out,
):
    tokens = part.shape[0]
    half = own.shape[1]
    piece = half // 4
    spot = place[1]
    for j in range(4):
        at = pl.multiple_of((spot ^ j) * piece, piece)
        far_out[:, j * piece : (j + 1) * piece] = far[:, pl.ds(at, piece)]
    h2_out[:, :half] = own[0:tokens].astype(F32) + (part[:, :half] + came[:, :half])
    h2_out[:, half:] = far_out[0:tokens].astype(F32) + (part[:, half:] + came[:, half:])
    h2 = h2_out[...]
    n2 = (h2 * norm_factor(h2) * gain[...]).astype(BF16)
    n2_out[...] = n2[:, :half]
    gu_far = jnp.concatenate(
        [gu_first[...], gu_pair[0:piece], gu_second[...], gu_pair[piece:]], axis=0
    )
    ff = tall.shape[0] - inner
    gate_up = dot(n2[:, :half], gu[...]) + dot(n2[:, half:], gu_far)
    grad_act = dot_bt(own[tokens:], tall[inner:]) + dot_bt(
        far_out[tokens:], tall_far(first, second, pair, inner, ff)
    )
    gate = gate_up[:, :ff]
    up = gate_up[:, ff:]
    silu, silu_grad = silu_turn(gate)
    act = (silu * up).astype(BF16)
    act_out[...] = act
    ggu_out[:, :ff] = (grad_act * up * silu_grad).astype(BF16)
    ggu_out[:, ff:] = (grad_act * silu).astype(BF16)
    ggu = ggu_out[...]
    n2p_out[:, :half] = dot_bt(ggu, gu[...])
    n2p_out[:, half:] = dot_bt(ggu, gu_far)
    down_out[...] = dot(act, tall[inner:])


def permuted(left, source):
    width = left.shape[1]
    hot = jnp.where(iota((width, source.shape[1]), 0) == source, 1.0, 0.0).astype(BF16)
    return dot(left, hot).astype(BF16)


def feed_grad_kernel(n2, act, ggu, own, order, order2, send_out, keep_out):
    tokens = n2.shape[0]
    half = n2.shape[1] // 2
    wide = ggu.shape[1]
    left = permuted(n2[...], order[...])
    keep_out[:, :wide] = dot_at(left[:, :half], ggu[...])
    send_out[:, :wide] = dot_at(left[:, half:], ggu[...]).astype(BF16)
    left = permuted(act[...], order2[...])
    right = own[tokens:]
    width = right.shape[1]
    for s in (0, 1):
        at = wide + s * width
        cut = 2 * s * half
        keep_out[:, at : at + width] = dot_at(left[:, cut : cut + half], right)
        send_out[:, at : at + width] = dot_at(left[:, cut + half : cut + 2 * half], right).astype(BF16)


def turn_kernel(
    full_width, own, far, h2, part, came, gain, mixed, tall, first, second, pair, order,
    dym_out, resid_out, gain_out, send_out, keep_out,
):
    tokens = h2.shape[0]
    half = own.shape[1]
    inner = mixed.shape[1]
    value = h2[...]
    factor = norm_factor(value)
    dn2 = part[...] + came[...]
    gained = dn2 * gain[...]
    inner_sum = jnp.sum(gained * value, axis=1, keepdims=True)
    gain_out[...] = jnp.broadcast_to(
        jnp.sum(dn2[:, :half] * value[:, :half] * factor, axis=0, keepdims=True), gain_out.shape
    )
    slope = factor * factor * factor * inner_sum / full_width
    change = factor * gained - value * slope
    dh_own = own[tokens:].astype(F32) + change[:, :half]
    dh_far = far[tokens:].astype(F32) + change[:, half:]
    resid_out[...] = dh_own
    low_own = dh_own.astype(BF16)
    dym_out[...] = dot_bt(low_own, tall[0:inner]) + dot_bt(
        dh_far.astype(BF16), tall_far(first, second, pair, 0, inner)
    )
    left = permuted(mixed[...], order[...])
    rows = half // 2
    for s in (0, 1):
        at = s * half
        cut = 2 * s * rows
        keep_out[:, at : at + half] = dot_at(left[:, cut : cut + rows], low_own)
        send_out[:, at : at + half] = dot_at(
            left[:, cut + rows : cut + 2 * rows], low_own
        ).astype(BF16)


def grad_two_kernel(n1, g_two, gx, gdt, wx, wd, wg, wq, wk, order, send_out, keep_out, n1p_out):
    rows = n1.shape[1] // 2
    left = permuted(n1[...], order[...])
    send_out[...] = dot_at(left[:, rows:], g_two[...]).astype(BF16)
    keep_out[...] = dot_at(left[:, :rows], g_two[...])
    ch = wg.shape[1]
    nq = wq.shape[1]
    total = dot_bt(gx[...], wx[...]) + dot_bt(gdt[...], wd[...])
    total = total + dot_bt(g_two[:, :ch], wg[...]) + dot_bt(g_two[:, ch : ch + nq], wq[...])
    n1p_out[...] = total + dot_bt(g_two[:, ch + nq :], wk[...])


def grad_one_kernel(n1, gx, gdt, gbc, gbc_came, wb, order, send_out, keep_out, n1b_out):
    tokens = n1.shape[0]
    rows = n1.shape[1] // 2
    ch = gx.shape[1]
    nbc = gbc.shape[1]
    left = permuted(n1[...], order[...])
    both = (gbc[0:tokens] + gbc_came[0:tokens]).astype(BF16)
    at = 0
    for right in (gx[...], both, gdt[...]):
        size = right.shape[1]
        send_out[:, at : at + size] = dot_at(left[:, rows:], right).astype(BF16)
        keep_out[:, at : at + size] = dot_at(left[:, :rows], right)
        at += size
    n1b_out[...] = dot_bt(both, wb[...])


def close_kernel(own, part, came, n1b, gain, gbc, gbc_came, dn1_out, gain_out, rows_out):
    tokens = part.shape[0]
    hid = own[0:tokens].astype(F32)
    dn1 = (part[...] + came[...]) + n1b[...]
    dn1_out[...] = dn1
    rows_out[0:8, :] = token_sums(dn1 * gain[...] * hid)
    rows_out[8:16, :] = gbc[tokens:] + gbc_came[tokens:]


def end_kernel(
    full_width, place, own, sums, sums_far, resid, dn1, gain, rows, rows_far, small, gain2,
    hidden_out, vector_out,
):
    tokens = dn1.shape[0]
    half = dn1.shape[1]
    quarter = hidden_out.shape[1]
    hid = own[0:tokens].astype(F32)
    mean = column(sums[...] + sums_far[...])[:, :1] / full_width
    factor = lax.rsqrt(mean + NORM_EPS)
    inner_sum = column(rows[0:8] + rows_far[0:8])[:, :1]
    value = dn1[...]
    change = resid[...] + factor * (value * gain[...]) - hid * (
        factor * factor * factor * inner_sum / full_width
    )
    first = place[0] == 0
    hidden_out[...] = jnp.where(first, change[:, :quarter], change[:, quarter:])
    count = small.shape[0]
    vector_out[...] = jnp.zeros_like(vector_out)
    vector_out[0:count] = small[...]
    vector_out[count : count + 8, 0 : rows.shape[1]] = jnp.where(
        place[2] == 0, rows[8:16], rows_far[8:16]
    )
    vector_out[count + 8 : count + 9, 0:half] = jnp.sum(value * hid * factor, axis=0, keepdims=True)
    vector_out[count + 9 : count + 10, 0:half] = gain2[0:1]


def halving_order(count):
    order = [0]
    step = count // 2
    while step >= 1:
        order = order + [o | step for o in order]
        step //= 2
    return order


def dp_rest(keep, came, step=2):
    total = keep + came.astype(F32)
    while step < lax.axis_size("dp"):
        half = total.shape[0] // 2
        came = swap(total[half:].astype(BF16), "dp", step)
        total = total[:half] + came.astype(F32)
        step *= 2
    return total


def shards(
    hidden,
    segment_ids,
    norm1_gain,
    w_gate,
    w_xin,
    w_dt,
    w_bc,
    w_query,
    w_kv,
    convx_weight,
    convx_bias,
    convbc_weight,
    convbc_bias,
    dt_bias,
    a_log,
    d_skip,
    w_mixout,
    w_attnout,
    norm2_gain,
    w_gateup,
    w_down,
    cotangent,
):
    row = lax.axis_index("row")
    col = lax.axis_index("col")
    me = lax.axis_index("dp")
    count = lax.axis_size("dp")
    spot = me & 3
    place = jnp.stack([col, spot, row]).astype(jnp.int32)
    tokens, quarter = hidden.shape
    half = 2 * quarter
    full_width = 4 * quarter
    piece = half // 4
    ch = w_xin.shape[1]
    nq = w_query.shape[1]
    nkv = w_kv.shape[2]
    nbc = w_bc.shape[1]
    heads = w_dt.shape[1]
    ff = w_down.shape[0]
    cq = convx_bias.shape[0]
    hq = dt_bias.shape[0]

    both = jnp.concatenate([hidden, cotangent], 0)
    own, sums = call(
        open_kernel,
        [((2 * tokens, half), BF16), ((8, tokens), F32)],
        place,
        both,
        swap(both, "col"),
        smem=(0,),
    )
    sums_far = swap(sums, "row")

    small = jnp.concatenate(
        [convx_weight.T.reshape(-1), convx_bias, dt_bias, a_log, d_skip, norm2_gain]
    )
    small_far = swap(small, "row")
    far = swap(own, "row")

    tall = jnp.concatenate([w_mixout, w_attnout, w_down], 0)
    gu = w_gateup.reshape(half, 2 * ff)
    tall_mine = lax.dynamic_slice_in_dim(tall, spot * piece, piece, 1)
    gu_mine = lax.dynamic_slice_in_dim(gu, spot * piece, piece, 0)
    t_first = swap(tall_mine, "row")
    g_first = swap(gu_mine, "row")
    t_second = swap(t_first, "dp", 1)
    g_second = swap(g_first, "dp", 2)
    t_pair = swap(jnp.concatenate([t_first, t_second], 1), "dp", 2)
    g_pair = swap(jnp.concatenate([g_first, g_second], 0), "dp", 1)

    def joined(start, size):
        a = small[start : start + size]
        b = small_far[start : start + size]
        first = row == 0
        return jnp.concatenate([jnp.where(first, a, b), jnp.where(first, b, a)], 0).astype(F32)

    at = TAPS * cq
    x_par = jnp.stack(
        [joined(k * cq, cq) for k in range(TAPS + 1)]
        + [jnp.repeat(joined(at + cq + 2 * hq, hq), HEAD)]
        + [jnp.zeros((ch,), F32)] * 2
    )
    bc_par = jnp.concatenate(
        [convbc_weight.T, convbc_bias[None], jnp.zeros((3, nbc), BF16)], 0
    ).astype(F32)
    head_par = jnp.stack(
        [jnp.pad(joined(at + cq + k * hq, hq), (0, LANES - heads)) for k in (0, 1)]
        + [jnp.zeros((LANES,), F32)] * 6
    )
    gain2_far = jnp.concatenate(
        [
            lax.dynamic_slice_in_dim(small_far, at + cq + 3 * hq + (spot ^ j) * piece, piece, 0)
            for j in range(4)
        ]
    )
    gain_one = norm1_gain.astype(F32)[None]
    gain_two = jnp.concatenate([norm2_gain, gain2_far]).astype(F32)[None]
    seg_row = segment_ids.astype(F32)
    seg_col = jnp.broadcast_to(segment_ids[0].astype(F32)[:, None], (tokens, LANES))
    wk = w_kv.reshape(half, nkv)
    wd = jnp.pad(w_dt, ((0, 0), (0, LANES - heads)))

    blocks = np.array(halving_order(count))
    order_block = jnp.asarray(np.repeat(blocks, half // count), jnp.int32) ^ me
    within = jnp.asarray(np.tile(np.arange(half // count), count), jnp.int32)
    size = half // count
    order = (order_block * size + within)[None]
    both_within = jnp.concatenate([within, within + size])
    both_block = jnp.concatenate([order_block, order_block])
    order_down = (both_block * (ff // count) + both_within)[None]
    m_rows = ch // count
    a_rows = nq // count
    order_mix = jnp.where(
        both_within < m_rows,
        both_block * m_rows + both_within,
        ch + both_block * a_rows + both_within - m_rows,
    )[None]

    cols = ch + nbc + LANES + ch + nq + nkv
    n1, part, part_low = call(
        lambda *refs: project_kernel(full_width, *refs),
        [((tokens, half), BF16), ((tokens, cols), F32), ((tokens, cols), BF16)],
        own, sums, sums_far, gain_one, w_xin, w_bc, wd, w_gate, w_query, wk,
    )
    mixed, raw, pre, ys = call(
        lambda *refs: mix_kernel(ch, nq, *refs),
        [
            ((tokens, ch + nq), BF16),
            ((tokens, cols), F32),
            ((tokens, ch + nbc), F32),
            ((tokens, ch), F32),
        ],
        seg_row, seg_col, part, swap(part_low, "row"), x_par, bc_par, head_par,
    )
    mix_part = call(
        out_kernel, [((tokens, full_width), F32)], mixed, tall, t_first, t_second, t_pair
    )[0]
    h2, n2, act, ggu, n2_part, down, far_order = call(
        lambda *refs: feed_kernel(ch + nq, *refs),
        [
            ((tokens, full_width), F32),
            ((tokens, half), BF16),
            ((tokens, ff), BF16),
            ((tokens, 2 * ff), BF16),
            ((tokens, full_width), F32),
            ((tokens, half), F32),
            ((2 * tokens, half), BF16),
        ],
        place, own, far, mix_part, swap(mix_part, "col"), gain_two,
        gu, g_first, g_second, g_pair, tall, t_first, t_second, t_pair,
        smem=(0,),
    )
    n2_came = swap(n2_part, "col")
    send_feed, keep_feed = call(
        feed_grad_kernel,
        [((half // 2, 2 * ff + 2 * half), BF16), ((half // 2, 2 * ff + 2 * half), F32)],
        n2, act, ggu, own, order, order_down,
    )
    came_feed = swap(send_feed, "dp", 1)
    down_came = swap(lax.dynamic_slice_in_dim(down, (1 - col) * quarter, quarter, 1), "col")

    dym, resid, gain2_sum, send_mix, keep_mix = call(
        lambda *refs: turn_kernel(full_width, *refs),
        [
            ((tokens, ch + nq), F32),
            ((tokens, half), F32),
            ((8, half), F32),
            ((half // 2, 2 * half), BF16),
            ((half // 2, 2 * half), F32),
        ],
        own, far_order, h2, n2_part, n2_came, gain_two, mixed, tall, t_first, t_second, t_pair,
        order_mix,
    )
    came_mix = swap(send_mix, "dp", 1)
    gx, g_two, gdt, gbc, small_sum = call(
        lambda *refs: unmix_kernel(ch, nq, *refs),
        [
            ((tokens, ch), BF16),
            ((tokens, ch + nq + nkv), BF16),
            ((tokens, LANES), BF16),
            ((tokens + 8, nbc), F32),
            ((16, ch), F32),
        ],
        seg_row, seg_col, raw, pre, ys, dym, x_par, bc_par, head_par,
        scratch=[((tokens, ch), F32), ((tokens, ch), F32), ((tokens, tokens), F32)],
    )
    gbc_came = swap(gbc, "col")
    send_two, keep_two, n1_part = call(
        grad_two_kernel,
        [
            ((half // 2, ch + nq + nkv), BF16),
            ((half // 2, ch + nq + nkv), F32),
            ((tokens, half), F32),
        ],
        n1, g_two, gx, gdt, w_xin, wd, w_gate, w_query, wk, order,
    )
    came_two = swap(send_two, "dp", 1)
    n1_came = swap(n1_part, "col")
    send_one, keep_one, n1_bc = call(
        grad_one_kernel,
        [
            ((half // 2, ch + nbc + LANES), BF16),
            ((half // 2, ch + nbc + LANES), F32),
            ((tokens, half), F32),
        ],
        n1, gx, gdt, gbc, gbc_came, w_bc, order,
    )
    came_one = swap(send_one, "dp", 1)
    dn1, _, rows = call(
        close_kernel,
        [((tokens, half), F32), ((8, half), F32), ((16, tokens), F32)],
        own, n1_part, n1_came, n1_bc, gain_one, gbc, gbc_came,
    )
    grad_hidden, vector = call(
        lambda *refs: end_kernel(full_width, *refs),
        [((tokens, quarter), F32), ((32, ch), F32)],
        place, own, sums, sums_far, resid, dn1, gain_one, rows, swap(rows, "row"), small_sum, gain2_sum,
        smem=(0,),
    )
    step = 1
    while step < count:
        vector = vector + swap(vector, "dp", step)
        step *= 2

    start = col * quarter
    output = (
        lax.dynamic_slice_in_dim(h2, start, quarter, 1)
        + (lax.dynamic_slice_in_dim(down, start, quarter, 1) + down_came)
    ).astype(BF16)

    r_feed = dp_rest(keep_feed, came_feed)
    r_mix = dp_rest(keep_mix, came_mix)
    r_two = dp_rest(keep_two, came_two)
    r_one = dp_rest(keep_one, came_one)
    r_down = jnp.concatenate([r_feed[:, 2 * ff : 2 * ff + half], r_feed[:, 2 * ff + half :]], 0)
    r_tall = jnp.concatenate([r_mix[:, :half], r_mix[:, half:]], 0)

    def mine(values, width):
        return lax.dynamic_slice_in_dim(values, row * width, width, values.ndim - 1)

    return (
        output,
        grad_hidden,
        vector[24, :half],
        r_two[:, :ch],
        r_one[:, :ch],
        r_one[:, ch + nbc : ch + nbc + heads],
        r_one[:, ch : ch + nbc],
        r_two[:, ch : ch + nq],
        r_two[:, ch + nq :].reshape(size, 1, nkv),
        mine(vector[0:TAPS], cq).T,
        mine(vector[TAPS], cq),
        vector[16 : 16 + TAPS, :nbc].T,
        vector[16 + TAPS, :nbc],
        mine(vector[12, :heads], hq),
        mine(vector[12, LANES : LANES + heads], hq),
        mine(vector[12, 2 * LANES : 2 * LANES + heads], hq),
        r_tall[:m_rows],
        r_tall[m_rows:],
        vector[25, :half],
        r_feed[:, : 2 * ff].reshape(size, 2, ff),
        r_down,
    )


def solution(mesh):
    placed = (
        P("dp", ("row", "col")),
        P("dp", None),
        P("row"),
        P("row", "col"),
        P("row", "col"),
        P("row", "col"),
        P("row", None),
        P("row", "col"),
        P("row", "col", None),
        P(("col", "row"), None),
        P(("col", "row")),
        P(),
        P(),
        P(("col", "row")),
        P(("col", "row")),
        P(("col", "row")),
        P("col", "row"),
        P("col", "row"),
        P("row"),
        P("row", None, "col"),
        P("col", "row"),
        P("dp", ("row", "col")),
    )
    return jax.shard_map(
        shards,
        mesh=mesh,
        in_specs=placed,
        out_specs=(
            P("dp", ("row", "col")),
            P("dp", ("row", "col")),
            P("row"),
            P(("row", "dp"), "col"),
            P(("row", "dp"), "col"),
            P(("row", "dp"), "col"),
            P(("row", "dp"), None),
            P(("row", "dp"), "col"),
            P(("row", "dp"), "col", None),
            P(("col", "row"), None),
            P(("col", "row")),
            P(),
            P(),
            P(("col", "row")),
            P(("col", "row")),
            P(("col", "row")),
            P(("col", "dp"), "row"),
            P(("col", "dp"), "row"),
            P("row"),
            P(("row", "dp"), None, "col"),
            P(("col", "dp"), "row"),
        ),
        check_vma=False,
    )
```

profile of v0, /device:TPU:0, one launch (start us, length us, event | category | flops | bytes accessed | tf_op | source)
XLA Modules:
  0.0 254.3 jit_solution(6901067768566227499)
XLA Ops:
  3.2 3.0 %collective-permute-start.5 = (bf16[2048,128]{1,0:T(8,128)(2,1)S(1)}, bf16[2048,128]{1,0:T(8,128)(2,1)S(1)}, u32[]{:S(2)}, u32[]{:S(2)}) collective-permute-start(bf16[2048,128]{1,0:T(8,128)(2,1)S(1)} %constant_dynamic-slice_fusion.6), channel_id=1, source_target_pairs={{0,2},{2,0},{1,3},{3,1},{4,6},{6,4},{5,7},{7,5},{8,10},{10,8},{9,1... | collective-permute-start | bytes 1572872 | tf_op jit(solution)/shard_map/ppermute | solution.py:20
  8.4 2.2 copy.48
  12.8 1.7 collective-permute-start.9
  14.6 4.4 %collective-permute-done.5.first.refs_11_.refs_8_ = bf16[2048,128]{1,0:T(8,128)(2,1)S(1)} collective-permute-done((bf16[2048,128]{1,0:T(8,128)(2,1)S(1)}, bf16[2048,128]{1,0:T(8,128)(2,1)S(1)}, u32[]{:S(2)}, u32[]{:S(2)}) %collective-permute-start.5) | collective-permute-done | bytes 524320 | tf_op jit(solution)/shard_map/ppermute | solution.py:20
  19.0 2.0 collective-permute-start.6
  23.9 2.1 shard_map.391
  27.5 2.3 collective-permute-done.2.refs_2_.refs_3_
  30.5 5.0 %shard_map.392 = (bf16[256,512]{1,0:T(8,128)(2,1)}, f32[256,2304]{1,0:T(8,128)}, bf16[256,2304]{1,0:T(8,128)(2,1)}) custom-call(bf16[512,512]{1,0:T(8,128)(2,1)} %get-tuple-element.59.refs_0_.refs_1_.own, f32[8,256]{1,0:T(8,128)} %get-tuple-element.60.refs_1_.refs_2_, f32[8,256]{1,0:T(8,128)} %copy-done.21, f32[1,512]{1,0:T(1,128)} %bitcast.55, ...), custom_call_target="tpu_custom_call" | custom-call | tf_op jit(solution)/shard_map/pallas_call | solution.py:46
  42.2 31.2 %collective-permute-done.10.refs_8_ = bf16[128,2048]{1,0:T(8,128)(2,1)S(1)} collective-permute-done((bf16[128,2048]{1,0:T(8,128)(2,1)S(1)}, bf16[128,2048]{1,0:T(8,128)(2,1)S(1)}, u32[]{:S(2)}, u32[]{:S(2)}) %collective-permute-start.10) | collective-permute-done | bytes 524320 | tf_op jit(solution)/shard_map/ppermute | solution.py:20
  76.8 6.9 %shard_map.393 = (bf16[256,1024]{1,0:T(8,128)(2,1)}, f32[256,2304]{1,0:T(8,128)}, f32[256,1024]{1,0:T(8,128)}, f32[256,768]{1,0:T(8,128)}) custom-call(f32[1,256]{1,0:T(1,128)} %copy-done.24, f32[256,128]{1,0:T(8,128)} %broadcast_in_dim.26.refs_1_, f32[256,2304]{1,0:T(8,128)} %get-tuple-element.61.refs_2_, bf16[256,2304]{1,0:T(8,128)(2,1)} %collective-permute-done.3.refs_3_, ...), custom_call_target="tpu_custom_call" | custom-call | tf_op jit(solution)/shard_map/pallas_call | solution.py:46
  84.7 4.1 %shard_map.394.refs_3_ = f32[256,1024]{1,0:T(8,128)} custom-call(bf16[256,1024]{1,0:T(8,128)(2,1)} %get-tuple-element.63.mixed.refs_6_, bf16[2048,512]{1,0:T(8,128)(2,1)} %copy-done, bf16[2048,128]{1,0:T(8,128)(2,1)} %copy-done.4, bf16[2048,128]{1,0:T(8,128)(2,1)} %copy-done.5, bf16[2048,256]{1,0:T(8,128)(2,1)} %copy-done.3), custom_call_target="tpu_custom_call" | custom-call | tf_op jit(solution)/shard_map/pallas_call | solution.py:46
  90.8 12.9 %collective-permute-done.1.refs_2_ = bf16[512,512]{1,0:T(8,128)(2,1)S(1)} collective-permute-done((bf16[512,512]{1,0:T(8,128)(2,1)S(1)}, bf16[512,512]{1,0:T(8,128)(2,1)S(1)}, u32[]{:S(2)}, u32[]{:S(2)}) %collective-permute-start.1) | collective-permute-done | bytes 524320 | tf_op jit(solution)/shard_map/ppermute | solution.py:20
  105.6 9.0 %shard_map.395 = (f32[256,1024]{1,0:T(8,128)}, bf16[256,512]{1,0:T(8,128)(2,1)}, bf16[256,1024]{1,0:T(8,128)(2,1)}, bf16[256,2048]{1,0:T(8,128)(2,1)}, f32[256,1...) custom-call(s32[3]{0:T(128)} %pad_add_fusion.1.place.refs_0_, ...), custom_call_target="tpu_custom_call" | custom-call | tf_op jit(solution)/shard_map/pallas_call | solution.py:46
  115.2 5.8 %shard_map.402 = (bf16[256,3072]{1,0:T(8,128)(2,1)}, f32[256,3072]{1,0:T(8,128)}) custom-call(bf16[256,512]{1,0:T(8,128)(2,1)} %get-tuple-element.92.n2, bf16[256,1024]{1,0:T(8,128)(2,1)} %get-tuple-element.93.act, bf16[256,2048]{1,0:T(8,128)(2,1)} %get-tuple-element.94.ggu, bf16[512,512]{1,0:T(8,128)(2,1)} %get-tuple-element.59.refs_0_.refs_1_.own, ...), custom_call_target="tpu_custom_call" | custom-call | tf_op jit(solution)/shard_map/pallas_call | solution.py:46
  122.5 6.7 %shard_map.396 = (f32[256,1024]{1,0:T(8,128)}, f32[256,512]{1,0:T(8,128)}, f32[8,512]{1,0:T(8,128)}, bf16[256,1024]{1,0:T(8,128)(2,1)}, f32[256,1024]{1,0:T(8,128)}) custom-call(bf16[512,512]{1,0:T(8,128)(2,1)} %get-tuple-element.59.refs_0_.refs_1_.own, bf16[512,512]{1,0:T(8,128)(2,1)} %get-tuple-element.66.refs_1_, f32[256,1024]{1,0:T(8,128)} %get-tuple-element.64.refs_2_, ...), custom_call_target="tpu_custom_call" | custom-call | tf_op jit(solution)/shard_map/pallas_call | solution.py:46
  129.2 11.0 %shard_map.397 = (bf16[256,768]{1,0:T(8,128)(2,1)}, bf16[256,1152]{1,0:T(8,128)(2,1)}, bf16[256,128]{1,0:T(8,128)(2,1)}, f32[264,256]{1,0:T(8,128)}, f32[16,768]{1,0:T(8,128)}) custom-call(f32[1,256]{1,0:T(1,128)} %copy-done.24, f32[256,128]{1,0:T(8,128)} %broadcast_in_dim.26.refs_1_, f32[256,2304]{1,0:T(8,128)} %get-tuple-element.70.refs_2_, ...), custom_call_target="tpu_custom_call" | custom-call | tf_op jit(solution)/shard_map/pallas_call | solution.py:46
  140.2 4.2 %shard_map.398 = (bf16[256,1152]{1,0:T(8,128)(2,1)}, f32[256,1152]{1,0:T(8,128)}, f32[256,512]{1,0:T(8,128)}) custom-call(bf16[256,512]{1,0:T(8,128)(2,1)} %get-tuple-element.69.n1, bf16[256,1152]{1,0:T(8,128)(2,1)} %get-tuple-element.74.g_two, bf16[256,768]{1,0:T(8,128)(2,1)} %get-tuple-element.75.gx, bf16[256,128]{1,0:T(8,128)(2,1)} %get-tuple-element.76.gdt, ...), custom_call_target="tpu_custom_call" | custom-call | tf_op jit(solution)/shard_map/pallas_call | solution.py:46
  145.2 1.8 collective-permute-done.12
  147.0 1.7 add_convert_fusion
  150.7 3.8 %shard_map.399 = (bf16[256,1152]{1,0:T(8,128)(2,1)}, f32[256,1152]{1,0:T(8,128)}, f32[256,512]{1,0:T(8,128)}) custom-call(bf16[256,512]{1,0:T(8,128)(2,1)} %get-tuple-element.69.n1, bf16[256,768]{1,0:T(8,128)(2,1)} %get-tuple-element.75.gx, bf16[256,128]{1,0:T(8,128)(2,1)} %get-tuple-element.76.gdt, f32[264,256]{1,0:T(8,128)} %get-tuple-element.78.gbc, ...), custom_call_target="tpu_custom_call" | custom-call | tf_op jit(solution)/shard_map/pallas_call | solution.py:46
  156.0 2.9 %shard_map.400 = (f32[256,512]{1,0:T(8,128)}, f32[8,512]{1,0:T(8,128)}, f32[16,256]{1,0:T(8,128)}) custom-call(bf16[512,512]{1,0:T(8,128)(2,1)} %get-tuple-element.59.refs_0_.refs_1_.own, f32[256,512]{1,0:T(8,128)} %get-tuple-element.77.part, f32[256,512]{1,0:T(8,128)} %collective-permute-done.14.came, f32[256,512]{1,0:T(8,128)} %get-tuple-element.79.n1b, ...), custom_call_target="tpu_custom_call" | custom-call | tf_op jit(solution)/shard_map/pallas_call | solution.py:46
  163.4 2.8 %shard_map.401 = (f32[256,256]{1,0:T(8,128)}, f32[32,768]{1,0:T(8,128)}) custom-call(s32[3]{0:T(128)} %pad_add_fusion.1.place.refs_0_, bf16[512,512]{1,0:T(8,128)(2,1)} %get-tuple-element.59.refs_0_.refs_1_.own, f32[8,256]{1,0:T(8,128)} %get-tuple-element.60.refs_1_.refs_2_, f32[8,256]{1,0:T(8,128)} %copy-done.21, f32[256,512]{1,0:T(8,128)} %get-tuple-element.68.refs_4_, ...), custom_call_target="tpu_custom_call" | custom-call | tf_op jit(solution)/shard_map/pallas_call | solution.py:46
  166.8 2.9 %collective-permute-done.26 = bf16[256,1024]{1,0:T(8,128)(2,1)} collective-permute-done((bf16[256,1024]{1,0:T(8,128)(2,1)}, bf16[256,1024]{1,0:T(8,128)(2,1)}, u32[]{:S(2)}, u32[]{:S(2)}) %collective-permute-start.26) | collective-permute-done | bytes 524320 | tf_op jit(solution)/shard_map/ppermute | solution.py:20
  172.6 24.0 %collective-permute-done.17 = f32[32,768]{1,0:T(8,128)S(1)} collective-permute-done((f32[32,768]{1,0:T(8,128)}, f32[32,768]{1,0:T(8,128)S(1)}, u32[]{:S(2)}, u32[]{:S(2)}) %collective-permute-start.17) | collective-permute-done | bytes 98336 | tf_op jit(solution)/shard_map/ppermute | solution.py:20
  201.3 2.7 %collective-permute-start.19 = (f32[32,768]{1,0:T(8,128)S(1)}, f32[32,768]{1,0:T(8,128)S(1)}, u32[]{:S(2)}, u32[]{:S(2)}) collective-permute-start(f32[32,768]{1,0:T(8,128)S(1)} %add.189), channel_id=1, source_target_pairs={{0,16},{4,20},{8,24},{12,28},{16,0},{20,4},{24,8},{28,12},{1,17},{... | collective-permute-start | bytes 294920 | tf_op jit(solution)/shard_map/ppermute | solution.py:20
  204.5 5.3 %collective-permute-done.19 = f32[32,768]{1,0:T(8,128)S(1)} collective-permute-done((f32[32,768]{1,0:T(8,128)S(1)}, f32[32,768]{1,0:T(8,128)S(1)}, u32[]{:S(2)}, u32[]{:S(2)}) %collective-permute-start.19) | collective-permute-done | bytes 98336 | tf_op jit(solution)/shard_map/ppermute | solution.py:20
  215.7 4.3 %collective-permute-start.24 = (bf16[128,1152]{1,0:T(8,128)(2,1)S(1)}, bf16[128,1152]{1,0:T(8,128)(2,1)S(1)}, u32[]{:S(2)}, u32[]{:S(2)}) collective-permute-start(bf16[128,1152]{1,0:T(8,128)(2,1)S(1)} %slice.313), channel_id=1, source_target_pairs={{0,8},{4,12},{8,0},{12,4},{16,24},{20,28},{24,16},{28,20},{1,9},{5... | collective-permute-start | bytes 884744 | tf_op jit(solution)/shard_map/ppermute | solution.py:20
  220.1 2.8 %collective-permute-start.22 = (bf16[64,1152]{1,0:T(8,128)(2,1)S(1)}, bf16[64,1152]{1,0:T(8,128)(2,1)S(1)}, u32[]{:S(2)}, u32[]{:S(2)}) collective-permute-start(bf16[64,1152]{1,0:T(8,128)(2,1)S(1)} %slice.317), channel_id=1, source_target_pairs={{0,16},{4,20},{8,24},{12,28},{16,0},{20,4},{24,8},{28,12},{1,17},{... | collective-permute-start | bytes 442376 | tf_op jit(solution)/shard_map/ppermute | solution.py:20
  224.3 2.1 collective-permute-done.22
  228.5 3.5 %collective-permute-start.25 = (bf16[64,1152]{1,0:T(8,128)(2,1)S(1)}, bf16[64,1152]{1,0:T(8,128)(2,1)S(1)}, u32[]{:S(2)}, u32[]{:S(2)}) collective-permute-start(bf16[64,1152]{1,0:T(8,128)(2,1)S(1)} %slice.316), channel_id=1, source_target_pairs={{0,16},{4,20},{8,24},{12,28},{16,0},{20,4},{24,8},{28,12},{1,17},{... | collective-permute-start | bytes 442376 | tf_op jit(solution)/shard_map/ppermute | solution.py:20
  232.3 12.7 %collective-permute-done.25 = bf16[64,1152]{1,0:T(8,128)(2,1)S(1)} collective-permute-done((bf16[64,1152]{1,0:T(8,128)(2,1)S(1)}, bf16[64,1152]{1,0:T(8,128)(2,1)S(1)}, u32[]{:S(2)}, u32[]{:S(2)}) %collective-permute-start.25) | collective-permute-done | bytes 147488 | tf_op jit(solution)/shard_map/ppermute | solution.py:20
  247.1 5.1 %collective-permute-done.31 = bf16[64,3072]{1,0:T(8,128)(2,1)S(1)} collective-permute-done((bf16[64,3072]{1,0:T(8,128)(2,1)S(1)}, bf16[64,3072]{1,0:T(8,128)(2,1)S(1)}, u32[]{:S(2)}, u32[]{:S(2)}) %collective-permute-start.31) | collective-permute-done | bytes 393248 | tf_op jit(solution)/shard_map/ppermute | solution.py:20
  (237 shorter events, 60.0 us)
Async XLA Ops:
  3.2 15.8 %collective-permute-start.5 = (bf16[2048,128]{1,0:T(8,128)(2,1)S(1)}, bf16[2048,128]{1,0:T(8,128)(2,1)S(1)}, u32[]{:S(2)}, u32[]{:S(2)}) collective-permute-start(bf16[2048,128]{1,0:T(8,128)(2,1)S(1)} %constant_dynamic-slice_fusion.6), channel_id=1, source_target_pairs={{0,2},{2,0},{1,3},{3,1},{4,6},{6,4},{5,7},{7,5},{8,10},{10,8},{9,1... | collective-permute-start | bytes 1572872 | tf_op jit(solution)/shard_map/ppermute | solution.py:20
  7.0 20.5 %collective-permute-start.4 = (bf16[2450]{0:T(1024)(128)(2,1)}, bf16[2450]{0:T(1024)(128)(2,1)S(1)}, u32[]{:S(2)}, u32[]{:S(2)}) collective-permute-start(bf16[2450]{0:T(1024)(128)(2,1)} %concatenate.182), channel_id=1, source_target_pairs={{0,2},{2,0},{1,3},{3,1},{4,6},{6,4},{5,7},{7,5},{8,10},{10,8},{9,1... | collective-permute-start | bytes 14708 | tf_op jit(solution)/shard_map/ppermute | solution.py:20
  8.3 15.7 %collective-permute-start = (bf16[512,256]{1,0:T(8,128)(2,1)S(1)}, bf16[512,256]{1,0:T(8,128)(2,1)}, u32[]{:S(2)}, u32[]{:S(2)}) collective-permute-start(bf16[512,256]{1,0:T(8,128)(2,1)S(1)} %constant_dynamic-update-slice_fusion.mine), channel_id=1, source_target_pairs={{0,1},{1,0},{2,3},{3,2},{4,5},{5,4},{6,7},{7,6},{8,9},{9,8},{10,11... | collective-permute-start | bytes 786440 | tf_op jit(solution)/shard_map/ppermute | solution.py:20
  12.8 27.5 %collective-permute-start.9 = (bf16[128,2048]{1,0:T(8,128)(2,1)}, bf16[128,2048]{1,0:T(8,128)(2,1)S(1)}, u32[]{:S(2)}, u32[]{:S(2)}) collective-permute-start(bf16[128,2048]{1,0:T(8,128)(2,1)} %constant_dynamic-slice_fusion.5), channel_id=1, source_target_pairs={{0,2},{2,0},{1,3},{3,1},{4,6},{6,4},{5,7},{7,5},{8,10},{10,8},{9,1... | collective-permute-start | bytes 1572872 | tf_op jit(solution)/shard_map/ppermute | solution.py:20
  19.0 18.0 %collective-permute-start.6 = (bf16[2048,128]{1,0:T(8,128)(2,1)S(1)}, bf16[2048,128]{1,0:T(8,128)(2,1)S(1)}, u32[]{:S(2)}, u32[]{:S(2)}) collective-permute-start(bf16[2048,128]{1,0:T(8,128)(2,1)S(1)} %collective-permute-done.5.first.refs_11_.refs_8_), channel_id=1, source_target_pairs={{0,4},{4,0},{8,12},{12,8},{16,20},{20,16},{24,28},{28,24},{1,5},{5... | collective-permute-start | bytes 1572872 | tf_op jit(solution)/shard_map/ppermute | solution.py:20
  26.0 3.9 %collective-permute-start.2 = (f32[8,256]{1,0:T(8,128)}, f32[8,256]{1,0:T(8,128)S(1)}, u32[]{:S(2)}, u32[]{:S(2)}) collective-permute-start(f32[8,256]{1,0:T(8,128)} %get-tuple-element.60.refs_1_.refs_2_), channel_id=1, source_target_pairs={{0,2},{2,0},{1,3},{3,1},{4,6},{6,4},{5,7},{7,5},{8,10},{10,8},{9,1... | collective-permute-start | bytes 24584 | tf_op jit(solution)/shard_map/ppermute | solution.py:20
  35.4 40.7 %collective-permute-start.3 = (bf16[256,2304]{1,0:T(8,128)(2,1)}, bf16[256,2304]{1,0:T(8,128)(2,1)}, u32[]{:S(2)}, u32[]{:S(2)}) collective-permute-start(bf16[256,2304]{1,0:T(8,128)(2,1)} %get-tuple-element.62), channel_id=1, source_target_pairs={{0,2},{2,0},{1,3},{3,1},{4,6},{6,4},{5,7},{7,5},{8,10},{10,8},{9,1... | collective-permute-start | bytes 3538952 | tf_op jit(solution)/shard_map/ppermute | solution.py:20
  38.3 45.5 %collective-permute-start.7 = (bf16[2048,256]{1,0:T(8,128)(2,1)}, bf16[2048,256]{1,0:T(8,128)(2,1)S(1)}, u32[]{:S(2)}, u32[]{:S(2)}) collective-permute-start(bf16[2048,256]{1,0:T(8,128)(2,1)} %pad_maximum_fusion), channel_id=1, source_target_pairs={{0,8},{4,12},{8,0},{12,4},{16,24},{20,28},{24,16},{28,20},{1,9},{5... | collective-permute-start | bytes 3145736 | tf_op jit(solution)/shard_map/ppermute | solution.py:20
  40.3 33.2 %collective-permute-start.10 = (bf16[128,2048]{1,0:T(8,128)(2,1)S(1)}, bf16[128,2048]{1,0:T(8,128)(2,1)S(1)}, u32[]{:S(2)}, u32[]{:S(2)}) collective-permute-start(bf16[128,2048]{1,0:T(8,128)(2,1)S(1)} %collective-permute-done.9.refs_7_), channel_id=1, source_target_pairs={{0,8},{4,12},{8,0},{12,4},{16,24},{20,28},{24,16},{28,20},{1,9},{5... | collective-permute-start | bytes 1572872 | tf_op jit(solution)/shard_map/ppermute | solution.py:20
  74.6 29.2 %collective-permute-start.11 = (bf16[256,2048]{1,0:T(8,128)(2,1)}, bf16[256,2048]{1,0:T(8,128)(2,1)}, u32[]{:S(2)}, u32[]{:S(2)}) collective-permute-start(bf16[256,2048]{1,0:T(8,128)(2,1)} %pad_maximum_fusion.1), channel_id=1, source_target_pairs={{0,4},{4,0},{8,12},{12,8},{16,20},{20,16},{24,28},{28,24},{1,5},{5... | collective-permute-start | bytes 3145736 | tf_op jit(solution)/shard_map/ppermute | solution.py:20
  88.8 14.9 %collective-permute-start.8 = (f32[256,1024]{1,0:T(8,128)}, f32[256,1024]{1,0:T(8,128)S(1)}, u32[]{:S(2)}, u32[]{:S(2)}) collective-permute-start(f32[256,1024]{1,0:T(8,128)} %shard_map.394.refs_3_), channel_id=1, source_target_pairs={{0,1},{1,0},{2,3},{3,2},{4,5},{5,4},{6,7},{7,6},{8,9},{9,8},{10,11... | collective-permute-start | bytes 3145736 | tf_op jit(solution)/shard_map/ppermute | solution.py:20
  89.4 14.3 %collective-permute-start.1 = (bf16[512,512]{1,0:T(8,128)(2,1)S(1)}, bf16[512,512]{1,0:T(8,128)(2,1)S(1)}, u32[]{:S(2)}, u32[]{:S(2)}) collective-permute-start(bf16[512,512]{1,0:T(8,128)(2,1)S(1)} %copy-done.1), channel_id=1, source_target_pairs={{0,2},{2,0},{1,3},{3,1},{4,6},{6,4},{5,7},{7,5},{8,10},{10,8},{9,1... | collective-permute-start | bytes 1572872 | tf_op jit(solution)/shard_map/ppermute | solution.py:20
  114.6 7.0 %collective-permute-start.13 = (f32[256,1024]{1,0:T(8,128)}, f32[256,1024]{1,0:T(8,128)S(1)}, u32[]{:S(2)}, u32[]{:S(2)}) collective-permute-start(f32[256,1024]{1,0:T(8,128)} %get-tuple-element.67.refs_3_), channel_id=1, source_target_pairs={{0,1},{1,0},{2,3},{3,2},{4,5},{5,4},{6,7},{7,6},{8,9},{9,8},{10,11... | collective-permute-start | bytes 3145736 | tf_op jit(solution)/shard_map/ppermute | solution.py:20
  121.0 38.4 %collective-permute-start.29 = (bf16[256,3072]{1,0:T(8,128)(2,1)}, bf16[256,3072]{1,0:T(8,128)(2,1)S(1)}, u32[]{:S(2)}, u32[]{:S(2)}) collective-permute-start(bf16[256,3072]{1,0:T(8,128)(2,1)} %get-tuple-element.96), channel_id=1, source_target_pairs={{0,4},{4,0},{8,12},{12,8},{16,20},{20,16},{24,28},{28,24},{1,5},{5... | collective-permute-start | bytes 4718600 | tf_op jit(solution)/shard_map/ppermute | solution.py:20
  144.4 11.6 %collective-permute-start.14 = (f32[256,512]{1,0:T(8,128)}, f32[256,512]{1,0:T(8,128)}, u32[]{:S(2)}, u32[]{:S(2)}) collective-permute-start(f32[256,512]{1,0:T(8,128)} %get-tuple-element.77.part), channel_id=1, source_target_pairs={{0,1},{1,0},{2,3},{3,2},{4,5},{5,4},{6,7},{7,6},{8,9},{9,8},{10,11... | collective-permute-start | bytes 1572872 | tf_op jit(solution)/shard_map/ppermute | solution.py:20
  144.6 2.4 collective-permute-start.12
  145.0 5.7 %collective-permute-start.15 = (f32[264,256]{1,0:T(8,128)S(1)}, f32[264,256]{1,0:T(8,128)}, u32[]{:S(2)}, u32[]{:S(2)}) collective-permute-start(f32[264,256]{1,0:T(8,128)S(1)} %copy-done.11), channel_id=1, source_target_pairs={{0,1},{1,0},{2,3},{3,2},{4,5},{5,4},{6,7},{7,6},{8,9},{9,8},{10,11... | collective-permute-start | bytes 811016 | tf_op jit(solution)/shard_map/ppermute | solution.py:20
  148.7 21.1 %collective-permute-start.26 = (bf16[256,1024]{1,0:T(8,128)(2,1)}, bf16[256,1024]{1,0:T(8,128)(2,1)}, u32[]{:S(2)}, u32[]{:S(2)}) collective-permute-start(bf16[256,1024]{1,0:T(8,128)(2,1)} %get-tuple-element.91), channel_id=1, source_target_pairs={{0,4},{4,0},{8,12},{12,8},{16,20},{20,16},{24,28},{28,24},{1,5},{5... | collective-permute-start | bytes 1572872 | tf_op jit(solution)/shard_map/ppermute | solution.py:20
  150.2 48.1 %collective-permute-start.20 = (bf16[256,1152]{1,0:T(8,128)(2,1)}, bf16[256,1152]{1,0:T(8,128)(2,1)}, u32[]{:S(2)}, u32[]{:S(2)}) collective-permute-start(bf16[256,1152]{1,0:T(8,128)(2,1)} %get-tuple-element.87), channel_id=1, source_target_pairs={{0,4},{4,0},{8,12},{12,8},{16,20},{20,16},{24,28},{28,24},{1,5},{5... | collective-permute-start | bytes 1769480 | tf_op jit(solution)/shard_map/ppermute | solution.py:20
  154.5 60.0 %collective-permute-start.23 = (bf16[256,1152]{1,0:T(8,128)(2,1)}, bf16[256,1152]{1,0:T(8,128)(2,1)}, u32[]{:S(2)}, u32[]{:S(2)}) collective-permute-start(bf16[256,1152]{1,0:T(8,128)(2,1)} %get-tuple-element.89), channel_id=1, source_target_pairs={{0,4},{4,0},{8,12},{12,8},{16,20},{20,16},{24,28},{28,24},{1,5},{5... | collective-permute-start | bytes 1769480 | tf_op jit(solution)/shard_map/ppermute | solution.py:20
  158.9 3.9 %collective-permute-start.16 = (f32[16,256]{1,0:T(8,128)}, f32[16,256]{1,0:T(8,128)S(1)}, u32[]{:S(2)}, u32[]{:S(2)}) collective-permute-start(f32[16,256]{1,0:T(8,128)} %get-tuple-element.81.refs_7_), channel_id=1, source_target_pairs={{0,2},{2,0},{1,3},{3,1},{4,6},{6,4},{5,7},{7,5},{8,10},{10,8},{9,1... | collective-permute-start | bytes 49160 | tf_op jit(solution)/shard_map/ppermute | solution.py:20
  160.1 71.9 %collective-permute-start.30 = (bf16[128,3072]{1,0:T(8,128)(2,1)S(1)}, bf16[128,3072]{1,0:T(8,128)(2,1)S(1)}, u32[]{:S(2)}, u32[]{:S(2)}) collective-permute-start(bf16[128,3072]{1,0:T(8,128)(2,1)S(1)} %slice.311), channel_id=1, source_target_pairs={{0,8},{4,12},{8,0},{12,4},{16,24},{20,28},{24,16},{28,20},{1,9},{5... | collective-permute-start | bytes 2359304 | tf_op jit(solution)/shard_map/ppermute | solution.py:20
  166.2 30.4 %collective-permute-start.17 = (f32[32,768]{1,0:T(8,128)}, f32[32,768]{1,0:T(8,128)S(1)}, u32[]{:S(2)}, u32[]{:S(2)}) collective-permute-start(f32[32,768]{1,0:T(8,128)} %get-tuple-element.85), channel_id=1, source_target_pairs={{0,4},{4,0},{8,12},{12,8},{16,20},{20,16},{24,28},{28,24},{1,5},{5... | collective-permute-start | bytes 294920 | tf_op jit(solution)/shard_map/ppermute | solution.py:20
  171.0 33.0 %collective-permute-start.27 = (bf16[128,1024]{1,0:T(8,128)(2,1)S(1)}, bf16[128,1024]{1,0:T(8,128)(2,1)S(1)}, u32[]{:S(2)}, u32[]{:S(2)}) collective-permute-start(bf16[128,1024]{1,0:T(8,128)(2,1)S(1)} %slice.315), channel_id=1, source_target_pairs={{0,8},{4,12},{8,0},{12,4},{16,24},{20,28},{24,16},{28,20},{1,9},{5... | collective-permute-start | bytes 786440 | tf_op jit(solution)/shard_map/ppermute | solution.py:20
  196.6 4.7 %collective-permute-start.18 = (f32[32,768]{1,0:T(8,128)S(1)}, f32[32,768]{1,0:T(8,128)S(1)}, u32[]{:S(2)}, u32[]{:S(2)}) collective-permute-start(f32[32,768]{1,0:T(8,128)S(1)} %add.188), channel_id=1, source_target_pairs={{0,8},{4,12},{8,0},{12,4},{16,24},{20,28},{24,16},{28,20},{1,9},{5... | collective-permute-start | bytes 294920 | tf_op jit(solution)/shard_map/ppermute | solution.py:20
  199.5 20.5 %collective-permute-start.21 = (bf16[128,1152]{1,0:T(8,128)(2,1)S(1)}, bf16[128,1152]{1,0:T(8,128)(2,1)S(1)}, u32[]{:S(2)}, u32[]{:S(2)}) collective-permute-start(bf16[128,1152]{1,0:T(8,128)(2,1)S(1)} %slice.314), channel_id=1, source_target_pairs={{0,8},{4,12},{8,0},{12,4},{16,24},{20,28},{24,16},{28,20},{1,9},{5... | collective-permute-start | bytes 884744 | tf_op jit(solution)/shard_map/ppermute | solution.py:20
  201.3 8.4 %collective-permute-start.19 = (f32[32,768]{1,0:T(8,128)S(1)}, f32[32,768]{1,0:T(8,128)S(1)}, u32[]{:S(2)}, u32[]{:S(2)}) collective-permute-start(f32[32,768]{1,0:T(8,128)S(1)} %add.189), channel_id=1, source_target_pairs={{0,16},{4,20},{8,24},{12,28},{16,0},{20,4},{24,8},{28,12},{1,17},{... | collective-permute-start | bytes 294920 | tf_op jit(solution)/shard_map/ppermute | solution.py:20
  204.1 18.8 %collective-permute-start.28 = (bf16[64,1024]{1,0:T(8,128)(2,1)S(1)}, bf16[64,1024]{1,0:T(8,128)(2,1)S(1)}, u32[]{:S(2)}, u32[]{:S(2)}) collective-permute-start(bf16[64,1024]{1,0:T(8,128)(2,1)S(1)} %slice.318), channel_id=1, source_target_pairs={{0,16},{4,20},{8,24},{12,28},{16,0},{20,4},{24,8},{28,12},{1,17},{... | collective-permute-start | bytes 393224 | tf_op jit(solution)/shard_map/ppermute | solution.py:20
  215.7 12.7 %collective-permute-start.24 = (bf16[128,1152]{1,0:T(8,128)(2,1)S(1)}, bf16[128,1152]{1,0:T(8,128)(2,1)S(1)}, u32[]{:S(2)}, u32[]{:S(2)}) collective-permute-start(bf16[128,1152]{1,0:T(8,128)(2,1)S(1)} %slice.313), channel_id=1, source_target_pairs={{0,8},{4,12},{8,0},{12,4},{16,24},{20,28},{24,16},{28,20},{1,9},{5... | collective-permute-start | bytes 884744 | tf_op jit(solution)/shard_map/ppermute | solution.py:20
  220.1 6.3 %collective-permute-start.22 = (bf16[64,1152]{1,0:T(8,128)(2,1)S(1)}, bf16[64,1152]{1,0:T(8,128)(2,1)S(1)}, u32[]{:S(2)}, u32[]{:S(2)}) collective-permute-start(bf16[64,1152]{1,0:T(8,128)(2,1)S(1)} %slice.317), channel_id=1, source_target_pairs={{0,16},{4,20},{8,24},{12,28},{16,0},{20,4},{24,8},{28,12},{1,17},{... | collective-permute-start | bytes 442376 | tf_op jit(solution)/shard_map/ppermute | solution.py:20
  228.5 16.5 %collective-permute-start.25 = (bf16[64,1152]{1,0:T(8,128)(2,1)S(1)}, bf16[64,1152]{1,0:T(8,128)(2,1)S(1)}, u32[]{:S(2)}, u32[]{:S(2)}) collective-permute-start(bf16[64,1152]{1,0:T(8,128)(2,1)S(1)} %slice.316), channel_id=1, source_target_pairs={{0,16},{4,20},{8,24},{12,28},{16,0},{20,4},{24,8},{28,12},{1,17},{... | collective-permute-start | bytes 442376 | tf_op jit(solution)/shard_map/ppermute | solution.py:20
  232.2 20.0 %collective-permute-start.31 = (bf16[64,3072]{1,0:T(8,128)(2,1)S(1)}, bf16[64,3072]{1,0:T(8,128)(2,1)S(1)}, u32[]{:S(2)}, u32[]{:S(2)}) collective-permute-start(bf16[64,3072]{1,0:T(8,128)(2,1)S(1)} %slice.312), channel_id=1, source_target_pairs={{0,16},{4,20},{8,24},{12,28},{16,0},{20,4},{24,8},{28,12},{1,17},{... | collective-permute-start | bytes 1179656 | tf_op jit(solution)/shard_map/ppermute | solution.py:20
  (43 other events, 490.6 us)
where the time goes:
time: 255 us; the launch traced here: 254 us
  waiting for transfers between devices  107 us (42%)
  Pallas kernels  64.1 us (25%)
  starting transfers between devices  39.5 us (15%)
  local copies, waits for them, and re-layouts  27.5 us (11%)
  other arithmetic  14.5 us (6%)
    ppermute x32, waiting for transfers between devices, swap(): return lax.ppermute(values, axis, [(i, i ^ step) for i in range(count)])  107 us
    pallas_call x12, Pallas kernels, call(): pl.pallas_call(kernel, out_shape=[jax.ShapeDtypeStruct(s, d) for s, d in...  64.1 us
    ppermute x32, starting transfers between devices, swap(): return lax.ppermute(values, axis, [(i, i ^ step) for i in range(count)])  39.5 us
    unnamed x96, local copies, waits for them, and re-layouts  12 us
  transfers between devices with their start and end apart: 32, of which 13 were waited for; matrix products, arithmetic and copies ran while one was open for 12% of the time, Pallas kernels for 22%

commit v1 on v0

v1 whole, which is shorter than its diff:
```python
import jax
import jax.numpy as jnp
import numpy as np
from jax import lax
from jax.experimental import pallas as pl
from jax.experimental.pallas import tpu as pltpu
from jax.sharding import PartitionSpec as P

NORM_EPS = 1e-05
F32 = jnp.float32
BF16 = jnp.bfloat16
HEAD = 64
LANES = 128
TAPS = 4
FAR = -1e30


def swap(values, axis, step=1):
    count = lax.axis_size(axis)
    return lax.ppermute(values, axis, [(i, i ^ step) for i in range(count)])


def dot(left, right):
    return jnp.dot(left, right, preferred_element_type=F32)


def dot_bt(left, right):
    return lax.dot_general(left, right, (((1,), (1,)), ((), ())), preferred_element_type=F32)


def dot_at(left, right):
    return lax.dot_general(left, right, (((0,), (0,)), ((), ())), preferred_element_type=F32)


def fine(left, right, dims=((1,), (0,))):
    return lax.dot_general(
        left, right, (dims, ((), ())), precision=lax.Precision.HIGHEST, preferred_element_type=F32
    )


class Chain:
    def __init__(self):
        self.token = jnp.zeros((8, LANES), F32)

    def __call__(self, kernel, outs, *args, scratch=(), smem=(), direct=False, after=()):
        plain = pl.ANY if direct else pltpu.VMEM
        specs = [
            pl.BlockSpec(memory_space=pltpu.SMEM if i in smem else plain)
            for i in range(len(args))
        ]
        extra = (self.token,) + tuple(after)
        count = len(args)
        held = count + len(extra)

        def body(*refs):
            refs[held][...] = jnp.zeros((8, LANES), F32)
            kernel(*refs[:count], *refs[held + 1 :])

        results = pl.pallas_call(
            body,
            out_shape=[jax.ShapeDtypeStruct((8, LANES), F32)]
            + [jax.ShapeDtypeStruct(s, d) for s, d in outs],
            in_specs=specs + [pl.BlockSpec(memory_space=pl.ANY)] * len(extra),
            out_specs=[pl.BlockSpec(memory_space=pltpu.VMEM)]
            + [pl.BlockSpec(memory_space=plain)] * len(outs),
            scratch_shapes=[pltpu.VMEM(s, d) if d is not None else s for s, d in scratch],
            compiler_params=pltpu.CompilerParams(vmem_limit_bytes=56 << 20),
            cost_estimate=pl.CostEstimate(flops=0, bytes_accessed=0, transcendentals=0),
        )(*args, *extra)
        self.token = results[0]
        return results[1:]


def iota(shape, dim):
    return lax.broadcasted_iota(jnp.int32, shape, dim)


def column(row_vector):
    ones = jnp.full((row_vector.shape[0], LANES), 1.0 / row_vector.shape[0], F32)
    return fine(row_vector, ones, ((0,), (0,)))


def token_sums(values):
    return fine(jnp.ones((8, values.shape[1]), F32), values, ((1,), (1,)))


def pieces_kernel(place, wm, wa, wd, gu, cot, t_out, g_out, c_out, sem):
    piece = t_out.shape[1]
    at = pl.multiple_of(place[1] * piece, piece)
    parts = []
    row = 0
    for w in (wm, wa, wd):
        size = w.shape[0]
        parts.append((w.at[:, pl.ds(at, piece)], t_out.at[row : row + size]))
        row += size
    parts.append((gu.at[pl.ds(at, piece)], g_out))
    parts.append((cot, c_out))
    copies = [pltpu.make_async_copy(s, d, sem.at[i]) for i, (s, d) in enumerate(parts)]
    for copy in copies:
        copy.start()
    for copy in copies:
        copy.wait()


def gather_quarters(place, mine, over_col, over_row, over_both, own_out, far_out, far_tmp):
    width = mine.shape[1]
    piece = width // 2
    first = place[0] == 0
    for a, b, out in ((mine, over_col, own_out), (over_row, over_both, far_tmp)):
        out[:, :width] = jnp.where(first, a[...], b[...])
        out[:, width:] = jnp.where(first, b[...], a[...])
    for j in range(4):
        at = pl.multiple_of((place[1] ^ j) * piece, piece)
        far_out[:, j * piece : (j + 1) * piece] = far_tmp[:, pl.ds(at, piece)]


def project_kernel(
    place, mine, over_col, over_row, over_both, gain, wx, wb, wd, wg, wq, wk,
    n1_out, p_out, low_out, own_out, far_out, factor_out, far_tmp,
):
    gather_quarters(place, mine, over_col, over_row, over_both, own_out, far_out, far_tmp)
    own = own_out[...].astype(F32)
    far = far_tmp[...].astype(F32)
    mean = jnp.sum(own * own + far * far, axis=1, keepdims=True) / (2 * own.shape[1])
    factor = lax.rsqrt(mean + NORM_EPS)
    factor_out[...] = jnp.broadcast_to(factor, factor_out.shape)
    n1 = (own * factor * gain[...]).astype(BF16)
    n1_out[...] = n1
    at = 0
    for w in (wx, wb, wd, wg, wq, wk):
        size = w.shape[1]
        part = dot(n1, w[...])
        p_out[:, at : at + size] = part
        low_out[:, at : at + size] = part.astype(BF16)
        at += size


def hop_kernel(t_first, t_second, g_first, g_second, t_out, g_out):
    t_piece = t_first.shape[1]
    g_piece = g_first.shape[0]
    t_out[:, :t_piece] = t_first[...]
    t_out[:, t_piece:] = t_second[...]
    g_out[:g_piece] = g_first[...]
    g_out[g_piece:] = g_second[...]


def masks(seg_row, seg_col, turned):
    tokens = seg_row.shape[1]
    i = iota((tokens, tokens), 1 if turned else 0)
    j = iota((tokens, tokens), 0 if turned else 1)
    same = seg_col[:, :1] == seg_row[...]
    return jnp.where((i >= j) & same, 0.0, FAR)


def valids(seg_col):
    seg = seg_col[...]
    t = iota(seg.shape, 0)
    return [
        jnp.where((t >= k) & (pltpu.roll(seg, k, 0) == seg), 1.0, 0.0) for k in range(1, TAPS)
    ]


def conv(block, taps, bias, valid):
    total = block * taps[TAPS - 1 : TAPS] + bias
    for k in range(1, TAPS):
        total = total + (pltpu.roll(block, k, 0) * valid[k - 1]) * taps[TAPS - 1 - k : TAPS - k]
    return total


def conv_turn(grad, block, taps, valid):
    tokens = grad.shape[0]
    back = grad * taps[TAPS - 1 : TAPS]
    rows = [None] * TAPS
    rows[TAPS - 1] = jnp.sum(grad * block, axis=0, keepdims=True)
    for k in range(1, TAPS):
        kept = grad * valid[k - 1]
        back = back + pltpu.roll(kept, tokens - k, 0) * taps[TAPS - 1 - k : TAPS - k]
        rows[TAPS - 1 - k] = jnp.sum(kept * pltpu.roll(block, k, 0), axis=0, keepdims=True)
    rows.append(jnp.sum(grad, axis=0, keepdims=True))
    rows.append(jnp.zeros((8 - len(rows), grad.shape[1]), F32))
    return back, jnp.concatenate(rows, 0)


def silu_turn(value):
    sig = jax.nn.sigmoid(value)
    return value * sig, sig * (1.0 + value * (1.0 - sig))


def steps(dt_raw, head_par):
    shifted = dt_raw + head_par[0:1]
    return jnp.maximum(shifted, 0.0) + jnp.log1p(jnp.exp(-jnp.abs(shifted)))


def mix_kernel(
    ch, nq, seg_row, seg_col, own, came, x_par, bc_par, head_par, wm, wa, first, second, pair,
    mixed_out, sums_out, pre_out, y_out, part_out,
):
    tokens = own.shape[0]
    nbc = bc_par.shape[1]
    state = nbc // 2
    sums_out[...] = own[...] + came[...].astype(F32)
    lane = iota((tokens, LANES), 1)
    low = lane < HEAD
    mask = masks(seg_row, seg_col, False)
    valid = valids(seg_col)
    for b in range(nbc // LANES):
        at = ch + b * LANES
        part = slice(b * LANES, (b + 1) * LANES)
        pre_out[:, at : at + LANES] = conv(
            sums_out[:, at : at + LANES], bc_par[0:TAPS, part], bc_par[TAPS : TAPS + 1, part], valid
        )
    bcc = pre_out[:, ch : ch + nbc]
    bcc = bcc * jax.nn.sigmoid(bcc)
    inner = fine(bcc[:, state:], bcc[:, :state], ((1,), (1,)))
    dt = steps(sums_out[:, ch + nbc : ch + nbc + LANES], head_par)
    tri = jnp.where(iota((tokens, tokens), 0) >= iota((tokens, tokens), 1), 1.0, 0.0)
    cum = fine(tri, dt * -jnp.exp(head_par[1:2]))
    cum_row = cum.T
    base = ch + nbc + LANES
    for p in range(ch // LANES):
        part = slice(p * LANES, (p + 1) * LANES)
        pre = conv(sums_out[:, part], x_par[0:TAPS, part], x_par[TAPS : TAPS + 1, part], valid)
        pre_out[:, part] = pre
        xc = pre * jax.nn.sigmoid(pre)
        h = 2 * p
        xdt = (xc * jnp.where(low, dt[:, h : h + 1], dt[:, h + 1 : h + 2])).astype(BF16)
        ys = []
        for e in (h, h + 1):
            decay = jnp.exp((cum[:, e : e + 1] - cum_row[e : e + 1]) + mask)
            ys.append(dot((inner * decay).astype(BF16), xdt))
        y = jnp.where(low, ys[0], ys[1])
        y_out[:, part] = y
        y = y + x_par[TAPS + 1 : TAPS + 2, part] * xc
        z = sums_out[:, base + p * LANES : base + (p + 1) * LANES]
        mixed_out[:, part] = (y * (z * jax.nn.sigmoid(z))).astype(BF16)
    at = base + ch
    kv = sums_out[:, at + nq : at + nq + LANES].astype(BF16)
    kv_turn = pltpu.roll(sums_out[:, at + nq : at + nq + LANES], HEAD, 1).astype(BF16)
    keys = jnp.where(low, kv, kv_turn)
    vals = jnp.where(low, kv_turn, kv)
    for p in range(nq // LANES):
        query = sums_out[:, at + p * LANES : at + (p + 1) * LANES] * (HEAD ** -0.5)
        outs = []
        for side in (low, ~low):
            score = dot_bt(jnp.where(side, query, 0.0).astype(BF16), keys) + mask
            score = jnp.exp(score - jnp.max(score, axis=1, keepdims=True))
            total = jnp.sum(score, axis=1, keepdims=True)
            outs.append(dot(score.astype(BF16), vals) / total)
        mixed_out[:, ch + p * LANES : ch + (p + 1) * LANES] = jnp.where(
            low, outs[0], outs[1]
        ).astype(BF16)
    half = wm.shape[1]
    value = mixed_out[...]
    part_out[:, :half] = dot(value[:, :ch], wm[...]) + dot(value[:, ch:], wa[...])
    part_out[:, half:] = dot(value, tall_far(first, second, pair, 0, ch + nq))


def unmix_two_kernel(ch, nq, seg_row, seg_col, sums, pre, ys, dym, x_par, gtwo_out):
    tokens = sums.shape[0]
    base = sums.shape[1] - (ch + nq + LANES)
    low = iota((tokens, LANES), 1) < HEAD
    mask = masks(seg_row, seg_col, True)
    for p in range(ch // LANES):
        part = slice(p * LANES, (p + 1) * LANES)
        value = pre[:, part]
        xc = value * jax.nn.sigmoid(value)
        _, gate_turn = silu_turn(sums[:, base + p * LANES : base + (p + 1) * LANES])
        y = ys[:, part] + x_par[TAPS + 1 : TAPS + 2, part] * xc
        gtwo_out[:, part] = (dym[:, part] * y * gate_turn).astype(BF16)
    at = base + ch
    kv = sums[:, at + nq : at + nq + LANES]
    kv_turn = pltpu.roll(kv, HEAD, 1)
    keys = jnp.where(low, kv, kv_turn).astype(BF16)
    vals = jnp.where(low, kv_turn, kv).astype(BF16)
    dk = jnp.zeros((tokens, LANES), F32)
    dv = jnp.zeros((tokens, LANES), F32)
    for p in range(nq // LANES):
        query = sums[:, at + p * LANES : at + (p + 1) * LANES] * (HEAD ** -0.5)
        grad = dym[:, ch + p * LANES : ch + (p + 1) * LANES]
        dqs = []
        for side in (low, ~low):
            q_low = jnp.where(side, query, 0.0).astype(BF16)
            g_low = jnp.where(side, grad, 0.0).astype(BF16)
            score = dot_bt(keys, q_low) + mask
            score = jnp.exp(score - jnp.max(score, axis=0, keepdims=True))
            prob = score * (1.0 / jnp.sum(score, axis=0, keepdims=True))
            dprob = dot_bt(vals, g_low)
            dv = dv + dot(prob.astype(BF16), g_low)
            inner_sum = jnp.sum(prob * dprob, axis=0, keepdims=True)
            dscore = (prob * (dprob - inner_sum)).astype(BF16)
            dk = dk + dot(dscore, q_low)
            dqs.append(dot_at(dscore, keys))
        gtwo_out[:, ch + p * LANES : ch + (p + 1) * LANES] = (
            jnp.where(low, dqs[0], dqs[1]) * (HEAD ** -0.5)
        ).astype(BF16)
    dk = dk + pltpu.roll(dk, HEAD, 1)
    dv = dv + pltpu.roll(dv, HEAD, 1)
    gtwo_out[:, ch + nq : ch + nq + LANES] = jnp.where(low, dk, dv).astype(BF16)

def unmix_one_kernel(
    ch, nq, seg_row, seg_col, sums, pre, ys, dym, x_par, bc_par, head_par,
    gx_out, gdt_out, gbc_out, small_out, prod_a, prod_b, turned,
):
    tokens = sums.shape[0]
    nbc = bc_par.shape[1]
    state = nbc // 2
    lane = iota((tokens, LANES), 1)
    low = lane < HEAD
    mask = masks(seg_row, seg_col, True)
    valid = valids(seg_col)
    bc_pre = pre[:, ch : ch + nbc]
    bcc, bcc_turn = silu_turn(bc_pre)
    b_in = bcc[:, :state]
    c_in = bcc[:, state:]
    inner = fine(b_in, c_in, ((1,), (1,)))
    dt_raw = sums[:, ch + nbc : ch + nbc + LANES]
    dt = steps(dt_raw, head_par)
    rate = jnp.exp(head_par[1:2])
    tri = jnp.where(iota((tokens, tokens), 0) >= iota((tokens, tokens), 1), 1.0, 0.0)
    cum = fine(tri, dt * -rate)
    cum_row = cum.T
    base = ch + nbc + LANES
    small_out[...] = jnp.zeros_like(small_out)
    turned[...] = jnp.zeros_like(turned)
    for p in range(ch // LANES):
        part = slice(p * LANES, (p + 1) * LANES)
        xc, xc_turn = silu_turn(pre[:, part])
        skip = x_par[TAPS + 1 : TAPS + 2, part]
        z = sums[:, base + p * LANES : base + (p + 1) * LANES]
        gate = z * jax.nn.sigmoid(z)
        dy_in = dym[:, part]
        y = ys[:, part]
        dy = dy_in * gate
        h = 2 * p
        dt_pair = jnp.where(low, dt[:, h : h + 1], dt[:, h + 1 : h + 2])
        xdt = xc * dt_pair
        dy_low = dy.astype(BF16)
        x_low = xdt.astype(BF16)
        sides = []
        for e, side in ((h, low), (h + 1, ~low)):
            decay = jnp.exp((cum_row[e : e + 1] - cum[:, e : e + 1]) + mask)
            turned[...] += dot_bt(jnp.where(side, xdt, 0.0).astype(BF16), dy_low) * decay
            sides.append(dot((inner * decay).astype(BF16), dy_low))
        dxdt = jnp.where(low, sides[0], sides[1])
        prod_a[:, part] = dy_low.astype(F32) * y - x_low.astype(F32) * dxdt
        prod_b[:, part] = dxdt * xc
        small_out[8 + TAPS + 1 : 8 + TAPS + 2, part] = jnp.sum(dy * xc, axis=0, keepdims=True)
        dpre = (skip * dy + dxdt * dt_pair) * xc_turn
        back, rows = conv_turn(dpre, sums[:, part], x_par[0:TAPS, part], valid)
        gx_out[:, part] = back.astype(BF16)
        small_out[0:8, part] = rows
    pick = jnp.where(iota((ch, LANES), 0) // HEAD == iota((ch, LANES), 1), 1.0, 0.0)
    dcum = fine(prod_a[...], pick)
    ddt = fine(prod_b[...], pick)
    after = fine(tri, dcum, ((0,), (0,)))
    ddt = ddt - rate * after
    ddt = ddt * jax.nn.sigmoid(dt_raw + head_par[0:1])
    gdt_out[...] = ddt.astype(BF16)
    small_out[8 + TAPS : 8 + TAPS + 1, 0:LANES] = jnp.sum(ddt, axis=0, keepdims=True)
    small_out[8 + TAPS : 8 + TAPS + 1, LANES : 2 * LANES] = jnp.sum(
        after * (-dt * rate), axis=0, keepdims=True
    )
    skip_sum = jnp.broadcast_to(small_out[8 + TAPS + 1 : 8 + TAPS + 2, :], (8, ch))
    small_out[8 + TAPS : 8 + TAPS + 1, 2 * LANES : 3 * LANES] = fine(skip_sum, pick)[0:1]
    dinner = turned[...]
    d_b = fine(dinner, c_in) * bcc_turn[:, :state]
    d_c = fine(dinner, b_in, ((0,), (0,))) * bcc_turn[:, state:]
    for b, grad in enumerate((d_b, d_c)):
        at = ch + b * LANES
        part = slice(b * LANES, (b + 1) * LANES)
        back, rows = conv_turn(grad, sums[:, at : at + LANES], bc_par[0:TAPS, part], valid)
        gbc_out[0:tokens, part] = back
        gbc_out[tokens : tokens + 8, part] = rows


def tall_far(first, second, pair, start, size):
    return jnp.concatenate(
        [r[start : start + size] for r in (first, second, pair)], axis=1
    )


def norm_factor(value):
    return lax.rsqrt(jnp.mean(value * value, axis=1, keepdims=True) + NORM_EPS)


def act_grad_kernel(
    inner, place, mine, over_col, over_row, over_both, wd, first, second, pair,
    own_out, far_out, ga_out, far_tmp,
):
    gather_quarters(place, mine, over_col, over_row, over_both, own_out, far_out, far_tmp)
    ff = wd.shape[0]
    ga_out[...] = dot_bt(own_out[...], wd[...]) + dot_bt(
        far_out[...], tall_far(first, second, pair, inner, ff)
    )


def feed_kernel(
    place, own, far, part, came, gain, gu, gu_first, gu_second, gu_pair, grad_act, wd,
    h2_out, n2_out, act_out, ggu_out, n2p_out, keep_out, send_out,
):
    half = own.shape[1]
    quarter = half // 2
    piece = half // 4
    h2_out[:, :half] = own[...].astype(F32) + (part[:, :half] + came[:, :half])
    h2_out[:, half:] = far[...].astype(F32) + (part[:, half:] + came[:, half:])
    h2 = h2_out[...]
    n2 = (h2 * norm_factor(h2) * gain[...]).astype(BF16)
    n2_out[...] = n2[:, :half]
    gu_far = jnp.concatenate(
        [gu_first[...], gu_pair[0:piece], gu_second[...], gu_pair[piece:]], axis=0
    )
    ff = wd.shape[0]
    gate_up = dot(n2[:, :half], gu[...]) + dot(n2[:, half:], gu_far)
    gate = gate_up[:, :ff]
    up = gate_up[:, ff:]
    silu, silu_grad = silu_turn(gate)
    act = (silu * up).astype(BF16)
    act_out[...] = act
    ga = grad_act[...]
    ggu_out[:, :ff] = (ga * up * silu_grad).astype(BF16)
    ggu_out[:, ff:] = (ga * silu).astype(BF16)
    ggu = ggu_out[...]
    n2p_out[:, :half] = dot_bt(ggu, gu[...])
    n2p_out[:, half:] = dot_bt(ggu, gu_far)
    down = dot(act, wd[...])
    first = place[0] == 0
    keep_out[...] = jnp.where(first, down[:, :quarter], down[:, quarter:])
    send_out[...] = jnp.where(first, down[:, quarter:], down[:, :quarter])


def permuted(left, source):
    width = left.shape[1]
    hot = jnp.where(iota((width, source.shape[1]), 0) == source, 1.0, 0.0).astype(BF16)
    return dot(left, hot).astype(BF16)


def pair_grad(left, right, send_out, keep_out, at, cut, rows):
    size = right.shape[1]
    send_out[:, at : at + size] = dot_at(left[:, cut + rows : cut + 2 * rows], right).astype(BF16)
    keep_out[:, at : at + size] = dot_at(left[:, cut : cut + rows], right)


def feed_grad_kernel(n2, act, ggu, dy, order, order2, g_send, g_keep, d_send, d_keep):
    rows = g_keep.shape[0]
    width = dy.shape[1]
    pair_grad(permuted(n2[...], order[...]), ggu[...], g_send, g_keep, 0, 0, rows)
    left = permuted(act[...], order2[...])
    for s in (0, 1):
        pair_grad(left, dy[...], d_send, d_keep, s * width, 2 * s * rows, rows)


def turn_kernel(
    place, dy_own, dy_far, h2, part, came, gain, wm, wa, first, second, pair, d_keep, d_came,
    dym_out, resid_out, low_out, gain_out, output_out,
):
    half = dy_own.shape[1]
    quarter = half // 2
    ch = wm.shape[0]
    value = h2[...]
    output_out[...] = (
        jnp.where(place[0] == 0, value[:, :quarter], value[:, quarter:half])
        + (d_keep[...] + d_came[...])
    ).astype(BF16)
    factor = norm_factor(value)
    dn2 = part[...] + came[...]
    gained = dn2 * gain[...]
    inner_sum = jnp.sum(gained * value, axis=1, keepdims=True)
    gain_out[...] = jnp.broadcast_to(
        jnp.sum(dn2[:, :half] * value[:, :half] * factor, axis=0, keepdims=True), gain_out.shape
    )
    slope = factor * factor * factor * inner_sum / (2 * half)
    change = factor * gained - value * slope
    dh_own = dy_own[...].astype(F32) + change[:, :half]
    dh_far = dy_far[...].astype(F32) + change[:, half:]
    resid_out[...] = dh_own
    low_own = dh_own.astype(BF16)
    low_out[...] = low_own
    dym = dot_bt(dh_far.astype(BF16), tall_far(first, second, pair, 0, dym_out.shape[1]))
    dym_out[:, :ch] = dym[:, :ch] + dot_bt(low_own, wm[...])
    dym_out[:, ch:] = dym[:, ch:] + dot_bt(low_own, wa[...])


def mix_grad_kernel(mixed, low, order, send_out, keep_out):
    rows = keep_out.shape[0]
    width = low.shape[1]
    left = permuted(mixed[...], order[...])
    for s in (0, 1):
        pair_grad(left, low[...], send_out, keep_out, s * width, 2 * s * rows, rows)


def grad_two_kernel(n1, g_two, order, send_out, keep_out):
    pair_grad(permuted(n1[...], order[...]), g_two[...], send_out, keep_out, 0, 0, keep_out.shape[0])


def back_kernel(g_two, gx, gdt, both, wx, wb, wd, wg, wq, wk, n1p_out, n1b_out):
    ch = wg.shape[1]
    nq = wq.shape[1]
    total = dot_bt(gx[...], wx[...]) + dot_bt(gdt[...], wd[...])
    total = total + dot_bt(g_two[:, :ch], wg[...]) + dot_bt(g_two[:, ch : ch + nq], wq[...])
    n1p_out[...] = total + dot_bt(g_two[:, ch + nq :], wk[...])
    n1b_out[...] = dot_bt(both[...], wb[...])


def grad_one_kernel(n1, gx, gdt, gbc, gbc_came, order, send_out, keep_out, both_out):
    tokens = n1.shape[0]
    left = permuted(n1[...], order[...])
    both = (gbc[0:tokens] + gbc_came[0:tokens]).astype(BF16)
    both_out[...] = both
    at = 0
    for right in (gx[...], both, gdt[...]):
        pair_grad(left, right, send_out, keep_out, at, 0, keep_out.shape[0])
        at += right.shape[1]


def close_kernel(own, part, came, n1b, gain, gbc, gbc_came, dn1_out, rows_out):
    tokens = part.shape[0]
    dn1 = (part[...] + came[...]) + n1b[...]
    dn1_out[...] = dn1
    rows_out[0:8, :] = token_sums(dn1 * gain[...] * own[...].astype(F32))
    rows_out[8:16, :] = gbc[tokens:] + gbc_came[tokens:]


def end_kernel(
    place, own, factor1, resid, dn1, gain, rows, rows_far, small, gain2, hidden_out, vector_out
):
    half = dn1.shape[1]
    quarter = half // 2
    hid = own[...].astype(F32)
    factor = factor1[:, :1]
    inner_sum = column(rows[0:8] + rows_far[0:8])[:, :1]
    value = dn1[...]
    change = resid[...] + factor * (value * gain[...]) - hid * (
        factor * factor * factor * inner_sum / (2 * half)
    )
    hidden_out[...] = jnp.where(place[0] == 0, change[:, :quarter], change[:, quarter:])
    count = small.shape[0]
    vector_out[...] = jnp.zeros_like(vector_out)
    vector_out[0:count] = small[...]
    vector_out[count : count + 8, 0 : rows.shape[1]] = jnp.where(
        place[2] == 0, rows[8:16], rows_far[8:16]
    )
    vector_out[count + 8 : count + 9, 0:half] = jnp.sum(value * hid * factor, axis=0, keepdims=True)
    vector_out[count + 9 : count + 10, 0:half] = gain2[0:1]


def stage_kernel(keep, came, send_out, keep_out):
    rows = keep_out.shape[0]
    total = keep[...] + came[...].astype(F32)
    send_out[...] = total[rows:].astype(BF16)
    keep_out[...] = total[:rows]


def stage_sum_kernel(keep, came, vector, vector_came, send_out, keep_out, vector_out):
    stage_kernel(keep, came, send_out, keep_out)
    vector_out[...] = vector[...] + vector_came[...]


def last_kernel(keep, came, *outs):
    total = keep[...] + came[...].astype(F32)
    at = 0
    for out in outs:
        out[...] = total[:, at : at + out.shape[1]]
        at += out.shape[1]


def last_tall_kernel(keep, came, *outs):
    total = keep[...] + came[...].astype(F32)
    width = outs[0].shape[1]
    tall = jnp.concatenate([total[:, :width], total[:, width:]], axis=0)
    at = 0
    for out in outs:
        out[...] = tall[at : at + out.shape[0]]
        at += out.shape[0]


def halving_order(steps):
    order = [0]
    for step in reversed(steps):
        order = order + [o | step for o in order]
    return order


class Scatter:
    def __init__(self, run, steps, send, keep, last, outs, vector=None):
        self.run, self.steps, self.last, self.outs = run, steps, last, outs
        self.at, self.keep, self.vector = 0, keep, vector
        self.came = swap(send, "dp", steps[0])
        self.results = None

    def add_vector(self, vector):
        self.vector = vector
        self.vector_came = swap(vector, "dp", self.steps[0])

    def advance(self):
        if self.results is not None:
            return
        self.at += 1
        if self.at == len(self.steps):
            self.results = self.run(self.last, self.outs, self.keep, self.came)
            if self.vector is not None:
                self.vector = self.vector + self.vector_came
            return
        rows, cols = self.keep.shape
        outs = [((rows // 2, cols), BF16), ((rows // 2, cols), F32)]
        step = self.steps[self.at]
        if self.vector is None:
            send, self.keep = self.run(stage_kernel, outs, self.keep, self.came)
        else:
            send, self.keep, self.vector = self.run(
                stage_sum_kernel,
                outs + [(self.vector.shape, F32)],
                self.keep, self.came, self.vector, self.vector_came,
            )
            self.vector_came = swap(self.vector, "dp", step)
        self.came = swap(send, "dp", step)


def shards(
    hidden,
    segment_ids,
    norm1_gain,
    w_gate,
    w_xin,
    w_dt,
    w_bc,
    w_query,
    w_kv,
    convx_weight,
    convx_bias,
    convbc_weight,
    convbc_bias,
    dt_bias,
    a_log,
    d_skip,
    w_mixout,
    w_attnout,
    norm2_gain,
    w_gateup,
    w_down,
    cotangent,
):
    row = lax.axis_index("row")
    col = lax.axis_index("col")
    me = lax.axis_index("dp")
    count = lax.axis_size("dp")
    spot = me & 3
    place = jnp.stack([col, spot, row]).astype(jnp.int32)
    tokens, quarter = hidden.shape
    half = 2 * quarter
    full_width = 4 * quarter
    piece = half // 4
    ch = w_xin.shape[1]
    nq = w_query.shape[1]
    nkv = w_kv.shape[2]
    nbc = w_bc.shape[1]
    heads = w_dt.shape[1]
    ff = w_down.shape[0]
    cq = convx_bias.shape[0]
    hq = dt_bias.shape[0]

    run = Chain()
    cols = ch + nbc + LANES + ch + nq + nkv
    inner = ch + nq
    over_row = swap(hidden, "row")
    over_col = swap(hidden, "col")
    over_both = swap(over_row, "col")

    gu = w_gateup.reshape(half, 2 * ff)
    t_mine, g_mine, cot = run(
        pieces_kernel,
        [((inner + ff, piece), BF16), ((piece, 2 * ff), BF16), ((tokens, quarter), BF16)],
        place, w_mixout, w_attnout, w_down, gu, cotangent,
        smem=(0,), direct=True, after=(over_row,), scratch=[(pltpu.SemaphoreType.DMA((5,)), None)],
    )
    t_first = swap(t_mine, "row")
    g_first = swap(g_mine, "row")
    wk = w_kv.reshape(half, nkv)
    wd = jnp.pad(w_dt, ((0, 0), (0, LANES - heads)))
    gain_one = norm1_gain.astype(F32)[None]
    n1, part, part_low, own, far, factor1 = run(
        project_kernel,
        [
            ((tokens, half), BF16),
            ((tokens, cols), F32),
            ((tokens, cols), BF16),
            ((tokens, half), BF16),
            ((tokens, half), BF16),
            ((tokens, LANES), F32),
        ],
        place, hidden, over_col, over_row, over_both, gain_one, w_xin, w_bc, wd, w_gate, w_query, wk,
        smem=(0,), scratch=[((tokens, half), BF16)],
    )
    part_came = swap(part_low, "row")
    cot_row = swap(cot, "row")
    cot_col = swap(cot, "col")
    cot_both = swap(cot_row, "col")
    t_second = swap(t_first, "dp", 1)
    g_second = swap(g_first, "dp", 2)
    t_cat, g_cat = run(
        hop_kernel,
        [((inner + ff, 2 * piece), BF16), ((2 * piece, 2 * ff), BF16)],
        t_first, t_second, g_first, g_second,
    )
    t_pair = swap(t_cat, "dp", 2)
    g_pair = swap(g_cat, "dp", 1)

    small = jnp.concatenate(
        [convx_weight.T.reshape(-1), convx_bias, dt_bias, a_log, d_skip, norm2_gain]
    )
    small_far = swap(small, "row")

    def joined(start, size):
        a = small[start : start + size]
        b = small_far[start : start + size]
        first = row == 0
        return jnp.concatenate([jnp.where(first, a, b), jnp.where(first, b, a)], 0).astype(F32)

    at = TAPS * cq
    x_par = jnp.stack(
        [joined(k * cq, cq) for k in range(TAPS + 1)]
        + [jnp.repeat(joined(at + cq + 2 * hq, hq), HEAD)]
        + [jnp.zeros((ch,), F32)] * 2
    )
    bc_par = jnp.concatenate(
        [convbc_weight.T, convbc_bias[None], jnp.zeros((3, nbc), BF16)], 0
    ).astype(F32)
    head_par = jnp.stack(
        [jnp.pad(joined(at + cq + k * hq, hq), (0, LANES - heads)) for k in (0, 1)]
        + [jnp.zeros((LANES,), F32)] * 6
    )
    gain2_far = jnp.concatenate(
        [
            lax.dynamic_slice_in_dim(small_far, at + cq + 3 * hq + (spot ^ j) * piece, piece, 0)
            for j in range(4)
        ]
    )
    gain_two = jnp.concatenate([norm2_gain, gain2_far]).astype(F32)[None]
    seg_row = segment_ids.astype(F32)
    seg_col = jnp.broadcast_to(segment_ids[0].astype(F32)[:, None], (tokens, LANES))

    near = [1 << b for b in range(count.bit_length() - 1)]
    turned = [near[1], near[0]] + near[2:]
    size = half // count
    within = jnp.asarray(np.tile(np.arange(size), count), jnp.int32)
    both_within = jnp.concatenate([within, within + size])

    def block_order(steps):
        return jnp.asarray(np.repeat(np.array(halving_order(steps)), size), jnp.int32) ^ me

    near_block = block_order(near)
    turned_block = block_order(turned)
    order_near = (near_block * size + within)[None]
    order_turned = (turned_block * size + within)[None]
    order_down = (jnp.concatenate([turned_block] * 2) * (ff // count) + both_within)[None]
    m_rows = ch // count
    a_rows = nq // count
    near_both = jnp.concatenate([near_block] * 2)
    order_mix = jnp.where(
        both_within < m_rows,
        near_both * m_rows + both_within,
        ch + near_both * a_rows + both_within - m_rows,
    )[None]

    dy_own, dy_far, grad_act = run(
        lambda *refs: act_grad_kernel(inner, *refs),
        [((tokens, half), BF16), ((tokens, half), BF16), ((tokens, ff), F32)],
        place, cot, cot_col, cot_row, cot_both, w_down, t_first, t_second, t_pair,
        smem=(0,), scratch=[((tokens, half), BF16)],
    )
    mixed, raw, pre, ys, mix_part = run(
        lambda *refs: mix_kernel(ch, nq, *refs),
        [
            ((tokens, inner), BF16),
            ((tokens, cols), F32),
            ((tokens, ch + nbc), F32),
            ((tokens, ch), F32),
            ((tokens, full_width), F32),
        ],
        seg_row, seg_col, part, part_came, x_par, bc_par, head_par,
        w_mixout, w_attnout, t_first, t_second, t_pair,
    )
    h2, n2, act, ggu, n2_part, down_keep, down_send = run(
        feed_kernel,
        [
            ((tokens, full_width), F32),
            ((tokens, half), BF16),
            ((tokens, ff), BF16),
            ((tokens, 2 * ff), BF16),
            ((tokens, full_width), F32),
            ((tokens, quarter), F32),
            ((tokens, quarter), F32),
        ],
        place, own, far, mix_part, swap(mix_part, "col"), gain_two,
        gu, g_first, g_second, g_pair, grad_act, w_down,
        smem=(0,),
    )
    n2_came = swap(n2_part, "col")
    down_came = swap(down_send, "col")
    rows = half // 2

    def halves(width):
        return [((rows, width), BF16), ((rows, width), F32)]

    g_send, g_keep, d_send, d_keep = run(
        feed_grad_kernel, halves(2 * ff) + halves(2 * half), n2, act, ggu, dy_own, order_near, order_down
    )
    s_gu = Scatter(run, near, g_send, g_keep, last_kernel, [((size, 2 * ff), F32)])
    s_down = Scatter(
        run, turned, d_send, d_keep, last_tall_kernel, [((2 * size, half), F32)]
    )
    dym, resid, low, gain2_sum, output = run(
        turn_kernel,
        [
            ((tokens, inner), F32),
            ((tokens, half), F32),
            ((tokens, half), BF16),
            ((8, half), F32),
            ((tokens, quarter), BF16),
        ],
        place, dy_own, dy_far, h2, n2_part, n2_came, gain_two,
        w_mixout, w_attnout, t_first, t_second, t_pair, down_keep, down_came,
        smem=(0,),
    )
    g_two = run(
        lambda *refs: unmix_two_kernel(ch, nq, *refs),
        [((tokens, ch + nq + nkv), BF16)],
        seg_row, seg_col, raw, pre, ys, dym, x_par,
    )[0]
    two_send, two_keep = run(grad_two_kernel, halves(ch + nq + nkv), n1, g_two, order_near)
    s_two = Scatter(
        run, near, two_send, two_keep, last_kernel,
        [((size, ch), F32), ((size, nq), F32), ((size, nkv), F32)],
    )
    s_down.advance()
    gx, gdt, gbc, small_sum = run(
        lambda *refs: unmix_one_kernel(ch, nq, *refs),
        [
            ((tokens, ch), BF16),
            ((tokens, LANES), BF16),
            ((tokens + 8, nbc), F32),
            ((16, ch), F32),
        ],
        seg_row, seg_col, raw, pre, ys, dym, x_par, bc_par, head_par,
        scratch=[((tokens, ch), F32), ((tokens, ch), F32), ((tokens, tokens), F32)],
    )
    gbc_came = swap(gbc, "col")
    m_send, m_keep = run(mix_grad_kernel, halves(2 * half), mixed, low, order_mix)
    s_mix = Scatter(
        run, near, m_send, m_keep, last_tall_kernel,
        [((m_rows, half), F32), ((a_rows, half), F32)],
    )
    one_send, one_keep, gbc_both = run(
        grad_one_kernel,
        halves(ch + nbc + LANES) + [((tokens, nbc), BF16)],
        n1, gx, gdt, gbc, gbc_came, order_turned,
    )
    s_one = Scatter(
        run, turned, one_send, one_keep, last_kernel,
        [((size, ch), F32), ((size, nbc), F32), ((size, LANES), F32)],
    )
    s_gu.advance()
    n1_part, n1_bc = run(
        back_kernel,
        [((tokens, half), F32), ((tokens, half), F32)],
        g_two, gx, gdt, gbc_both, w_xin, w_bc, wd, w_gate, w_query, wk,
    )
    n1_came = swap(n1_part, "col")
    s_two.advance()
    dn1, sum_rows = run(
        close_kernel,
        [((tokens, half), F32), ((16, tokens), F32)],
        own, n1_part, n1_came, n1_bc, gain_one, gbc, gbc_came,
    )
    rows_far = swap(sum_rows, "row")
    s_gu.advance()
    s_down.advance()
    grad_hidden, vector = run(
        end_kernel,
        [((tokens, quarter), F32), ((32, ch), F32)],
        place, own, factor1, resid, dn1, gain_one, sum_rows, rows_far, small_sum, gain2_sum,
        smem=(0,),
    )
    s_one.add_vector(vector)
    s_one.advance()
    s_mix.advance()
    scatters = (s_two, s_gu, s_down, s_one, s_mix)
    while any(s.results is None for s in scatters):
        for s in scatters:
            s.advance()
    vector = s_one.vector
    r_gate, r_query, r_kv = s_two.results
    r_xin, r_bc, r_dt = s_one.results
    r_mixout, r_attnout = s_mix.results

    def mine(values, width):
        return lax.dynamic_slice_in_dim(values, row * width, width, values.ndim - 1)

    return (
        output,
        grad_hidden,
        vector[24, :half],
        r_gate,
        r_xin,
        r_dt[:, :heads],
        r_bc,
        r_query,
        r_kv.reshape(size, 1, nkv),
        mine(vector[0:TAPS], cq).T,
        mine(vector[TAPS], cq),
        vector[16 : 16 + TAPS, :nbc].T,
        vector[16 + TAPS, :nbc],
        mine(vector[12, :heads], hq),
        mine(vector[12, LANES : LANES + heads], hq),
        mine(vector[12, 2 * LANES : 2 * LANES + heads], hq),
        r_mixout,
        r_attnout,
        vector[25, :half],
        s_gu.results[0].reshape(size, 2, ff),
        s_down.results[0],
    )


def solution(mesh):
    placed = (
        P("dp", ("row", "col")),
        P("dp", None),
        P("row"),
        P("row", "col"),
        P("row", "col"),
        P("row", "col"),
        P("row", None),
        P("row", "col"),
        P("row", "col", None),
        P(("col", "row"), None),
        P(("col", "row")),
        P(),
        P(),
        P(("col", "row")),
        P(("col", "row")),
        P(("col", "row")),
        P("col", "row"),
        P("col", "row"),
        P("row"),
        P("row", None, "col"),
        P("col", "row"),
        P("dp", ("row", "col")),
    )
    return jax.shard_map(
        shards,
        mesh=mesh,
        in_specs=placed,
        out_specs=(
            P("dp", ("row", "col")),
            P("dp", ("row", "col")),
            P("row"),
            P(("row", "dp"), "col"),
            P(("row", "dp"), "col"),
            P(("row", "dp"), "col"),
            P(("row", "dp"), None),
            P(("row", "dp"), "col"),
            P(("row", "dp"), "col", None),
            P(("col", "row"), None),
            P(("col", "row")),
            P(),
            P(),
            P(("col", "row")),
            P(("col", "row")),
            P(("col", "row")),
            P(("col", "dp"), "row"),
            P(("col", "dp"), "row"),
            P("row"),
            P(("row", "dp"), None, "col"),
            P(("col", "dp"), "row"),
        ),
        check_vma=False,
    )
```

time: 255 us -> 288 us (1.13)
  Pallas kernels: 64.1 us -> 141 us
  waiting for transfers between devices: 107 us -> 68.6 us
  other arithmetic: 14.5 us -> 4.54 us
  local copies, waits for them, and re-layouts: 27.5 us -> 32.8 us
    pallas_call x12 -> x31, Pallas kernels: 64.1 us -> 141 us  [__call__(): pl.pallas_call(body, out_shape=[jax.ShapeDtypeStruct((8, LANES), F32)] +...]
    ppermute x32 -> x38, waiting for transfers between devices: 107 us -> 68.6 us  [swap(): return lax.ppermute(values, axis, [(i, i ^ step) for i in range(count)])]
    unnamed x96 -> x133, local copies, waits for them, and re-layouts: 12 us -> 22.5 us
    add x17 -> x1, other arithmetic: 5.72 us -> 0.01 us  [advance(): self.vector = self.vector + self.vector_came]
    slice x18 -> x0, local copies, waits for them, and re-layouts: 4.27 us -> none  [the longest x1 0.69 us: shards(): r_two[:, :ch]]
    concatenate x4 -> x0, other arithmetic: 3.75 us -> none  [the longest x1 1.22 us: shards(): t_pair = swap(jnp.concatenate([t_first, t_second], 1), 'dp', 2)]
    ppermute x32 -> x38, starting transfers between devices: 39.5 us -> 38.3 us  [swap(): return lax.ppermute(values, axis, [(i, i ^ step) for i in range(count)])]
  transfers between devices with their start and end apart: 32 -> 38, of which waited for: 13 -> 9; matrix products, arithmetic and copies ran while one was open for 12% -> 7% of each run, Pallas kernels for 22% -> 33%
where the time goes in v1:
time: 288 us; the launch traced here: 287 us
  Pallas kernels  141 us (49%)
  waiting for transfers between devices  68.6 us (24%)
  starting transfers between devices  38.3 us (13%)
  local copies, waits for them, and re-layouts  32.8 us (11%)
  other arithmetic  4.54 us (2%)
    pallas_call x31, Pallas kernels, __call__(): pl.pallas_call(body, out_shape=[jax.ShapeDtypeStruct((8, LANES), F32)] +...  141 us
    ppermute x38, waiting for transfers between devices, swap(): return lax.ppermute(values, axis, [(i, i ^ step) for i in range(count)])  68.6 us
    ppermute x38, starting transfers between devices, swap(): return lax.ppermute(values, axis, [(i, i ^ step) for i in range(count)])  38.3 us
    unnamed x133, local copies, waits for them, and re-layouts  22.5 us
  transfers between devices with their start and end apart: 38, of which 9 were waited for; matrix products, arithmetic and copies ran while one was open for 7% of the time, Pallas kernels for 33%

profile of v1, /device:TPU:0, one launch (start us, length us, event | category | flops | bytes accessed | tf_op | source)
XLA Modules:
  0.0 286.9 jit_solution(3167324707511960964)
XLA Ops:
  0.7 3.0 %collective-permute-start = (bf16[256,256]{1,0:T(8,128)(2,1)}, bf16[256,256]{1,0:T(8,128)(2,1)S(1)}, u32[]{:S(2)}, u32[]{:S(2)}) collective-permute-start(bf16[256,256]{1,0:T(8,128)(2,1)} %refs_1_.3), channel_id=1, source_target_pairs={{0,2},{2,0},{1,3},{3,1},{4,6},{6,4},{5,7},{7,5},{8,10},{10,8},{9,1... | collective-permute-start | bytes 393224 | tf_op jit(solution)/shard_map/ppermute | solution.py:20
  3.7 3.6 %copy.49 = bf16[64,8,2,1024]{3,1,2,0:T(8,128)(2,1)} copy(bf16[64,8,2,1024]{3,2,1,0:T(2,128)(2,1)} %bitcast.51) | data formatting | bytes 4194304
  8.6 38.3 %shard_map.400 = (f32[8,128]{1,0:T(8,128)}, bf16[2048,128]{1,0:T(8,128)(2,1)}, bf16[128,2048]{1,0:T(8,128)(2,1)}, bf16[256,256]{1,0:T(8,128)(2,1)}) custom-call(s32[3]{0:T(128)} %pad_add_fusion.1.refs_0_, bf16[768,512]{1,0:T(8,128)(2,1)} %refs_7_.6, bf16[256,512]{1,0:T(8,128)(2,1)} %refs_8_.4, bf16[1024,512]{1,0:T(8,128)(2,1)} %refs_11_.1, ...), custom_call_target="tpu_custom_call" | custom-call | tf_op jit(solution)/shard_map/pallas_call | solution.py:59
  49.0 13.0 %collective-permute-done.4.refs_0_.refs_6_.refs_9_ = bf16[2048,128]{1,0:T(8,128)(2,1)S(1)} collective-permute-done((bf16[2048,128]{1,0:T(8,128)(2,1)}, bf16[2048,128]{1,0:T(8,128)(2,1)S(1)}, u32[]{:S(2)}, u32[]{:S(2)}) %collective-permute-start.4) | collective-permute-done | bytes 524320 | tf_op jit(solution)/shard_map/ppermute | solution.py:20
  63.5 8.3 %collective-permute-done.6.refs_2_.refs_7_ = bf16[128,2048]{1,0:T(8,128)(2,1)S(1)} collective-permute-done((bf16[128,2048]{1,0:T(8,128)(2,1)}, bf16[128,2048]{1,0:T(8,128)(2,1)S(1)}, u32[]{:S(2)}, u32[]{:S(2)}) %collective-permute-start.6) | collective-permute-done | bytes 524320 | tf_op jit(solution)/shard_map/ppermute | solution.py:20
  77.6 4.8 %shard_map.401 = (f32[8,128]{1,0:T(8,128)}, bf16[256,512]{1,0:T(8,128)(2,1)}, f32[256,2304]{1,0:T(8,128)}, bf16[256,2304]{1,0:T(8,128)(2,1)}, bf16[256,512]{1,0:...) custom-call(s32[3]{0:T(128)} %pad_add_fusion.1.refs_0_, bf16[256,256]{1,0:T(8,128)(2,1)} %refs_1_.3, ...), custom_call_target="tpu_custom_call" | custom-call | tf_op jit(solution)/shard_map/pallas_call | solution.py:59
  85.0 3.1 %shard_map.402 = (f32[8,128]{1,0:T(8,128)}, bf16[2048,256]{1,0:T(8,128)(2,1)}, bf16[256,2048]{1,0:T(8,128)(2,1)}) custom-call(bf16[2048,128]{1,0:T(8,128)(2,1)} %copy-done.1, bf16[2048,128]{1,0:T(8,128)(2,1)} %copy-done.2, bf16[128,2048]{1,0:T(8,128)(2,1)} %copy-done.3, bf16[128,2048]{1,0:T(8,128)(2,1)} %copy-done.4, f32[8,128]{1,0:T(8,128)} %get-tuple-element.140.refs_4_), custom_call_target="tpu_custom_call" | custom-call | tf_op jit(solution)/shard_map/pallas_call | solution.py:59
  91.1 22.5 %collective-permute-done.2.refs_3_ = bf16[256,256]{1,0:T(8,128)(2,1)S(1)} collective-permute-done((bf16[256,256]{1,0:T(8,128)(2,1)S(1)}, bf16[256,256]{1,0:T(8,128)(2,1)S(1)}, u32[]{:S(2)}, u32[]{:S(2)}) %collective-permute-start.2) | collective-permute-done | bytes 131104 | tf_op jit(solution)/shard_map/ppermute | solution.py:20
  116.7 3.8 %shard_map.403 = (f32[8,128]{1,0:T(8,128)}, bf16[256,512]{1,0:T(8,128)(2,1)}, bf16[256,512]{1,0:T(8,128)(2,1)}, f32[256,1024]{1,0:T(8,128)}) custom-call(s32[3]{0:T(128)} %pad_add_fusion.1.refs_0_, bf16[256,256]{1,0:T(8,128)(2,1)} %get-tuple-element.136.refs_1_, bf16[256,256]{1,0:T(8,128)(2,1)} %copy-done.32, bf16[256,256]{1,0:T(8,128)(2,1)} %copy-done.28, ...), custom_call_target="tpu_custom_call" | custom-call | tf_op jit(solution)/shard_map/pallas_call | solution.py:59
  121.3 7.9 %shard_map.404 = (f32[8,128]{1,0:T(8,128)}, bf16[256,1024]{1,0:T(8,128)(2,1)}, f32[256,2304]{1,0:T(8,128)}, f32[256,1024]{1,0:T(8,128)}, f32[256,768]{1,0:T(8,128)}, /*index=5*/f32[256,1024]{1,0:T(8,128)}) custom-call(f32[1,256]{1,0:T(1,128)} %copy-done.38, f32[256,128]{1,0:T(8,128)} %broadcast_in_dim.35.refs_1_, f32[256,2304]{1,0:T(8,128)} %get-tuple-element.147.refs_2_, ...), custom_call_target="tpu_custom_call" | custom-call | tf_op jit(solution)/shard_map/pallas_call | solution.py:59
  130.4 9.6 %collective-permute-done.14.refs_9_ = bf16[256,2048]{1,0:T(8,128)(2,1)S(1)} collective-permute-done((bf16[256,2048]{1,0:T(8,128)(2,1)}, bf16[256,2048]{1,0:T(8,128)(2,1)S(1)}, u32[]{:S(2)}, u32[]{:S(2)}) %collective-permute-start.14) | collective-permute-done | bytes 1048608 | tf_op jit(solution)/shard_map/ppermute | solution.py:20
  141.3 7.8 %shard_map.405 = (f32[8,128]{1,0:T(8,128)}, f32[256,1024]{1,0:T(8,128)}, bf16[256,512]{1,0:T(8,128)(2,1)}, bf16[256,1024]{1,0:T(8,128)(2,1)}, bf16[256,2048]{1,0...) custom-call(s32[3]{0:T(128)} %pad_add_fusion.1.refs_0_, ...), custom_call_target="tpu_custom_call" | custom-call | tf_op jit(solution)/shard_map/pallas_call | solution.py:59
  150.4 5.4 %shard_map.406 = (f32[8,128]{1,0:T(8,128)}, bf16[256,2048]{1,0:T(8,128)(2,1)}, f32[256,2048]{1,0:T(8,128)}, bf16[256,1024]{1,0:T(8,128)(2,1)}, f32[256,1024]{1,0:T(8,128)}) custom-call(bf16[256,512]{1,0:T(8,128)(2,1)} %get-tuple-element.158.refs_0_, bf16[256,1024]{1,0:T(8,128)(2,1)} %get-tuple-element.159.refs_1_, ...), custom_call_target="tpu_custom_call" | custom-call | tf_op jit(solution)/shard_map/pallas_call | solution.py:59
  160.4 5.3 %shard_map.407 = (f32[8,128]{1,0:T(8,128)}, f32[256,1024]{1,0:T(8,128)}, f32[256,512]{1,0:T(8,128)}, bf16[256,512]{1,0:T(8,128)(2,1)}, f32[8,512]{1,0:T(8,128)}, /*index=5*/bf16[256,256]{1,0:T(8,128)(2,1)}) custom-call(s32[3]{0:T(128)} %pad_add_fusion.1.refs_0_, bf16[256,512]{1,0:T(8,128)(2,1)} %get-tuple-element.143.refs_3_.refs_1_, ...), custom_call_target="tpu_custom_call" | custom-call | tf_op jit(solution)/shard_map/pallas_call | solution.py:59
  165.7 5.6 %shard_map.408 = (f32[8,128]{1,0:T(8,128)}, bf16[256,1152]{1,0:T(8,128)(2,1)}) custom-call(f32[1,256]{1,0:T(1,128)} %copy-done.38, f32[256,128]{1,0:T(8,128)} %broadcast_in_dim.35.refs_1_, f32[256,2304]{1,0:T(8,128)} %get-tuple-element.166.refs_2_, f32[256,1024]{1,0:T(8,128)} %get-tuple-element.167.refs_3_, f32[256,768]{1,0:T(8,128)} %get-tuple-element.168.refs_4_, ...), custom_call_target="tpu_custom_call" | custom-call | tf_op jit(solution)/shard_map/pallas_call | solution.py:59
  171.3 3.0 %shard_map.409 = (f32[8,128]{1,0:T(8,128)}, bf16[256,1152]{1,0:T(8,128)(2,1)}, f32[256,1152]{1,0:T(8,128)}) custom-call(bf16[256,512]{1,0:T(8,128)(2,1)} %get-tuple-element.174.refs_0_, bf16[256,1152]{1,0:T(8,128)(2,1)} %get-tuple-element.171.refs_1_.refs_0_, s32[1,512]{1,0:T(1,128)} %bitcast.62, f32[8,128]{1,0:T(8,128)} %get-tuple-element.175.refs_3_), custom_call_target="tpu_custom_call" | custom-call | tf_op jit(solution)/shard_map/pallas_call | solution.py:59
  178.0 9.0 %shard_map.411 = (f32[8,128]{1,0:T(8,128)}, bf16[256,768]{1,0:T(8,128)(2,1)}, bf16[256,128]{1,0:T(8,128)(2,1)}, f32[264,256]{1,0:T(8,128)}, f32[16,768]{1,0:T(8,128)}) custom-call(f32[1,256]{1,0:T(1,128)} %copy-done.38, f32[256,128]{1,0:T(8,128)} %broadcast_in_dim.35.refs_1_, f32[256,2304]{1,0:T(8,128)} %get-tuple-element.166.refs_2_, ...), custom_call_target="tpu_custom_call" | custom-call | tf_op jit(solution)/shard_map/pallas_call | solution.py:59
  187.0 3.3 %shard_map.412 = (f32[8,128]{1,0:T(8,128)}, bf16[256,1024]{1,0:T(8,128)(2,1)}, f32[256,1024]{1,0:T(8,128)}) custom-call(bf16[256,1024]{1,0:T(8,128)(2,1)} %get-tuple-element.181.refs_0_, bf16[256,512]{1,0:T(8,128)(2,1)} %get-tuple-element.182.refs_1_, s32[1,1024]{1,0:T(1,128)} %get-tuple-element.309.refs_2_, f32[8,128]{1,0:T(8,128)} %get-tuple-element.183.refs_3_), custom_call_target="tpu_custom_call" | custom-call | tf_op jit(solution)/shard_map/pallas_call | solution.py:59
  190.9 3.3 %shard_map.413 = (f32[8,128]{1,0:T(8,128)}, bf16[256,1152]{1,0:T(8,128)(2,1)}, f32[256,1152]{1,0:T(8,128)}, bf16[256,256]{1,0:T(8,128)(2,1)}) custom-call(bf16[256,512]{1,0:T(8,128)(2,1)} %get-tuple-element.174.refs_0_, bf16[256,768]{1,0:T(8,128)(2,1)} %get-tuple-element.178.refs_1_, bf16[256,128]{1,0:T(8,128)(2,1)} %get-tuple-element.179.refs_2_, ...), custom_call_target="tpu_custom_call" | custom-call | tf_op jit(solution)/shard_map/pallas_call | solution.py:59
  195.3 3.4 %shard_map.414 = (f32[8,128]{1,0:T(8,128)}, bf16[128,2048]{1,0:T(8,128)(2,1)}, f32[128,2048]{1,0:T(8,128)}) custom-call(f32[256,2048]{1,0:T(8,128)} %get-tuple-element.186.refs_0_, bf16[256,2048]{1,0:T(8,128)(2,1)} %copy-done.6, f32[8,128]{1,0:T(8,128)} %get-tuple-element.188.refs_2_), custom_call_target="tpu_custom_call" | custom-call | tf_op jit(solution)/shard_map/pallas_call | solution.py:59
  198.7 3.9 %shard_map.415 = (f32[8,128]{1,0:T(8,128)}, f32[256,512]{1,0:T(8,128)}, f32[256,512]{1,0:T(8,128)}) custom-call(bf16[256,1152]{1,0:T(8,128)(2,1)} %get-tuple-element.171.refs_1_.refs_0_, bf16[256,768]{1,0:T(8,128)(2,1)} %get-tuple-element.178.refs_1_, bf16[256,128]{1,0:T(8,128)(2,1)} %get-tuple-element.179.refs_2_, ...), custom_call_target="tpu_custom_call" | custom-call | tf_op jit(solution)/shard_map/pallas_call | solution.py:59
  207.4 2.4 shard_map.416
  210.6 2.8 shard_map.417
  214.7 3.1 %collective-permute-done.24.refs_1_ = bf16[128,2048]{1,0:T(8,128)(2,1)S(1)} collective-permute-done((bf16[128,2048]{1,0:T(8,128)(2,1)S(1)}, bf16[128,2048]{1,0:T(8,128)(2,1)S(1)}, u32[]{:S(2)}, u32[]{:S(2)}) %collective-permute-start.24) | collective-permute-done | bytes 524320 | tf_op jit(solution)/shard_map/ppermute | solution.py:20
  218.7 2.3 shard_map.418
  221.0 3.1 %collective-permute-done.23.refs_1_ = bf16[128,1024]{1,0:T(8,128)(2,1)S(1)} collective-permute-done((bf16[128,1024]{1,0:T(8,128)(2,1)S(1)}, bf16[128,1024]{1,0:T(8,128)(2,1)S(1)}, u32[]{:S(2)}, u32[]{:S(2)}) %collective-permute-start.23) | collective-permute-done | bytes 262176 | tf_op jit(solution)/shard_map/ppermute | solution.py:20
  227.3 2.6 shard_map.420
  231.9 2.6 collective-permute-start.30
  234.5 6.8 %collective-permute-done.26.refs_3_ = f32[32,768]{1,0:T(8,128)S(1)} collective-permute-done((f32[32,768]{1,0:T(8,128)}, f32[32,768]{1,0:T(8,128)S(1)}, u32[]{:S(2)}, u32[]{:S(2)}) %collective-permute-start.26) | collective-permute-done | bytes 98336 | tf_op jit(solution)/shard_map/ppermute | solution.py:20
  241.9 2.4 shard_map.421
  246.6 2.3 shard_map.422
  249.0 4.2 %collective-permute-start.29 = (bf16[64,1024]{1,0:T(8,128)(2,1)S(1)}, bf16[64,1024]{1,0:T(8,128)(2,1)S(1)}, u32[]{:S(2)}, u32[]{:S(2)}) collective-permute-start(bf16[64,1024]{1,0:T(8,128)(2,1)S(1)} %copy-done.61), channel_id=1, source_target_pairs={{0,16},{4,20},{8,24},{12,28},{16,0},{20,4},{24,8},{28,12},{1,17},{... | collective-permute-start | bytes 393224 | tf_op jit(solution)/shard_map/ppermute | solution.py:20
  (264 shorter events, 83.3 us)
Async XLA Ops:
  46.9 15.1 %collective-permute-start.4 = (bf16[2048,128]{1,0:T(8,128)(2,1)}, bf16[2048,128]{1,0:T(8,128)(2,1)S(1)}, u32[]{:S(2)}, u32[]{:S(2)}) collective-permute-start(bf16[2048,128]{1,0:T(8,128)(2,1)} %get-tuple-element.137), channel_id=1, source_target_pairs={{0,2},{2,0},{1,3},{3,1},{4,6},{6,4},{5,7},{7,5},{8,10},{10,8},{9,1... | collective-permute-start | bytes 1572872 | tf_op jit(solution)/shard_map/ppermute | solution.py:20
  48.2 23.5 %collective-permute-start.6 = (bf16[128,2048]{1,0:T(8,128)(2,1)}, bf16[128,2048]{1,0:T(8,128)(2,1)S(1)}, u32[]{:S(2)}, u32[]{:S(2)}) collective-permute-start(bf16[128,2048]{1,0:T(8,128)(2,1)} %get-tuple-element.138), channel_id=1, source_target_pairs={{0,2},{2,0},{1,3},{3,1},{4,6},{6,4},{5,7},{7,5},{8,10},{10,8},{9,1... | collective-permute-start | bytes 1572872 | tf_op jit(solution)/shard_map/ppermute | solution.py:20
  62.0 21.6 %collective-permute-start.5 = (bf16[2048,128]{1,0:T(8,128)(2,1)S(1)}, bf16[2048,128]{1,0:T(8,128)(2,1)S(1)}, u32[]{:S(2)}, u32[]{:S(2)}) collective-permute-start(bf16[2048,128]{1,0:T(8,128)(2,1)S(1)} %collective-permute-done.4.refs_0_.refs_6_.refs_9_), channel_id=1, source_target_pairs={{0,4},{4,0},{8,12},{12,8},{16,20},{20,16},{24,28},{28,24},{1,5},{5... | collective-permute-start | bytes 1572872 | tf_op jit(solution)/shard_map/ppermute | solution.py:20
  71.8 12.5 %collective-permute-start.7 = (bf16[128,2048]{1,0:T(8,128)(2,1)S(1)}, bf16[128,2048]{1,0:T(8,128)(2,1)S(1)}, u32[]{:S(2)}, u32[]{:S(2)}) collective-permute-start(bf16[128,2048]{1,0:T(8,128)(2,1)S(1)} %collective-permute-done.6.refs_2_.refs_7_), channel_id=1, source_target_pairs={{0,8},{4,12},{8,0},{12,4},{16,24},{20,28},{24,16},{28,20},{1,9},{5... | collective-permute-start | bytes 1572872 | tf_op jit(solution)/shard_map/ppermute | solution.py:20
  73.5 16.2 %collective-permute-start.12 = (bf16[2450]{0:T(1024)(128)(2,1)S(1)}, bf16[2450]{0:T(1024)(128)(2,1)S(1)}, u32[]{:S(2)}, u32[]{:S(2)}) collective-permute-start(bf16[2450]{0:T(1024)(128)(2,1)S(1)} %concatenate.168), channel_id=1, source_target_pairs={{0,2},{2,0},{1,3},{3,1},{4,6},{6,4},{5,7},{7,5},{8,10},{10,8},{9,1... | collective-permute-start | bytes 14708 | tf_op jit(solution)/shard_map/ppermute | solution.py:20
  82.3 38.2 %collective-permute-start.11 = (bf16[256,2304]{1,0:T(8,128)(2,1)}, bf16[256,2304]{1,0:T(8,128)(2,1)}, u32[]{:S(2)}, u32[]{:S(2)}) collective-permute-start(bf16[256,2304]{1,0:T(8,128)(2,1)} %get-tuple-element.148), channel_id=1, source_target_pairs={{0,2},{2,0},{1,3},{3,1},{4,6},{6,4},{5,7},{7,5},{8,10},{10,8},{9,1... | collective-permute-start | bytes 3538952 | tf_op jit(solution)/shard_map/ppermute | solution.py:20
  88.1 27.6 %collective-permute-start.10 = (bf16[2048,256]{1,0:T(8,128)(2,1)}, bf16[2048,256]{1,0:T(8,128)(2,1)S(1)}, u32[]{:S(2)}, u32[]{:S(2)}) collective-permute-start(bf16[2048,256]{1,0:T(8,128)(2,1)} %get-tuple-element.141), channel_id=1, source_target_pairs={{0,8},{4,12},{8,0},{12,4},{16,24},{20,28},{24,16},{28,20},{1,9},{5... | collective-permute-start | bytes 3145736 | tf_op jit(solution)/shard_map/ppermute | solution.py:20
  90.0 23.6 %collective-permute-start.2 = (bf16[256,256]{1,0:T(8,128)(2,1)S(1)}, bf16[256,256]{1,0:T(8,128)(2,1)S(1)}, u32[]{:S(2)}, u32[]{:S(2)}) collective-permute-start(bf16[256,256]{1,0:T(8,128)(2,1)S(1)} %copy-done.26), channel_id=1, source_target_pairs={{0,2},{2,0},{1,3},{3,1},{4,6},{6,4},{5,7},{7,5},{8,10},{10,8},{9,1... | collective-permute-start | bytes 393224 | tf_op jit(solution)/shard_map/ppermute | solution.py:20
  91.0 24.6 %collective-permute-start.1 = (bf16[256,256]{1,0:T(8,128)(2,1)S(1)}, bf16[256,256]{1,0:T(8,128)(2,1)S(1)}, u32[]{:S(2)}, u32[]{:S(2)}) collective-permute-start(bf16[256,256]{1,0:T(8,128)(2,1)S(1)} %copy-done.26), channel_id=1, source_target_pairs={{0,1},{1,0},{2,3},{3,2},{4,5},{5,4},{6,7},{7,6},{8,9},{9,8},{10,11... | collective-permute-start | bytes 393224 | tf_op jit(solution)/shard_map/ppermute | solution.py:20
  114.2 25.8 %collective-permute-start.14 = (bf16[256,2048]{1,0:T(8,128)(2,1)}, bf16[256,2048]{1,0:T(8,128)(2,1)S(1)}, u32[]{:S(2)}, u32[]{:S(2)}) collective-permute-start(bf16[256,2048]{1,0:T(8,128)(2,1)} %get-tuple-element.151), channel_id=1, source_target_pairs={{0,4},{4,0},{8,12},{12,8},{16,20},{20,16},{24,28},{28,24},{1,5},{5... | collective-permute-start | bytes 3145736 | tf_op jit(solution)/shard_map/ppermute | solution.py:20
  129.2 10.8 %collective-permute-start.13 = (f32[256,1024]{1,0:T(8,128)}, f32[256,1024]{1,0:T(8,128)S(1)}, u32[]{:S(2)}, u32[]{:S(2)}) collective-permute-start(f32[256,1024]{1,0:T(8,128)} %get-tuple-element.150.refs_3_), channel_id=1, source_target_pairs={{0,1},{1,0},{2,3},{3,2},{4,5},{5,4},{6,7},{7,6},{8,9},{9,8},{10,11... | collective-permute-start | bytes 3145736 | tf_op jit(solution)/shard_map/ppermute | solution.py:20
  149.1 10.2 %collective-permute-start.15 = (f32[256,1024]{1,0:T(8,128)}, f32[256,1024]{1,0:T(8,128)S(1)}, u32[]{:S(2)}, u32[]{:S(2)}) collective-permute-start(f32[256,1024]{1,0:T(8,128)} %get-tuple-element.155.refs_4_), channel_id=1, source_target_pairs={{0,1},{1,0},{2,3},{3,2},{4,5},{5,4},{6,7},{7,6},{8,9},{9,8},{10,11... | collective-permute-start | bytes 3145736 | tf_op jit(solution)/shard_map/ppermute | solution.py:20
  155.8 38.4 %collective-permute-start.19 = (bf16[256,2048]{1,0:T(8,128)(2,1)}, bf16[256,2048]{1,0:T(8,128)(2,1)S(1)}, u32[]{:S(2)}, u32[]{:S(2)}) collective-permute-start(bf16[256,2048]{1,0:T(8,128)(2,1)} %get-tuple-element.187), channel_id=1, source_target_pairs={{0,4},{4,0},{8,12},{12,8},{16,20},{20,16},{24,28},{28,24},{1,5},{5... | collective-permute-start | bytes 3145736 | tf_op jit(solution)/shard_map/ppermute | solution.py:20
  157.3 17.6 %collective-permute-start.17 = (bf16[256,1024]{1,0:T(8,128)(2,1)}, bf16[256,1024]{1,0:T(8,128)(2,1)S(1)}, u32[]{:S(2)}, u32[]{:S(2)}) collective-permute-start(bf16[256,1024]{1,0:T(8,128)(2,1)} %get-tuple-element.173), channel_id=1, source_target_pairs={{0,8},{4,12},{8,0},{12,4},{16,24},{20,28},{24,16},{28,20},{1,9},{5... | collective-permute-start | bytes 1572872 | tf_op jit(solution)/shard_map/ppermute | solution.py:20
  174.4 32.3 %collective-permute-start.21 = (bf16[256,1152]{1,0:T(8,128)(2,1)}, bf16[256,1152]{1,0:T(8,128)(2,1)S(1)}, u32[]{:S(2)}, u32[]{:S(2)}) collective-permute-start(bf16[256,1152]{1,0:T(8,128)(2,1)} %get-tuple-element.193), channel_id=1, source_target_pairs={{0,4},{4,0},{8,12},{12,8},{16,20},{20,16},{24,28},{28,24},{1,5},{5... | collective-permute-start | bytes 1769480 | tf_op jit(solution)/shard_map/ppermute | solution.py:20
  202.6 7.2 %collective-permute-start.20 = (f32[256,512]{1,0:T(8,128)}, f32[256,512]{1,0:T(8,128)S(1)}, u32[]{:S(2)}, u32[]{:S(2)}) collective-permute-start(f32[256,512]{1,0:T(8,128)} %get-tuple-element.190.refs_1_), channel_id=1, source_target_pairs={{0,1},{1,0},{2,3},{3,2},{4,5},{5,4},{6,7},{7,6},{8,9},{9,8},{10,11... | collective-permute-start | bytes 1572872 | tf_op jit(solution)/shard_map/ppermute | solution.py:20
  203.1 14.8 %collective-permute-start.24 = (bf16[128,2048]{1,0:T(8,128)(2,1)S(1)}, bf16[128,2048]{1,0:T(8,128)(2,1)S(1)}, u32[]{:S(2)}, u32[]{:S(2)}) collective-permute-start(bf16[128,2048]{1,0:T(8,128)(2,1)S(1)} %copy-done.56), channel_id=1, source_target_pairs={{0,8},{4,12},{8,0},{12,4},{16,24},{20,28},{24,16},{28,20},{1,9},{5... | collective-permute-start | bytes 1572872 | tf_op jit(solution)/shard_map/ppermute | solution.py:20
  204.7 29.8 %collective-permute-start.25 = (bf16[256,1152]{1,0:T(8,128)(2,1)S(1)}, bf16[256,1152]{1,0:T(8,128)(2,1)S(1)}, u32[]{:S(2)}, u32[]{:S(2)}) collective-permute-start(bf16[256,1152]{1,0:T(8,128)(2,1)S(1)} %copy-done.54), channel_id=1, source_target_pairs={{0,8},{4,12},{8,0},{12,4},{16,24},{20,28},{24,16},{28,20},{1,9},{5... | collective-permute-start | bytes 1769480 | tf_op jit(solution)/shard_map/ppermute | solution.py:20
  205.1 40.7 %collective-permute-start.32 = (bf16[256,1024]{1,0:T(8,128)(2,1)S(1)}, bf16[256,1024]{1,0:T(8,128)(2,1)S(1)}, u32[]{:S(2)}, u32[]{:S(2)}) collective-permute-start(bf16[256,1024]{1,0:T(8,128)(2,1)S(1)} %copy-done.55), channel_id=1, source_target_pairs={{0,4},{4,0},{8,12},{12,8},{16,20},{20,16},{24,28},{28,24},{1,5},{5... | collective-permute-start | bytes 1572872 | tf_op jit(solution)/shard_map/ppermute | solution.py:20
  206.6 17.5 %collective-permute-start.23 = (bf16[128,1024]{1,0:T(8,128)(2,1)S(1)}, bf16[128,1024]{1,0:T(8,128)(2,1)S(1)}, u32[]{:S(2)}, u32[]{:S(2)}) collective-permute-start(bf16[128,1024]{1,0:T(8,128)(2,1)S(1)} %copy-done.58), channel_id=1, source_target_pairs={{0,4},{4,0},{8,12},{12,8},{16,20},{20,16},{24,28},{28,24},{1,5},{5... | collective-permute-start | bytes 786440 | tf_op jit(solution)/shard_map/ppermute | solution.py:20
  213.4 13.2 %collective-permute-start.22 = (f32[16,256]{1,0:T(8,128)}, f32[16,256]{1,0:T(8,128)S(1)}, u32[]{:S(2)}, u32[]{:S(2)}) collective-permute-start(f32[16,256]{1,0:T(8,128)} %get-tuple-element.197.refs_6_), channel_id=1, source_target_pairs={{0,2},{2,0},{1,3},{3,1},{4,6},{6,4},{5,7},{7,5},{8,10},{10,8},{9,1... | collective-permute-start | bytes 49160 | tf_op jit(solution)/shard_map/ppermute | solution.py:20
  229.9 11.4 %collective-permute-start.26 = (f32[32,768]{1,0:T(8,128)}, f32[32,768]{1,0:T(8,128)S(1)}, u32[]{:S(2)}, u32[]{:S(2)}) collective-permute-start(f32[32,768]{1,0:T(8,128)} %get-tuple-element.210.refs_2_), channel_id=1, source_target_pairs={{0,8},{4,12},{8,0},{12,4},{16,24},{20,28},{24,16},{28,20},{1,9},{5... | collective-permute-start | bytes 294920 | tf_op jit(solution)/shard_map/ppermute | solution.py:20
  231.5 21.7 %collective-permute-start.31 = (bf16[128,1152]{1,0:T(8,128)(2,1)S(1)}, bf16[128,1152]{1,0:T(8,128)(2,1)S(1)}, u32[]{:S(2)}, u32[]{:S(2)}) collective-permute-start(bf16[128,1152]{1,0:T(8,128)(2,1)S(1)} %copy-done.57), channel_id=1, source_target_pairs={{0,8},{4,12},{8,0},{12,4},{16,24},{20,28},{24,16},{28,20},{1,9},{5... | collective-permute-start | bytes 884744 | tf_op jit(solution)/shard_map/ppermute | solution.py:20
  231.9 23.9 %collective-permute-start.30 = (bf16[64,2048]{1,0:T(8,128)(2,1)S(1)}, bf16[64,2048]{1,0:T(8,128)(2,1)S(1)}, u32[]{:S(2)}, u32[]{:S(2)}) collective-permute-start(bf16[64,2048]{1,0:T(8,128)(2,1)S(1)} %copy-done.59), channel_id=1, source_target_pairs={{0,16},{4,20},{8,24},{12,28},{16,0},{20,4},{24,8},{28,12},{1,17},{... | collective-permute-start | bytes 786440 | tf_op jit(solution)/shard_map/ppermute | solution.py:20
  244.4 16.5 %collective-permute-start.27 = (bf16[128,1152]{1,0:T(8,128)(2,1)}, bf16[128,1152]{1,0:T(8,128)(2,1)S(1)}, u32[]{:S(2)}, u32[]{:S(2)}) collective-permute-start(bf16[128,1152]{1,0:T(8,128)(2,1)} %get-tuple-element.213), channel_id=1, source_target_pairs={{0,4},{4,0},{8,12},{12,8},{16,20},{20,16},{24,28},{28,24},{1,5},{5... | collective-permute-start | bytes 884744 | tf_op jit(solution)/shard_map/ppermute | solution.py:20
  249.0 19.8 %collective-permute-start.35 = (bf16[128,1024]{1,0:T(8,128)(2,1)}, bf16[128,1024]{1,0:T(8,128)(2,1)S(1)}, u32[]{:S(2)}, u32[]{:S(2)}) collective-permute-start(bf16[128,1024]{1,0:T(8,128)(2,1)} %get-tuple-element.232), channel_id=1, source_target_pairs={{0,8},{4,12},{8,0},{12,4},{16,24},{20,28},{24,16},{28,20},{1,9},{5... | collective-permute-start | bytes 786440 | tf_op jit(solution)/shard_map/ppermute | solution.py:20
  249.0 9.5 %collective-permute-start.29 = (bf16[64,1024]{1,0:T(8,128)(2,1)S(1)}, bf16[64,1024]{1,0:T(8,128)(2,1)S(1)}, u32[]{:S(2)}, u32[]{:S(2)}) collective-permute-start(bf16[64,1024]{1,0:T(8,128)(2,1)S(1)} %copy-done.61), channel_id=1, source_target_pairs={{0,16},{4,20},{8,24},{12,28},{16,0},{20,4},{24,8},{28,12},{1,17},{... | collective-permute-start | bytes 393224 | tf_op jit(solution)/shard_map/ppermute | solution.py:20
  253.1 7.7 %collective-permute-start.28 = (f32[32,768]{1,0:T(8,128)}, f32[32,768]{1,0:T(8,128)S(1)}, u32[]{:S(2)}, u32[]{:S(2)}) collective-permute-start(f32[32,768]{1,0:T(8,128)} %get-tuple-element.214.refs_2_), channel_id=1, source_target_pairs={{0,4},{4,0},{8,12},{12,8},{16,20},{20,16},{24,28},{28,24},{1,5},{5... | collective-permute-start | bytes 294920 | tf_op jit(solution)/shard_map/ppermute | solution.py:20
  255.8 17.8 %collective-permute-start.34 = (bf16[64,1152]{1,0:T(8,128)(2,1)}, bf16[64,1152]{1,0:T(8,128)(2,1)S(1)}, u32[]{:S(2)}, u32[]{:S(2)}) collective-permute-start(bf16[64,1152]{1,0:T(8,128)(2,1)} %get-tuple-element.230), channel_id=1, source_target_pairs={{0,16},{4,20},{8,24},{12,28},{16,0},{20,4},{24,8},{28,12},{1,17},{... | collective-permute-start | bytes 442376 | tf_op jit(solution)/shard_map/ppermute | solution.py:20
  263.6 12.4 %collective-permute-start.33 = (f32[32,768]{1,0:T(8,128)}, f32[32,768]{1,0:T(8,128)S(1)}, u32[]{:S(2)}, u32[]{:S(2)}) collective-permute-start(f32[32,768]{1,0:T(8,128)} %get-tuple-element.228), channel_id=1, source_target_pairs={{0,16},{4,20},{8,24},{12,28},{16,0},{20,4},{24,8},{28,12},{1,17},{... | collective-permute-start | bytes 294920 | tf_op jit(solution)/shard_map/ppermute | solution.py:20
  268.1 12.6 %collective-permute-start.36 = (bf16[64,1152]{1,0:T(8,128)(2,1)}, bf16[64,1152]{1,0:T(8,128)(2,1)S(1)}, u32[]{:S(2)}, u32[]{:S(2)}) collective-permute-start(bf16[64,1152]{1,0:T(8,128)(2,1)} %get-tuple-element.237), channel_id=1, source_target_pairs={{0,16},{4,20},{8,24},{12,28},{16,0},{20,4},{24,8},{28,12},{1,17},{... | collective-permute-start | bytes 442376 | tf_op jit(solution)/shard_map/ppermute | solution.py:20
  271.4 13.2 %collective-permute-start.37 = (bf16[64,1024]{1,0:T(8,128)(2,1)}, bf16[64,1024]{1,0:T(8,128)(2,1)S(1)}, u32[]{:S(2)}, u32[]{:S(2)}) collective-permute-start(bf16[64,1024]{1,0:T(8,128)(2,1)} %get-tuple-element.245), channel_id=1, source_target_pairs={{0,16},{4,20},{8,24},{12,28},{16,0},{20,4},{24,8},{28,12},{1,17},{... | collective-permute-start | bytes 393224 | tf_op jit(solution)/shard_map/ppermute | solution.py:20
  (69 other events, 1067.4 us)

commit v2 on v1

--- a/solution.py
+++ b/solution.py
@@ -42,7 +42,7 @@
     def __init__(self):
         self.token = jnp.zeros((8, LANES), F32)
 
-    def __call__(self, kernel, outs, *args, scratch=(), smem=(), direct=False, after=()):
+    def __call__(self, kernel, outs, *args, scratch=(), smem=(), direct=False, after=(), alias=None):
         plain = pl.ANY if direct else pltpu.VMEM
         specs = [
             pl.BlockSpec(memory_space=pltpu.SMEM if i in smem else plain)
@@ -66,10 +66,16 @@
             scratch_shapes=[pltpu.VMEM(s, d) if d is not None else s for s, d in scratch],
             compiler_params=pltpu.CompilerParams(vmem_limit_bytes=56 << 20),
             cost_estimate=pl.CostEstimate(flops=0, bytes_accessed=0, transcendentals=0),
+            input_output_aliases=alias or {},
         )(*args, *extra)
         self.token = results[0]
         return results[1:]
 
+    def touch(self, value):
+        return self(
+            lambda *refs: None, [(value.shape, value.dtype)], value, direct=True, alias={0: 1}
+        )[0]
+
 
 def iota(shape, dim):
     return lax.broadcasted_iota(jnp.int32, shape, dim)
@@ -84,41 +90,54 @@
     return fine(jnp.ones((8, values.shape[1]), F32), values, ((1,), (1,)))
 
 
-def pieces_kernel(place, wm, wa, wd, gu, cot, t_out, g_out, c_out, sem):
-    piece = t_out.shape[1]
+def pieces_kernel(place, wm, wa, wd, cot, hid, out):
+    piece = out.shape[1]
     at = pl.multiple_of(place[1] * piece, piece)
-    parts = []
     row = 0
     for w in (wm, wa, wd):
-        size = w.shape[0]
-        parts.append((w.at[:, pl.ds(at, piece)], t_out.at[row : row + size]))
-        row += size
-    parts.append((gu.at[pl.ds(at, piece)], g_out))
-    parts.append((cot, c_out))
-    copies = [pltpu.make_async_copy(s, d, sem.at[i]) for i, (s, d) in enumerate(parts)]
-    for copy in copies:
-        copy.start()
-    for copy in copies:
-        copy.wait()
-
-
-def gather_quarters(place, mine, over_col, over_row, over_both, own_out, far_out, far_tmp):
-    width = mine.shape[1]
+        out[row : row + w.shape[0]] = w[:, pl.ds(at, piece)]
+        row += w.shape[0]
+    for value in (cot, hid):
+        for j in range(value.shape[1] // piece):
+            out[row : row + value.shape[0]] = value[:, j * piece : (j + 1) * piece]
+            row += value.shape[0]
+
+
+def split_kernel(got, cot, hid, first_out, pair_out):
+    size = first_out.shape[0]
+    tokens = cot.shape[0]
+    piece = got.shape[1]
+    first_out[...] = got[0:size]
+    for i, value in enumerate((cot, hid)):
+        at = 2 * i * tokens
+        pair_out[at : at + tokens] = value[...]
+        for j in range(value.shape[1] // piece):
+            pair_out[at + tokens : at + 2 * tokens, j * piece : (j + 1) * piece] = got[
+                size + at + j * tokens : size + at + (j + 1) * tokens
+            ]
+
+
+def gather_quarters(place, mine, came, at, own_out, far_out, far_tmp):
+    width = own_out.shape[1] // 2
     piece = width // 2
     first = place[0] == 0
-    for a, b, out in ((mine, over_col, own_out), (over_row, over_both, far_tmp)):
-        out[:, :width] = jnp.where(first, a[...], b[...])
-        out[:, width:] = jnp.where(first, b[...], a[...])
+    tokens = own_out.shape[0]
+    for i, out in enumerate((own_out, far_tmp)):
+        rows = slice((at + i) * tokens, (at + i + 1) * tokens)
+        a = mine[rows]
+        b = came[rows]
+        out[:, :width] = jnp.where(first, a, b)
+        out[:, width:] = jnp.where(first, b, a)
     for j in range(4):
         at = pl.multiple_of((place[1] ^ j) * piece, piece)
         far_out[:, j * piece : (j + 1) * piece] = far_tmp[:, pl.ds(at, piece)]
 
 
 def project_kernel(
-    place, mine, over_col, over_row, over_both, gain, wx, wb, wd, wg, wq, wk,
+    place, mine, came, gain, wx, wb, wd, wg, wq, wk,
     n1_out, p_out, low_out, own_out, far_out, factor_out, far_tmp,
 ):
-    gather_quarters(place, mine, over_col, over_row, over_both, own_out, far_out, far_tmp)
+    gather_quarters(place, mine, came, 2, own_out, far_out, far_tmp)
     own = own_out[...].astype(F32)
     far = far_tmp[...].astype(F32)
     mean = jnp.sum(own * own + far * far, axis=1, keepdims=True) / (2 * own.shape[1])
@@ -192,8 +211,8 @@
 
 
 def mix_kernel(
-    ch, nq, seg_row, seg_col, own, came, x_par, bc_par, head_par, wm, wa, first, second, pair,
-    mixed_out, sums_out, pre_out, y_out, part_out,
+    ch, nq, seg_row, seg_col, own, came, x_par, bc_par, head_par,
+    mixed_out, sums_out, pre_out, y_out,
 ):
     tokens = own.shape[0]
     nbc = bc_par.shape[1]
@@ -249,10 +268,6 @@
         mixed_out[:, ch + p * LANES : ch + (p + 1) * LANES] = jnp.where(
             low, outs[0], outs[1]
         ).astype(BF16)
-    half = wm.shape[1]
-    value = mixed_out[...]
-    part_out[:, :half] = dot(value[:, :ch], wm[...]) + dot(value[:, ch:], wa[...])
-    part_out[:, half:] = dot(value, tall_far(first, second, pair, 0, ch + nq))
 
 
 def unmix_two_kernel(ch, nq, seg_row, seg_col, sums, pre, ys, dym, x_par, gtwo_out):
@@ -379,15 +394,22 @@
     )
 
 
+def out_kernel(mixed, wm, wa, first, second, pair, part_out):
+    half = wm.shape[1]
+    ch = wm.shape[0]
+    value = mixed[...]
+    part_out[:, :half] = dot(value[:, :ch], wm[...]) + dot(value[:, ch:], wa[...])
+    part_out[:, half:] = dot(value, tall_far(first, second, pair, 0, value.shape[1]))
+
+
 def norm_factor(value):
     return lax.rsqrt(jnp.mean(value * value, axis=1, keepdims=True) + NORM_EPS)
 
 
 def act_grad_kernel(
-    inner, place, mine, over_col, over_row, over_both, wd, first, second, pair,
-    own_out, far_out, ga_out, far_tmp,
+    inner, place, mine, came, wd, first, second, pair, own_out, far_out, ga_out, far_tmp
 ):
-    gather_quarters(place, mine, over_col, over_row, over_both, own_out, far_out, far_tmp)
+    gather_quarters(place, mine, came, 0, own_out, far_out, far_tmp)
     ff = wd.shape[0]
     ga_out[...] = dot_bt(own_out[...], wd[...]) + dot_bt(
         far_out[...], tall_far(first, second, pair, inner, ff)
@@ -492,22 +514,24 @@
     pair_grad(permuted(n1[...], order[...]), g_two[...], send_out, keep_out, 0, 0, keep_out.shape[0])
 
 
-def back_kernel(g_two, gx, gdt, both, wx, wb, wd, wg, wq, wk, n1p_out, n1b_out):
+def back_kernel(
+    g_two, gx, gdt, gbc, gbc_came, wx, wb, wd, wg, wq, wk, n1p_out, n1b_out, both_out
+):
+    tokens = gx.shape[0]
+    both = (gbc[0:tokens] + gbc_came[0:tokens]).astype(BF16)
+    both_out[...] = both
     ch = wg.shape[1]
     nq = wq.shape[1]
     total = dot_bt(gx[...], wx[...]) + dot_bt(gdt[...], wd[...])
     total = total + dot_bt(g_two[:, :ch], wg[...]) + dot_bt(g_two[:, ch : ch + nq], wq[...])
     n1p_out[...] = total + dot_bt(g_two[:, ch + nq :], wk[...])
-    n1b_out[...] = dot_bt(both[...], wb[...])
-
-
-def grad_one_kernel(n1, gx, gdt, gbc, gbc_came, order, send_out, keep_out, both_out):
-    tokens = n1.shape[0]
+    n1b_out[...] = dot_bt(both, wb[...])
+
+
+def grad_one_kernel(n1, gx, gdt, both, order, send_out, keep_out):
     left = permuted(n1[...], order[...])
-    both = (gbc[0:tokens] + gbc_came[0:tokens]).astype(BF16)
-    both_out[...] = both
     at = 0
-    for right in (gx[...], both, gdt[...]):
+    for right in (gx[...], both[...], gdt[...]):
         pair_grad(left, right, send_out, keep_out, at, 0, keep_out.shape[0])
         at += right.shape[1]
 
@@ -555,6 +579,15 @@
     vector_out[...] = vector[...] + vector_came[...]
 
 
+def join_kernel(keep_a, came_a, keep_b, came_b, send_out, keep_out):
+    rows, width = keep_out.shape
+    width = width // 2
+    for i, (keep, came) in enumerate(((keep_a, came_a), (keep_b, came_b))):
+        total = keep[...] + came[...].astype(F32)
+        send_out[:, i * width : (i + 1) * width] = total[rows:].astype(BF16)
+        keep_out[:, i * width : (i + 1) * width] = total[:rows]
+
+
 def last_kernel(keep, came, *outs):
     total = keep[...] + came[...].astype(F32)
     at = 0
@@ -566,11 +599,11 @@
 def last_tall_kernel(keep, came, *outs):
     total = keep[...] + came[...].astype(F32)
     width = outs[0].shape[1]
-    tall = jnp.concatenate([total[:, :width], total[:, width:]], axis=0)
-    at = 0
-    for out in outs:
-        out[...] = tall[at : at + out.shape[0]]
-        at += out.shape[0]
+    outs[0][...] = jnp.concatenate([total[:, :width], total[:, width : 2 * width]], axis=0)
+    tall = jnp.concatenate([total[:, 2 * width : 3 * width], total[:, 3 * width :]], axis=0)
+    size = outs[1].shape[0]
+    outs[1][...] = tall[:size]
+    outs[2][...] = tall[size:]
 
 
 def halving_order(steps):
@@ -581,10 +614,10 @@
 
 
 class Scatter:
-    def __init__(self, run, steps, send, keep, last, outs, vector=None):
+    def __init__(self, run, steps, send, keep, last=None, outs=(), at=0):
         self.run, self.steps, self.last, self.outs = run, steps, last, outs
-        self.at, self.keep, self.vector = 0, keep, vector
-        self.came = swap(send, "dp", steps[0])
+        self.at, self.keep, self.vector = at, keep, None
+        self.came = swap(send, "dp", steps[at])
         self.results = None
 
     def add_vector(self, vector):
@@ -661,22 +694,26 @@
     run = Chain()
     cols = ch + nbc + LANES + ch + nq + nkv
     inner = ch + nq
-    over_row = swap(hidden, "row")
-    over_col = swap(hidden, "col")
-    over_both = swap(over_row, "col")
-
+
+    t_mine = run(
+        pieces_kernel,
+        [((inner + ff + 4 * tokens, piece), BF16)],
+        place, w_mixout, w_attnout, w_down, cotangent, hidden,
+        smem=(0,),
+    )[0]
+    t_got = swap(t_mine, "row")
     gu = w_gateup.reshape(half, 2 * ff)
-    t_mine, g_mine, cot = run(
-        pieces_kernel,
-        [((inner + ff, piece), BF16), ((piece, 2 * ff), BF16), ((tokens, quarter), BF16)],
-        place, w_mixout, w_attnout, w_down, gu, cotangent,
-        smem=(0,), direct=True, after=(over_row,), scratch=[(pltpu.SemaphoreType.DMA((5,)), None)],
-    )
-    t_first = swap(t_mine, "row")
-    g_first = swap(g_mine, "row")
+    g_first = swap(lax.dynamic_slice_in_dim(gu, spot * piece, piece, 0), "row")
     wk = w_kv.reshape(half, nkv)
     wd = jnp.pad(w_dt, ((0, 0), (0, LANES - heads)))
     gain_one = norm1_gain.astype(F32)[None]
+    t_first, in_pair = run(
+        split_kernel,
+        [((inner + ff, piece), BF16), ((4 * tokens, quarter), BF16)],
+        t_got, cotangent, hidden,
+    )
+    t_second = swap(t_first, "dp", 1)
+    in_came = swap(in_pair, "col")
     n1, part, part_low, own, far, factor1 = run(
         project_kernel,
         [
@@ -687,14 +724,11 @@
             ((tokens, half), BF16),
             ((tokens, LANES), F32),
         ],
-        place, hidden, over_col, over_row, over_both, gain_one, w_xin, w_bc, wd, w_gate, w_query, wk,
+        place, in_pair, in_came, gain_one, w_xin, w_bc, wd, w_gate, w_query, wk,
         smem=(0,), scratch=[((tokens, half), BF16)],
     )
     part_came = swap(part_low, "row")
-    cot_row = swap(cot, "row")
-    cot_col = swap(cot, "col")
-    cot_both = swap(cot_row, "col")
-    t_second = swap(t_first, "dp", 1)
+    g_first = run.touch(g_first)
     g_second = swap(g_first, "dp", 2)
     t_cat, g_cat = run(
         hop_kernel,
@@ -749,35 +783,38 @@
 
     near_block = block_order(near)
     turned_block = block_order(turned)
+    turned_both = jnp.concatenate([turned_block] * 2)
     order_near = (near_block * size + within)[None]
-    order_turned = (turned_block * size + within)[None]
-    order_down = (jnp.concatenate([turned_block] * 2) * (ff // count) + both_within)[None]
+    order_down = (turned_both * (ff // count) + both_within)[None]
     m_rows = ch // count
     a_rows = nq // count
-    near_both = jnp.concatenate([near_block] * 2)
     order_mix = jnp.where(
         both_within < m_rows,
-        near_both * m_rows + both_within,
-        ch + near_both * a_rows + both_within - m_rows,
+        turned_both * m_rows + both_within,
+        ch + turned_both * a_rows + both_within - m_rows,
     )[None]
 
-    dy_own, dy_far, grad_act = run(
-        lambda *refs: act_grad_kernel(inner, *refs),
-        [((tokens, half), BF16), ((tokens, half), BF16), ((tokens, ff), F32)],
-        place, cot, cot_col, cot_row, cot_both, w_down, t_first, t_second, t_pair,
-        smem=(0,), scratch=[((tokens, half), BF16)],
-    )
-    mixed, raw, pre, ys, mix_part = run(
+    mixed, raw, pre, ys = run(
         lambda *refs: mix_kernel(ch, nq, *refs),
         [
             ((tokens, inner), BF16),
             ((tokens, cols), F32),
             ((tokens, ch + nbc), F32),
             ((tokens, ch), F32),
-            ((tokens, full_width), F32),
         ],
         seg_row, seg_col, part, part_came, x_par, bc_par, head_par,
-        w_mixout, w_attnout, t_first, t_second, t_pair,
+    )
+    mix_part = run(
+        out_kernel,
+        [((tokens, full_width), F32)],
+        mixed, w_mixout, w_attnout, t_first, t_second, t_pair,
+    )[0]
+    mix_came = swap(mix_part, "col")
+    dy_own, dy_far, grad_act = run(
+        lambda *refs: act_grad_kernel(inner, *refs),
+        [((tokens, half), BF16), ((tokens, half), BF16), ((tokens, ff), F32)],
+        place, in_pair, in_came, w_down, t_first, t_second, t_pair,
+        smem=(0,), scratch=[((tokens, half), BF16)],
     )
     h2, n2, act, ggu, n2_part, down_keep, down_send = run(
         feed_kernel,
@@ -790,7 +827,7 @@
             ((tokens, quarter), F32),
             ((tokens, quarter), F32),
         ],
-        place, own, far, mix_part, swap(mix_part, "col"), gain_two,
+        place, own, far, mix_part, mix_came, gain_two,
         gu, g_first, g_second, g_pair, grad_act, w_down,
         smem=(0,),
     )
@@ -805,9 +842,7 @@
         feed_grad_kernel, halves(2 * ff) + halves(2 * half), n2, act, ggu, dy_own, order_near, order_down
     )
     s_gu = Scatter(run, near, g_send, g_keep, last_kernel, [((size, 2 * ff), F32)])
-    s_down = Scatter(
-        run, turned, d_send, d_keep, last_tall_kernel, [((2 * size, half), F32)]
-    )
+    s_down = Scatter(run, turned, d_send, d_keep)
     dym, resid, low, gain2_sum, output = run(
         turn_kernel,
         [
@@ -831,6 +866,8 @@
         run, near, two_send, two_keep, last_kernel,
         [((size, ch), F32), ((size, nq), F32), ((size, nkv), F32)],
     )
+    m_send, m_keep = run(mix_grad_kernel, halves(2 * half), mixed, low, order_mix)
+    s_mix = Scatter(run, turned, m_send, m_keep)
     s_down.advance()
     gx, gdt, gbc, small_sum = run(
         lambda *refs: unmix_one_kernel(ch, nq, *refs),
@@ -844,28 +881,22 @@
         scratch=[((tokens, ch), F32), ((tokens, ch), F32), ((tokens, tokens), F32)],
     )
     gbc_came = swap(gbc, "col")
-    m_send, m_keep = run(mix_grad_kernel, halves(2 * half), mixed, low, order_mix)
-    s_mix = Scatter(
-        run, near, m_send, m_keep, last_tall_kernel,
-        [((m_rows, half), F32), ((a_rows, half), F32)],
-    )
-    one_send, one_keep, gbc_both = run(
-        grad_one_kernel,
-        halves(ch + nbc + LANES) + [((tokens, nbc), BF16)],
-        n1, gx, gdt, gbc, gbc_came, order_turned,
+    n1_part, n1_bc, gbc_both = run(
+        back_kernel,
+        [((tokens, half), F32), ((tokens, half), F32), ((tokens, nbc), BF16)],
+        g_two, gx, gdt, gbc, gbc_came, w_xin, w_bc, wd, w_gate, w_query, wk,
+    )
+    n1_came = swap(n1_part, "col")
+    s_gu.advance()
+    s_mix.advance()
+    s_two.advance()
+    one_send, one_keep = run(
+        grad_one_kernel, halves(ch + nbc + LANES), n1, gx, gdt, gbc_both, order_near
     )
     s_one = Scatter(
-        run, turned, one_send, one_keep, last_kernel,
+        run, near, one_send, one_keep, last_kernel,
         [((size, ch), F32), ((size, nbc), F32), ((size, LANES), F32)],
     )
-    s_gu.advance()
-    n1_part, n1_bc = run(
-        back_kernel,
-        [((tokens, half), F32), ((tokens, half), F32)],
-        g_two, gx, gdt, gbc_both, w_xin, w_bc, wd, w_gate, w_query, wk,
-    )
-    n1_came = swap(n1_part, "col")
-    s_two.advance()
     dn1, sum_rows = run(
         close_kernel,
         [((tokens, half), F32), ((16, tokens), F32)],
@@ -873,7 +904,6 @@
     )
     rows_far = swap(sum_rows, "row")
     s_gu.advance()
-    s_down.advance()
     grad_hidden, vector = run(
         end_kernel,
         [((tokens, quarter), F32), ((32, ch), F32)],
@@ -882,15 +912,24 @@
     )
     s_one.add_vector(vector)
     s_one.advance()
-    s_mix.advance()
-    scatters = (s_two, s_gu, s_down, s_one, s_mix)
+    tall_send, tall_keep = run(
+        join_kernel,
+        [((rows // 4, 4 * half), BF16), ((rows // 4, 4 * half), F32)],
+        s_down.keep, s_down.came, s_mix.keep, s_mix.came,
+    )
+    s_tall = Scatter(
+        run, turned, tall_send, tall_keep, last_tall_kernel,
+        [((2 * size, half), F32), ((m_rows, half), F32), ((a_rows, half), F32)],
+        at=2,
+    )
+    scatters = (s_two, s_gu, s_one, s_tall)
     while any(s.results is None for s in scatters):
         for s in scatters:
             s.advance()
     vector = s_one.vector
     r_gate, r_query, r_kv = s_two.results
     r_xin, r_bc, r_dt = s_one.results
-    r_mixout, r_attnout = s_mix.results
+    r_down, r_mixout, r_attnout = s_tall.results
 
     def mine(values, width):
         return lax.dynamic_slice_in_dim(values, row * width, width, values.ndim - 1)
@@ -916,7 +955,7 @@
         r_attnout,
         vector[25, :half],
         s_gu.results[0].reshape(size, 2, ff),
-        s_down.results[0],
+        r_down,
     )
 
 

time: 288 us -> 251 us (0.87)
  Pallas kernels: 141 us -> 108 us
    pallas_call x31 -> x32, Pallas kernels: 141 us -> 108 us  [__call__(): pl.pallas_call(body, out_shape=[jax.ShapeDtypeStruct((8, LANES), F32)] +...]
    ppermute x38 -> x32, waiting for transfers between devices: 68.6 us -> 66.4 us  [swap(): return lax.ppermute(values, axis, [(i, i ^ step) for i in range(count)])]
    unnamed x133 -> x113, local copies, waits for them, and re-layouts: 22.5 us -> 20.7 us
    ppermute x38 -> x32, starting transfers between devices: 38.3 us -> 37.8 us  [swap(): return lax.ppermute(values, axis, [(i, i ^ step) for i in range(count)])]
  transfers between devices with their start and end apart: 38 -> 32, of which waited for: 9 -> 11; matrix products, arithmetic and copies ran while one was open for 7% -> 6% of each run, Pallas kernels for 33% -> 37%
where the time goes in v2:
time: 251 us; the launch traced here: 250 us
  Pallas kernels  108 us (43%)
  waiting for transfers between devices  66.4 us (26%)
  starting transfers between devices  37.8 us (15%)
  local copies, waits for them, and re-layouts  31.8 us (13%)
  other arithmetic  4.58 us (2%)
    pallas_call x32, Pallas kernels, __call__(): pl.pallas_call(body, out_shape=[jax.ShapeDtypeStruct((8, LANES), F32)] +...  108 us
    ppermute x32, waiting for transfers between devices, swap(): return lax.ppermute(values, axis, [(i, i ^ step) for i in range(count)])  66.4 us
    ppermute x32, starting transfers between devices, swap(): return lax.ppermute(values, axis, [(i, i ^ step) for i in range(count)])  37.8 us
    unnamed x113, local copies, waits for them, and re-layouts  20.7 us
  transfers between devices with their start and end apart: 32, of which 11 were waited for; matrix products, arithmetic and copies ran while one was open for 6% of the time, Pallas kernels for 37%

profile of v2, /device:TPU:0, one launch (start us, length us, event | category | flops | bytes accessed | tf_op | source)
XLA Modules:
  0.0 249.7 jit_solution(7316710030029990253)
XLA Ops:
  1.9 2.6 %shard_map.400 = (f32[8,128]{1,0:T(8,128)}, bf16[3072,128]{1,0:T(8,128)(2,1)}) custom-call(s32[3]{0:T(128)} %pad_add_fusion.1.refs_0_, bf16[768,512]{1,0:T(8,128)(2,1)} %refs_7_.3, bf16[256,512]{1,0:T(8,128)(2,1)} %refs_8_.4, bf16[1024,512]{1,0:T(8,128)(2,1)} %refs_11_.1, bf16[256,256]{1,0:T(8,128)(2,1)} %refs_1_.4, bf16[256,256]{1,0:T(8,128)(2,1)} %refs_2_.4, ...), custom_call_target="tpu_custom_call" | custom-call | tf_op jit(solution)/shard_map/pallas_call | solution.py:59
  4.5 3.0 %collective-permute-start = (bf16[3072,128]{1,0:T(8,128)(2,1)}, bf16[3072,128]{1,0:T(8,128)(2,1)S(1)}, u32[]{:S(2)}, u32[]{:S(2)}) collective-permute-start(bf16[3072,128]{1,0:T(8,128)(2,1)} %get-tuple-element.136), channel_id=1, source_target_pairs={{0,2},{2,0},{1,3},{3,1},{4,6},{6,4},{5,7},{7,5},{8,10},{10,8},{9,1... | collective-permute-start | bytes 2359304 | tf_op jit(solution)/shard_map/ppermute | solution.py:20
  8.1 17.1 %collective-permute-done.refs_0_ = bf16[3072,128]{1,0:T(8,128)(2,1)S(1)} collective-permute-done((bf16[3072,128]{1,0:T(8,128)(2,1)}, bf16[3072,128]{1,0:T(8,128)(2,1)S(1)}, u32[]{:S(2)}, u32[]{:S(2)}) %collective-permute-start) | collective-permute-done | bytes 786464 | tf_op jit(solution)/shard_map/ppermute | solution.py:20
  34.0 4.9 %shard_map.402 = (f32[8,128]{1,0:T(8,128)}, bf16[256,512]{1,0:T(8,128)(2,1)}, f32[256,2304]{1,0:T(8,128)}, bf16[256,2304]{1,0:T(8,128)(2,1)}, bf16[256,512]{1,0:...) custom-call(s32[3]{0:T(128)} %pad_add_fusion.1.refs_0_, bf16[1024,256]{1,0:T(8,128)(2,1)} %get-tuple-element.138.refs_1_, ...), custom_call_target="tpu_custom_call" | custom-call | tf_op jit(solution)/shard_map/pallas_call | solution.py:59
  38.8 4.9 %collective-permute-done.3.refs_0_ = bf16[128,2048]{1,0:T(8,128)(2,1)S(1)} collective-permute-done((bf16[128,2048]{1,0:T(8,128)(2,1)}, bf16[128,2048]{1,0:T(8,128)(2,1)S(1)}, u32[]{:S(2)}, u32[]{:S(2)}) %collective-permute-start.3) | collective-permute-done | bytes 524320 | tf_op jit(solution)/shard_map/ppermute | solution.py:20
  50.1 8.8 %collective-permute-done.4.refs_3_.refs_8_ = bf16[128,2048]{1,0:T(8,128)(2,1)S(1)} collective-permute-done((bf16[128,2048]{1,0:T(8,128)(2,1)}, bf16[128,2048]{1,0:T(8,128)(2,1)S(1)}, u32[]{:S(2)}, u32[]{:S(2)}) %collective-permute-start.4) | collective-permute-done | bytes 524320 | tf_op jit(solution)/shard_map/ppermute | solution.py:20
  59.8 3.0 %shard_map.404 = (f32[8,128]{1,0:T(8,128)}, bf16[2048,256]{1,0:T(8,128)(2,1)}, bf16[256,2048]{1,0:T(8,128)(2,1)}) custom-call(bf16[2048,128]{1,0:T(8,128)(2,1)} %get-tuple-element.139.refs_0_.refs_3_.refs_4_.refs_9_, bf16[2048,128]{1,0:T(8,128)(2,1)} %copy-done.2, bf16[128,2048]{1,0:T(8,128)(2,1)} %get-tuple-element.142.refs_2_.refs_7_, ...), custom_call_target="tpu_custom_call" | custom-call | tf_op jit(solution)/shard_map/pallas_call | solution.py:59
  67.9 9.0 %collective-permute-done.6.refs_3_ = bf16[256,2304]{1,0:T(8,128)(2,1)} collective-permute-done((bf16[256,2304]{1,0:T(8,128)(2,1)}, bf16[256,2304]{1,0:T(8,128)(2,1)}, u32[]{:S(2)}, u32[]{:S(2)}) %collective-permute-start.6) | collective-permute-done | bytes 1179680 | tf_op jit(solution)/shard_map/ppermute | solution.py:20
  77.7 6.7 %shard_map.405 = (f32[8,128]{1,0:T(8,128)}, bf16[256,1024]{1,0:T(8,128)(2,1)}, f32[256,2304]{1,0:T(8,128)}, f32[256,1024]{1,0:T(8,128)}, f32[256,768]{1,0:T(8,128)}) custom-call(f32[1,256]{1,0:T(1,128)} %copy-done.31, f32[256,128]{1,0:T(8,128)} %broadcast_in_dim.32.refs_1_, f32[256,2304]{1,0:T(8,128)} %get-tuple-element.145.refs_2_, ...), custom_call_target="tpu_custom_call" | custom-call | tf_op jit(solution)/shard_map/pallas_call | solution.py:59
  84.4 2.7 %collective-permute-done.5.refs_5_.refs_6_.refs_11_ = bf16[2048,256]{1,0:T(8,128)(2,1)S(1)} collective-permute-done((bf16[2048,256]{1,0:T(8,128)(2,1)}, bf16[2048,256]{1,0:T(8,128)(2,1)S(1)}, u32[]{:S(2)}, u32[]{:S(2)}) %collective-permute-start.5) | collective-permute-done | bytes 1048608 | tf_op jit(solution)/shard_map/ppermute | solution.py:20
  88.1 3.7 %shard_map.406 = (f32[8,128]{1,0:T(8,128)}, f32[256,1024]{1,0:T(8,128)}) custom-call(bf16[256,1024]{1,0:T(8,128)(2,1)} %get-tuple-element.148.refs_0_, bf16[768,512]{1,0:T(8,128)(2,1)} %refs_7_.3, bf16[256,512]{1,0:T(8,128)(2,1)} %refs_8_.4, bf16[2048,128]{1,0:T(8,128)(2,1)} %get-tuple-element.139.refs_0_.refs_3_.refs_4_.refs_9_, ...), custom_call_target="tpu_custom_call" | custom-call | tf_op jit(solution)/shard_map/pallas_call | solution.py:59
  92.8 3.9 %shard_map.407 = (f32[8,128]{1,0:T(8,128)}, bf16[256,512]{1,0:T(8,128)(2,1)}, bf16[256,512]{1,0:T(8,128)(2,1)}, f32[256,1024]{1,0:T(8,128)}) custom-call(s32[3]{0:T(128)} %pad_add_fusion.1.refs_0_, bf16[1024,256]{1,0:T(8,128)(2,1)} %get-tuple-element.138.refs_1_, bf16[1024,256]{1,0:T(8,128)(2,1)} %collective-permute-done.1.refs_2_, ...), custom_call_target="tpu_custom_call" | custom-call | tf_op jit(solution)/shard_map/pallas_call | solution.py:59
  98.1 7.8 %shard_map.408 = (f32[8,128]{1,0:T(8,128)}, f32[256,1024]{1,0:T(8,128)}, bf16[256,512]{1,0:T(8,128)(2,1)}, bf16[256,1024]{1,0:T(8,128)(2,1)}, bf16[256,2048]{1,0...) custom-call(s32[3]{0:T(128)} %pad_add_fusion.1.refs_0_, ...), custom_call_target="tpu_custom_call" | custom-call | tf_op jit(solution)/shard_map/pallas_call | solution.py:59
  107.7 5.4 %shard_map.409 = (f32[8,128]{1,0:T(8,128)}, bf16[256,2048]{1,0:T(8,128)(2,1)}, f32[256,2048]{1,0:T(8,128)}, bf16[256,1024]{1,0:T(8,128)(2,1)}, f32[256,1024]{1,0:T(8,128)}) custom-call(bf16[256,512]{1,0:T(8,128)(2,1)} %get-tuple-element.163.refs_0_, bf16[256,1024]{1,0:T(8,128)(2,1)} %get-tuple-element.164.refs_1_, ...), custom_call_target="tpu_custom_call" | custom-call | tf_op jit(solution)/shard_map/pallas_call | solution.py:59
  117.4 5.3 %shard_map.410 = (f32[8,128]{1,0:T(8,128)}, f32[256,1024]{1,0:T(8,128)}, f32[256,512]{1,0:T(8,128)}, bf16[256,512]{1,0:T(8,128)(2,1)}, f32[8,512]{1,0:T(8,128)}, /*index=5*/bf16[256,256]{1,0:T(8,128)(2,1)}) custom-call(s32[3]{0:T(128)} %pad_add_fusion.1.refs_0_, bf16[256,512]{1,0:T(8,128)(2,1)} %get-tuple-element.151.refs_3_.refs_1_, ...), custom_call_target="tpu_custom_call" | custom-call | tf_op jit(solution)/shard_map/pallas_call | solution.py:59
  122.7 5.6 %shard_map.411 = (f32[8,128]{1,0:T(8,128)}, bf16[256,1152]{1,0:T(8,128)(2,1)}) custom-call(f32[1,256]{1,0:T(1,128)} %copy-done.31, f32[256,128]{1,0:T(8,128)} %broadcast_in_dim.32.refs_1_, f32[256,2304]{1,0:T(8,128)} %get-tuple-element.171.refs_2_, f32[256,1024]{1,0:T(8,128)} %get-tuple-element.172.refs_3_, f32[256,768]{1,0:T(8,128)} %get-tuple-element.173.refs_4_, ...), custom_call_target="tpu_custom_call" | custom-call | tf_op jit(solution)/shard_map/pallas_call | solution.py:59
  128.3 3.1 %shard_map.412 = (f32[8,128]{1,0:T(8,128)}, bf16[256,1152]{1,0:T(8,128)(2,1)}, f32[256,1152]{1,0:T(8,128)}) custom-call(bf16[256,512]{1,0:T(8,128)(2,1)} %get-tuple-element.180.refs_0_, bf16[256,1152]{1,0:T(8,128)(2,1)} %get-tuple-element.176.refs_1_.refs_0_, s32[1,512]{1,0:T(1,128)} %bitcast.53, f32[8,128]{1,0:T(8,128)} %get-tuple-element.181.refs_3_), custom_call_target="tpu_custom_call" | custom-call | tf_op jit(solution)/shard_map/pallas_call | solution.py:59
  131.9 3.3 %shard_map.413 = (f32[8,128]{1,0:T(8,128)}, bf16[256,1024]{1,0:T(8,128)(2,1)}, f32[256,1024]{1,0:T(8,128)}) custom-call(bf16[256,1024]{1,0:T(8,128)(2,1)} %get-tuple-element.148.refs_0_, bf16[256,512]{1,0:T(8,128)(2,1)} %get-tuple-element.179.refs_1_, s32[1,1024]{1,0:T(1,128)} %get-tuple-element.297.refs_2_, f32[8,128]{1,0:T(8,128)} %get-tuple-element.182.refs_3_), custom_call_target="tpu_custom_call" | custom-call | tf_op jit(solution)/shard_map/pallas_call | solution.py:59
  139.8 9.0 %shard_map.415 = (f32[8,128]{1,0:T(8,128)}, bf16[256,768]{1,0:T(8,128)(2,1)}, bf16[256,128]{1,0:T(8,128)(2,1)}, f32[264,256]{1,0:T(8,128)}, f32[16,768]{1,0:T(8,128)}) custom-call(f32[1,256]{1,0:T(1,128)} %copy-done.31, f32[256,128]{1,0:T(8,128)} %broadcast_in_dim.32.refs_1_, f32[256,2304]{1,0:T(8,128)} %get-tuple-element.171.refs_2_, ...), custom_call_target="tpu_custom_call" | custom-call | tf_op jit(solution)/shard_map/pallas_call | solution.py:59
  151.3 3.8 %shard_map.416 = (f32[8,128]{1,0:T(8,128)}, f32[256,512]{1,0:T(8,128)}, f32[256,512]{1,0:T(8,128)}, bf16[256,256]{1,0:T(8,128)(2,1)}) custom-call(bf16[256,1152]{1,0:T(8,128)(2,1)} %get-tuple-element.176.refs_1_.refs_0_, bf16[256,768]{1,0:T(8,128)(2,1)} %get-tuple-element.185.refs_1_, bf16[256,128]{1,0:T(8,128)(2,1)} %get-tuple-element.186.refs_2_, ...), custom_call_target="tpu_custom_call" | custom-call | tf_op jit(solution)/shard_map/pallas_call | solution.py:59
  156.2 3.1 %shard_map.417 = (f32[8,128]{1,0:T(8,128)}, bf16[128,2048]{1,0:T(8,128)(2,1)}, f32[128,2048]{1,0:T(8,128)}) custom-call(f32[256,2048]{1,0:T(8,128)} %get-tuple-element.196.refs_0_, bf16[256,2048]{1,0:T(8,128)(2,1)} %copy-done.7, f32[8,128]{1,0:T(8,128)} %get-tuple-element.198.refs_2_), custom_call_target="tpu_custom_call" | custom-call | tf_op jit(solution)/shard_map/pallas_call | solution.py:59
  160.7 2.3 shard_map.418
  163.9 2.4 shard_map.419
  166.2 3.2 %shard_map.420 = (f32[8,128]{1,0:T(8,128)}, bf16[256,1152]{1,0:T(8,128)(2,1)}, f32[256,1152]{1,0:T(8,128)}) custom-call(bf16[256,512]{1,0:T(8,128)(2,1)} %get-tuple-element.180.refs_0_, bf16[256,768]{1,0:T(8,128)(2,1)} %get-tuple-element.185.refs_1_, bf16[256,128]{1,0:T(8,128)(2,1)} %get-tuple-element.186.refs_2_, ...), custom_call_target="tpu_custom_call" | custom-call | tf_op jit(solution)/shard_map/pallas_call | solution.py:59
  173.7 2.8 %shard_map.421 = (f32[8,128]{1,0:T(8,128)}, f32[256,512]{1,0:T(8,128)}, f32[16,256]{1,0:T(8,128)}) custom-call(bf16[256,512]{1,0:T(8,128)(2,1)} %get-tuple-element.153.refs_1_.refs_0_, f32[256,512]{1,0:T(8,128)} %get-tuple-element.189.refs_1_, f32[256,512]{1,0:T(8,128)} %copy-done.17, f32[256,512]{1,0:T(8,128)} %get-tuple-element.190.refs_3_, ...), custom_call_target="tpu_custom_call" | custom-call | tf_op jit(solution)/shard_map/pallas_call | solution.py:59
  181.8 2.6 %shard_map.423 = (f32[8,128]{1,0:T(8,128)}, f32[256,256]{1,0:T(8,128)}, f32[32,768]{1,0:T(8,128)}) custom-call(s32[3]{0:T(128)} %pad_add_fusion.1.refs_0_, bf16[256,512]{1,0:T(8,128)(2,1)} %get-tuple-element.153.refs_1_.refs_0_, f32[256,128]{1,0:T(8,128)} %get-tuple-element.169.refs_2_, f32[256,512]{1,0:T(8,128)} %get-tuple-element.170.refs_3_, ...), custom_call_target="tpu_custom_call" | custom-call | tf_op jit(solution)/shard_map/pallas_call | solution.py:59
  186.4 11.9 %collective-permute-done.21.refs_3_ = f32[32,768]{1,0:T(8,128)S(1)} collective-permute-done((f32[32,768]{1,0:T(8,128)}, f32[32,768]{1,0:T(8,128)S(1)}, u32[]{:S(2)}, u32[]{:S(2)}) %collective-permute-start.21) | collective-permute-done | bytes 98336 | tf_op jit(solution)/shard_map/ppermute | solution.py:20
  199.1 2.4 shard_map.424
  203.1 2.6 %collective-permute-start.24 = (bf16[64,2048]{1,0:T(8,128)(2,1)S(1)}, bf16[64,2048]{1,0:T(8,128)(2,1)S(1)}, u32[]{:S(2)}, u32[]{:S(2)}) collective-permute-start(bf16[64,2048]{1,0:T(8,128)(2,1)S(1)} %copy-done.50), channel_id=1, source_target_pairs={{0,16},{4,20},{8,24},{12,28},{16,0},{20,4},{24,8},{28,12},{1,17},{... | collective-permute-start | bytes 786440 | tf_op jit(solution)/shard_map/ppermute | solution.py:20
  212.3 2.6 %collective-permute-start.29 = (bf16[64,1152]{1,0:T(8,128)(2,1)}, bf16[64,1152]{1,0:T(8,128)(2,1)S(1)}, u32[]{:S(2)}, u32[]{:S(2)}) collective-permute-start(bf16[64,1152]{1,0:T(8,128)(2,1)} %get-tuple-element.233), channel_id=1, source_target_pairs={{0,16},{4,20},{8,24},{12,28},{16,0},{20,4},{24,8},{28,12},{1,17},{... | collective-permute-start | bytes 442376 | tf_op jit(solution)/shard_map/ppermute | solution.py:20
  219.1 5.0 %collective-permute-done.23.refs_3_ = f32[32,768]{1,0:T(8,128)S(1)} collective-permute-done((f32[32,768]{1,0:T(8,128)}, f32[32,768]{1,0:T(8,128)S(1)}, u32[]{:S(2)}, u32[]{:S(2)}) %collective-permute-start.23) | collective-permute-done | bytes 98336 | tf_op jit(solution)/shard_map/ppermute | solution.py:20
  226.8 3.4 %collective-permute-start.28 = (f32[32,768]{1,0:T(8,128)}, f32[32,768]{1,0:T(8,128)S(1)}, u32[]{:S(2)}, u32[]{:S(2)}) collective-permute-start(f32[32,768]{1,0:T(8,128)} %get-tuple-element.231), channel_id=1, source_target_pairs={{0,16},{4,20},{8,24},{12,28},{16,0},{20,4},{24,8},{28,12},{1,17},{... | collective-permute-start | bytes 294920 | tf_op jit(solution)/shard_map/ppermute | solution.py:20
  (235 shorter events, 90.6 us)
Async XLA Ops:
  4.5 20.7 %collective-permute-start = (bf16[3072,128]{1,0:T(8,128)(2,1)}, bf16[3072,128]{1,0:T(8,128)(2,1)S(1)}, u32[]{:S(2)}, u32[]{:S(2)}) collective-permute-start(bf16[3072,128]{1,0:T(8,128)(2,1)} %get-tuple-element.136), channel_id=1, source_target_pairs={{0,2},{2,0},{1,3},{3,1},{4,6},{6,4},{5,7},{7,5},{8,10},{10,8},{9,1... | collective-permute-start | bytes 2359304 | tf_op jit(solution)/shard_map/ppermute | solution.py:20
  28.4 5.6 %collective-permute-start.1 = (bf16[1024,256]{1,0:T(8,128)(2,1)}, bf16[1024,256]{1,0:T(8,128)(2,1)}, u32[]{:S(2)}, u32[]{:S(2)}) collective-permute-start(bf16[1024,256]{1,0:T(8,128)(2,1)} %get-tuple-element.138.refs_1_), channel_id=1, source_target_pairs={{0,1},{1,0},{2,3},{3,2},{4,5},{5,4},{6,7},{7,6},{8,9},{9,8},{10,11... | collective-permute-start | bytes 1572872 | tf_op jit(solution)/shard_map/ppermute | solution.py:20
  29.2 14.5 %collective-permute-start.3 = (bf16[128,2048]{1,0:T(8,128)(2,1)}, bf16[128,2048]{1,0:T(8,128)(2,1)S(1)}, u32[]{:S(2)}, u32[]{:S(2)}) collective-permute-start(bf16[128,2048]{1,0:T(8,128)(2,1)} %constant_dynamic-slice_fusion.3), channel_id=1, source_target_pairs={{0,2},{2,0},{1,3},{3,1},{4,6},{6,4},{5,7},{7,5},{8,10},{10,8},{9,1... | collective-permute-start | bytes 1572872 | tf_op jit(solution)/shard_map/ppermute | solution.py:20
  32.5 17.6 %collective-permute-start.2 = (bf16[2048,128]{1,0:T(8,128)(2,1)}, bf16[2048,128]{1,0:T(8,128)(2,1)S(1)}, u32[]{:S(2)}, u32[]{:S(2)}) collective-permute-start(bf16[2048,128]{1,0:T(8,128)(2,1)} %get-tuple-element.139.refs_0_.refs_3_.refs_4_.refs_9_), channel_id=1, source_target_pairs={{0,4},{4,0},{8,12},{12,8},{16,20},{20,16},{24,28},{28,24},{1,5},{5... | collective-permute-start | bytes 1572872 | tf_op jit(solution)/shard_map/ppermute | solution.py:20
  45.1 13.8 %collective-permute-start.4 = (bf16[128,2048]{1,0:T(8,128)(2,1)}, bf16[128,2048]{1,0:T(8,128)(2,1)S(1)}, u32[]{:S(2)}, u32[]{:S(2)}) collective-permute-start(bf16[128,2048]{1,0:T(8,128)(2,1)} %get-tuple-element.142.refs_2_.refs_7_), channel_id=1, source_target_pairs={{0,8},{4,12},{8,0},{12,4},{16,24},{20,28},{24,16},{28,20},{1,9},{5... | collective-permute-start | bytes 1572872 | tf_op jit(solution)/shard_map/ppermute | solution.py:20
  47.1 17.5 %collective-permute-start.7 = (bf16[2450]{0:T(1024)(128)(2,1)S(1)}, bf16[2450]{0:T(1024)(128)(2,1)S(1)}, u32[]{:S(2)}, u32[]{:S(2)}) collective-permute-start(bf16[2450]{0:T(1024)(128)(2,1)S(1)} %concatenate.163), channel_id=1, source_target_pairs={{0,2},{2,0},{1,3},{3,1},{4,6},{6,4},{5,7},{7,5},{8,10},{10,8},{9,1... | collective-permute-start | bytes 14708 | tf_op jit(solution)/shard_map/ppermute | solution.py:20
  49.6 27.4 %collective-permute-start.6 = (bf16[256,2304]{1,0:T(8,128)(2,1)}, bf16[256,2304]{1,0:T(8,128)(2,1)}, u32[]{:S(2)}, u32[]{:S(2)}) collective-permute-start(bf16[256,2304]{1,0:T(8,128)(2,1)} %get-tuple-element.146), channel_id=1, source_target_pairs={{0,2},{2,0},{1,3},{3,1},{4,6},{6,4},{5,7},{7,5},{8,10},{10,8},{9,1... | collective-permute-start | bytes 3538952 | tf_op jit(solution)/shard_map/ppermute | solution.py:20
  62.8 24.3 %collective-permute-start.5 = (bf16[2048,256]{1,0:T(8,128)(2,1)}, bf16[2048,256]{1,0:T(8,128)(2,1)S(1)}, u32[]{:S(2)}, u32[]{:S(2)}) collective-permute-start(bf16[2048,256]{1,0:T(8,128)(2,1)} %get-tuple-element.144), channel_id=1, source_target_pairs={{0,8},{4,12},{8,0},{12,4},{16,24},{20,28},{24,16},{28,20},{1,9},{5... | collective-permute-start | bytes 3145736 | tf_op jit(solution)/shard_map/ppermute | solution.py:20
  66.4 30.3 %collective-permute-start.9 = (bf16[256,2048]{1,0:T(8,128)(2,1)}, bf16[256,2048]{1,0:T(8,128)(2,1)S(1)}, u32[]{:S(2)}, u32[]{:S(2)}) collective-permute-start(bf16[256,2048]{1,0:T(8,128)(2,1)} %get-tuple-element.156), channel_id=1, source_target_pairs={{0,4},{4,0},{8,12},{12,8},{16,20},{20,16},{24,28},{28,24},{1,5},{5... | collective-permute-start | bytes 3145736 | tf_op jit(solution)/shard_map/ppermute | solution.py:20
  91.8 4.9 %collective-permute-start.8 = (f32[256,1024]{1,0:T(8,128)}, f32[256,1024]{1,0:T(8,128)S(1)}, u32[]{:S(2)}, u32[]{:S(2)}) collective-permute-start(f32[256,1024]{1,0:T(8,128)} %get-tuple-element.155.refs_3_), channel_id=1, source_target_pairs={{0,1},{1,0},{2,3},{3,2},{4,5},{5,4},{6,7},{7,6},{8,9},{9,8},{10,11... | collective-permute-start | bytes 3145736 | tf_op jit(solution)/shard_map/ppermute | solution.py:20
  105.9 10.4 %collective-permute-start.10 = (f32[256,1024]{1,0:T(8,128)}, f32[256,1024]{1,0:T(8,128)S(1)}, u32[]{:S(2)}, u32[]{:S(2)}) collective-permute-start(f32[256,1024]{1,0:T(8,128)} %get-tuple-element.160.refs_4_), channel_id=1, source_target_pairs={{0,1},{1,0},{2,3},{3,2},{4,5},{5,4},{6,7},{7,6},{8,9},{9,8},{10,11... | collective-permute-start | bytes 3145736 | tf_op jit(solution)/shard_map/ppermute | solution.py:20
  113.1 42.1 %collective-permute-start.17 = (bf16[256,2048]{1,0:T(8,128)(2,1)}, bf16[256,2048]{1,0:T(8,128)(2,1)S(1)}, u32[]{:S(2)}, u32[]{:S(2)}) collective-permute-start(bf16[256,2048]{1,0:T(8,128)(2,1)} %get-tuple-element.197), channel_id=1, source_target_pairs={{0,4},{4,0},{8,12},{12,8},{16,20},{20,16},{24,28},{28,24},{1,5},{5... | collective-permute-start | bytes 3145736 | tf_op jit(solution)/shard_map/ppermute | solution.py:20
  114.7 1.6 collective-permute-start.11
  114.7 22.0 %collective-permute-start.12 = (bf16[256,1024]{1,0:T(8,128)(2,1)}, bf16[256,1024]{1,0:T(8,128)(2,1)S(1)}, u32[]{:S(2)}, u32[]{:S(2)}) collective-permute-start(bf16[256,1024]{1,0:T(8,128)(2,1)} %get-tuple-element.178), channel_id=1, source_target_pairs={{0,8},{4,12},{8,0},{12,4},{16,24},{20,28},{24,16},{28,20},{1,9},{5... | collective-permute-start | bytes 1572872 | tf_op jit(solution)/shard_map/ppermute | solution.py:20
  131.3 31.7 %collective-permute-start.15 = (bf16[256,1152]{1,0:T(8,128)(2,1)}, bf16[256,1152]{1,0:T(8,128)(2,1)S(1)}, u32[]{:S(2)}, u32[]{:S(2)}) collective-permute-start(bf16[256,1152]{1,0:T(8,128)(2,1)} %get-tuple-element.193), channel_id=1, source_target_pairs={{0,4},{4,0},{8,12},{12,8},{16,20},{20,16},{24,28},{28,24},{1,5},{5... | collective-permute-start | bytes 1769480 | tf_op jit(solution)/shard_map/ppermute | solution.py:20
  135.2 24.7 %collective-permute-start.16 = (bf16[256,1024]{1,0:T(8,128)(2,1)}, bf16[256,1024]{1,0:T(8,128)(2,1)S(1)}, u32[]{:S(2)}, u32[]{:S(2)}) collective-permute-start(bf16[256,1024]{1,0:T(8,128)(2,1)} %get-tuple-element.195), channel_id=1, source_target_pairs={{0,8},{4,12},{8,0},{12,4},{16,24},{20,28},{24,16},{28,20},{1,9},{5... | collective-permute-start | bytes 1572872 | tf_op jit(solution)/shard_map/ppermute | solution.py:20
  148.8 1.8 collective-permute-start.13
  155.1 17.8 %collective-permute-start.14 = (f32[256,512]{1,0:T(8,128)}, f32[256,512]{1,0:T(8,128)S(1)}, u32[]{:S(2)}, u32[]{:S(2)}) collective-permute-start(f32[256,512]{1,0:T(8,128)} %get-tuple-element.189.refs_1_), channel_id=1, source_target_pairs={{0,1},{1,0},{2,3},{3,2},{4,5},{5,4},{6,7},{7,6},{8,9},{9,8},{10,11... | collective-permute-start | bytes 1572872 | tf_op jit(solution)/shard_map/ppermute | solution.py:20
  159.4 18.7 %collective-permute-start.19 = (bf16[128,2048]{1,0:T(8,128)(2,1)}, bf16[128,2048]{1,0:T(8,128)(2,1)S(1)}, u32[]{:S(2)}, u32[]{:S(2)}) collective-permute-start(bf16[128,2048]{1,0:T(8,128)(2,1)} %get-tuple-element.208), channel_id=1, source_target_pairs={{0,8},{4,12},{8,0},{12,4},{16,24},{20,28},{24,16},{28,20},{1,9},{5... | collective-permute-start | bytes 1572872 | tf_op jit(solution)/shard_map/ppermute | solution.py:20
  169.4 28.9 %collective-permute-start.20 = (bf16[256,1152]{1,0:T(8,128)(2,1)}, bf16[256,1152]{1,0:T(8,128)(2,1)S(1)}, u32[]{:S(2)}, u32[]{:S(2)}) collective-permute-start(bf16[256,1152]{1,0:T(8,128)(2,1)} %get-tuple-element.213), channel_id=1, source_target_pairs={{0,4},{4,0},{8,12},{12,8},{16,20},{20,16},{24,28},{28,24},{1,5},{5... | collective-permute-start | bytes 1769480 | tf_op jit(solution)/shard_map/ppermute | solution.py:20
  170.9 34.8 %collective-permute-start.26 = (bf16[128,1024]{1,0:T(8,128)(2,1)S(1)}, bf16[128,1024]{1,0:T(8,128)(2,1)S(1)}, u32[]{:S(2)}, u32[]{:S(2)}) collective-permute-start(bf16[128,1024]{1,0:T(8,128)(2,1)S(1)} %copy-done.48), channel_id=1, source_target_pairs={{0,4},{4,0},{8,12},{12,8},{16,20},{20,16},{24,28},{28,24},{1,5},{5... | collective-permute-start | bytes 786440 | tf_op jit(solution)/shard_map/ppermute | solution.py:20
  171.4 34.3 %collective-permute-start.27 = (bf16[128,1024]{1,0:T(8,128)(2,1)S(1)}, bf16[128,1024]{1,0:T(8,128)(2,1)S(1)}, u32[]{:S(2)}, u32[]{:S(2)}) collective-permute-start(bf16[128,1024]{1,0:T(8,128)(2,1)S(1)} %copy-done.49), channel_id=1, source_target_pairs={{0,4},{4,0},{8,12},{12,8},{16,20},{20,16},{24,28},{28,24},{1,5},{5... | collective-permute-start | bytes 786440 | tf_op jit(solution)/shard_map/ppermute | solution.py:20
  176.5 4.6 %collective-permute-start.18 = (f32[16,256]{1,0:T(8,128)}, f32[16,256]{1,0:T(8,128)S(1)}, u32[]{:S(2)}, u32[]{:S(2)}) collective-permute-start(f32[16,256]{1,0:T(8,128)} %get-tuple-element.204.refs_6_), channel_id=1, source_target_pairs={{0,2},{2,0},{1,3},{3,1},{4,6},{6,4},{5,7},{7,5},{8,10},{10,8},{9,1... | collective-permute-start | bytes 49160 | tf_op jit(solution)/shard_map/ppermute | solution.py:20
  184.3 13.9 %collective-permute-start.21 = (f32[32,768]{1,0:T(8,128)}, f32[32,768]{1,0:T(8,128)S(1)}, u32[]{:S(2)}, u32[]{:S(2)}) collective-permute-start(f32[32,768]{1,0:T(8,128)} %get-tuple-element.214.refs_2_), channel_id=1, source_target_pairs={{0,4},{4,0},{8,12},{12,8},{16,20},{20,16},{24,28},{28,24},{1,5},{5... | collective-permute-start | bytes 294920 | tf_op jit(solution)/shard_map/ppermute | solution.py:20
  184.9 24.7 %collective-permute-start.25 = (bf16[128,1152]{1,0:T(8,128)(2,1)S(1)}, bf16[128,1152]{1,0:T(8,128)(2,1)S(1)}, u32[]{:S(2)}, u32[]{:S(2)}) collective-permute-start(bf16[128,1152]{1,0:T(8,128)(2,1)S(1)} %copy-done.47), channel_id=1, source_target_pairs={{0,8},{4,12},{8,0},{12,4},{16,24},{20,28},{24,16},{28,20},{1,9},{5... | collective-permute-start | bytes 884744 | tf_op jit(solution)/shard_map/ppermute | solution.py:20
  201.6 22.5 %collective-permute-start.22 = (bf16[128,1152]{1,0:T(8,128)(2,1)}, bf16[128,1152]{1,0:T(8,128)(2,1)S(1)}, u32[]{:S(2)}, u32[]{:S(2)}) collective-permute-start(bf16[128,1152]{1,0:T(8,128)(2,1)} %get-tuple-element.217), channel_id=1, source_target_pairs={{0,8},{4,12},{8,0},{12,4},{16,24},{20,28},{24,16},{28,20},{1,9},{5... | collective-permute-start | bytes 884744 | tf_op jit(solution)/shard_map/ppermute | solution.py:20
  203.1 13.3 %collective-permute-start.24 = (bf16[64,2048]{1,0:T(8,128)(2,1)S(1)}, bf16[64,2048]{1,0:T(8,128)(2,1)S(1)}, u32[]{:S(2)}, u32[]{:S(2)}) collective-permute-start(bf16[64,2048]{1,0:T(8,128)(2,1)S(1)} %copy-done.50), channel_id=1, source_target_pairs={{0,16},{4,20},{8,24},{12,28},{16,0},{20,4},{24,8},{28,12},{1,17},{... | collective-permute-start | bytes 786440 | tf_op jit(solution)/shard_map/ppermute | solution.py:20
  208.8 25.7 %collective-permute-start.30 = (bf16[64,2048]{1,0:T(8,128)(2,1)}, bf16[64,2048]{1,0:T(8,128)(2,1)S(1)}, u32[]{:S(2)}, u32[]{:S(2)}) collective-permute-start(bf16[64,2048]{1,0:T(8,128)(2,1)} %get-tuple-element.235), channel_id=1, source_target_pairs={{0,16},{4,20},{8,24},{12,28},{16,0},{20,4},{24,8},{28,12},{1,17},{... | collective-permute-start | bytes 786440 | tf_op jit(solution)/shard_map/ppermute | solution.py:20
  209.1 14.9 %collective-permute-start.23 = (f32[32,768]{1,0:T(8,128)}, f32[32,768]{1,0:T(8,128)S(1)}, u32[]{:S(2)}, u32[]{:S(2)}) collective-permute-start(f32[32,768]{1,0:T(8,128)} %get-tuple-element.218.refs_2_), channel_id=1, source_target_pairs={{0,8},{4,12},{8,0},{12,4},{16,24},{20,28},{24,16},{28,20},{1,9},{5... | collective-permute-start | bytes 294920 | tf_op jit(solution)/shard_map/ppermute | solution.py:20
  212.3 26.5 %collective-permute-start.29 = (bf16[64,1152]{1,0:T(8,128)(2,1)}, bf16[64,1152]{1,0:T(8,128)(2,1)S(1)}, u32[]{:S(2)}, u32[]{:S(2)}) collective-permute-start(bf16[64,1152]{1,0:T(8,128)(2,1)} %get-tuple-element.233), channel_id=1, source_target_pairs={{0,16},{4,20},{8,24},{12,28},{16,0},{20,4},{24,8},{28,12},{1,17},{... | collective-permute-start | bytes 442376 | tf_op jit(solution)/shard_map/ppermute | solution.py:20
  226.8 14.3 %collective-permute-start.28 = (f32[32,768]{1,0:T(8,128)}, f32[32,768]{1,0:T(8,128)S(1)}, u32[]{:S(2)}, u32[]{:S(2)}) collective-permute-start(f32[32,768]{1,0:T(8,128)} %get-tuple-element.231), channel_id=1, source_target_pairs={{0,16},{4,20},{8,24},{12,28},{16,0},{20,4},{24,8},{28,12},{1,17},{... | collective-permute-start | bytes 294920 | tf_op jit(solution)/shard_map/ppermute | solution.py:20
  232.5 13.3 %collective-permute-start.31 = (bf16[64,1152]{1,0:T(8,128)(2,1)}, bf16[64,1152]{1,0:T(8,128)(2,1)S(1)}, u32[]{:S(2)}, u32[]{:S(2)}) collective-permute-start(bf16[64,1152]{1,0:T(8,128)(2,1)} %get-tuple-element.240), channel_id=1, source_target_pairs={{0,16},{4,20},{8,24},{12,28},{16,0},{20,4},{24,8},{28,12},{1,17},{... | collective-permute-start | bytes 442376 | tf_op jit(solution)/shard_map/ppermute | solution.py:20
  (53 other events, 400.9 us)

commit v3 on v2

--- a/solution.py
+++ b/solution.py
@@ -42,8 +42,8 @@
     def __init__(self):
         self.token = jnp.zeros((8, LANES), F32)
 
-    def __call__(self, kernel, outs, *args, scratch=(), smem=(), direct=False, after=(), alias=None):
-        plain = pl.ANY if direct else pltpu.VMEM
+    def __call__(self, kernel, outs, *args, scratch=(), smem=(), after=()):
+        plain = pltpu.VMEM
         specs = [
             pl.BlockSpec(memory_space=pltpu.SMEM if i in smem else plain)
             for i in range(len(args))
@@ -66,16 +66,10 @@
             scratch_shapes=[pltpu.VMEM(s, d) if d is not None else s for s, d in scratch],
             compiler_params=pltpu.CompilerParams(vmem_limit_bytes=56 << 20),
             cost_estimate=pl.CostEstimate(flops=0, bytes_accessed=0, transcendentals=0),
-            input_output_aliases=alias or {},
         )(*args, *extra)
         self.token = results[0]
         return results[1:]
 
-    def touch(self, value):
-        return self(
-            lambda *refs: None, [(value.shape, value.dtype)], value, direct=True, alias={0: 1}
-        )[0]
-
 
 def iota(shape, dim):
     return lax.broadcasted_iota(jnp.int32, shape, dim)
@@ -90,31 +84,71 @@
     return fine(jnp.ones((8, values.shape[1]), F32), values, ((1,), (1,)))
 
 
-def pieces_kernel(place, wm, wa, wd, cot, hid, out):
+def pieces_kernel(place, wm, wa, wd, gu, cot, hid, small, out):
     piece = out.shape[1]
     at = pl.multiple_of(place[1] * piece, piece)
     row = 0
     for w in (wm, wa, wd):
         out[row : row + w.shape[0]] = w[:, pl.ds(at, piece)]
         row += w.shape[0]
-    for value in (cot, hid):
+    for value in (gu[pl.ds(at, piece), :], cot[...], hid[...]):
         for j in range(value.shape[1] // piece):
             out[row : row + value.shape[0]] = value[:, j * piece : (j + 1) * piece]
             row += value.shape[0]
-
-
-def split_kernel(got, cot, hid, first_out, pair_out):
-    size = first_out.shape[0]
+    out[row:] = small[...]
+
+
+def join_small(place, heads, own, far, x_par_out, head_out, gain_out):
+    first = place[2] == 0
+    a = jnp.where(first, own, far)
+    b = jnp.where(first, far, own)
+    width = x_par_out.shape[1] // 2
+    count = width // LANES
+    x_par_out[...] = jnp.zeros_like(x_par_out)
+    for k in range(TAPS + 1):
+        for i in range(count):
+            at = k * count + i
+            x_par_out[k : k + 1, i * LANES : (i + 1) * LANES] = a[at : at + 1]
+            x_par_out[k : k + 1, width + i * LANES : width + (i + 1) * LANES] = b[at : at + 1]
+    row = (TAPS + 1) * count
+    pieces = gain_out.shape[1] // (2 * LANES)
+    for j in range(pieces):
+        gain_out[:, j * LANES : (j + 1) * LANES] = own[row + j : row + j + 1]
+        block = jnp.zeros((1, LANES), F32)
+        for i in range(pieces):
+            block = block + jnp.where((place[1] ^ j) == i, far[row + i : row + i + 1], 0.0)
+        at = (pieces + j) * LANES
+        gain_out[:, at : at + LANES] = block
+    row += pieces
+    joined = a[row : row + 8] + pltpu.roll(b[row : row + 8], heads // 2, 1)
+    head_out[...] = joined
+    pick = jnp.where(
+        iota((LANES, 2 * width), 0) == iota((LANES, 2 * width), 1) // HEAD, 1.0, 0.0
+    )
+    x_par_out[TAPS + 1 : TAPS + 2] = fine(joined, pick)[2:3]
+
+
+def split_kernel(
+    heads, place, got, cot, hid, small, t_out, g_out, pair_out, x_par_out, head_out, gain_out
+):
+    piece = got.shape[1]
     tokens = cot.shape[0]
-    piece = got.shape[1]
-    first_out[...] = got[0:size]
+    row = t_out.shape[0]
+    t_out[...] = got[0:row]
+    for j in range(g_out.shape[1] // piece):
+        g_out[:, j * piece : (j + 1) * piece] = got[row : row + piece]
+        row += piece
     for i, value in enumerate((cot, hid)):
         at = 2 * i * tokens
         pair_out[at : at + tokens] = value[...]
         for j in range(value.shape[1] // piece):
             pair_out[at + tokens : at + 2 * tokens, j * piece : (j + 1) * piece] = got[
-                size + at + j * tokens : size + at + (j + 1) * tokens
+                row : row + tokens
             ]
+            row += tokens
+    own = small[...].astype(F32)
+    far = got[row:].astype(F32)
+    join_small(place, heads, own, far, x_par_out, head_out, gain_out)
 
 
 def gather_quarters(place, mine, came, at, own_out, far_out, far_tmp):
@@ -154,13 +188,14 @@
         at += size
 
 
-def hop_kernel(t_first, t_second, g_first, g_second, t_out, g_out):
+def hop_kernel(t_first, t_second, g_first, g_second, n1, order, t_out, g_out, left_out):
     t_piece = t_first.shape[1]
     g_piece = g_first.shape[0]
     t_out[:, :t_piece] = t_first[...]
     t_out[:, t_piece:] = t_second[...]
     g_out[:g_piece] = g_first[...]
     g_out[g_piece:] = g_second[...]
+    left_out[...] = permuted(n1[...], order[...])
 
 
 def masks(seg_row, seg_col, turned):
@@ -456,28 +491,30 @@
     return dot(left, hot).astype(BF16)
 
 
-def pair_grad(left, right, send_out, keep_out, at, cut, rows):
-    size = right.shape[1]
-    send_out[:, at : at + size] = dot_at(left[:, cut + rows : cut + 2 * rows], right).astype(BF16)
-    keep_out[:, at : at + size] = dot_at(left[:, cut : cut + rows], right)
-
-
-def feed_grad_kernel(n2, act, ggu, dy, order, order2, g_send, g_keep, d_send, d_keep):
-    rows = g_keep.shape[0]
+def feed_grad_kernel(
+    n2, act, ggu, dy, order, order2, g_send, d_send, g_left, d_left
+):
+    rows = g_send.shape[0]
     width = dy.shape[1]
-    pair_grad(permuted(n2[...], order[...]), ggu[...], g_send, g_keep, 0, 0, rows)
+    left = permuted(n2[...], order[...])
+    g_send[...] = dot_at(left[:, rows:], ggu[...]).astype(BF16)
+    g_left[...] = left[:, :rows]
     left = permuted(act[...], order2[...])
     for s in (0, 1):
-        pair_grad(left, dy[...], d_send, d_keep, s * width, 2 * s * rows, rows)
+        cut = 2 * s * rows
+        d_send[:, s * width : (s + 1) * width] = dot_at(
+            left[:, cut + rows : cut + 2 * rows], dy[...]
+        ).astype(BF16)
+        d_left[:, s * rows : (s + 1) * rows] = left[:, cut : cut + rows]
 
 
 def turn_kernel(
-    place, dy_own, dy_far, h2, part, came, gain, wm, wa, first, second, pair, d_keep, d_came,
-    dym_out, resid_out, low_out, gain_out, output_out,
+    ch, nq, place, dy_own, dy_far, h2, part, came, gain, wm, wa, first, second, pair, d_keep, d_came,
+    mixed, order_mix, seg_row, seg_col, sums, pre, ys, x_par, left1,
+    dym_out, resid_out, low_out, gain_out, output_out, m_send, m_left, gtwo_out, two_send,
 ):
     half = dy_own.shape[1]
     quarter = half // 2
-    ch = wm.shape[0]
     value = h2[...]
     output_out[...] = (
         jnp.where(place[0] == 0, value[:, :quarter], value[:, quarter:half])
@@ -500,26 +537,32 @@
     dym = dot_bt(dh_far.astype(BF16), tall_far(first, second, pair, 0, dym_out.shape[1]))
     dym_out[:, :ch] = dym[:, :ch] + dot_bt(low_own, wm[...])
     dym_out[:, ch:] = dym[:, ch:] + dot_bt(low_own, wa[...])
-
-
-def mix_grad_kernel(mixed, low, order, send_out, keep_out):
-    rows = keep_out.shape[0]
-    width = low.shape[1]
-    left = permuted(mixed[...], order[...])
+    unmix_two_kernel(ch, nq, seg_row, seg_col, sums, pre, ys, dym_out, x_par, gtwo_out)
+    rows = two_send.shape[0]
+    two_send[...] = dot_at(left1[:, rows:], gtwo_out[...]).astype(BF16)
+    left = permuted(mixed[...], order_mix[...])
     for s in (0, 1):
-        pair_grad(left, low[...], send_out, keep_out, s * width, 2 * s * rows, rows)
-
-
-def grad_two_kernel(n1, g_two, order, send_out, keep_out):
-    pair_grad(permuted(n1[...], order[...]), g_two[...], send_out, keep_out, 0, 0, keep_out.shape[0])
+        cut = 2 * s * rows
+        m_send[:, s * half : (s + 1) * half] = dot_at(
+            left[:, cut + rows : cut + 2 * rows], low_own
+        ).astype(BF16)
+        m_left[:, s * rows : (s + 1) * rows] = left[:, cut : cut + rows]
 
 
 def back_kernel(
-    g_two, gx, gdt, gbc, gbc_came, wx, wb, wd, wg, wq, wk, n1p_out, n1b_out, both_out
+    g_two, gx, gdt, gbc, gbc_came, wx, wb, wd, wg, wq, wk, left1,
+    n1p_out, n1b_out, both_out, one_send,
 ):
     tokens = gx.shape[0]
     both = (gbc[0:tokens] + gbc_came[0:tokens]).astype(BF16)
     both_out[...] = both
+    rows = one_send.shape[0]
+    left = left1[:, rows:]
+    at = 0
+    for right in (gx[...], both, gdt[...]):
+        size = right.shape[1]
+        one_send[:, at : at + size] = dot_at(left, right).astype(BF16)
+        at += size
     ch = wg.shape[1]
     nq = wq.shape[1]
     total = dot_bt(gx[...], wx[...]) + dot_bt(gdt[...], wd[...])
@@ -528,12 +571,92 @@
     n1b_out[...] = dot_bt(both, wb[...])
 
 
-def grad_one_kernel(n1, gx, gdt, both, order, send_out, keep_out):
-    left = permuted(n1[...], order[...])
+def store_halves(total, at, send_out, keep_out, skip=0):
+    rows = keep_out.shape[0]
+    size = total.shape[1]
+    send_out[skip:, at : at + size] = total[rows:].astype(BF16)
+    keep_out[:, at : at + size] = total[:rows]
+
+
+def wide_kernel(left, right, came, send_out, keep_out):
+    total = dot_at(left[:, : came.shape[0]], right[...]) + came[...].astype(F32)
+    store_halves(total, 0, send_out, keep_out)
+
+
+def tall_kernel(d_left, dy, d_came, m_left, low, m_came, send_out, keep_out):
+    at = 0
+    for left, right, came in ((d_left, dy, d_came), (m_left, low, m_came)):
+        rows = came.shape[0]
+        width = right.shape[1]
+        for s in (0, 1):
+            total = dot_at(left[:, s * rows : (s + 1) * rows], right[...])
+            total = total + came[:, s * width : (s + 1) * width].astype(F32)
+            store_halves(total, at, send_out, keep_out)
+            at += width
+
+
+def pack_vector(value, out):
+    rows, width = value.shape
+    high = value.astype(BF16)
+    low = (value - high.astype(F32)).astype(BF16)
+    out[0:rows, 0:width] = high
+    out[rows : 2 * rows, 0:width] = low
+    out[0 : 2 * rows, width:] = jnp.zeros((2 * rows, out.shape[1] - width), BF16)
+    return high.astype(F32) + low.astype(F32)
+
+
+def read_vector(came, shape):
+    rows, width = shape
+    return came[0:rows, 0:width].astype(F32) + came[rows : 2 * rows, 0:width].astype(F32)
+
+
+def one_kernel(left1, gx, both, gdt, came, vector, vector_came, send_out, keep_out, vector_out):
+    left = left1[:, : came.shape[0]]
+    skip = 2 * vector.shape[0]
     at = 0
     for right in (gx[...], both[...], gdt[...]):
-        pair_grad(left, right, send_out, keep_out, at, 0, keep_out.shape[0])
-        at += right.shape[1]
+        size = right.shape[1]
+        total = dot_at(left, right) + came[:, at : at + size].astype(F32)
+        store_halves(total, at, send_out, keep_out, skip)
+        at += size
+    vector_out[...] = pack_vector(vector[...] + vector_came[...], send_out)
+
+
+def one_stage_kernel(keep, came, vector, send_out, keep_out, vector_out):
+    skip = 2 * vector.shape[0]
+    total = keep[...] + came[skip:].astype(F32)
+    store_halves(total, 0, send_out, keep_out, skip)
+    vector_out[...] = pack_vector(vector[...] + read_vector(came, vector.shape), send_out)
+
+
+def one_last_kernel(
+    heads, place, keep, came, vector, x_out, bc_out, dt_out,
+    n1_out, n2_out, xw_out, xb_out, bw_out, bb_out, dtb_out, alog_out, skip_out,
+):
+    skip = 2 * vector.shape[0]
+    total = keep[...] + came[skip:].astype(F32)
+    ch = x_out.shape[1]
+    nbc = bc_out.shape[1]
+    x_out[...] = total[:, :ch]
+    bc_out[...] = total[:, ch : ch + nbc]
+    dt_out[...] = total[:, ch + nbc : ch + nbc + heads]
+    value = vector[...] + read_vector(came, vector.shape)
+    first = place[2] == 0
+    half = n1_out.shape[1]
+    cq = xb_out.shape[1]
+    n1_out[...] = value[24:25, :half]
+    n2_out[...] = value[25:26, :half]
+    mine = jnp.where(first, value[0:8, :cq], value[0:8, cq : 2 * cq])
+    xw_out[...] = mine[0:TAPS]
+    xb_out[...] = mine[TAPS : TAPS + 1]
+    bw_out[...] = value[16 : 16 + TAPS, :nbc]
+    bb_out[...] = value[16 + TAPS : 17 + TAPS, :nbc]
+    hq = dtb_out.shape[1]
+    for i, out in enumerate((dtb_out, alog_out, skip_out)):
+        at = i * LANES
+        out[...] = jnp.where(
+            first, value[12:13, at : at + hq], value[12:13, at + hq : at + 2 * hq]
+        )
 
 
 def close_kernel(own, part, came, n1b, gain, gbc, gbc_came, dn1_out, rows_out):
@@ -574,20 +697,6 @@
     keep_out[...] = total[:rows]
 
 
-def stage_sum_kernel(keep, came, vector, vector_came, send_out, keep_out, vector_out):
-    stage_kernel(keep, came, send_out, keep_out)
-    vector_out[...] = vector[...] + vector_came[...]
-
-
-def join_kernel(keep_a, came_a, keep_b, came_b, send_out, keep_out):
-    rows, width = keep_out.shape
-    width = width // 2
-    for i, (keep, came) in enumerate(((keep_a, came_a), (keep_b, came_b))):
-        total = keep[...] + came[...].astype(F32)
-        send_out[:, i * width : (i + 1) * width] = total[rows:].astype(BF16)
-        keep_out[:, i * width : (i + 1) * width] = total[:rows]
-
-
 def last_kernel(keep, came, *outs):
     total = keep[...] + came[...].astype(F32)
     at = 0
@@ -613,39 +722,18 @@
     return order
 
 
-class Scatter:
-    def __init__(self, run, steps, send, keep, last=None, outs=(), at=0):
-        self.run, self.steps, self.last, self.outs = run, steps, last, outs
-        self.at, self.keep, self.vector = at, keep, None
-        self.came = swap(send, "dp", steps[at])
-        self.results = None
-
-    def add_vector(self, vector):
-        self.vector = vector
-        self.vector_came = swap(vector, "dp", self.steps[0])
-
-    def advance(self):
-        if self.results is not None:
-            return
-        self.at += 1
-        if self.at == len(self.steps):
-            self.results = self.run(self.last, self.outs, self.keep, self.came)
-            if self.vector is not None:
-                self.vector = self.vector + self.vector_came
-            return
-        rows, cols = self.keep.shape
-        outs = [((rows // 2, cols), BF16), ((rows // 2, cols), F32)]
-        step = self.steps[self.at]
-        if self.vector is None:
-            send, self.keep = self.run(stage_kernel, outs, self.keep, self.came)
-        else:
-            send, self.keep, self.vector = self.run(
-                stage_sum_kernel,
-                outs + [(self.vector.shape, F32)],
-                self.keep, self.came, self.vector, self.vector_came,
-            )
-            self.vector_came = swap(self.vector, "dp", step)
-        self.came = swap(send, "dp", step)
+def halve(run, steps, at, send, keep, last, outs):
+    while True:
+        came = swap(send, "dp", steps[at])
+        yield None
+        at += 1
+        if at == len(steps):
+            break
+        rows, cols = keep.shape
+        send, keep = run(
+            stage_kernel, [((rows // 2, cols), BF16), ((rows // 2, cols), F32)], keep, came
+        )
+    yield run(last, outs, keep, came)
 
 
 def shards(
@@ -695,24 +783,61 @@
     cols = ch + nbc + LANES + ch + nq + nkv
     inner = ch + nq
 
-    t_mine = run(
+    near = [1 << b for b in range(count.bit_length() - 1)]
+    turned = [near[1], near[0]] + near[2:]
+    size = half // count
+    within = jnp.asarray(np.tile(np.arange(size), count), jnp.int32)
+    both_within = jnp.concatenate([within, within + size])
+
+    def block_order(steps):
+        return jnp.asarray(np.repeat(np.array(halving_order(steps)), size), jnp.int32) ^ me
+
+    near_block = block_order(near)
+    turned_both = jnp.concatenate([block_order(turned)] * 2)
+    order_near = (near_block * size + within)[None]
+    order_down = (turned_both * (ff // count) + both_within)[None]
+    m_rows = ch // count
+    a_rows = nq // count
+    order_mix = jnp.where(
+        both_within < m_rows,
+        turned_both * m_rows + both_within,
+        ch + turned_both * a_rows + both_within - m_rows,
+    )[None]
+
+    def padded(value):
+        return jnp.pad(value, (0, LANES - hq))
+
+    small = jnp.concatenate(
+        [convx_weight.T.reshape(-1), convx_bias, norm2_gain, padded(dt_bias), padded(a_log), padded(d_skip)]
+    )
+    small_rows = 16 * pl.cdiv(small.shape[0] // LANES + 8, 16)
+    small = jnp.pad(small, (0, small_rows * LANES - small.shape[0])).reshape(small_rows, LANES)
+    gu = w_gateup.reshape(half, 2 * ff)
+    mine = run(
         pieces_kernel,
-        [((inner + ff + 4 * tokens, piece), BF16)],
-        place, w_mixout, w_attnout, w_down, cotangent, hidden,
+        [((inner + 3 * ff + 4 * tokens + small_rows, piece), BF16)],
+        place, w_mixout, w_attnout, w_down, gu, cotangent, hidden, small,
         smem=(0,),
     )[0]
-    t_got = swap(t_mine, "row")
-    gu = w_gateup.reshape(half, 2 * ff)
-    g_first = swap(lax.dynamic_slice_in_dim(gu, spot * piece, piece, 0), "row")
+    got = swap(mine, "row")
     wk = w_kv.reshape(half, nkv)
     wd = jnp.pad(w_dt, ((0, 0), (0, LANES - heads)))
     gain_one = norm1_gain.astype(F32)[None]
-    t_first, in_pair = run(
-        split_kernel,
-        [((inner + ff, piece), BF16), ((4 * tokens, quarter), BF16)],
-        t_got, cotangent, hidden,
+    t_first, g_first, in_pair, x_par, head_par, gain_two = run(
+        lambda *refs: split_kernel(heads, *refs),
+        [
+            ((inner + ff, piece), BF16),
+            ((piece, 2 * ff), BF16),
+            ((4 * tokens, quarter), BF16),
+            ((8, ch), F32),
+            ((8, LANES), F32),
+            ((1, full_width), F32),
+        ],
+        place, got, cotangent, hidden, small,
+        smem=(0,),
     )
     t_second = swap(t_first, "dp", 1)
+    g_second = swap(g_first, "dp", 2)
     in_came = swap(in_pair, "col")
     n1, part, part_low, own, far, factor1 = run(
         project_kernel,
@@ -728,71 +853,19 @@
         smem=(0,), scratch=[((tokens, half), BF16)],
     )
     part_came = swap(part_low, "row")
-    g_first = run.touch(g_first)
-    g_second = swap(g_first, "dp", 2)
-    t_cat, g_cat = run(
+    t_cat, g_cat, left1 = run(
         hop_kernel,
-        [((inner + ff, 2 * piece), BF16), ((2 * piece, 2 * ff), BF16)],
-        t_first, t_second, g_first, g_second,
+        [((inner + ff, 2 * piece), BF16), ((2 * piece, 2 * ff), BF16), ((tokens, half), BF16)],
+        t_first, t_second, g_first, g_second, n1, order_near,
     )
     t_pair = swap(t_cat, "dp", 2)
     g_pair = swap(g_cat, "dp", 1)
 
-    small = jnp.concatenate(
-        [convx_weight.T.reshape(-1), convx_bias, dt_bias, a_log, d_skip, norm2_gain]
-    )
-    small_far = swap(small, "row")
-
-    def joined(start, size):
-        a = small[start : start + size]
-        b = small_far[start : start + size]
-        first = row == 0
-        return jnp.concatenate([jnp.where(first, a, b), jnp.where(first, b, a)], 0).astype(F32)
-
-    at = TAPS * cq
-    x_par = jnp.stack(
-        [joined(k * cq, cq) for k in range(TAPS + 1)]
-        + [jnp.repeat(joined(at + cq + 2 * hq, hq), HEAD)]
-        + [jnp.zeros((ch,), F32)] * 2
-    )
     bc_par = jnp.concatenate(
         [convbc_weight.T, convbc_bias[None], jnp.zeros((3, nbc), BF16)], 0
     ).astype(F32)
-    head_par = jnp.stack(
-        [jnp.pad(joined(at + cq + k * hq, hq), (0, LANES - heads)) for k in (0, 1)]
-        + [jnp.zeros((LANES,), F32)] * 6
-    )
-    gain2_far = jnp.concatenate(
-        [
-            lax.dynamic_slice_in_dim(small_far, at + cq + 3 * hq + (spot ^ j) * piece, piece, 0)
-            for j in range(4)
-        ]
-    )
-    gain_two = jnp.concatenate([norm2_gain, gain2_far]).astype(F32)[None]
     seg_row = segment_ids.astype(F32)
     seg_col = jnp.broadcast_to(segment_ids[0].astype(F32)[:, None], (tokens, LANES))
-
-    near = [1 << b for b in range(count.bit_length() - 1)]
-    turned = [near[1], near[0]] + near[2:]
-    size = half // count
-    within = jnp.asarray(np.tile(np.arange(size), count), jnp.int32)
-    both_within = jnp.concatenate([within, within + size])
-
-    def block_order(steps):
-        return jnp.asarray(np.repeat(np.array(halving_order(steps)), size), jnp.int32) ^ me
-
-    near_block = block_order(near)
-    turned_block = block_order(turned)
-    turned_both = jnp.concatenate([turned_block] * 2)
-    order_near = (near_block * size + within)[None]
-    order_down = (turned_both * (ff // count) + both_within)[None]
-    m_rows = ch // count
-    a_rows = nq // count
-    order_mix = jnp.where(
-        both_within < m_rows,
-        turned_both * m_rows + both_within,
-        ch + turned_both * a_rows + both_within - m_rows,
-    )[None]
 
     mixed, raw, pre, ys = run(
         lambda *refs: mix_kernel(ch, nq, *refs),
@@ -835,40 +908,38 @@
     down_came = swap(down_send, "col")
     rows = half // 2
 
-    def halves(width):
-        return [((rows, width), BF16), ((rows, width), F32)]
-
-    g_send, g_keep, d_send, d_keep = run(
-        feed_grad_kernel, halves(2 * ff) + halves(2 * half), n2, act, ggu, dy_own, order_near, order_down
-    )
-    s_gu = Scatter(run, near, g_send, g_keep, last_kernel, [((size, 2 * ff), F32)])
-    s_down = Scatter(run, turned, d_send, d_keep)
-    dym, resid, low, gain2_sum, output = run(
-        turn_kernel,
+    g_send, d_send, g_left, d_left = run(
+        feed_grad_kernel,
+        [
+            ((rows, 2 * ff), BF16),
+            ((rows, 2 * half), BF16),
+            ((tokens, rows), BF16),
+            ((tokens, half), BF16),
+        ],
+        n2, act, ggu, dy_own, order_near, order_down,
+    )
+    g_came = swap(g_send, "dp", near[0])
+    d_came = swap(d_send, "dp", turned[0])
+    dym, resid, low, gain2_sum, output, m_send, m_left, g_two, two_send = run(
+        lambda *refs: turn_kernel(ch, nq, *refs),
         [
             ((tokens, inner), F32),
             ((tokens, half), F32),
             ((tokens, half), BF16),
             ((8, half), F32),
             ((tokens, quarter), BF16),
+            ((rows, 2 * half), BF16),
+            ((tokens, half), BF16),
+            ((tokens, ch + nq + nkv), BF16),
+            ((rows, ch + nq + nkv), BF16),
         ],
         place, dy_own, dy_far, h2, n2_part, n2_came, gain_two,
         w_mixout, w_attnout, t_first, t_second, t_pair, down_keep, down_came,
+        mixed, order_mix, seg_row, seg_col, raw, pre, ys, x_par, left1,
         smem=(0,),
     )
-    g_two = run(
-        lambda *refs: unmix_two_kernel(ch, nq, *refs),
-        [((tokens, ch + nq + nkv), BF16)],
-        seg_row, seg_col, raw, pre, ys, dym, x_par,
-    )[0]
-    two_send, two_keep = run(grad_two_kernel, halves(ch + nq + nkv), n1, g_two, order_near)
-    s_two = Scatter(
-        run, near, two_send, two_keep, last_kernel,
-        [((size, ch), F32), ((size, nq), F32), ((size, nkv), F32)],
-    )
-    m_send, m_keep = run(mix_grad_kernel, halves(2 * half), mixed, low, order_mix)
-    s_mix = Scatter(run, turned, m_send, m_keep)
-    s_down.advance()
+    two_came = swap(two_send, "dp", near[0])
+    m_came = swap(m_send, "dp", turned[0])
     gx, gdt, gbc, small_sum = run(
         lambda *refs: unmix_one_kernel(ch, nq, *refs),
         [
@@ -881,80 +952,123 @@
         scratch=[((tokens, ch), F32), ((tokens, ch), F32), ((tokens, tokens), F32)],
     )
     gbc_came = swap(gbc, "col")
-    n1_part, n1_bc, gbc_both = run(
+
+    def quarters(width):
+        return [((rows // 2, width), BF16), ((rows // 2, width), F32)]
+
+    g_send, g_keep = run(wide_kernel, quarters(2 * ff), g_left, ggu, g_came)
+    s_gu = halve(run, near, 1, g_send, g_keep, last_kernel, [((size, 2 * ff), F32)])
+    next(s_gu)
+    n1_part, n1_bc, gbc_both, one_send = run(
         back_kernel,
-        [((tokens, half), F32), ((tokens, half), F32), ((tokens, nbc), BF16)],
-        g_two, gx, gdt, gbc, gbc_came, w_xin, w_bc, wd, w_gate, w_query, wk,
-    )
+        [
+            ((tokens, half), F32),
+            ((tokens, half), F32),
+            ((tokens, nbc), BF16),
+            ((rows, ch + nbc + LANES), BF16),
+        ],
+        g_two, gx, gdt, gbc, gbc_came, w_xin, w_bc, wd, w_gate, w_query, wk, left1,
+    )
+    one_came = swap(one_send, "dp", near[0])
     n1_came = swap(n1_part, "col")
-    s_gu.advance()
-    s_mix.advance()
-    s_two.advance()
-    one_send, one_keep = run(
-        grad_one_kernel, halves(ch + nbc + LANES), n1, gx, gdt, gbc_both, order_near
-    )
-    s_one = Scatter(
-        run, near, one_send, one_keep, last_kernel,
-        [((size, ch), F32), ((size, nbc), F32), ((size, LANES), F32)],
-    )
+    tall_send, tall_keep = run(
+        tall_kernel, quarters(4 * half), d_left, dy_own, d_came, m_left, low, m_came
+    )
+    s_tall = halve(
+        run, turned, 1, tall_send, tall_keep, last_tall_kernel,
+        [((2 * size, half), F32), ((m_rows, half), F32), ((a_rows, half), F32)],
+    )
+    next(s_tall)
+    two_send, two_keep = run(wide_kernel, quarters(ch + nq + nkv), left1, g_two, two_came)
+    s_two = halve(
+        run, near, 1, two_send, two_keep, last_kernel,
+        [((size, ch), F32), ((size, nq), F32), ((size, nkv), F32)],
+    )
+    next(s_two)
     dn1, sum_rows = run(
         close_kernel,
         [((tokens, half), F32), ((16, tokens), F32)],
         own, n1_part, n1_came, n1_bc, gain_one, gbc, gbc_came,
     )
     rows_far = swap(sum_rows, "row")
-    s_gu.advance()
+    r_gu = next(s_gu)
     grad_hidden, vector = run(
         end_kernel,
         [((tokens, quarter), F32), ((32, ch), F32)],
         place, own, factor1, resid, dn1, gain_one, sum_rows, rows_far, small_sum, gain2_sum,
         smem=(0,),
     )
-    s_one.add_vector(vector)
-    s_one.advance()
-    tall_send, tall_keep = run(
-        join_kernel,
-        [((rows // 4, 4 * half), BF16), ((rows // 4, 4 * half), F32)],
-        s_down.keep, s_down.came, s_mix.keep, s_mix.came,
-    )
-    s_tall = Scatter(
-        run, turned, tall_send, tall_keep, last_tall_kernel,
-        [((2 * size, half), F32), ((m_rows, half), F32), ((a_rows, half), F32)],
-        at=2,
-    )
-    scatters = (s_two, s_gu, s_one, s_tall)
-    while any(s.results is None for s in scatters):
-        for s in scatters:
-            s.advance()
-    vector = s_one.vector
-    r_gate, r_query, r_kv = s_two.results
-    r_xin, r_bc, r_dt = s_one.results
-    r_down, r_mixout, r_attnout = s_tall.results
-
-    def mine(values, width):
-        return lax.dynamic_slice_in_dim(values, row * width, width, values.ndim - 1)
-
+    vector_came = swap(vector, "dp", near[0])
+    r_two = next(s_two)
+    r_gu = r_gu or next(s_gu)
+    r_two = r_two or next(s_two)
+    r_tall = next(s_tall)
+
+    def one_outs(keep):
+        width = ch + nbc + LANES
+        return [((keep + 64, width), BF16), ((keep, width), F32), ((32, ch), F32)]
+
+    one_send, one_keep, vector = run(
+        one_kernel, one_outs(rows // 2),
+        left1, gx, gbc_both, gdt, one_came, vector, vector_came,
+    )
+    r_tall = r_tall or next(s_tall)
+    for step in near[1:-1]:
+        one_came = swap(one_send, "dp", step)
+        one_send, one_keep, vector = run(
+            one_stage_kernel, one_outs(one_keep.shape[0] // 2), one_keep, one_came, vector
+        )
+        r_gu = r_gu or next(s_gu)
+        r_tall = r_tall or next(s_tall)
+        r_two = r_two or next(s_two)
+    one_came = swap(one_send, "dp", near[-1])
+    r_gu = r_gu or next(s_gu)
+    r_tall = r_tall or next(s_tall)
+    r_two = r_two or next(s_two)
+    (
+        r_xin, r_bc, r_dt, o_norm1, o_norm2, o_cxw, o_cxb, o_cbw, o_cbb, o_dtb, o_alog, o_dsk
+    ) = run(
+        lambda *refs: one_last_kernel(heads, *refs),
+        [
+            ((size, ch), F32),
+            ((size, nbc), F32),
+            ((size, heads), F32),
+            ((1, half), F32),
+            ((1, half), F32),
+            ((TAPS, cq), F32),
+            ((1, cq), F32),
+            ((TAPS, nbc), F32),
+            ((1, nbc), F32),
+            ((1, hq), F32),
+            ((1, hq), F32),
+            ((1, hq), F32),
+        ],
+        place, one_keep, one_came, vector,
+        smem=(0,),
+    )
+    r_gate, r_query, r_kv = r_two
+    r_down, r_mixout, r_attnout = r_tall
     return (
         output,
         grad_hidden,
-        vector[24, :half],
+        o_norm1[0],
         r_gate,
         r_xin,
-        r_dt[:, :heads],
+        r_dt,
         r_bc,
         r_query,
         r_kv.reshape(size, 1, nkv),
-        mine(vector[0:TAPS], cq).T,
-        mine(vector[TAPS], cq),
-        vector[16 : 16 + TAPS, :nbc].T,
-        vector[16 + TAPS, :nbc],
-        mine(vector[12, :heads], hq),
-        mine(vector[12, LANES : LANES + heads], hq),
-        mine(vector[12, 2 * LANES : 2 * LANES + heads], hq),
+        o_cxw.T,
+        o_cxb[0],
+        o_cbw.T,
+        o_cbb[0],
+        o_dtb[0],
+        o_alog[0],
+        o_dsk[0],
         r_mixout,
         r_attnout,
-        vector[25, :half],
-        s_gu.results[0].reshape(size, 2, ff),
+        o_norm2[0],
+        r_gu[0].reshape(size, 2, ff),
         r_down,
     )
 

time: 251 us -> 239 us (0.952)
  waiting for transfers between devices: 66.4 us -> 79.7 us
  Pallas kernels: 108 us -> 96.6 us
  starting transfers between devices: 37.8 us -> 29 us
  local copies, waits for them, and re-layouts: 31.8 us -> 28.2 us
    ppermute x32 -> x27, waiting for transfers between devices: 66.4 us -> 79.7 us  [swap(): return lax.ppermute(values, axis, [(i, i ^ step) for i in range(count)])]
    pallas_call x32 -> x26, Pallas kernels: 108 us -> 96.6 us  [__call__(): pl.pallas_call(body, out_shape=[jax.ShapeDtypeStruct((8, LANES), F32)] +...]
    ppermute x32 -> x27, starting transfers between devices: 37.8 us -> 29 us  [swap(): return lax.ppermute(values, axis, [(i, i ^ step) for i in range(count)])]
    unnamed x113 -> x106, local copies, waits for them, and re-layouts: 20.7 us -> 23.8 us
    dynamic_slice x5 -> x0, local copies, waits for them, and re-layouts: 3.17 us -> none  [the longest x4 2.34 us: mine(): return lax.dynamic_slice_in_dim(values, row * width, width, values.ndim - 1)]
  transfers between devices with their start and end apart: 32 -> 27, of which waited for: 11 -> 12; matrix products, arithmetic and copies ran while one was open for 6% -> 2% of each run, Pallas kernels for 37% -> 32%
where the time goes in v3:
time: 239 us
  Pallas kernels  96.6 us (40%)
  waiting for transfers between devices  79.7 us (33%)
  starting transfers between devices  29 us (12%)
  local copies, waits for them, and re-layouts  28.2 us (12%)
  other arithmetic  4.24 us (2%)
    pallas_call x26, Pallas kernels, __call__(): pl.pallas_call(body, out_shape=[jax.ShapeDtypeStruct((8, LANES), F32)] +...  96.6 us
    ppermute x27, waiting for transfers between devices, swap(): return lax.ppermute(values, axis, [(i, i ^ step) for i in range(count)])  79.7 us
    ppermute x27, starting transfers between devices, swap(): return lax.ppermute(values, axis, [(i, i ^ step) for i in range(count)])  29 us
    unnamed x106, local copies, waits for them, and re-layouts  23.8 us
  transfers between devices with their start and end apart: 27, of which 12 were waited for; matrix products, arithmetic and copies ran while one was open for 2% of the time, Pallas kernels for 32%

profile of v3, /device:TPU:0, one launch (start us, length us, event | category | flops | bytes accessed | tf_op | source)
XLA Modules:
  0.0 238.7 jit_solution(17259834003511764442)
XLA Ops:
  0.7 3.6 %copy.49 = bf16[64,8,2,1024]{3,1,2,0:T(8,128)(2,1)} copy(bf16[64,8,2,1024]{3,2,1,0:T(2,128)(2,1)} %bitcast.27) | data formatting | bytes 4194304
  7.4 3.5 %shard_map.400 = (f32[8,128]{1,0:T(8,128)}, bf16[5152,128]{1,0:T(8,128)(2,1)}) custom-call(s32[3]{0:T(128)} %pad_add_fusion.1.refs_0_, bf16[768,512]{1,0:T(8,128)(2,1)} %refs_7_.3, bf16[256,512]{1,0:T(8,128)(2,1)} %refs_8_.4, bf16[1024,512]{1,0:T(8,128)(2,1)} %refs_11_.1, bf16[512,2048]{1,0:T(8,128)(2,1)} %bitcast.25, bf16[256,256]{1,0:T(8,128)(2,1)} %refs_2_.4, ...), custom_call_target="tpu_custom_call" | custom-call | tf_op jit(solution)/shard_map/pallas_call | solution.py:59
  11.0 3.0 %collective-permute-start = (bf16[5152,128]{1,0:T(8,128)(2,1)}, bf16[5152,128]{1,0:T(8,128)(2,1)S(1)}, u32[]{:S(2)}, u32[]{:S(2)}) collective-permute-start(bf16[5152,128]{1,0:T(8,128)(2,1)} %get-tuple-element.139), channel_id=1, source_target_pairs={{0,2},{2,0},{1,3},{3,1},{4,6},{6,4},{5,7},{7,5},{8,10},{10,8},{9,1... | collective-permute-start | bytes 3956744 | tf_op jit(solution)/shard_map/ppermute | solution.py:20
  13.9 29.2 %collective-permute-done.refs_1_ = bf16[5152,128]{1,0:T(8,128)(2,1)S(1)} collective-permute-done((bf16[5152,128]{1,0:T(8,128)(2,1)}, bf16[5152,128]{1,0:T(8,128)(2,1)S(1)}, u32[]{:S(2)}, u32[]{:S(2)}) %collective-permute-start) | collective-permute-done | bytes 1318944 | tf_op jit(solution)/shard_map/ppermute | solution.py:20
  44.1 2.8 %shard_map.401 = (f32[8,128]{1,0:T(8,128)}, bf16[2048,128]{1,0:T(8,128)(2,1)}, bf16[128,2048]{1,0:T(8,128)(2,1)}, bf16[1024,256]{1,0:T(8,128)(2,1)}, f32[8,768]{...) custom-call(s32[3]{0:T(128)} %pad_add_fusion.1.refs_0_, bf16[5152,128]{1,0:T(8,128)(2,1)} %copy-done.4, ...), custom_call_target="tpu_custom_call" | custom-call | tf_op jit(solution)/shard_map/pallas_call | solution.py:59
  52.6 4.9 %shard_map.402 = (f32[8,128]{1,0:T(8,128)}, bf16[256,512]{1,0:T(8,128)(2,1)}, f32[256,2304]{1,0:T(8,128)}, bf16[256,2304]{1,0:T(8,128)(2,1)}, bf16[256,512]{1,0:...) custom-call(s32[3]{0:T(128)} %pad_add_fusion.1.refs_0_, bf16[1024,256]{1,0:T(8,128)(2,1)} %get-tuple-element.141.refs_1_, ...), custom_call_target="tpu_custom_call" | custom-call | tf_op jit(solution)/shard_map/pallas_call | solution.py:59
  63.8 3.4 %shard_map.403 = (f32[8,128]{1,0:T(8,128)}, bf16[2048,256]{1,0:T(8,128)(2,1)}, bf16[256,2048]{1,0:T(8,128)(2,1)}, bf16[256,512]{1,0:T(8,128)(2,1)}) custom-call(bf16[2048,128]{1,0:T(8,128)(2,1)} %get-tuple-element.142.refs_0_.refs_3_.refs_4_.refs_9_, bf16[2048,128]{1,0:T(8,128)(2,1)} %copy-done.1, bf16[128,2048]{1,0:T(8,128)(2,1)} %get-tuple-element.143.refs_2_.refs_7_, ...), custom_call_target="tpu_custom_call" | custom-call | tf_op jit(solution)/shard_map/pallas_call | solution.py:59
  70.1 15.3 %collective-permute-done.5.refs_3_ = bf16[256,2304]{1,0:T(8,128)(2,1)S(1)} collective-permute-done((bf16[256,2304]{1,0:T(8,128)(2,1)}, bf16[256,2304]{1,0:T(8,128)(2,1)S(1)}, u32[]{:S(2)}, u32[]{:S(2)}) %collective-permute-start.5) | collective-permute-done | bytes 1179680 | tf_op jit(solution)/shard_map/ppermute | solution.py:20
  86.6 6.7 %shard_map.404 = (f32[8,128]{1,0:T(8,128)}, bf16[256,1024]{1,0:T(8,128)(2,1)}, f32[256,2304]{1,0:T(8,128)}, f32[256,1024]{1,0:T(8,128)}, f32[256,768]{1,0:T(8,128)}) custom-call(f32[1,256]{1,0:T(1,128)} %copy-done.27, f32[256,128]{1,0:T(8,128)} %broadcast_in_dim.29.refs_1_.refs_17_, f32[256,2304]{1,0:T(8,128)} %get-tuple-element.148.refs_2_, ...), custom_call_target="tpu_custom_call" | custom-call | tf_op jit(solution)/shard_map/pallas_call | solution.py:59
  94.2 3.7 %shard_map.405 = (f32[8,128]{1,0:T(8,128)}, f32[256,1024]{1,0:T(8,128)}) custom-call(bf16[256,1024]{1,0:T(8,128)(2,1)} %get-tuple-element.153.refs_0_.refs_14_, bf16[768,512]{1,0:T(8,128)(2,1)} %refs_7_.3, bf16[256,512]{1,0:T(8,128)(2,1)} %refs_8_.4, bf16[2048,128]{1,0:T(8,128)(2,1)} %get-tuple-element.142.refs_0_.refs_3_.refs_4_.refs_9_, ...), custom_call_target="tpu_custom_call" | custom-call | tf_op jit(solution)/shard_map/pallas_call | solution.py:59
  97.9 4.0 %shard_map.406 = (f32[8,128]{1,0:T(8,128)}, bf16[256,512]{1,0:T(8,128)(2,1)}, bf16[256,512]{1,0:T(8,128)(2,1)}, f32[256,1024]{1,0:T(8,128)}) custom-call(s32[3]{0:T(128)} %pad_add_fusion.1.refs_0_, bf16[1024,256]{1,0:T(8,128)(2,1)} %get-tuple-element.141.refs_1_, bf16[1024,256]{1,0:T(8,128)(2,1)} %copy-done.2, bf16[1024,512]{1,0:T(8,128)(2,1)} %refs_11_.1, ...), custom_call_target="tpu_custom_call" | custom-call | tf_op jit(solution)/shard_map/pallas_call | solution.py:59
  103.2 7.8 %shard_map.407 = (f32[8,128]{1,0:T(8,128)}, f32[256,1024]{1,0:T(8,128)}, bf16[256,512]{1,0:T(8,128)(2,1)}, bf16[256,1024]{1,0:T(8,128)(2,1)}, bf16[256,2048]{1,0...) custom-call(s32[3]{0:T(128)} %pad_add_fusion.1.refs_0_, ...), custom_call_target="tpu_custom_call" | custom-call | tf_op jit(solution)/shard_map/pallas_call | solution.py:59
  112.3 3.9 %shard_map.408 = (f32[8,128]{1,0:T(8,128)}, bf16[256,2048]{1,0:T(8,128)(2,1)}, bf16[256,1024]{1,0:T(8,128)(2,1)}, bf16[256,256]{1,0:T(8,128)(2,1)}, bf16[256,512]{1,0:T(8,128)(2,1)}) custom-call(bf16[256,512]{1,0:T(8,128)(2,1)} %get-tuple-element.173.refs_0_, bf16[256,1024]{1,0:T(8,128)(2,1)} %get-tuple-element.174.refs_1_, ...), custom_call_target="tpu_custom_call" | custom-call | tf_op jit(solution)/shard_map/pallas_call | solution.py:59
  119.3 9.5 %shard_map.409 = (f32[8,128]{1,0:T(8,128)}, f32[256,1024]{1,0:T(8,128)}, f32[256,512]{1,0:T(8,128)}, bf16[256,512]{1,0:T(8,128)(2,1)}, f32[8,512]{1,0:T(8,128)},...) custom-call(s32[3]{0:T(128)} %pad_add_fusion.1.refs_0_, ...), custom_call_target="tpu_custom_call" | custom-call | tf_op jit(solution)/shard_map/pallas_call | solution.py:59
  128.9 9.1 %shard_map.410 = (f32[8,128]{1,0:T(8,128)}, bf16[256,768]{1,0:T(8,128)(2,1)}, bf16[256,128]{1,0:T(8,128)(2,1)}, f32[264,256]{1,0:T(8,128)}, f32[16,768]{1,0:T(8,128)}) custom-call(f32[1,256]{1,0:T(1,128)} %copy-done.27, f32[256,128]{1,0:T(8,128)} %broadcast_in_dim.29.refs_1_.refs_17_, f32[256,2304]{1,0:T(8,128)} %get-tuple-element.169.refs_18_.refs_2_, ...), custom_call_target="tpu_custom_call" | custom-call | tf_op jit(solution)/shard_map/pallas_call | solution.py:59
  142.6 3.2 %shard_map.411 = (f32[8,128]{1,0:T(8,128)}, bf16[128,2048]{1,0:T(8,128)(2,1)}, f32[128,2048]{1,0:T(8,128)}) custom-call(bf16[256,256]{1,0:T(8,128)(2,1)} %get-tuple-element.187.refs_0_, bf16[256,2048]{1,0:T(8,128)(2,1)} %get-tuple-element.175.refs_2_.refs_1_, bf16[256,2048]{1,0:T(8,128)(2,1)} %copy-done.8, f32[8,128]{1,0:T(8,128)} %get-tuple-element.189.refs_3_), custom_call_target="tpu_custom_call" | custom-call | tf_op jit(solution)/shard_map/pallas_call | solution.py:59
  146.5 4.2 %shard_map.412 = (f32[8,128]{1,0:T(8,128)}, f32[256,512]{1,0:T(8,128)}, f32[256,512]{1,0:T(8,128)}, bf16[256,256]{1,0:T(8,128)(2,1)}, bf16[256,1152]{1,0:T(8,128)(2,1)}) custom-call(bf16[256,1152]{1,0:T(8,128)(2,1)} %get-tuple-element.181.refs_0_.refs_1_, bf16[256,768]{1,0:T(8,128)(2,1)} %get-tuple-element.184.refs_1_, ...), custom_call_target="tpu_custom_call" | custom-call | tf_op jit(solution)/shard_map/pallas_call | solution.py:59
  153.1 3.1 %shard_map.413 = (f32[8,128]{1,0:T(8,128)}, bf16[128,2048]{1,0:T(8,128)(2,1)}, f32[128,2048]{1,0:T(8,128)}) custom-call(bf16[256,512]{1,0:T(8,128)(2,1)} %get-tuple-element.194.refs_0_, bf16[256,512]{1,0:T(8,128)(2,1)} %get-tuple-element.156.refs_3_.refs_1_, bf16[256,1024]{1,0:T(8,128)(2,1)} %copy-done.16, bf16[256,512]{1,0:T(8,128)(2,1)} %get-tuple-element.196.refs_3_, ...), custom_call_target="tpu_custom_call" | custom-call | tf_op jit(solution)/shard_map/pallas_call | solution.py:59
  158.5 2.6 %shard_map.414 = (f32[8,128]{1,0:T(8,128)}, bf16[128,1152]{1,0:T(8,128)(2,1)}, f32[128,1152]{1,0:T(8,128)}) custom-call(bf16[256,512]{1,0:T(8,128)(2,1)} %get-tuple-element.172.refs_22_.refs_11_.refs_0_, bf16[256,1152]{1,0:T(8,128)(2,1)} %get-tuple-element.181.refs_0_.refs_1_, bf16[256,1152]{1,0:T(8,128)(2,1)} %copy-done.12, f32[8,128]{1,0:T(8,128)} %get-tuple-element.200.refs_3_), custom_call_target="tpu_custom_call" | custom-call | tf_op jit(solution)/shard_map/pallas_call | solution.py:59
  163.0 2.8 %shard_map.415 = (f32[8,128]{1,0:T(8,128)}, f32[256,512]{1,0:T(8,128)}, f32[16,256]{1,0:T(8,128)}) custom-call(bf16[256,512]{1,0:T(8,128)(2,1)} %get-tuple-element.158.refs_1_.refs_0_, f32[256,512]{1,0:T(8,128)} %get-tuple-element.191.refs_1_, f32[256,512]{1,0:T(8,128)} %copy-done.17, f32[256,512]{1,0:T(8,128)} %get-tuple-element.192.refs_3_, ...), custom_call_target="tpu_custom_call" | custom-call | tf_op jit(solution)/shard_map/pallas_call | solution.py:59
  166.6 2.3 shard_map.416
  169.0 2.6 %collective-permute-start.23 = (bf16[64,2048]{1,0:T(8,128)(2,1)}, bf16[64,2048]{1,0:T(8,128)(2,1)S(1)}, u32[]{:S(2)}, u32[]{:S(2)}) collective-permute-start(bf16[64,2048]{1,0:T(8,128)(2,1)} %get-tuple-element.222), channel_id=1, source_target_pairs={{0,16},{4,20},{8,24},{12,28},{16,0},{20,4},{24,8},{28,12},{1,17},{... | collective-permute-start | bytes 786440 | tf_op jit(solution)/shard_map/ppermute | solution.py:20
  173.1 2.5 %collective-permute-done.16.refs_7_ = f32[16,256]{1,0:T(8,128)S(1)} collective-permute-done((f32[16,256]{1,0:T(8,128)}, f32[16,256]{1,0:T(8,128)S(1)}, u32[]{:S(2)}, u32[]{:S(2)}) %collective-permute-start.16) | collective-permute-done | bytes 16416 | tf_op jit(solution)/shard_map/ppermute | solution.py:20
  176.1 2.6 %shard_map.417 = (f32[8,128]{1,0:T(8,128)}, f32[256,256]{1,0:T(8,128)}, f32[32,768]{1,0:T(8,128)}) custom-call(s32[3]{0:T(128)} %pad_add_fusion.1.refs_0_, bf16[256,512]{1,0:T(8,128)(2,1)} %get-tuple-element.158.refs_1_.refs_0_, f32[256,128]{1,0:T(8,128)} %get-tuple-element.179.refs_2_, f32[256,512]{1,0:T(8,128)} %get-tuple-element.180.refs_3_, ...), custom_call_target="tpu_custom_call" | custom-call | tf_op jit(solution)/shard_map/pallas_call | solution.py:59
  185.9 3.7 %collective-permute-done.22.refs_1_ = bf16[64,1152]{1,0:T(8,128)(2,1)S(1)} collective-permute-done((bf16[64,1152]{1,0:T(8,128)(2,1)}, bf16[64,1152]{1,0:T(8,128)(2,1)S(1)}, u32[]{:S(2)}, u32[]{:S(2)}) %collective-permute-start.22) | collective-permute-done | bytes 147488 | tf_op jit(solution)/shard_map/ppermute | solution.py:20
  192.7 2.3 shard_map.421
  195.9 2.7 %shard_map.422 = (f32[8,128]{1,0:T(8,128)}, bf16[192,1152]{1,0:T(8,128)(2,1)}, f32[128,1152]{1,0:T(8,128)}, f32[32,768]{1,0:T(8,128)}) custom-call(bf16[256,512]{1,0:T(8,128)(2,1)} %get-tuple-element.172.refs_22_.refs_11_.refs_0_, bf16[256,768]{1,0:T(8,128)(2,1)} %get-tuple-element.184.refs_1_, bf16[256,256]{1,0:T(8,128)(2,1)} %get-tuple-element.211.refs_2_, ...), custom_call_target="tpu_custom_call" | custom-call | tf_op jit(solution)/shard_map/pallas_call | solution.py:59
  199.1 3.3 %collective-permute-start.25 = (bf16[64,2048]{1,0:T(8,128)(2,1)}, bf16[64,2048]{1,0:T(8,128)(2,1)S(1)}, u32[]{:S(2)}, u32[]{:S(2)}) collective-permute-start(bf16[64,2048]{1,0:T(8,128)(2,1)} %get-tuple-element.231), channel_id=1, source_target_pairs={{0,16},{4,20},{8,24},{12,28},{16,0},{20,4},{24,8},{28,12},{1,17},{... | collective-permute-start | bytes 786440 | tf_op jit(solution)/shard_map/ppermute | solution.py:20
  202.3 10.9 %collective-permute-done.25.refs_1_ = bf16[64,2048]{1,0:T(8,128)(2,1)S(1)} collective-permute-done((bf16[64,2048]{1,0:T(8,128)(2,1)}, bf16[64,2048]{1,0:T(8,128)(2,1)S(1)}, u32[]{:S(2)}, u32[]{:S(2)}) %collective-permute-start.25) | collective-permute-done | bytes 262176 | tf_op jit(solution)/shard_map/ppermute | solution.py:20
  216.6 2.1 shard_map.424
  218.7 3.3 %collective-permute-start.26 = (bf16[128,1152]{1,0:T(8,128)(2,1)}, bf16[128,1152]{1,0:T(8,128)(2,1)S(1)}, u32[]{:S(2)}, u32[]{:S(2)}) collective-permute-start(bf16[128,1152]{1,0:T(8,128)(2,1)} %get-tuple-element.235), channel_id=1, source_target_pairs={{0,16},{4,20},{8,24},{12,28},{16,0},{20,4},{24,8},{28,12},{1,17},{... | collective-permute-start | bytes 884744 | tf_op jit(solution)/shard_map/ppermute | solution.py:20
  223.2 10.2 %collective-permute-done.26.refs_2_ = bf16[128,1152]{1,0:T(8,128)(2,1)S(1)} collective-permute-done((bf16[128,1152]{1,0:T(8,128)(2,1)}, bf16[128,1152]{1,0:T(8,128)(2,1)S(1)}, u32[]{:S(2)}, u32[]{:S(2)}) %collective-permute-start.26) | collective-permute-done | bytes 294944 | tf_op jit(solution)/shard_map/ppermute | solution.py:20
  (176 shorter events, 63.1 us)
Async XLA Ops:
  7.4 42.9 %copy-start.37 = (bf16[512]{0:T(512)(128)(2,1)S(1)}, bf16[512]{0:T(512)(128)(2,1)}, u32[]{:S(2)}) copy-start(bf16[512]{0:T(512)(128)(2,1)} %param.27) | copy-start | bytes 3076
  7.4 43.5 %copy-start.29 = (bf16[512,12]{0,1:T(8,128)(2,1)S(1)}, bf16[512,12]{0,1:T(8,128)(2,1)}, u32[]{:S(2)}) copy-start(bf16[512,12]{0,1:T(8,128)(2,1)} %param.30) | copy-start | bytes 36868
  11.0 32.1 %collective-permute-start = (bf16[5152,128]{1,0:T(8,128)(2,1)}, bf16[5152,128]{1,0:T(8,128)(2,1)S(1)}, u32[]{:S(2)}, u32[]{:S(2)}) collective-permute-start(bf16[5152,128]{1,0:T(8,128)(2,1)} %get-tuple-element.139), channel_id=1, source_target_pairs={{0,2},{2,0},{1,3},{3,1},{4,6},{6,4},{5,7},{7,5},{8,10},{10,8},{9,1... | collective-permute-start | bytes 3956744 | tf_op jit(solution)/shard_map/ppermute | solution.py:20
  46.9 4.9 %collective-permute-start.1 = (bf16[1024,256]{1,0:T(8,128)(2,1)}, bf16[1024,256]{1,0:T(8,128)(2,1)S(1)}, u32[]{:S(2)}, u32[]{:S(2)}) collective-permute-start(bf16[1024,256]{1,0:T(8,128)(2,1)} %get-tuple-element.141.refs_1_), channel_id=1, source_target_pairs={{0,1},{1,0},{2,3},{3,2},{4,5},{5,4},{6,7},{7,6},{8,9},{9,8},{10,11... | collective-permute-start | bytes 1572872 | tf_op jit(solution)/shard_map/ppermute | solution.py:20
  47.0 14.6 %collective-permute-start.2 = (bf16[2048,128]{1,0:T(8,128)(2,1)}, bf16[2048,128]{1,0:T(8,128)(2,1)S(1)}, u32[]{:S(2)}, u32[]{:S(2)}) collective-permute-start(bf16[2048,128]{1,0:T(8,128)(2,1)} %get-tuple-element.142.refs_0_.refs_3_.refs_4_.refs_9_), channel_id=1, source_target_pairs={{0,4},{4,0},{8,12},{12,8},{16,20},{20,16},{24,28},{28,24},{1,5},{5... | collective-permute-start | bytes 1572872 | tf_op jit(solution)/shard_map/ppermute | solution.py:20
  48.8 14.2 %collective-permute-start.3 = (bf16[128,2048]{1,0:T(8,128)(2,1)}, bf16[128,2048]{1,0:T(8,128)(2,1)S(1)}, u32[]{:S(2)}, u32[]{:S(2)}) collective-permute-start(bf16[128,2048]{1,0:T(8,128)(2,1)} %get-tuple-element.143.refs_2_.refs_7_), channel_id=1, source_target_pairs={{0,8},{4,12},{8,0},{12,4},{16,24},{20,28},{24,16},{28,20},{1,9},{5... | collective-permute-start | bytes 1572872 | tf_op jit(solution)/shard_map/ppermute | solution.py:20
  52.6 16.3 %copy-start.36 = (bf16[256,4]{0,1:T(4,128)(2,1)S(1)}, bf16[256,4]{0,1:T(4,128)(2,1)}, u32[]{:S(2)}) copy-start(bf16[256,4]{0,1:T(4,128)(2,1)} %param.36) | copy-start | bytes 6148
  57.5 28.0 %collective-permute-start.5 = (bf16[256,2304]{1,0:T(8,128)(2,1)}, bf16[256,2304]{1,0:T(8,128)(2,1)S(1)}, u32[]{:S(2)}, u32[]{:S(2)}) collective-permute-start(bf16[256,2304]{1,0:T(8,128)(2,1)} %get-tuple-element.149), channel_id=1, source_target_pairs={{0,2},{2,0},{1,3},{3,1},{4,6},{6,4},{5,7},{7,5},{8,10},{10,8},{9,1... | collective-permute-start | bytes 3538952 | tf_op jit(solution)/shard_map/ppermute | solution.py:20
  67.2 26.0 %collective-permute-start.4 = (bf16[2048,256]{1,0:T(8,128)(2,1)}, bf16[2048,256]{1,0:T(8,128)(2,1)S(1)}, u32[]{:S(2)}, u32[]{:S(2)}) collective-permute-start(bf16[2048,256]{1,0:T(8,128)(2,1)} %get-tuple-element.147), channel_id=1, source_target_pairs={{0,8},{4,12},{8,0},{12,4},{16,24},{20,28},{24,16},{28,20},{1,9},{5... | collective-permute-start | bytes 3145736 | tf_op jit(solution)/shard_map/ppermute | solution.py:20
  68.8 17.5 %copy-start.27 = (f32[1,256]{1,0:T(1,128)}, f32[1,256]{1,0:T(1,128)S(1)}, u32[]{:S(2)}) copy-start(f32[1,256]{1,0:T(1,128)S(1)} %convert_element_type.23.refs_0_.refs_16_) | copy-start | bytes 3076
  69.6 32.4 %collective-permute-start.7 = (bf16[256,2048]{1,0:T(8,128)(2,1)}, bf16[256,2048]{1,0:T(8,128)(2,1)S(1)}, u32[]{:S(2)}, u32[]{:S(2)}) collective-permute-start(bf16[256,2048]{1,0:T(8,128)(2,1)} %get-tuple-element.162), channel_id=1, source_target_pairs={{0,4},{4,0},{8,12},{12,8},{16,20},{20,16},{24,28},{28,24},{1,5},{5... | collective-permute-start | bytes 3145736 | tf_op jit(solution)/shard_map/ppermute | solution.py:20
  97.9 4.0 %collective-permute-start.6 = (f32[256,1024]{1,0:T(8,128)}, f32[256,1024]{1,0:T(8,128)S(1)}, u32[]{:S(2)}, u32[]{:S(2)}) collective-permute-start(f32[256,1024]{1,0:T(8,128)} %get-tuple-element.160.refs_3_), channel_id=1, source_target_pairs={{0,1},{1,0},{2,3},{3,2},{4,5},{5,4},{6,7},{7,6},{8,9},{9,8},{10,11... | collective-permute-start | bytes 3145736 | tf_op jit(solution)/shard_map/ppermute | solution.py:20
  111.1 7.2 %collective-permute-start.8 = (f32[256,1024]{1,0:T(8,128)}, f32[256,1024]{1,0:T(8,128)S(1)}, u32[]{:S(2)}, u32[]{:S(2)}) collective-permute-start(f32[256,1024]{1,0:T(8,128)} %get-tuple-element.166.refs_4_), channel_id=1, source_target_pairs={{0,1},{1,0},{2,3},{3,2},{4,5},{5,4},{6,7},{7,6},{8,9},{9,8},{10,11... | collective-permute-start | bytes 3145736 | tf_op jit(solution)/shard_map/ppermute | solution.py:20
  116.2 25.5 %collective-permute-start.11 = (bf16[256,2048]{1,0:T(8,128)(2,1)}, bf16[256,2048]{1,0:T(8,128)(2,1)S(1)}, u32[]{:S(2)}, u32[]{:S(2)}) collective-permute-start(bf16[256,2048]{1,0:T(8,128)(2,1)} %get-tuple-element.188), channel_id=1, source_target_pairs={{0,4},{4,0},{8,12},{12,8},{16,20},{20,16},{24,28},{28,24},{1,5},{5... | collective-permute-start | bytes 3145736 | tf_op jit(solution)/shard_map/ppermute | solution.py:20
  116.7 1.5 collective-permute-start.9
  116.7 34.3 %collective-permute-start.14 = (bf16[256,1024]{1,0:T(8,128)(2,1)}, bf16[256,1024]{1,0:T(8,128)(2,1)S(1)}, u32[]{:S(2)}, u32[]{:S(2)}) collective-permute-start(bf16[256,1024]{1,0:T(8,128)(2,1)} %get-tuple-element.195), channel_id=1, source_target_pairs={{0,8},{4,12},{8,0},{12,4},{16,24},{20,28},{24,16},{28,20},{1,9},{5... | collective-permute-start | bytes 1572872 | tf_op jit(solution)/shard_map/ppermute | solution.py:20
  137.9 7.9 %collective-permute-start.10 = (f32[264,256]{1,0:T(8,128)}, f32[264,256]{1,0:T(8,128)S(1)}, u32[]{:S(2)}, u32[]{:S(2)}) collective-permute-start(f32[264,256]{1,0:T(8,128)} %get-tuple-element.186.refs_3_.refs_5_), channel_id=1, source_target_pairs={{0,1},{1,0},{2,3},{3,2},{4,5},{5,4},{6,7},{7,6},{8,9},{9,8},{10,11... | collective-permute-start | bytes 811016 | tf_op jit(solution)/shard_map/ppermute | solution.py:20
  138.1 14.2 %collective-permute-start.15 = (bf16[256,1024]{1,0:T(8,128)(2,1)S(1)}, bf16[256,1024]{1,0:T(8,128)(2,1)S(1)}, u32[]{:S(2)}, u32[]{:S(2)}) collective-permute-start(bf16[256,1024]{1,0:T(8,128)(2,1)S(1)} %copy-done.42), channel_id=1, source_target_pairs={{0,8},{4,12},{8,0},{12,4},{16,24},{20,28},{24,16},{28,20},{1,9},{5... | collective-permute-start | bytes 1572872 | tf_op jit(solution)/shard_map/ppermute | solution.py:20
  138.7 19.0 %collective-permute-start.13 = (bf16[256,1152]{1,0:T(8,128)(2,1)S(1)}, bf16[256,1152]{1,0:T(8,128)(2,1)S(1)}, u32[]{:S(2)}, u32[]{:S(2)}) collective-permute-start(bf16[256,1152]{1,0:T(8,128)(2,1)S(1)} %copy-done.41), channel_id=1, source_target_pairs={{0,4},{4,0},{8,12},{12,8},{16,20},{20,16},{24,28},{28,24},{1,5},{5... | collective-permute-start | bytes 1769480 | tf_op jit(solution)/shard_map/ppermute | solution.py:20
  150.7 11.5 %collective-permute-start.12 = (f32[256,512]{1,0:T(8,128)}, f32[256,512]{1,0:T(8,128)S(1)}, u32[]{:S(2)}, u32[]{:S(2)}) collective-permute-start(f32[256,512]{1,0:T(8,128)} %get-tuple-element.191.refs_1_), channel_id=1, source_target_pairs={{0,1},{1,0},{2,3},{3,2},{4,5},{5,4},{6,7},{7,6},{8,9},{9,8},{10,11... | collective-permute-start | bytes 1572872 | tf_op jit(solution)/shard_map/ppermute | solution.py:20
  150.7 15.1 %collective-permute-start.17 = (bf16[128,2048]{1,0:T(8,128)(2,1)S(1)}, bf16[128,2048]{1,0:T(8,128)(2,1)S(1)}, u32[]{:S(2)}, u32[]{:S(2)}) collective-permute-start(bf16[128,2048]{1,0:T(8,128)(2,1)S(1)} %copy-done.43), channel_id=1, source_target_pairs={{0,8},{4,12},{8,0},{12,4},{16,24},{20,28},{24,16},{28,20},{1,9},{5... | collective-permute-start | bytes 1572872 | tf_op jit(solution)/shard_map/ppermute | solution.py:20
  151.1 44.0 %collective-permute-start.18 = (bf16[256,1152]{1,0:T(8,128)(2,1)}, bf16[256,1152]{1,0:T(8,128)(2,1)S(1)}, u32[]{:S(2)}, u32[]{:S(2)}) collective-permute-start(bf16[256,1152]{1,0:T(8,128)(2,1)} %get-tuple-element.212), channel_id=1, source_target_pairs={{0,4},{4,0},{8,12},{12,8},{16,20},{20,16},{24,28},{28,24},{1,5},{5... | collective-permute-start | bytes 1769480 | tf_op jit(solution)/shard_map/ppermute | solution.py:20
  156.2 35.8 %collective-permute-start.20 = (bf16[128,2048]{1,0:T(8,128)(2,1)}, bf16[128,2048]{1,0:T(8,128)(2,1)S(1)}, u32[]{:S(2)}, u32[]{:S(2)}) collective-permute-start(bf16[128,2048]{1,0:T(8,128)(2,1)} %get-tuple-element.215), channel_id=1, source_target_pairs={{0,4},{4,0},{8,12},{12,8},{16,20},{20,16},{24,28},{28,24},{1,5},{5... | collective-permute-start | bytes 1572872 | tf_op jit(solution)/shard_map/ppermute | solution.py:20
  161.1 17.6 %collective-permute-start.21 = (bf16[128,1152]{1,0:T(8,128)(2,1)}, bf16[128,1152]{1,0:T(8,128)(2,1)S(1)}, u32[]{:S(2)}, u32[]{:S(2)}) collective-permute-start(bf16[128,1152]{1,0:T(8,128)(2,1)} %get-tuple-element.217), channel_id=1, source_target_pairs={{0,8},{4,12},{8,0},{12,4},{16,24},{20,28},{24,16},{28,20},{1,9},{5... | collective-permute-start | bytes 884744 | tf_op jit(solution)/shard_map/ppermute | solution.py:20
  169.0 14.3 %collective-permute-start.23 = (bf16[64,2048]{1,0:T(8,128)(2,1)}, bf16[64,2048]{1,0:T(8,128)(2,1)S(1)}, u32[]{:S(2)}, u32[]{:S(2)}) collective-permute-start(bf16[64,2048]{1,0:T(8,128)(2,1)} %get-tuple-element.222), channel_id=1, source_target_pairs={{0,16},{4,20},{8,24},{12,28},{16,0},{20,4},{24,8},{28,12},{1,17},{... | collective-permute-start | bytes 786440 | tf_op jit(solution)/shard_map/ppermute | solution.py:20
  171.6 3.9 %collective-permute-start.16 = (f32[16,256]{1,0:T(8,128)}, f32[16,256]{1,0:T(8,128)S(1)}, u32[]{:S(2)}, u32[]{:S(2)}) collective-permute-start(f32[16,256]{1,0:T(8,128)} %get-tuple-element.203.refs_6_), channel_id=1, source_target_pairs={{0,2},{2,0},{1,3},{3,1},{4,6},{6,4},{5,7},{7,5},{8,10},{10,8},{9,1... | collective-permute-start | bytes 49160 | tf_op jit(solution)/shard_map/ppermute | solution.py:20
  181.3 8.2 %collective-permute-start.22 = (bf16[64,1152]{1,0:T(8,128)(2,1)}, bf16[64,1152]{1,0:T(8,128)(2,1)S(1)}, u32[]{:S(2)}, u32[]{:S(2)}) collective-permute-start(bf16[64,1152]{1,0:T(8,128)(2,1)} %get-tuple-element.220), channel_id=1, source_target_pairs={{0,16},{4,20},{8,24},{12,28},{16,0},{20,4},{24,8},{28,12},{1,17},{... | collective-permute-start | bytes 442376 | tf_op jit(solution)/shard_map/ppermute | solution.py:20
  181.7 13.4 %collective-permute-start.19 = (f32[32,768]{1,0:T(8,128)}, f32[32,768]{1,0:T(8,128)S(1)}, u32[]{:S(2)}, u32[]{:S(2)}) collective-permute-start(f32[32,768]{1,0:T(8,128)} %get-tuple-element.213.refs_5_), channel_id=1, source_target_pairs={{0,4},{4,0},{8,12},{12,8},{16,20},{20,16},{24,28},{28,24},{1,5},{5... | collective-permute-start | bytes 294920 | tf_op jit(solution)/shard_map/ppermute | solution.py:20
  195.0 27.0 %copy-start.15 = (f32[64,2048]{1,0:T(8,128)S(1)}, f32[64,2048]{1,0:T(8,128)}, u32[]{:S(2)}) copy-start(f32[64,2048]{1,0:T(8,128)} %get-tuple-element.255) | copy-start | bytes 1572868
  198.6 17.3 %collective-permute-start.24 = (bf16[192,1152]{1,0:T(8,128)(2,1)}, bf16[192,1152]{1,0:T(8,128)(2,1)S(1)}, u32[]{:S(2)}, u32[]{:S(2)}) collective-permute-start(bf16[192,1152]{1,0:T(8,128)(2,1)} %get-tuple-element.228), channel_id=1, source_target_pairs={{0,8},{4,12},{8,0},{12,4},{16,24},{20,28},{24,16},{28,20},{1,9},{5... | collective-permute-start | bytes 1327112 | tf_op jit(solution)/shard_map/ppermute | solution.py:20
  199.1 14.2 %collective-permute-start.25 = (bf16[64,2048]{1,0:T(8,128)(2,1)}, bf16[64,2048]{1,0:T(8,128)(2,1)S(1)}, u32[]{:S(2)}, u32[]{:S(2)}) collective-permute-start(bf16[64,2048]{1,0:T(8,128)(2,1)} %get-tuple-element.231), channel_id=1, source_target_pairs={{0,16},{4,20},{8,24},{12,28},{16,0},{20,4},{24,8},{28,12},{1,17},{... | collective-permute-start | bytes 786440 | tf_op jit(solution)/shard_map/ppermute | solution.py:20
  218.7 14.7 %collective-permute-start.26 = (bf16[128,1152]{1,0:T(8,128)(2,1)}, bf16[128,1152]{1,0:T(8,128)(2,1)S(1)}, u32[]{:S(2)}, u32[]{:S(2)}) collective-permute-start(bf16[128,1152]{1,0:T(8,128)(2,1)} %get-tuple-element.235), channel_id=1, source_target_pairs={{0,16},{4,20},{8,24},{12,28},{16,0},{20,4},{24,8},{28,12},{1,17},{... | collective-permute-start | bytes 884744 | tf_op jit(solution)/shard_map/ppermute | solution.py:20
  (44 other events, 156.9 us)

commit v4 on v3

--- a/solution.py
+++ b/solution.py
@@ -64,11 +64,20 @@
             out_specs=[pl.BlockSpec(memory_space=pltpu.VMEM)]
             + [pl.BlockSpec(memory_space=plain)] * len(outs),
             scratch_shapes=[pltpu.VMEM(s, d) if d is not None else s for s, d in scratch],
-            compiler_params=pltpu.CompilerParams(vmem_limit_bytes=56 << 20),
+            compiler_params=pltpu.CompilerParams(vmem_limit_bytes=62 << 20),
             cost_estimate=pl.CostEstimate(flops=0, bytes_accessed=0, transcendentals=0),
         )(*args, *extra)
         self.token = results[0]
         return results[1:]
+
+
+def two_parts(value):
+    high = value.astype(BF16)
+    return high, (value - high.astype(F32)).astype(BF16)
+
+
+def dot_three(product, left, right):
+    return product(left[0], right[0]) + (product(left[1], right[0]) + product(left[0], right[1]))
 
 
 def iota(shape, dim):
@@ -91,7 +100,7 @@
     for w in (wm, wa, wd):
         out[row : row + w.shape[0]] = w[:, pl.ds(at, piece)]
         row += w.shape[0]
-    for value in (gu[pl.ds(at, piece), :], cot[...], hid[...]):
+    for value in (gu, cot, hid):
         for j in range(value.shape[1] // piece):
             out[row : row + value.shape[0]] = value[:, j * piece : (j + 1) * piece]
             row += value.shape[0]
@@ -129,7 +138,7 @@
 
 
 def split_kernel(
-    heads, place, got, cot, hid, small, t_out, g_out, pair_out, x_par_out, head_out, gain_out
+    heads, place, got, cot, small, t_out, g_out, pair_out, x_par_out, head_out, gain_out
 ):
     piece = got.shape[1]
     tokens = cot.shape[0]
@@ -138,11 +147,10 @@
     for j in range(g_out.shape[1] // piece):
         g_out[:, j * piece : (j + 1) * piece] = got[row : row + piece]
         row += piece
-    for i, value in enumerate((cot, hid)):
-        at = 2 * i * tokens
-        pair_out[at : at + tokens] = value[...]
-        for j in range(value.shape[1] // piece):
-            pair_out[at + tokens : at + 2 * tokens, j * piece : (j + 1) * piece] = got[
+    pair_out[0:tokens] = cot[...]
+    for i in (1, 2):
+        for j in range(cot.shape[1] // piece):
+            pair_out[i * tokens : (i + 1) * tokens, j * piece : (j + 1) * piece] = got[
                 row : row + tokens
             ]
             row += tokens
@@ -151,51 +159,49 @@
     join_small(place, heads, own, far, x_par_out, head_out, gain_out)
 
 
-def gather_quarters(place, mine, came, at, own_out, far_out, far_tmp):
-    width = own_out.shape[1] // 2
-    piece = width // 2
-    first = place[0] == 0
-    tokens = own_out.shape[0]
-    for i, out in enumerate((own_out, far_tmp)):
-        rows = slice((at + i) * tokens, (at + i + 1) * tokens)
-        a = mine[rows]
-        b = came[rows]
-        out[:, :width] = jnp.where(first, a, b)
-        out[:, width:] = jnp.where(first, b, a)
+def far_order(place, value, out):
+    piece = value.shape[1] // 4
     for j in range(4):
         at = pl.multiple_of((place[1] ^ j) * piece, piece)
-        far_out[:, j * piece : (j + 1) * piece] = far_tmp[:, pl.ds(at, piece)]
-
-
-def project_kernel(
-    place, mine, came, gain, wx, wb, wd, wg, wq, wk,
-    n1_out, p_out, low_out, own_out, far_out, factor_out, far_tmp,
-):
-    gather_quarters(place, mine, came, 2, own_out, far_out, far_tmp)
-    own = own_out[...].astype(F32)
-    far = far_tmp[...].astype(F32)
-    mean = jnp.sum(own * own + far * far, axis=1, keepdims=True) / (2 * own.shape[1])
-    factor = lax.rsqrt(mean + NORM_EPS)
-    factor_out[...] = jnp.broadcast_to(factor, factor_out.shape)
-    n1 = (own * factor * gain[...]).astype(BF16)
-    n1_out[...] = n1
+        out[:, j * piece : (j + 1) * piece] = value[:, pl.ds(at, piece)]
+
+
+def side_by_side(place, a, b, out):
+    width = a.shape[1]
+    first = place[0] == 0
+    out[:, :width] = jnp.where(first, a, b)
+    out[:, width:] = jnp.where(first, b, a)
+
+
+def project_kernel(place, mine, came, gain, wx, wb, wd, wg, wq, wk, own_out, p_out, low_out):
+    side_by_side(place, mine[...], came[...], own_out)
+    high, low = two_parts(own_out[...].astype(F32) * gain[...])
     at = 0
     for w in (wx, wb, wd, wg, wq, wk):
         size = w.shape[1]
-        part = dot(n1, w[...])
+        part = dot(high, w[...]) + dot(low, w[...])
         p_out[:, at : at + size] = part
         low_out[:, at : at + size] = part.astype(BF16)
         at += size
 
 
-def hop_kernel(t_first, t_second, g_first, g_second, n1, order, t_out, g_out, left_out):
-    t_piece = t_first.shape[1]
-    g_piece = g_first.shape[0]
-    t_out[:, :t_piece] = t_first[...]
-    t_out[:, t_piece:] = t_second[...]
-    g_out[:g_piece] = g_first[...]
-    g_out[g_piece:] = g_second[...]
-    left_out[...] = permuted(n1[...], order[...])
+def norm_kernel(
+    place, pair, came, own, gain, order,
+    far_out, dy_own, dy_far, factor_out, n1_out, left_out, far_tmp,
+):
+    tokens = own.shape[0]
+    side_by_side(place, pair[0:tokens], came[0:tokens], dy_own)
+    side_by_side(place, pair[tokens : 2 * tokens], came[tokens : 2 * tokens], far_tmp)
+    far_order(place, far_tmp, dy_far)
+    side_by_side(place, pair[2 * tokens :], came[2 * tokens :], far_tmp)
+    far_order(place, far_tmp, far_out)
+    hid = own[...].astype(F32)
+    far = far_out[...].astype(F32)
+    mean = jnp.sum(hid * hid + far * far, axis=1, keepdims=True) / (2 * hid.shape[1])
+    factor = lax.rsqrt(mean + NORM_EPS)
+    factor_out[...] = jnp.broadcast_to(factor, factor_out.shape)
+    n1_out[...] = (hid * factor * gain[...]).astype(BF16)
+    left_out[...] = permuted(n1_out[...], order[...])
 
 
 def masks(seg_row, seg_col, turned):
@@ -246,13 +252,13 @@
 
 
 def mix_kernel(
-    ch, nq, seg_row, seg_col, own, came, x_par, bc_par, head_par,
+    ch, nq, seg_row, seg_col, factor, own, came, x_par, bc_par, head_par,
     mixed_out, sums_out, pre_out, y_out,
 ):
     tokens = own.shape[0]
     nbc = bc_par.shape[1]
     state = nbc // 2
-    sums_out[...] = own[...] + came[...].astype(F32)
+    sums_out[...] = factor[:, :1] * (own[...] + came[...].astype(F32))
     lane = iota((tokens, LANES), 1)
     low = lane < HEAD
     mask = masks(seg_row, seg_col, False)
@@ -288,18 +294,18 @@
         z = sums_out[:, base + p * LANES : base + (p + 1) * LANES]
         mixed_out[:, part] = (y * (z * jax.nn.sigmoid(z))).astype(BF16)
     at = base + ch
-    kv = sums_out[:, at + nq : at + nq + LANES].astype(BF16)
-    kv_turn = pltpu.roll(sums_out[:, at + nq : at + nq + LANES], HEAD, 1).astype(BF16)
-    keys = jnp.where(low, kv, kv_turn)
-    vals = jnp.where(low, kv_turn, kv)
+    kv = sums_out[:, at + nq : at + nq + LANES]
+    kv_turn = pltpu.roll(kv, HEAD, 1)
+    keys = two_parts(jnp.where(low, kv, kv_turn))
+    vals = two_parts(jnp.where(low, kv_turn, kv))
     for p in range(nq // LANES):
         query = sums_out[:, at + p * LANES : at + (p + 1) * LANES] * (HEAD ** -0.5)
         outs = []
         for side in (low, ~low):
-            score = dot_bt(jnp.where(side, query, 0.0).astype(BF16), keys) + mask
+            score = dot_three(dot_bt, two_parts(jnp.where(side, query, 0.0)), keys) + mask
             score = jnp.exp(score - jnp.max(score, axis=1, keepdims=True))
             total = jnp.sum(score, axis=1, keepdims=True)
-            outs.append(dot(score.astype(BF16), vals) / total)
+            outs.append(dot_three(dot, two_parts(score), vals) / total)
         mixed_out[:, ch + p * LANES : ch + (p + 1) * LANES] = jnp.where(
             low, outs[0], outs[1]
         ).astype(BF16)
@@ -423,49 +429,45 @@
         gbc_out[tokens : tokens + 8, part] = rows
 
 
-def tall_far(first, second, pair, start, size):
+def tall_far(fetch, start, size):
     return jnp.concatenate(
-        [r[start : start + size] for r in (first, second, pair)], axis=1
-    )
-
-
-def out_kernel(mixed, wm, wa, first, second, pair, part_out):
+        [r[start : start + size] for r in fetch], axis=1
+    )
+
+
+def out_kernel(mixed, wm, wa, t0, t1, t2, t3, part_out):
+    fetch = (t0, t1, t2, t3)
     half = wm.shape[1]
     ch = wm.shape[0]
     value = mixed[...]
     part_out[:, :half] = dot(value[:, :ch], wm[...]) + dot(value[:, ch:], wa[...])
-    part_out[:, half:] = dot(value, tall_far(first, second, pair, 0, value.shape[1]))
+    part_out[:, half:] = dot(value, tall_far(fetch, 0, value.shape[1]))
 
 
 def norm_factor(value):
     return lax.rsqrt(jnp.mean(value * value, axis=1, keepdims=True) + NORM_EPS)
 
 
-def act_grad_kernel(
-    inner, place, mine, came, wd, first, second, pair, own_out, far_out, ga_out, far_tmp
-):
-    gather_quarters(place, mine, came, 0, own_out, far_out, far_tmp)
+def act_grad_kernel(inner, dy_own, dy_far, wd, t0, t1, t2, t3, ga_out):
+    fetch = (t0, t1, t2, t3)
     ff = wd.shape[0]
-    ga_out[...] = dot_bt(own_out[...], wd[...]) + dot_bt(
-        far_out[...], tall_far(first, second, pair, inner, ff)
+    ga_out[...] = dot_bt(dy_own[...], wd[...]) + dot_bt(
+        dy_far[...], tall_far(fetch, inner, ff)
     )
 
 
 def feed_kernel(
-    place, own, far, part, came, gain, gu, gu_first, gu_second, gu_pair, grad_act, wd,
+    place, own, far, part, came, gain, gu, gu0, gu1, gu2, gu3, grad_act, wd,
     h2_out, n2_out, act_out, ggu_out, n2p_out, keep_out, send_out,
 ):
     half = own.shape[1]
     quarter = half // 2
-    piece = half // 4
     h2_out[:, :half] = own[...].astype(F32) + (part[:, :half] + came[:, :half])
     h2_out[:, half:] = far[...].astype(F32) + (part[:, half:] + came[:, half:])
     h2 = h2_out[...]
     n2 = (h2 * norm_factor(h2) * gain[...]).astype(BF16)
     n2_out[...] = n2[:, :half]
-    gu_far = jnp.concatenate(
-        [gu_first[...], gu_pair[0:piece], gu_second[...], gu_pair[piece:]], axis=0
-    )
+    gu_far = jnp.concatenate([gu0[...], gu1[...], gu2[...], gu3[...]], axis=0)
     ff = wd.shape[0]
     gate_up = dot(n2[:, :half], gu[...]) + dot(n2[:, half:], gu_far)
     gate = gate_up[:, :ff]
@@ -509,10 +511,11 @@
 
 
 def turn_kernel(
-    ch, nq, place, dy_own, dy_far, h2, part, came, gain, wm, wa, first, second, pair, d_keep, d_came,
+    ch, nq, place, dy_own, dy_far, h2, part, came, gain, wm, wa, t0, t1, t2, t3, d_keep, d_came,
     mixed, order_mix, seg_row, seg_col, sums, pre, ys, x_par, left1,
     dym_out, resid_out, low_out, gain_out, output_out, m_send, m_left, gtwo_out, two_send,
 ):
+    fetch = (t0, t1, t2, t3)
     half = dy_own.shape[1]
     quarter = half // 2
     value = h2[...]
@@ -534,7 +537,7 @@
     resid_out[...] = dh_own
     low_own = dh_own.astype(BF16)
     low_out[...] = low_own
-    dym = dot_bt(dh_far.astype(BF16), tall_far(first, second, pair, 0, dym_out.shape[1]))
+    dym = dot_bt(dh_far.astype(BF16), tall_far(fetch, 0, dym_out.shape[1]))
     dym_out[:, :ch] = dym[:, :ch] + dot_bt(low_own, wm[...])
     dym_out[:, ch:] = dym[:, ch:] + dot_bt(low_own, wa[...])
     unmix_two_kernel(ch, nq, seg_row, seg_col, sums, pre, ys, dym_out, x_par, gtwo_out)
@@ -644,18 +647,26 @@
     first = place[2] == 0
     half = n1_out.shape[1]
     cq = xb_out.shape[1]
-    n1_out[...] = value[24:25, :half]
-    n2_out[...] = value[25:26, :half]
+    n1_out[...] = value[6:7, :half]
+    n2_out[...] = value[7:8, :half]
     mine = jnp.where(first, value[0:8, :cq], value[0:8, cq : 2 * cq])
     xw_out[...] = mine[0:TAPS]
     xb_out[...] = mine[TAPS : TAPS + 1]
-    bw_out[...] = value[16 : 16 + TAPS, :nbc]
-    bb_out[...] = value[16 + TAPS : 17 + TAPS, :nbc]
+    bw_out[...] = jnp.concatenate(
+        [
+            value[6:7, half : half + nbc],
+            value[7:8, half : half + nbc],
+            value[8:9, :nbc],
+            value[8:9, nbc : 2 * nbc],
+        ],
+        axis=0,
+    )
+    bb_out[...] = value[5:6, 3 * LANES : 3 * LANES + nbc]
     hq = dtb_out.shape[1]
     for i, out in enumerate((dtb_out, alog_out, skip_out)):
         at = i * LANES
         out[...] = jnp.where(
-            first, value[12:13, at : at + hq], value[12:13, at + hq : at + 2 * hq]
+            first, value[5:6, at : at + hq], value[5:6, at + hq : at + 2 * hq]
         )
 
 
@@ -680,14 +691,19 @@
         factor * factor * factor * inner_sum / (2 * half)
     )
     hidden_out[...] = jnp.where(place[0] == 0, change[:, :quarter], change[:, quarter:])
-    count = small.shape[0]
+    shared = jnp.where(place[2] == 0, rows[8:16], rows_far[8:16])
+    nbc = rows.shape[1]
+    heads = 3 * LANES
     vector_out[...] = jnp.zeros_like(vector_out)
-    vector_out[0:count] = small[...]
-    vector_out[count : count + 8, 0 : rows.shape[1]] = jnp.where(
-        place[2] == 0, rows[8:16], rows_far[8:16]
-    )
-    vector_out[count + 8 : count + 9, 0:half] = jnp.sum(value * hid * factor, axis=0, keepdims=True)
-    vector_out[count + 9 : count + 10, 0:half] = gain2[0:1]
+    vector_out[0 : TAPS + 1] = small[0 : TAPS + 1]
+    vector_out[5:6, 0:heads] = small[8 + TAPS : 9 + TAPS, 0:heads]
+    vector_out[5:6, heads : heads + nbc] = shared[TAPS : TAPS + 1]
+    vector_out[6:7, 0:half] = jnp.sum(value * hid * factor, axis=0, keepdims=True)
+    vector_out[7:8, 0:half] = gain2[0:1]
+    vector_out[6:7, half : half + nbc] = shared[0:1]
+    vector_out[7:8, half : half + nbc] = shared[1:2]
+    vector_out[8:9, 0:nbc] = shared[2:3]
+    vector_out[8:9, nbc : 2 * nbc] = shared[3:4]
 
 
 def stage_kernel(keep, came, send_out, keep_out):
@@ -734,6 +750,13 @@
             stage_kernel, [((rows // 2, cols), BF16), ((rows // 2, cols), F32)], keep, came
         )
     yield run(last, outs, keep, came)
+
+
+def finish(steps):
+    result = None
+    while result is None:
+        result = next(steps)
+    return result
 
 
 def shards(
@@ -812,54 +835,60 @@
     )
     small_rows = 16 * pl.cdiv(small.shape[0] // LANES + 8, 16)
     small = jnp.pad(small, (0, small_rows * LANES - small.shape[0])).reshape(small_rows, LANES)
-    gu = w_gateup.reshape(half, 2 * ff)
+    gu_mine = lax.dynamic_slice_in_dim(w_gateup, spot * piece, piece, 0).reshape(piece, 2 * ff)
+    hid_came = swap(hidden, "col")
     mine = run(
         pieces_kernel,
         [((inner + 3 * ff + 4 * tokens + small_rows, piece), BF16)],
-        place, w_mixout, w_attnout, w_down, gu, cotangent, hidden, small,
+        place, w_mixout, w_attnout, w_down, gu_mine, cotangent, hidden, small,
         smem=(0,),
     )[0]
     got = swap(mine, "row")
     wk = w_kv.reshape(half, nkv)
     wd = jnp.pad(w_dt, ((0, 0), (0, LANES - heads)))
     gain_one = norm1_gain.astype(F32)[None]
+    own, part, part_low = run(
+        project_kernel,
+        [((tokens, half), BF16), ((tokens, cols), F32), ((tokens, cols), BF16)],
+        place, hidden, hid_came, gain_one, w_xin, w_bc, wd, w_gate, w_query, wk,
+        smem=(0,),
+    )
+    part_came = swap(part_low, "row")
     t_first, g_first, in_pair, x_par, head_par, gain_two = run(
         lambda *refs: split_kernel(heads, *refs),
         [
             ((inner + ff, piece), BF16),
             ((piece, 2 * ff), BF16),
-            ((4 * tokens, quarter), BF16),
+            ((3 * tokens, quarter), BF16),
             ((8, ch), F32),
             ((8, LANES), F32),
             ((1, full_width), F32),
         ],
-        place, got, cotangent, hidden, small,
+        place, got, cotangent, small,
         smem=(0,),
     )
     t_second = swap(t_first, "dp", 1)
     g_second = swap(g_first, "dp", 2)
+    t_third = swap(t_first, "dp", 2)
+    g_third = swap(g_first, "dp", 1)
     in_came = swap(in_pair, "col")
-    n1, part, part_low, own, far, factor1 = run(
-        project_kernel,
+    gu = w_gateup.reshape(half, 2 * ff)
+    far, dy_own, dy_far, factor1, n1, left1 = run(
+        norm_kernel,
         [
             ((tokens, half), BF16),
-            ((tokens, cols), F32),
-            ((tokens, cols), BF16),
             ((tokens, half), BF16),
             ((tokens, half), BF16),
             ((tokens, LANES), F32),
+            ((tokens, half), BF16),
+            ((tokens, half), BF16),
         ],
-        place, in_pair, in_came, gain_one, w_xin, w_bc, wd, w_gate, w_query, wk,
-        smem=(0,), scratch=[((tokens, half), BF16)],
-    )
-    part_came = swap(part_low, "row")
-    t_cat, g_cat, left1 = run(
-        hop_kernel,
-        [((inner + ff, 2 * piece), BF16), ((2 * piece, 2 * ff), BF16), ((tokens, half), BF16)],
-        t_first, t_second, g_first, g_second, n1, order_near,
-    )
-    t_pair = swap(t_cat, "dp", 2)
-    g_pair = swap(g_cat, "dp", 1)
+        place, in_pair, in_came, own, gain_one, order_near,
+        smem=(0,), scratch=[((tokens, half), BF16)], after=(t_second, g_second),
+    )
+    t_fourth = swap(t_second, "dp", 2)
+    g_fourth = swap(g_second, "dp", 1)
+    tall_fetch = (t_first, t_second, t_third, t_fourth)
 
     bc_par = jnp.concatenate(
         [convbc_weight.T, convbc_bias[None], jnp.zeros((3, nbc), BF16)], 0
@@ -875,20 +904,21 @@
             ((tokens, ch + nbc), F32),
             ((tokens, ch), F32),
         ],
-        seg_row, seg_col, part, part_came, x_par, bc_par, head_par,
+        seg_row, seg_col, factor1, part, part_came, x_par, bc_par, head_par,
+        after=(g_third,),
     )
     mix_part = run(
         out_kernel,
         [((tokens, full_width), F32)],
-        mixed, w_mixout, w_attnout, t_first, t_second, t_pair,
+        mixed, w_mixout, w_attnout, *tall_fetch,
+        after=(g_fourth,),
     )[0]
     mix_came = swap(mix_part, "col")
-    dy_own, dy_far, grad_act = run(
+    grad_act = run(
         lambda *refs: act_grad_kernel(inner, *refs),
-        [((tokens, half), BF16), ((tokens, half), BF16), ((tokens, ff), F32)],
-        place, in_pair, in_came, w_down, t_first, t_second, t_pair,
-        smem=(0,), scratch=[((tokens, half), BF16)],
-    )
+        [((tokens, ff), F32)],
+        dy_own, dy_far, w_down, *tall_fetch,
+    )[0]
     h2, n2, act, ggu, n2_part, down_keep, down_send = run(
         feed_kernel,
         [
@@ -901,7 +931,7 @@
             ((tokens, quarter), F32),
         ],
         place, own, far, mix_part, mix_came, gain_two,
-        gu, g_first, g_second, g_pair, grad_act, w_down,
+        gu, g_first, g_third, g_second, g_fourth, grad_act, w_down,
         smem=(0,),
     )
     n2_came = swap(n2_part, "col")
@@ -934,7 +964,7 @@
             ((rows, ch + nq + nkv), BF16),
         ],
         place, dy_own, dy_far, h2, n2_part, n2_came, gain_two,
-        w_mixout, w_attnout, t_first, t_second, t_pair, down_keep, down_came,
+        w_mixout, w_attnout, *tall_fetch, down_keep, down_came,
         mixed, order_mix, seg_row, seg_col, raw, pre, ys, x_par, left1,
         smem=(0,),
     )
@@ -971,6 +1001,10 @@
     )
     one_came = swap(one_send, "dp", near[0])
     n1_came = swap(n1_part, "col")
+    def one_outs(keep):
+        width = ch + nbc + LANES
+        return [((keep + 32, width), BF16), ((keep, width), F32), ((16, ch), F32)]
+
     tall_send, tall_keep = run(
         tall_kernel, quarters(4 * half), d_left, dy_own, d_came, m_left, low, m_came
     )
@@ -991,40 +1025,29 @@
         own, n1_part, n1_came, n1_bc, gain_one, gbc, gbc_came,
     )
     rows_far = swap(sum_rows, "row")
-    r_gu = next(s_gu)
+    next(s_gu)
     grad_hidden, vector = run(
         end_kernel,
-        [((tokens, quarter), F32), ((32, ch), F32)],
+        [((tokens, quarter), F32), ((16, ch), F32)],
         place, own, factor1, resid, dn1, gain_one, sum_rows, rows_far, small_sum, gain2_sum,
         smem=(0,),
     )
     vector_came = swap(vector, "dp", near[0])
-    r_two = next(s_two)
-    r_gu = r_gu or next(s_gu)
-    r_two = r_two or next(s_two)
-    r_tall = next(s_tall)
-
-    def one_outs(keep):
-        width = ch + nbc + LANES
-        return [((keep + 64, width), BF16), ((keep, width), F32), ((32, ch), F32)]
-
+    next(s_two)
+    r_gu = finish(s_gu)
     one_send, one_keep, vector = run(
         one_kernel, one_outs(rows // 2),
         left1, gx, gbc_both, gdt, one_came, vector, vector_came,
     )
-    r_tall = r_tall or next(s_tall)
+    next(s_tall)
+    r_two = finish(s_two)
     for step in near[1:-1]:
         one_came = swap(one_send, "dp", step)
         one_send, one_keep, vector = run(
             one_stage_kernel, one_outs(one_keep.shape[0] // 2), one_keep, one_came, vector
         )
-        r_gu = r_gu or next(s_gu)
-        r_tall = r_tall or next(s_tall)
-        r_two = r_two or next(s_two)
     one_came = swap(one_send, "dp", near[-1])
-    r_gu = r_gu or next(s_gu)
-    r_tall = r_tall or next(s_tall)
-    r_two = r_two or next(s_two)
+    r_tall = finish(s_tall)
     (
         r_xin, r_bc, r_dt, o_norm1, o_norm2, o_cxw, o_cxb, o_cbw, o_cbb, o_dtb, o_alog, o_dsk
     ) = run(

time: 239 us -> 221 us (0.925)
  waiting for transfers between devices: 79.7 us -> 58.8 us
  starting transfers between devices: 29 us -> 34.5 us
    ppermute x27 -> x30, waiting for transfers between devices: 79.7 us -> 58.8 us  [swap(): return lax.ppermute(values, axis, [(i, i ^ step) for i in range(count)])]
    ppermute x27 -> x30, starting transfers between devices: 29 us -> 34.5 us  [swap(): return lax.ppermute(values, axis, [(i, i ^ step) for i in range(count)])]
    unnamed x106 -> x95, local copies, waits for them, and re-layouts: 23.8 us -> 20.6 us
  transfers between devices with their start and end apart: 27 -> 30, of which waited for: 12 -> 12; matrix products, arithmetic and copies ran while one was open for 2% -> 4% of each run, Pallas kernels for 32% -> 36%
where the time goes in v4:
time: 221 us; the launch traced here: 220 us
  Pallas kernels  95.3 us (43%)
  waiting for transfers between devices  58.8 us (27%)
  starting transfers between devices  34.5 us (16%)
  local copies, waits for them, and re-layouts  26.2 us (12%)
  other arithmetic  4.31 us (2%)
    pallas_call x26, Pallas kernels, __call__(): pl.pallas_call(body, out_shape=[jax.ShapeDtypeStruct((8, LANES), F32)] +...  95.3 us
    ppermute x30, waiting for transfers between devices, swap(): return lax.ppermute(values, axis, [(i, i ^ step) for i in range(count)])  58.8 us
    ppermute x30, starting transfers between devices, swap(): return lax.ppermute(values, axis, [(i, i ^ step) for i in range(count)])  34.5 us
    unnamed x95, local copies, waits for them, and re-layouts  20.6 us
  transfers between devices with their start and end apart: 30, of which 12 were waited for; matrix products, arithmetic and copies ran while one was open for 4% of the time, Pallas kernels for 36%

profile of v4, /device:TPU:0, one launch (start us, length us, event | category | flops | bytes accessed | tf_op | source)
XLA Modules:
  0.0 220.1 jit_solution(13502833289833588665)
XLA Ops:
  6.3 3.1 %shard_map.400 = (f32[8,128]{1,0:T(8,128)}, bf16[5152,128]{1,0:T(8,128)(2,1)}) custom-call(s32[3]{0:T(128)} %pad_add_fusion.1.refs_0_, bf16[768,512]{1,0:T(8,128)(2,1)} %refs_7_.3, bf16[256,512]{1,0:T(8,128)(2,1)} %refs_8_.4, bf16[1024,512]{1,0:T(8,128)(2,1)} %refs_12_.1, bf16[128,2048]{1,0:T(8,128)(2,1)} %bitcast.29, bf16[256,256]{1,0:T(8,128)(2,1)} %refs_2_.5, ...), custom_call_target="tpu_custom_call" | custom-call | tf_op jit(solution)/shard_map/pallas_call | solution.py:59
  9.4 3.0 %collective-permute-start = (bf16[5152,128]{1,0:T(8,128)(2,1)}, bf16[5152,128]{1,0:T(8,128)(2,1)S(1)}, u32[]{:S(2)}, u32[]{:S(2)}) collective-permute-start(bf16[5152,128]{1,0:T(8,128)(2,1)} %get-tuple-element.136), channel_id=1, source_target_pairs={{0,2},{2,0},{1,3},{3,1},{4,6},{6,4},{5,7},{7,5},{8,10},{10,8},{9,1... | collective-permute-start | bytes 3956744 | tf_op jit(solution)/shard_map/ppermute | solution.py:20
  14.5 5.1 %shard_map.401 = (f32[8,128]{1,0:T(8,128)}, bf16[256,512]{1,0:T(8,128)(2,1)}, f32[256,2304]{1,0:T(8,128)}, bf16[256,2304]{1,0:T(8,128)(2,1)}) custom-call(s32[3]{0:T(128)} %pad_add_fusion.1.refs_0_, bf16[256,256]{1,0:T(8,128)(2,1)} %refs_1_.4, bf16[256,256]{1,0:T(8,128)(2,1)} %copy-done.21, f32[1,512]{1,0:T(1,128)} %bitcast.33, bf16[512,768]{1,0:T(8,128)(2,1)} %refs_5_.5, ...), custom_call_target="tpu_custom_call" | custom-call | tf_op jit(solution)/shard_map/pallas_call | solution.py:59
  19.7 22.7 %collective-permute-done.refs_1_ = bf16[5152,128]{1,0:T(8,128)(2,1)S(1)} collective-permute-done((bf16[5152,128]{1,0:T(8,128)(2,1)}, bf16[5152,128]{1,0:T(8,128)(2,1)S(1)}, u32[]{:S(2)}, u32[]{:S(2)}) %collective-permute-start) | collective-permute-done | bytes 1318944 | tf_op jit(solution)/shard_map/ppermute | solution.py:20
  43.4 2.7 %shard_map.402 = (f32[8,128]{1,0:T(8,128)}, bf16[2048,128]{1,0:T(8,128)(2,1)}, bf16[128,2048]{1,0:T(8,128)(2,1)}, bf16[768,256]{1,0:T(8,128)(2,1)}, f32[8,768]{1...) custom-call(s32[3]{0:T(128)} %pad_add_fusion.1.refs_0_, bf16[5152,128]{1,0:T(8,128)(2,1)} %copy-done.3, ...), custom_call_target="tpu_custom_call" | custom-call | tf_op jit(solution)/shard_map/pallas_call | solution.py:59
  52.1 9.1 %collective-permute-done.3.refs_7_.refs_4_.refs_10_ = bf16[2048,128]{1,0:T(8,128)(2,1)S(1)} collective-permute-done((bf16[2048,128]{1,0:T(8,128)(2,1)}, bf16[2048,128]{1,0:T(8,128)(2,1)S(1)}, u32[]{:S(2)}, u32[]{:S(2)}) %collective-permute-start.3) | collective-permute-done | bytes 524320 | tf_op jit(solution)/shard_map/ppermute | solution.py:20
  61.2 2.1 collective-permute-start.8
  66.2 2.5 %shard_map.403 = (f32[8,128]{1,0:T(8,128)}, bf16[256,512]{1,0:T(8,128)(2,1)}, bf16[256,512]{1,0:T(8,128)(2,1)}, bf16[256,512]{1,0:T(8,128)(2,1)}, f32[256,128]{1...) custom-call(s32[3]{0:T(128)} %pad_add_fusion.1.refs_0_, bf16[768,256]{1,0:T(8,128)(2,1)} %get-tuple-element.139.refs_1_, ...), custom_call_target="tpu_custom_call" | custom-call | tf_op jit(solution)/shard_map/pallas_call | solution.py:59
  68.7 3.9 %collective-permute-done.6.refs_9_.refs_8_ = bf16[128,2048]{1,0:T(8,128)(2,1)} collective-permute-done((bf16[128,2048]{1,0:T(8,128)(2,1)}, bf16[128,2048]{1,0:T(8,128)(2,1)}, u32[]{:S(2)}, u32[]{:S(2)}) %collective-permute-start.6) | collective-permute-done | bytes 524320 | tf_op jit(solution)/shard_map/ppermute | solution.py:20
  73.3 7.1 %shard_map.404 = (f32[8,128]{1,0:T(8,128)}, bf16[256,1024]{1,0:T(8,128)(2,1)}, f32[256,2304]{1,0:T(8,128)}, f32[256,1024]{1,0:T(8,128)}, f32[256,768]{1,0:T(8,128)}) custom-call(f32[1,256]{1,0:T(1,128)} %copy-done.23, f32[256,128]{1,0:T(8,128)} %broadcast_in_dim.29.refs_1_.refs_18_, f32[256,128]{1,0:T(8,128)} %get-tuple-element.147.refs_2_, ...), custom_call_target="tpu_custom_call" | custom-call | tf_op jit(solution)/shard_map/pallas_call | solution.py:59
  83.0 3.7 %shard_map.405 = (f32[8,128]{1,0:T(8,128)}, f32[256,1024]{1,0:T(8,128)}) custom-call(bf16[256,1024]{1,0:T(8,128)(2,1)} %get-tuple-element.153.refs_0_.refs_15_, bf16[768,512]{1,0:T(8,128)(2,1)} %refs_7_.3, bf16[256,512]{1,0:T(8,128)(2,1)} %refs_8_.4, bf16[2048,128]{1,0:T(8,128)(2,1)} %get-tuple-element.142.refs_3_.refs_9_, bf16[2048,128]{1,0:T(8,128)(2,1)} %copy-done, ...), custom_call_target="tpu_custom_call" | custom-call | tf_op jit(solution)/shard_map/pallas_call | solution.py:59
  86.7 3.5 %copy.50 = bf16[64,8,2,1024]{3,1,2,0:T(8,128)(2,1)} copy(bf16[64,8,2,1024]{3,2,1,0:T(2,128)(2,1)} %bitcast.28) | data formatting | bytes 4194304
  90.2 3.8 %shard_map.406 = (f32[8,128]{1,0:T(8,128)}, f32[256,1024]{1,0:T(8,128)}) custom-call(bf16[256,512]{1,0:T(8,128)(2,1)} %get-tuple-element.144.refs_0_.refs_3_.refs_1_, bf16[256,512]{1,0:T(8,128)(2,1)} %get-tuple-element.145.refs_1_.refs_2_, bf16[1024,512]{1,0:T(8,128)(2,1)} %refs_12_.1, bf16[2048,128]{1,0:T(8,128)(2,1)} %get-tuple-element.142.refs_3_.refs_9_, ...), custom_call_target="tpu_custom_call" | custom-call | tf_op jit(solution)/shard_map/pallas_call | solution.py:59
  95.0 7.8 %shard_map.407 = (f32[8,128]{1,0:T(8,128)}, f32[256,1024]{1,0:T(8,128)}, bf16[256,512]{1,0:T(8,128)(2,1)}, bf16[256,1024]{1,0:T(8,128)(2,1)}, bf16[256,2048]{1,0...) custom-call(s32[3]{0:T(128)} %pad_add_fusion.1.refs_0_, ...), custom_call_target="tpu_custom_call" | custom-call | tf_op jit(solution)/shard_map/pallas_call | solution.py:59
  104.0 4.1 %shard_map.408 = (f32[8,128]{1,0:T(8,128)}, bf16[256,2048]{1,0:T(8,128)(2,1)}, bf16[256,1024]{1,0:T(8,128)(2,1)}, bf16[256,256]{1,0:T(8,128)(2,1)}, bf16[256,512]{1,0:T(8,128)(2,1)}) custom-call(bf16[256,512]{1,0:T(8,128)(2,1)} %get-tuple-element.168.refs_0_, bf16[256,1024]{1,0:T(8,128)(2,1)} %get-tuple-element.169.refs_1_, ...), custom_call_target="tpu_custom_call" | custom-call | tf_op jit(solution)/shard_map/pallas_call | solution.py:59
  111.4 9.1 %shard_map.409 = (f32[8,128]{1,0:T(8,128)}, f32[256,1024]{1,0:T(8,128)}, f32[256,512]{1,0:T(8,128)}, bf16[256,512]{1,0:T(8,128)(2,1)}, f32[8,512]{1,0:T(8,128)},...) custom-call(s32[3]{0:T(128)} %pad_add_fusion.1.refs_0_, ...), custom_call_target="tpu_custom_call" | custom-call | tf_op jit(solution)/shard_map/pallas_call | solution.py:59
  120.5 9.0 %shard_map.410 = (f32[8,128]{1,0:T(8,128)}, bf16[256,768]{1,0:T(8,128)(2,1)}, bf16[256,128]{1,0:T(8,128)(2,1)}, f32[264,256]{1,0:T(8,128)}, f32[16,768]{1,0:T(8,128)}) custom-call(f32[1,256]{1,0:T(1,128)} %copy-done.23, f32[256,128]{1,0:T(8,128)} %broadcast_in_dim.29.refs_1_.refs_18_, f32[256,2304]{1,0:T(8,128)} %get-tuple-element.164.refs_19_.refs_2_, ...), custom_call_target="tpu_custom_call" | custom-call | tf_op jit(solution)/shard_map/pallas_call | solution.py:59
  134.1 3.2 %shard_map.411 = (f32[8,128]{1,0:T(8,128)}, bf16[128,2048]{1,0:T(8,128)(2,1)}, f32[128,2048]{1,0:T(8,128)}) custom-call(bf16[256,256]{1,0:T(8,128)(2,1)} %get-tuple-element.181.refs_0_, bf16[256,2048]{1,0:T(8,128)(2,1)} %get-tuple-element.170.refs_2_.refs_1_, bf16[256,2048]{1,0:T(8,128)(2,1)} %collective-permute-done.14.refs_2_, ...), custom_call_target="tpu_custom_call" | custom-call | tf_op jit(solution)/shard_map/pallas_call | solution.py:59
  138.0 4.1 %shard_map.412 = (f32[8,128]{1,0:T(8,128)}, f32[256,512]{1,0:T(8,128)}, f32[256,512]{1,0:T(8,128)}, bf16[256,256]{1,0:T(8,128)(2,1)}, bf16[256,1152]{1,0:T(8,128)(2,1)}) custom-call(bf16[256,1152]{1,0:T(8,128)(2,1)} %get-tuple-element.175.refs_0_.refs_1_, bf16[256,768]{1,0:T(8,128)(2,1)} %get-tuple-element.178.refs_1_, ...), custom_call_target="tpu_custom_call" | custom-call | tf_op jit(solution)/shard_map/pallas_call | solution.py:59
  145.3 3.4 %shard_map.413 = (f32[8,128]{1,0:T(8,128)}, bf16[128,2048]{1,0:T(8,128)(2,1)}, f32[128,2048]{1,0:T(8,128)}) custom-call(bf16[256,512]{1,0:T(8,128)(2,1)} %get-tuple-element.188.refs_0_, bf16[256,512]{1,0:T(8,128)(2,1)} %get-tuple-element.144.refs_0_.refs_3_.refs_1_, bf16[256,1024]{1,0:T(8,128)(2,1)} %collective-permute-done.17.refs_2_, ...), custom_call_target="tpu_custom_call" | custom-call | tf_op jit(solution)/shard_map/pallas_call | solution.py:59
  149.5 2.6 %shard_map.414 = (f32[8,128]{1,0:T(8,128)}, bf16[128,1152]{1,0:T(8,128)(2,1)}, f32[128,1152]{1,0:T(8,128)}) custom-call(bf16[256,512]{1,0:T(8,128)(2,1)} %get-tuple-element.167.refs_23_.refs_11_.refs_0_, bf16[256,1152]{1,0:T(8,128)(2,1)} %get-tuple-element.175.refs_0_.refs_1_, bf16[256,1152]{1,0:T(8,128)(2,1)} %copy-done.8, f32[8,128]{1,0:T(8,128)} %get-tuple-element.194.refs_3_), custom_call_target="tpu_custom_call" | custom-call | tf_op jit(solution)/shard_map/pallas_call | solution.py:59
  153.7 2.8 %shard_map.415 = (f32[8,128]{1,0:T(8,128)}, f32[256,512]{1,0:T(8,128)}, f32[16,256]{1,0:T(8,128)}) custom-call(bf16[256,512]{1,0:T(8,128)(2,1)} %get-tuple-element.140.refs_3_.refs_1_.refs_0_, f32[256,512]{1,0:T(8,128)} %get-tuple-element.185.refs_1_, f32[256,512]{1,0:T(8,128)} %collective-permute-done.15.refs_2_, f32[256,512]{1,0:T(8,128)} %get-tuple-element.186.refs_3_, ...), custom_call_target="tpu_custom_call" | custom-call | tf_op jit(solution)/shard_map/pallas_call | solution.py:59
  157.9 2.3 %shard_map.416 = (f32[8,128]{1,0:T(8,128)}, bf16[64,2048]{1,0:T(8,128)(2,1)}, f32[64,2048]{1,0:T(8,128)}) custom-call(f32[128,2048]{1,0:T(8,128)} %get-tuple-element.200.refs_0_, bf16[128,2048]{1,0:T(8,128)(2,1)} %copy-done.10, f32[8,128]{1,0:T(8,128)} %get-tuple-element.202.refs_2_), custom_call_target="tpu_custom_call" | custom-call | tf_op jit(solution)/shard_map/pallas_call | solution.py:59
  160.2 2.6 %collective-permute-start.23 = (bf16[64,2048]{1,0:T(8,128)(2,1)}, bf16[64,2048]{1,0:T(8,128)(2,1)S(1)}, u32[]{:S(2)}, u32[]{:S(2)}) collective-permute-start(bf16[64,2048]{1,0:T(8,128)(2,1)} %get-tuple-element.209), channel_id=1, source_target_pairs={{0,16},{4,20},{8,24},{12,28},{16,0},{20,4},{24,8},{28,12},{1,17},{... | collective-permute-start | bytes 786440 | tf_op jit(solution)/shard_map/ppermute | solution.py:20
  164.5 2.4 %collective-permute-done.19.refs_7_ = f32[16,256]{1,0:T(8,128)S(1)} collective-permute-done((f32[16,256]{1,0:T(8,128)}, f32[16,256]{1,0:T(8,128)S(1)}, u32[]{:S(2)}, u32[]{:S(2)}) %collective-permute-start.19) | collective-permute-done | bytes 16416 | tf_op jit(solution)/shard_map/ppermute | solution.py:20
  167.5 2.5 %shard_map.417 = (f32[8,128]{1,0:T(8,128)}, f32[256,256]{1,0:T(8,128)}, f32[16,768]{1,0:T(8,128)}) custom-call(s32[3]{0:T(128)} %pad_add_fusion.1.refs_0_, bf16[256,512]{1,0:T(8,128)(2,1)} %get-tuple-element.140.refs_3_.refs_1_.refs_0_, f32[256,128]{1,0:T(8,128)} %get-tuple-element.147.refs_2_, f32[256,512]{1,0:T(8,128)} %get-tuple-element.174.refs_3_, ...), custom_call_target="tpu_custom_call" | custom-call | tf_op jit(solution)/shard_map/pallas_call | solution.py:59
  178.1 2.7 %shard_map.420 = (f32[8,128]{1,0:T(8,128)}, bf16[160,1152]{1,0:T(8,128)(2,1)}, f32[128,1152]{1,0:T(8,128)}, f32[16,768]{1,0:T(8,128)}) custom-call(bf16[256,512]{1,0:T(8,128)(2,1)} %get-tuple-element.167.refs_23_.refs_11_.refs_0_, bf16[256,768]{1,0:T(8,128)(2,1)} %get-tuple-element.178.refs_1_, bf16[256,256]{1,0:T(8,128)(2,1)} %get-tuple-element.205.refs_2_, ...), custom_call_target="tpu_custom_call" | custom-call | tf_op jit(solution)/shard_map/pallas_call | solution.py:59
  182.5 2.2 collective-permute-start.26
  185.5 2.3 %shard_map.421 = (f32[8,128]{1,0:T(8,128)}, bf16[64,2048]{1,0:T(8,128)(2,1)}, f32[64,2048]{1,0:T(8,128)}) custom-call(f32[128,2048]{1,0:T(8,128)} %get-tuple-element.220.refs_0_, bf16[128,2048]{1,0:T(8,128)(2,1)} %copy-done.9, f32[8,128]{1,0:T(8,128)} %get-tuple-element.222.refs_2_), custom_call_target="tpu_custom_call" | custom-call | tf_op jit(solution)/shard_map/pallas_call | solution.py:59
  188.5 6.4 %collective-permute-done.26.refs_1_ = bf16[64,1152]{1,0:T(8,128)(2,1)S(1)} collective-permute-done((bf16[64,1152]{1,0:T(8,128)(2,1)S(1)}, bf16[64,1152]{1,0:T(8,128)(2,1)S(1)}, u32[]{:S(2)}, u32[]{:S(2)}) %collective-permute-start.26) | collective-permute-done | bytes 147488 | tf_op jit(solution)/shard_map/ppermute | solution.py:20
  200.1 3.4 %collective-permute-start.28 = (bf16[96,1152]{1,0:T(8,128)(2,1)}, bf16[96,1152]{1,0:T(8,128)(2,1)S(1)}, u32[]{:S(2)}, u32[]{:S(2)}) collective-permute-start(bf16[96,1152]{1,0:T(8,128)(2,1)} %get-tuple-element.226), channel_id=1, source_target_pairs={{0,16},{4,20},{8,24},{12,28},{16,0},{20,4},{24,8},{28,12},{1,17},{... | collective-permute-start | bytes 663560 | tf_op jit(solution)/shard_map/ppermute | solution.py:20
  204.8 6.9 %collective-permute-done.29.refs_1_ = bf16[64,2048]{1,0:T(8,128)(2,1)S(1)} collective-permute-done((bf16[64,2048]{1,0:T(8,128)(2,1)}, bf16[64,2048]{1,0:T(8,128)(2,1)S(1)}, u32[]{:S(2)}, u32[]{:S(2)}) %collective-permute-start.29) | collective-permute-done | bytes 262176 | tf_op jit(solution)/shard_map/ppermute | solution.py:20
  (172 shorter events, 67.0 us)
Async XLA Ops:
  9.4 33.0 %collective-permute-start = (bf16[5152,128]{1,0:T(8,128)(2,1)}, bf16[5152,128]{1,0:T(8,128)(2,1)S(1)}, u32[]{:S(2)}, u32[]{:S(2)}) collective-permute-start(bf16[5152,128]{1,0:T(8,128)(2,1)} %get-tuple-element.136), channel_id=1, source_target_pairs={{0,2},{2,0},{1,3},{3,1},{4,6},{6,4},{5,7},{7,5},{8,10},{10,8},{9,1... | collective-permute-start | bytes 3956744 | tf_op jit(solution)/shard_map/ppermute | solution.py:20
  12.4 1.5 collective-permute-start.1
  13.8 51.1 %copy-start.31 = (s32[512]{0:T(512)S(1)}, s32[512]{0:T(512)}, u32[]{:S(2)}) copy-start(s32[512]{0:T(512)} %constant.43.clone) | copy-start | bytes 6148
  13.8 51.7 %copy-start.32 = (bf16[256,4]{0,1:T(4,128)(2,1)S(1)}, bf16[256,4]{0,1:T(4,128)(2,1)}, u32[]{:S(2)}) copy-start(bf16[256,4]{0,1:T(4,128)(2,1)} %param.36) | copy-start | bytes 6148
  19.6 49.1 %collective-permute-start.5 = (bf16[256,2304]{1,0:T(8,128)(2,1)}, bf16[256,2304]{1,0:T(8,128)(2,1)}, u32[]{:S(2)}, u32[]{:S(2)}) collective-permute-start(bf16[256,2304]{1,0:T(8,128)(2,1)} %get-tuple-element.149), channel_id=1, source_target_pairs={{0,2},{2,0},{1,3},{3,1},{4,6},{6,4},{5,7},{7,5},{8,10},{10,8},{9,1... | collective-permute-start | bytes 3538952 | tf_op jit(solution)/shard_map/ppermute | solution.py:20
  46.1 15.1 %collective-permute-start.3 = (bf16[2048,128]{1,0:T(8,128)(2,1)}, bf16[2048,128]{1,0:T(8,128)(2,1)S(1)}, u32[]{:S(2)}, u32[]{:S(2)}) collective-permute-start(bf16[2048,128]{1,0:T(8,128)(2,1)} %get-tuple-element.142.refs_3_.refs_9_), channel_id=1, source_target_pairs={{0,4},{4,0},{8,12},{12,8},{16,20},{20,16},{24,28},{28,24},{1,5},{5... | collective-permute-start | bytes 1572872 | tf_op jit(solution)/shard_map/ppermute | solution.py:20
  48.1 15.2 %collective-permute-start.4 = (bf16[128,2048]{1,0:T(8,128)(2,1)}, bf16[128,2048]{1,0:T(8,128)(2,1)}, u32[]{:S(2)}, u32[]{:S(2)}) collective-permute-start(bf16[128,2048]{1,0:T(8,128)(2,1)} %get-tuple-element.143.refs_7_), channel_id=1, source_target_pairs={{0,8},{4,12},{8,0},{12,4},{16,24},{20,28},{24,16},{28,20},{1,9},{5... | collective-permute-start | bytes 1572872 | tf_op jit(solution)/shard_map/ppermute | solution.py:20
  49.7 1.9 collective-permute-start.2
  49.7 22.8 %collective-permute-start.6 = (bf16[128,2048]{1,0:T(8,128)(2,1)}, bf16[128,2048]{1,0:T(8,128)(2,1)}, u32[]{:S(2)}, u32[]{:S(2)}) collective-permute-start(bf16[128,2048]{1,0:T(8,128)(2,1)} %get-tuple-element.143.refs_7_), channel_id=1, source_target_pairs={{0,4},{4,0},{8,12},{12,8},{16,20},{20,16},{24,28},{28,24},{1,5},{5... | collective-permute-start | bytes 1572872 | tf_op jit(solution)/shard_map/ppermute | solution.py:20
  51.6 28.7 %collective-permute-start.7 = (bf16[2048,128]{1,0:T(8,128)(2,1)}, bf16[2048,128]{1,0:T(8,128)(2,1)S(1)}, u32[]{:S(2)}, u32[]{:S(2)}) collective-permute-start(bf16[2048,128]{1,0:T(8,128)(2,1)} %get-tuple-element.142.refs_3_.refs_9_), channel_id=1, source_target_pairs={{0,8},{4,12},{8,0},{12,4},{16,24},{20,28},{24,16},{28,20},{1,9},{5... | collective-permute-start | bytes 1572872 | tf_op jit(solution)/shard_map/ppermute | solution.py:20
  61.2 21.0 %collective-permute-start.8 = (bf16[2048,128]{1,0:T(8,128)(2,1)S(1)}, bf16[2048,128]{1,0:T(8,128)(2,1)S(1)}, u32[]{:S(2)}, u32[]{:S(2)}) collective-permute-start(bf16[2048,128]{1,0:T(8,128)(2,1)S(1)} %collective-permute-done.3.refs_7_.refs_4_.refs_10_), channel_id=1, source_target_pairs={{0,8},{4,12},{8,0},{12,4},{16,24},{20,28},{24,16},{28,20},{1,9},{5... | collective-permute-start | bytes 1572872 | tf_op jit(solution)/shard_map/ppermute | solution.py:20
  63.3 18.9 %collective-permute-start.9 = (bf16[128,2048]{1,0:T(8,128)(2,1)}, bf16[128,2048]{1,0:T(8,128)(2,1)}, u32[]{:S(2)}, u32[]{:S(2)}) collective-permute-start(bf16[128,2048]{1,0:T(8,128)(2,1)} %collective-permute-done.4.refs_8_.refs_9_), channel_id=1, source_target_pairs={{0,4},{4,0},{8,12},{12,8},{16,20},{20,16},{24,28},{28,24},{1,5},{5... | collective-permute-start | bytes 1572872 | tf_op jit(solution)/shard_map/ppermute | solution.py:20
  86.7 7.3 %collective-permute-start.10 = (f32[256,1024]{1,0:T(8,128)}, f32[256,1024]{1,0:T(8,128)S(1)}, u32[]{:S(2)}, u32[]{:S(2)}) collective-permute-start(f32[256,1024]{1,0:T(8,128)} %get-tuple-element.155.refs_3_), channel_id=1, source_target_pairs={{0,1},{1,0},{2,3},{3,2},{4,5},{5,4},{6,7},{7,6},{8,9},{9,8},{10,11... | collective-permute-start | bytes 3145736 | tf_op jit(solution)/shard_map/ppermute | solution.py:20
  102.8 7.5 %collective-permute-start.11 = (f32[256,1024]{1,0:T(8,128)}, f32[256,1024]{1,0:T(8,128)S(1)}, u32[]{:S(2)}, u32[]{:S(2)}) collective-permute-start(f32[256,1024]{1,0:T(8,128)} %get-tuple-element.161.refs_4_), channel_id=1, source_target_pairs={{0,1},{1,0},{2,3},{3,2},{4,5},{5,4},{6,7},{7,6},{8,9},{9,8},{10,11... | collective-permute-start | bytes 3145736 | tf_op jit(solution)/shard_map/ppermute | solution.py:20
  108.1 26.0 %collective-permute-start.14 = (bf16[256,2048]{1,0:T(8,128)(2,1)}, bf16[256,2048]{1,0:T(8,128)(2,1)}, u32[]{:S(2)}, u32[]{:S(2)}) collective-permute-start(bf16[256,2048]{1,0:T(8,128)(2,1)} %get-tuple-element.182), channel_id=1, source_target_pairs={{0,4},{4,0},{8,12},{12,8},{16,20},{20,16},{24,28},{28,24},{1,5},{5... | collective-permute-start | bytes 3145736 | tf_op jit(solution)/shard_map/ppermute | solution.py:20
  108.8 1.5 collective-permute-start.12
  108.8 35.1 %collective-permute-start.17 = (bf16[256,1024]{1,0:T(8,128)(2,1)}, bf16[256,1024]{1,0:T(8,128)(2,1)}, u32[]{:S(2)}, u32[]{:S(2)}) collective-permute-start(bf16[256,1024]{1,0:T(8,128)(2,1)} %get-tuple-element.189), channel_id=1, source_target_pairs={{0,8},{4,12},{8,0},{12,4},{16,24},{20,28},{24,16},{28,20},{1,9},{5... | collective-permute-start | bytes 1572872 | tf_op jit(solution)/shard_map/ppermute | solution.py:20
  129.5 7.8 %collective-permute-start.13 = (f32[264,256]{1,0:T(8,128)}, f32[264,256]{1,0:T(8,128)S(1)}, u32[]{:S(2)}, u32[]{:S(2)}) collective-permute-start(f32[264,256]{1,0:T(8,128)} %get-tuple-element.180.refs_3_.refs_5_), channel_id=1, source_target_pairs={{0,1},{1,0},{2,3},{3,2},{4,5},{5,4},{6,7},{7,6},{8,9},{9,8},{10,11... | collective-permute-start | bytes 811016 | tf_op jit(solution)/shard_map/ppermute | solution.py:20
  129.7 19.0 %collective-permute-start.16 = (bf16[256,1152]{1,0:T(8,128)(2,1)}, bf16[256,1152]{1,0:T(8,128)(2,1)S(1)}, u32[]{:S(2)}, u32[]{:S(2)}) collective-permute-start(bf16[256,1152]{1,0:T(8,128)(2,1)} %get-tuple-element.187), channel_id=1, source_target_pairs={{0,4},{4,0},{8,12},{12,8},{16,20},{20,16},{24,28},{28,24},{1,5},{5... | collective-permute-start | bytes 1769480 | tf_op jit(solution)/shard_map/ppermute | solution.py:20
  131.2 14.2 %collective-permute-start.18 = (bf16[256,1024]{1,0:T(8,128)(2,1)}, bf16[256,1024]{1,0:T(8,128)(2,1)}, u32[]{:S(2)}, u32[]{:S(2)}) collective-permute-start(bf16[256,1024]{1,0:T(8,128)(2,1)} %get-tuple-element.192), channel_id=1, source_target_pairs={{0,8},{4,12},{8,0},{12,4},{16,24},{20,28},{24,16},{28,20},{1,9},{5... | collective-permute-start | bytes 1572872 | tf_op jit(solution)/shard_map/ppermute | solution.py:20
  142.1 11.6 %collective-permute-start.15 = (f32[256,512]{1,0:T(8,128)}, f32[256,512]{1,0:T(8,128)}, u32[]{:S(2)}, u32[]{:S(2)}) collective-permute-start(f32[256,512]{1,0:T(8,128)} %get-tuple-element.185.refs_1_), channel_id=1, source_target_pairs={{0,1},{1,0},{2,3},{3,2},{4,5},{5,4},{6,7},{7,6},{8,9},{9,8},{10,11... | collective-permute-start | bytes 1572872 | tf_op jit(solution)/shard_map/ppermute | solution.py:20
  142.1 15.0 %collective-permute-start.20 = (bf16[128,2048]{1,0:T(8,128)(2,1)}, bf16[128,2048]{1,0:T(8,128)(2,1)S(1)}, u32[]{:S(2)}, u32[]{:S(2)}) collective-permute-start(bf16[128,2048]{1,0:T(8,128)(2,1)} %get-tuple-element.201), channel_id=1, source_target_pairs={{0,8},{4,12},{8,0},{12,4},{16,24},{20,28},{24,16},{28,20},{1,9},{5... | collective-permute-start | bytes 1572872 | tf_op jit(solution)/shard_map/ppermute | solution.py:20
  143.8 33.4 %collective-permute-start.21 = (bf16[256,1152]{1,0:T(8,128)(2,1)}, bf16[256,1152]{1,0:T(8,128)(2,1)S(1)}, u32[]{:S(2)}, u32[]{:S(2)}) collective-permute-start(bf16[256,1152]{1,0:T(8,128)(2,1)} %get-tuple-element.206), channel_id=1, source_target_pairs={{0,4},{4,0},{8,12},{12,8},{16,20},{20,16},{24,28},{28,24},{1,5},{5... | collective-permute-start | bytes 1769480 | tf_op jit(solution)/shard_map/ppermute | solution.py:20
  152.1 19.9 %collective-permute-start.24 = (bf16[128,1152]{1,0:T(8,128)(2,1)}, bf16[128,1152]{1,0:T(8,128)(2,1)S(1)}, u32[]{:S(2)}, u32[]{:S(2)}) collective-permute-start(bf16[128,1152]{1,0:T(8,128)(2,1)} %get-tuple-element.211), channel_id=1, source_target_pairs={{0,8},{4,12},{8,0},{12,4},{16,24},{20,28},{24,16},{28,20},{1,9},{5... | collective-permute-start | bytes 884744 | tf_op jit(solution)/shard_map/ppermute | solution.py:20
  160.2 14.4 %collective-permute-start.23 = (bf16[64,2048]{1,0:T(8,128)(2,1)}, bf16[64,2048]{1,0:T(8,128)(2,1)S(1)}, u32[]{:S(2)}, u32[]{:S(2)}) collective-permute-start(bf16[64,2048]{1,0:T(8,128)(2,1)} %get-tuple-element.209), channel_id=1, source_target_pairs={{0,16},{4,20},{8,24},{12,28},{16,0},{20,4},{24,8},{28,12},{1,17},{... | collective-permute-start | bytes 786440 | tf_op jit(solution)/shard_map/ppermute | solution.py:20
  162.9 21.8 %collective-permute-start.27 = (bf16[128,2048]{1,0:T(8,128)(2,1)}, bf16[128,2048]{1,0:T(8,128)(2,1)S(1)}, u32[]{:S(2)}, u32[]{:S(2)}) collective-permute-start(bf16[128,2048]{1,0:T(8,128)(2,1)} %get-tuple-element.221), channel_id=1, source_target_pairs={{0,4},{4,0},{8,12},{12,8},{16,20},{20,16},{24,28},{28,24},{1,5},{5... | collective-permute-start | bytes 1572872 | tf_op jit(solution)/shard_map/ppermute | solution.py:20
  163.0 3.9 %collective-permute-start.19 = (f32[16,256]{1,0:T(8,128)}, f32[16,256]{1,0:T(8,128)S(1)}, u32[]{:S(2)}, u32[]{:S(2)}) collective-permute-start(f32[16,256]{1,0:T(8,128)} %get-tuple-element.197.refs_6_), channel_id=1, source_target_pairs={{0,2},{2,0},{1,3},{3,1},{4,6},{6,4},{5,7},{7,5},{8,10},{10,8},{9,1... | collective-permute-start | bytes 49160 | tf_op jit(solution)/shard_map/ppermute | solution.py:20
  170.1 7.2 %collective-permute-start.22 = (f32[16,768]{1,0:T(8,128)}, f32[16,768]{1,0:T(8,128)S(1)}, u32[]{:S(2)}, u32[]{:S(2)}) collective-permute-start(f32[16,768]{1,0:T(8,128)} %get-tuple-element.207.refs_5_), channel_id=1, source_target_pairs={{0,4},{4,0},{8,12},{12,8},{16,20},{20,16},{24,28},{28,24},{1,5},{5... | collective-permute-start | bytes 147464 | tf_op jit(solution)/shard_map/ppermute | solution.py:20
  180.9 16.5 %collective-permute-start.25 = (bf16[160,1152]{1,0:T(8,128)(2,1)}, bf16[160,1152]{1,0:T(8,128)(2,1)S(1)}, u32[]{:S(2)}, u32[]{:S(2)}) collective-permute-start(bf16[160,1152]{1,0:T(8,128)(2,1)} %get-tuple-element.216), channel_id=1, source_target_pairs={{0,8},{4,12},{8,0},{12,4},{16,24},{20,28},{24,16},{28,20},{1,9},{5... | collective-permute-start | bytes 1105928 | tf_op jit(solution)/shard_map/ppermute | solution.py:20
  182.5 12.5 %collective-permute-start.26 = (bf16[64,1152]{1,0:T(8,128)(2,1)S(1)}, bf16[64,1152]{1,0:T(8,128)(2,1)S(1)}, u32[]{:S(2)}, u32[]{:S(2)}) collective-permute-start(bf16[64,1152]{1,0:T(8,128)(2,1)S(1)} %copy-done.38), channel_id=1, source_target_pairs={{0,16},{4,20},{8,24},{12,28},{16,0},{20,4},{24,8},{28,12},{1,17},{... | collective-permute-start | bytes 442376 | tf_op jit(solution)/shard_map/ppermute | solution.py:20
  187.8 23.9 %collective-permute-start.29 = (bf16[64,2048]{1,0:T(8,128)(2,1)}, bf16[64,2048]{1,0:T(8,128)(2,1)S(1)}, u32[]{:S(2)}, u32[]{:S(2)}) collective-permute-start(bf16[64,2048]{1,0:T(8,128)(2,1)} %get-tuple-element.229), channel_id=1, source_target_pairs={{0,16},{4,20},{8,24},{12,28},{16,0},{20,4},{24,8},{28,12},{1,17},{... | collective-permute-start | bytes 786440 | tf_op jit(solution)/shard_map/ppermute | solution.py:20
  200.1 14.7 %collective-permute-start.28 = (bf16[96,1152]{1,0:T(8,128)(2,1)}, bf16[96,1152]{1,0:T(8,128)(2,1)S(1)}, u32[]{:S(2)}, u32[]{:S(2)}) collective-permute-start(bf16[96,1152]{1,0:T(8,128)(2,1)} %get-tuple-element.226), channel_id=1, source_target_pairs={{0,16},{4,20},{8,24},{12,28},{16,0},{20,4},{24,8},{28,12},{1,17},{... | collective-permute-start | bytes 663560 | tf_op jit(solution)/shard_map/ppermute | solution.py:20
  (41 other events, 308.9 us)

commit v5 on v4

--- a/solution.py
+++ b/solution.py
@@ -64,7 +64,7 @@
             out_specs=[pl.BlockSpec(memory_space=pltpu.VMEM)]
             + [pl.BlockSpec(memory_space=plain)] * len(outs),
             scratch_shapes=[pltpu.VMEM(s, d) if d is not None else s for s, d in scratch],
-            compiler_params=pltpu.CompilerParams(vmem_limit_bytes=62 << 20),
+            compiler_params=pltpu.CompilerParams(vmem_limit_bytes=64 << 20),
             cost_estimate=pl.CostEstimate(flops=0, bytes_accessed=0, transcendentals=0),
         )(*args, *extra)
         self.token = results[0]
@@ -604,7 +604,6 @@
     low = (value - high.astype(F32)).astype(BF16)
     out[0:rows, 0:width] = high
     out[rows : 2 * rows, 0:width] = low
-    out[0 : 2 * rows, width:] = jnp.zeros((2 * rows, out.shape[1] - width), BF16)
     return high.astype(F32) + low.astype(F32)
 
 
@@ -642,31 +641,23 @@
     nbc = bc_out.shape[1]
     x_out[...] = total[:, :ch]
     bc_out[...] = total[:, ch : ch + nbc]
-    dt_out[...] = total[:, ch + nbc : ch + nbc + heads]
+    dt_out[...] = total[:, ch + nbc : ch + nbc + LANES].T[:heads]
     value = vector[...] + read_vector(came, vector.shape)
     first = place[2] == 0
     half = n1_out.shape[1]
     cq = xb_out.shape[1]
-    n1_out[...] = value[6:7, :half]
-    n2_out[...] = value[7:8, :half]
+    n1_out[...] = value[5:6, :half]
+    n2_out[...] = value[5:6, half : 2 * half]
     mine = jnp.where(first, value[0:8, :cq], value[0:8, cq : 2 * cq])
     xw_out[...] = mine[0:TAPS]
     xb_out[...] = mine[TAPS : TAPS + 1]
-    bw_out[...] = jnp.concatenate(
-        [
-            value[6:7, half : half + nbc],
-            value[7:8, half : half + nbc],
-            value[8:9, :nbc],
-            value[8:9, nbc : 2 * nbc],
-        ],
-        axis=0,
-    )
-    bb_out[...] = value[5:6, 3 * LANES : 3 * LANES + nbc]
+    bw_out[...] = value[1 : TAPS + 1, ch : ch + nbc]
+    bb_out[...] = value[6:7, :nbc]
     hq = dtb_out.shape[1]
     for i, out in enumerate((dtb_out, alog_out, skip_out)):
-        at = i * LANES
+        at = ch + i * LANES
         out[...] = jnp.where(
-            first, value[5:6, at : at + hq], value[5:6, at + hq : at + 2 * hq]
+            first, value[0:1, at : at + hq], value[0:1, at + hq : at + 2 * hq]
         )
 
 
@@ -693,17 +684,15 @@
     hidden_out[...] = jnp.where(place[0] == 0, change[:, :quarter], change[:, quarter:])
     shared = jnp.where(place[2] == 0, rows[8:16], rows_far[8:16])
     nbc = rows.shape[1]
+    ch = small.shape[1]
     heads = 3 * LANES
     vector_out[...] = jnp.zeros_like(vector_out)
-    vector_out[0 : TAPS + 1] = small[0 : TAPS + 1]
-    vector_out[5:6, 0:heads] = small[8 + TAPS : 9 + TAPS, 0:heads]
-    vector_out[5:6, heads : heads + nbc] = shared[TAPS : TAPS + 1]
-    vector_out[6:7, 0:half] = jnp.sum(value * hid * factor, axis=0, keepdims=True)
-    vector_out[7:8, 0:half] = gain2[0:1]
-    vector_out[6:7, half : half + nbc] = shared[0:1]
-    vector_out[7:8, half : half + nbc] = shared[1:2]
-    vector_out[8:9, 0:nbc] = shared[2:3]
-    vector_out[8:9, nbc : 2 * nbc] = shared[3:4]
+    vector_out[0 : TAPS + 1, 0:ch] = small[0 : TAPS + 1]
+    vector_out[0:1, ch : ch + heads] = small[8 + TAPS : 9 + TAPS, 0:heads]
+    vector_out[1 : TAPS + 1, ch : ch + nbc] = shared[0:TAPS]
+    vector_out[5:6, 0:half] = jnp.sum(value * hid * factor, axis=0, keepdims=True)
+    vector_out[5:6, half : 2 * half] = gain2[0:1]
+    vector_out[6:7, 0:nbc] = shared[TAPS : TAPS + 1]
 
 
 def stage_kernel(keep, came, send_out, keep_out):
@@ -844,6 +833,7 @@
         smem=(0,),
     )[0]
     got = swap(mine, "row")
+    gu = w_gateup.reshape(half, 2 * ff)
     wk = w_kv.reshape(half, nkv)
     wd = jnp.pad(w_dt, ((0, 0), (0, LANES - heads)))
     gain_one = norm1_gain.astype(F32)[None]
@@ -854,6 +844,11 @@
         smem=(0,),
     )
     part_came = swap(part_low, "row")
+    bc_par = jnp.concatenate(
+        [convbc_weight.T, convbc_bias[None], jnp.zeros((3, nbc), BF16)], 0
+    ).astype(F32)
+    seg_row = segment_ids.astype(F32)
+    seg_col = jnp.broadcast_to(segment_ids[0].astype(F32)[:, None], (tokens, LANES))
     t_first, g_first, in_pair, x_par, head_par, gain_two = run(
         lambda *refs: split_kernel(heads, *refs),
         [
@@ -865,14 +860,13 @@
             ((1, full_width), F32),
         ],
         place, got, cotangent, small,
-        smem=(0,),
+        smem=(0,), after=(gu, seg_row, seg_col, bc_par, order_near, order_down, order_mix),
     )
     t_second = swap(t_first, "dp", 1)
     g_second = swap(g_first, "dp", 2)
     t_third = swap(t_first, "dp", 2)
     g_third = swap(g_first, "dp", 1)
     in_came = swap(in_pair, "col")
-    gu = w_gateup.reshape(half, 2 * ff)
     far, dy_own, dy_far, factor1, n1, left1 = run(
         norm_kernel,
         [
@@ -890,12 +884,6 @@
     g_fourth = swap(g_second, "dp", 1)
     tall_fetch = (t_first, t_second, t_third, t_fourth)
 
-    bc_par = jnp.concatenate(
-        [convbc_weight.T, convbc_bias[None], jnp.zeros((3, nbc), BF16)], 0
-    ).astype(F32)
-    seg_row = segment_ids.astype(F32)
-    seg_col = jnp.broadcast_to(segment_ids[0].astype(F32)[:, None], (tokens, LANES))
-
     mixed, raw, pre, ys = run(
         lambda *refs: mix_kernel(ch, nq, *refs),
         [
@@ -905,13 +893,12 @@
             ((tokens, ch), F32),
         ],
         seg_row, seg_col, factor1, part, part_came, x_par, bc_par, head_par,
-        after=(g_third,),
     )
     mix_part = run(
         out_kernel,
         [((tokens, full_width), F32)],
         mixed, w_mixout, w_attnout, *tall_fetch,
-        after=(g_fourth,),
+        after=(g_third, g_fourth),
     )[0]
     mix_came = swap(mix_part, "col")
     grad_act = run(
@@ -1003,7 +990,7 @@
     n1_came = swap(n1_part, "col")
     def one_outs(keep):
         width = ch + nbc + LANES
-        return [((keep + 32, width), BF16), ((keep, width), F32), ((16, ch), F32)]
+        return [((keep + 16, width), BF16), ((keep, width), F32), ((8, ch + nbc + LANES), F32)]
 
     tall_send, tall_keep = run(
         tall_kernel, quarters(4 * half), d_left, dy_own, d_came, m_left, low, m_came
@@ -1019,21 +1006,21 @@
         [((size, ch), F32), ((size, nq), F32), ((size, nkv), F32)],
     )
     next(s_two)
+    next(s_gu)
     dn1, sum_rows = run(
         close_kernel,
         [((tokens, half), F32), ((16, tokens), F32)],
         own, n1_part, n1_came, n1_bc, gain_one, gbc, gbc_came,
     )
     rows_far = swap(sum_rows, "row")
-    next(s_gu)
+    next(s_two)
     grad_hidden, vector = run(
         end_kernel,
-        [((tokens, quarter), F32), ((16, ch), F32)],
+        [((tokens, quarter), F32), ((8, ch + nbc + LANES), F32)],
         place, own, factor1, resid, dn1, gain_one, sum_rows, rows_far, small_sum, gain2_sum,
         smem=(0,),
     )
     vector_came = swap(vector, "dp", near[0])
-    next(s_two)
     r_gu = finish(s_gu)
     one_send, one_keep, vector = run(
         one_kernel, one_outs(rows // 2),
@@ -1055,7 +1042,7 @@
         [
             ((size, ch), F32),
             ((size, nbc), F32),
-            ((size, heads), F32),
+            ((heads, size), F32),
             ((1, half), F32),
             ((1, half), F32),
             ((TAPS, cq), F32),
@@ -1077,7 +1064,7 @@
         o_norm1[0],
         r_gate,
         r_xin,
-        r_dt,
+        r_dt.T,
         r_bc,
         r_query,
         r_kv.reshape(size, 1, nkv),

time: 221 us -> 210 us (0.950)
  local copies, waits for them, and re-layouts: 26.2 us -> 18.2 us
  starting transfers between devices: 34.5 us -> 30.7 us
  other arithmetic: 4.31 us -> 6.98 us
    unnamed x95 -> x16, local copies, waits for them, and re-layouts: 20.6 us -> 7.64 us
    ppermute x30, starting transfers between devices: 34.5 us -> 30.7 us  [swap(): return lax.ppermute(values, axis, [(i, i ^ step) for i in range(count)])]
  transfers between devices with their start and end apart: 30 -> 30, of which waited for: 12 -> 16; matrix products, arithmetic and copies ran while one was open for 4% -> 7% of each run, Pallas kernels for 36% -> 38%
where the time goes in v5:
time: 210 us; the launch traced here: 209 us
  Pallas kernels  95 us (45%)
  waiting for transfers between devices  57.4 us (27%)
  starting transfers between devices  30.7 us (15%)
  local copies, waits for them, and re-layouts  18.2 us (9%)
  other arithmetic  6.98 us (3%)
    pallas_call x26, Pallas kernels, __call__(): pl.pallas_call(body, out_shape=[jax.ShapeDtypeStruct((8, LANES), F32)] +...  95 us
    ppermute x30, waiting for transfers between devices, swap(): return lax.ppermute(values, axis, [(i, i ^ step) for i in range(count)])  57.4 us
    ppermute x30, starting transfers between devices, swap(): return lax.ppermute(values, axis, [(i, i ^ step) for i in range(count)])  30.7 us
    unnamed x16, local copies, waits for them, and re-layouts  7.64 us
  transfers between devices with their start and end apart: 30, of which 16 were waited for; matrix products, arithmetic and copies ran while one was open for 7% of the time, Pallas kernels for 38%

profile of v5, /device:TPU:0, one launch (start us, length us, event | category | flops | bytes accessed | tf_op | source)
XLA Modules:
  0.0 209.2 jit_solution(7212198254839856475)
XLA Ops:
  10.0 3.2 %shard_map.400 = (f32[8,128]{1,0:T(8,128)}, bf16[5152,128]{1,0:T(8,128)(2,1)}) custom-call(s32[3]{0:T(128)} %pad_add_fusion.1.refs_0_, bf16[768,512]{1,0:T(8,128)(2,1)} %refs_7_.3, bf16[256,512]{1,0:T(8,128)(2,1)} %refs_8_.4, bf16[1024,512]{1,0:T(8,128)(2,1)} %refs_12_.1, bf16[128,2048]{1,0:T(8,128)(2,1)} %bitcast.31, bf16[256,256]{1,0:T(8,128)(2,1)} %refs_2_.5, ...), custom_call_target="tpu_custom_call" | custom-call | tf_op jit(solution)/shard_map/pallas_call | solution.py:59
  13.2 3.0 %collective-permute-start = (bf16[5152,128]{1,0:T(8,128)(2,1)}, bf16[5152,128]{1,0:T(8,128)(2,1)}, u32[]{:S(2)}, u32[]{:S(2)}) collective-permute-start(bf16[5152,128]{1,0:T(8,128)(2,1)} %get-tuple-element.136), channel_id=1, source_target_pairs={{0,2},{2,0},{1,3},{3,1},{4,6},{6,4},{5,7},{7,5},{8,10},{10,8},{9,1... | collective-permute-start | bytes 3956744 | tf_op jit(solution)/shard_map/ppermute | solution.py:20
  20.9 3.6 %copy.49 = bf16[64,8,2,1024]{3,1,2,0:T(8,128)(2,1)} copy(bf16[64,8,2,1024]{3,2,1,0:T(2,128)(2,1)} %bitcast.30) | data formatting | bytes 4194304
  25.8 5.0 %shard_map.401 = (f32[8,128]{1,0:T(8,128)}, bf16[256,512]{1,0:T(8,128)(2,1)}, f32[256,2304]{1,0:T(8,128)}, bf16[256,2304]{1,0:T(8,128)(2,1)}) custom-call(s32[3]{0:T(128)} %pad_add_fusion.1.refs_0_, bf16[256,256]{1,0:T(8,128)(2,1)} %refs_1_.4, bf16[256,256]{1,0:T(8,128)(2,1)} %collective-permute-done.1.refs_2_, f32[1,512]{1,0:T(1,128)} %bitcast.35, ...), custom_call_target="tpu_custom_call" | custom-call | tf_op jit(solution)/shard_map/pallas_call | solution.py:59
  32.1 14.1 %collective-permute-done.refs_1_ = bf16[5152,128]{1,0:T(8,128)(2,1)} collective-permute-done((bf16[5152,128]{1,0:T(8,128)(2,1)}, bf16[5152,128]{1,0:T(8,128)(2,1)}, u32[]{:S(2)}, u32[]{:S(2)}) %collective-permute-start) | collective-permute-done | bytes 1318944 | tf_op jit(solution)/shard_map/ppermute | solution.py:20
  47.7 2.7 %shard_map.402 = (f32[8,128]{1,0:T(8,128)}, bf16[2048,128]{1,0:T(8,128)(2,1)}, bf16[128,2048]{1,0:T(8,128)(2,1)}, bf16[768,256]{1,0:T(8,128)(2,1)}, f32[8,768]{1...) custom-call(s32[3]{0:T(128)} %pad_add_fusion.1.refs_0_, bf16[5152,128]{1,0:T(8,128)(2,1)} %collective-permute-done.refs_1_, ...), custom_call_target="tpu_custom_call" | custom-call | tf_op jit(solution)/shard_map/pallas_call | solution.py:59
  56.5 9.1 %collective-permute-done.4.refs_8_.refs_9_ = bf16[128,2048]{1,0:T(8,128)(2,1)} collective-permute-done((bf16[128,2048]{1,0:T(8,128)(2,1)}, bf16[128,2048]{1,0:T(8,128)(2,1)}, u32[]{:S(2)}, u32[]{:S(2)}) %collective-permute-start.4) | collective-permute-done | bytes 524320 | tf_op jit(solution)/shard_map/ppermute | solution.py:20
  69.2 2.5 %shard_map.403 = (f32[8,128]{1,0:T(8,128)}, bf16[256,512]{1,0:T(8,128)(2,1)}, bf16[256,512]{1,0:T(8,128)(2,1)}, bf16[256,512]{1,0:T(8,128)(2,1)}, f32[256,128]{1...) custom-call(s32[3]{0:T(128)} %pad_add_fusion.1.refs_0_, bf16[768,256]{1,0:T(8,128)(2,1)} %get-tuple-element.139.refs_1_, ...), custom_call_target="tpu_custom_call" | custom-call | tf_op jit(solution)/shard_map/pallas_call | solution.py:59
  71.7 7.1 %shard_map.404 = (f32[8,128]{1,0:T(8,128)}, bf16[256,1024]{1,0:T(8,128)(2,1)}, f32[256,2304]{1,0:T(8,128)}, f32[256,1024]{1,0:T(8,128)}, f32[256,768]{1,0:T(8,128)}) custom-call(f32[1,256]{1,0:T(1,128)} %convert_element_type.23.refs_6_.refs_0_.refs_17_, f32[256,128]{1,0:T(8,128)} %broadcast_in_dim.28.refs_7_.refs_1_.refs_18_, ...), custom_call_target="tpu_custom_call" | custom-call | tf_op jit(solution)/shard_map/pallas_call | solution.py:59
  78.9 7.7 %collective-permute-done.9.refs_9_.refs_10_ = bf16[128,2048]{1,0:T(8,128)(2,1)} collective-permute-done((bf16[128,2048]{1,0:T(8,128)(2,1)}, bf16[128,2048]{1,0:T(8,128)(2,1)}, u32[]{:S(2)}, u32[]{:S(2)}) %collective-permute-start.9) | collective-permute-done | bytes 524320 | tf_op jit(solution)/shard_map/ppermute | solution.py:20
  86.7 3.7 %shard_map.405 = (f32[8,128]{1,0:T(8,128)}, f32[256,1024]{1,0:T(8,128)}) custom-call(bf16[256,1024]{1,0:T(8,128)(2,1)} %get-tuple-element.153.refs_0_.refs_15_, bf16[768,512]{1,0:T(8,128)(2,1)} %refs_7_.3, bf16[256,512]{1,0:T(8,128)(2,1)} %refs_8_.4, bf16[2048,128]{1,0:T(8,128)(2,1)} %get-tuple-element.142.refs_3_.refs_9_, ...), custom_call_target="tpu_custom_call" | custom-call | tf_op jit(solution)/shard_map/pallas_call | solution.py:59
  90.3 3.7 %shard_map.406 = (f32[8,128]{1,0:T(8,128)}, f32[256,1024]{1,0:T(8,128)}) custom-call(bf16[256,512]{1,0:T(8,128)(2,1)} %get-tuple-element.144.refs_0_.refs_3_.refs_1_, bf16[256,512]{1,0:T(8,128)(2,1)} %get-tuple-element.145.refs_1_.refs_2_, bf16[1024,512]{1,0:T(8,128)(2,1)} %refs_12_.1, bf16[2048,128]{1,0:T(8,128)(2,1)} %get-tuple-element.142.refs_3_.refs_9_, ...), custom_call_target="tpu_custom_call" | custom-call | tf_op jit(solution)/shard_map/pallas_call | solution.py:59
  94.1 7.8 %shard_map.407 = (f32[8,128]{1,0:T(8,128)}, f32[256,1024]{1,0:T(8,128)}, bf16[256,512]{1,0:T(8,128)(2,1)}, bf16[256,1024]{1,0:T(8,128)(2,1)}, bf16[256,2048]{1,0...) custom-call(s32[3]{0:T(128)} %pad_add_fusion.1.refs_0_, ...), custom_call_target="tpu_custom_call" | custom-call | tf_op jit(solution)/shard_map/pallas_call | solution.py:59
  102.3 4.1 %shard_map.408 = (f32[8,128]{1,0:T(8,128)}, bf16[256,2048]{1,0:T(8,128)(2,1)}, bf16[256,1024]{1,0:T(8,128)(2,1)}, bf16[256,256]{1,0:T(8,128)(2,1)}, bf16[256,512]{1,0:T(8,128)(2,1)}) custom-call(bf16[256,512]{1,0:T(8,128)(2,1)} %get-tuple-element.168.refs_0_, bf16[256,1024]{1,0:T(8,128)(2,1)} %get-tuple-element.169.refs_1_, ...), custom_call_target="tpu_custom_call" | custom-call | tf_op jit(solution)/shard_map/pallas_call | solution.py:59
  109.8 9.2 %shard_map.409 = (f32[8,128]{1,0:T(8,128)}, f32[256,1024]{1,0:T(8,128)}, f32[256,512]{1,0:T(8,128)}, bf16[256,512]{1,0:T(8,128)(2,1)}, f32[8,512]{1,0:T(8,128)},...) custom-call(s32[3]{0:T(128)} %pad_add_fusion.1.refs_0_, ...), custom_call_target="tpu_custom_call" | custom-call | tf_op jit(solution)/shard_map/pallas_call | solution.py:59
  119.6 9.0 %shard_map.410 = (f32[8,128]{1,0:T(8,128)}, bf16[256,768]{1,0:T(8,128)(2,1)}, bf16[256,128]{1,0:T(8,128)(2,1)}, f32[264,256]{1,0:T(8,128)}, f32[16,768]{1,0:T(8,128)}) custom-call(f32[1,256]{1,0:T(1,128)} %convert_element_type.23.refs_6_.refs_0_.refs_17_, f32[256,128]{1,0:T(8,128)} %broadcast_in_dim.28.refs_7_.refs_1_.refs_18_, ...), custom_call_target="tpu_custom_call" | custom-call | tf_op jit(solution)/shard_map/pallas_call | solution.py:59
  129.1 3.7 %collective-permute-done.14.refs_2_ = bf16[256,2048]{1,0:T(8,128)(2,1)} collective-permute-done((bf16[256,2048]{1,0:T(8,128)(2,1)}, bf16[256,2048]{1,0:T(8,128)(2,1)}, u32[]{:S(2)}, u32[]{:S(2)}) %collective-permute-start.14) | collective-permute-done | bytes 1048608 | tf_op jit(solution)/shard_map/ppermute | solution.py:20
  132.8 3.2 %shard_map.411 = (f32[8,128]{1,0:T(8,128)}, bf16[128,2048]{1,0:T(8,128)(2,1)}, f32[128,2048]{1,0:T(8,128)}) custom-call(bf16[256,256]{1,0:T(8,128)(2,1)} %get-tuple-element.181.refs_0_, bf16[256,2048]{1,0:T(8,128)(2,1)} %get-tuple-element.170.refs_2_.refs_1_, bf16[256,2048]{1,0:T(8,128)(2,1)} %collective-permute-done.14.refs_2_, ...), custom_call_target="tpu_custom_call" | custom-call | tf_op jit(solution)/shard_map/pallas_call | solution.py:59
  136.5 4.1 %shard_map.412 = (f32[8,128]{1,0:T(8,128)}, f32[256,512]{1,0:T(8,128)}, f32[256,512]{1,0:T(8,128)}, bf16[256,256]{1,0:T(8,128)(2,1)}, bf16[256,1152]{1,0:T(8,128)(2,1)}) custom-call(bf16[256,1152]{1,0:T(8,128)(2,1)} %get-tuple-element.175.refs_0_.refs_1_, bf16[256,768]{1,0:T(8,128)(2,1)} %get-tuple-element.178.refs_1_, ...), custom_call_target="tpu_custom_call" | custom-call | tf_op jit(solution)/shard_map/pallas_call | solution.py:59
  143.6 3.2 %shard_map.413 = (f32[8,128]{1,0:T(8,128)}, bf16[128,2048]{1,0:T(8,128)(2,1)}, f32[128,2048]{1,0:T(8,128)}) custom-call(bf16[256,512]{1,0:T(8,128)(2,1)} %get-tuple-element.190.refs_0_, bf16[256,512]{1,0:T(8,128)(2,1)} %get-tuple-element.144.refs_0_.refs_3_.refs_1_, bf16[256,1024]{1,0:T(8,128)(2,1)} %collective-permute-done.18.refs_2_, ...), custom_call_target="tpu_custom_call" | custom-call | tf_op jit(solution)/shard_map/pallas_call | solution.py:59
  146.8 2.6 %shard_map.414 = (f32[8,128]{1,0:T(8,128)}, bf16[128,1152]{1,0:T(8,128)(2,1)}, f32[128,1152]{1,0:T(8,128)}) custom-call(bf16[256,512]{1,0:T(8,128)(2,1)} %get-tuple-element.167.refs_23_.refs_11_.refs_0_, bf16[256,1152]{1,0:T(8,128)(2,1)} %get-tuple-element.175.refs_0_.refs_1_, bf16[256,1152]{1,0:T(8,128)(2,1)} %collective-permute-done.17.refs_2_, ...), custom_call_target="tpu_custom_call" | custom-call | tf_op jit(solution)/shard_map/pallas_call | solution.py:59
  151.4 3.4 %collective-permute-done.16.refs_1_ = bf16[128,2048]{1,0:T(8,128)(2,1)} collective-permute-done((bf16[128,2048]{1,0:T(8,128)(2,1)}, bf16[128,2048]{1,0:T(8,128)(2,1)}, u32[]{:S(2)}, u32[]{:S(2)}) %collective-permute-start.16) | collective-permute-done | bytes 524320 | tf_op jit(solution)/shard_map/ppermute | solution.py:20
  154.9 2.3 %shard_map.415 = (f32[8,128]{1,0:T(8,128)}, bf16[64,2048]{1,0:T(8,128)(2,1)}, f32[64,2048]{1,0:T(8,128)}) custom-call(f32[128,2048]{1,0:T(8,128)} %get-tuple-element.187.refs_0_, bf16[128,2048]{1,0:T(8,128)(2,1)} %collective-permute-done.16.refs_1_, f32[8,128]{1,0:T(8,128)} %get-tuple-element.197.refs_2_), custom_call_target="tpu_custom_call" | custom-call | tf_op jit(solution)/shard_map/pallas_call | solution.py:59
  157.1 2.6 %collective-permute-start.24 = (bf16[64,2048]{1,0:T(8,128)(2,1)}, bf16[64,2048]{1,0:T(8,128)(2,1)}, u32[]{:S(2)}, u32[]{:S(2)}) collective-permute-start(bf16[64,2048]{1,0:T(8,128)(2,1)} %get-tuple-element.212), channel_id=1, source_target_pairs={{0,16},{4,20},{8,24},{12,28},{16,0},{20,4},{24,8},{28,12},{1,17},{... | collective-permute-start | bytes 786440 | tf_op jit(solution)/shard_map/ppermute | solution.py:20
  159.7 2.8 %shard_map.416 = (f32[8,128]{1,0:T(8,128)}, f32[256,512]{1,0:T(8,128)}, f32[16,256]{1,0:T(8,128)}) custom-call(bf16[256,512]{1,0:T(8,128)(2,1)} %get-tuple-element.140.refs_3_.refs_1_.refs_0_, f32[256,512]{1,0:T(8,128)} %get-tuple-element.185.refs_1_, f32[256,512]{1,0:T(8,128)} %collective-permute-done.15.refs_2_, f32[256,512]{1,0:T(8,128)} %get-tuple-element.186.refs_3_, ...), custom_call_target="tpu_custom_call" | custom-call | tf_op jit(solution)/shard_map/pallas_call | solution.py:59
  166.6 2.5 %shard_map.418 = (f32[8,128]{1,0:T(8,128)}, f32[256,256]{1,0:T(8,128)}, f32[8,1152]{1,0:T(8,128)}) custom-call(s32[3]{0:T(128)} %pad_add_fusion.1.refs_0_, bf16[256,512]{1,0:T(8,128)(2,1)} %get-tuple-element.140.refs_3_.refs_1_.refs_0_, f32[256,128]{1,0:T(8,128)} %get-tuple-element.147.refs_2_, f32[256,512]{1,0:T(8,128)} %get-tuple-element.174.refs_3_, ...), custom_call_target="tpu_custom_call" | custom-call | tf_op jit(solution)/shard_map/pallas_call | solution.py:59
  173.5 2.7 %shard_map.420 = (f32[8,128]{1,0:T(8,128)}, bf16[144,1152]{1,0:T(8,128)(2,1)}, f32[128,1152]{1,0:T(8,128)}, f32[8,1152]{1,0:T(8,128)}) custom-call(bf16[256,512]{1,0:T(8,128)(2,1)} %get-tuple-element.167.refs_23_.refs_11_.refs_0_, bf16[256,768]{1,0:T(8,128)(2,1)} %get-tuple-element.178.refs_1_, bf16[256,256]{1,0:T(8,128)(2,1)} %get-tuple-element.208.refs_2_, ...), custom_call_target="tpu_custom_call" | custom-call | tf_op jit(solution)/shard_map/pallas_call | solution.py:59
  176.5 2.7 %collective-permute-start.26 = (bf16[64,1152]{1,0:T(8,128)(2,1)}, bf16[64,1152]{1,0:T(8,128)(2,1)}, u32[]{:S(2)}, u32[]{:S(2)}) collective-permute-start(bf16[64,1152]{1,0:T(8,128)(2,1)} %get-tuple-element.219), channel_id=1, source_target_pairs={{0,16},{4,20},{8,24},{12,28},{16,0},{20,4},{24,8},{28,12},{1,17},{... | collective-permute-start | bytes 442376 | tf_op jit(solution)/shard_map/ppermute | solution.py:20
  179.2 2.3 %shard_map.421 = (f32[8,128]{1,0:T(8,128)}, bf16[64,2048]{1,0:T(8,128)(2,1)}, f32[64,2048]{1,0:T(8,128)}) custom-call(f32[128,2048]{1,0:T(8,128)} %get-tuple-element.220.refs_0_, bf16[128,2048]{1,0:T(8,128)(2,1)} %collective-permute-done.27.refs_1_, f32[8,128]{1,0:T(8,128)} %get-tuple-element.222.refs_2_), custom_call_target="tpu_custom_call" | custom-call | tf_op jit(solution)/shard_map/pallas_call | solution.py:59
  181.7 6.5 %collective-permute-done.26.refs_1_ = bf16[64,1152]{1,0:T(8,128)(2,1)} collective-permute-done((bf16[64,1152]{1,0:T(8,128)(2,1)}, bf16[64,1152]{1,0:T(8,128)(2,1)}, u32[]{:S(2)}, u32[]{:S(2)}) %collective-permute-start.26) | collective-permute-done | bytes 147488 | tf_op jit(solution)/shard_map/ppermute | solution.py:20
  192.1 3.4 %collective-permute-start.28 = (bf16[80,1152]{1,0:T(8,128)(2,1)}, bf16[80,1152]{1,0:T(8,128)(2,1)}, u32[]{:S(2)}, u32[]{:S(2)}) collective-permute-start(bf16[80,1152]{1,0:T(8,128)(2,1)} %get-tuple-element.226), channel_id=1, source_target_pairs={{0,16},{4,20},{8,24},{12,28},{16,0},{20,4},{24,8},{28,12},{1,17},{... | collective-permute-start | bytes 552968 | tf_op jit(solution)/shard_map/ppermute | solution.py:20
  197.7 5.9 %collective-permute-done.29.refs_1_ = bf16[64,2048]{1,0:T(8,128)(2,1)} collective-permute-done((bf16[64,2048]{1,0:T(8,128)(2,1)}, bf16[64,2048]{1,0:T(8,128)(2,1)}, u32[]{:S(2)}, u32[]{:S(2)}) %collective-permute-start.29) | collective-permute-done | bytes 262176 | tf_op jit(solution)/shard_map/ppermute | solution.py:20
  (93 shorter events, 59.0 us)
Async XLA Ops:
  13.2 33.1 %collective-permute-start = (bf16[5152,128]{1,0:T(8,128)(2,1)}, bf16[5152,128]{1,0:T(8,128)(2,1)}, u32[]{:S(2)}, u32[]{:S(2)}) collective-permute-start(bf16[5152,128]{1,0:T(8,128)(2,1)} %get-tuple-element.136), channel_id=1, source_target_pairs={{0,2},{2,0},{1,3},{3,1},{4,6},{6,4},{5,7},{7,5},{8,10},{10,8},{9,1... | collective-permute-start | bytes 3956744 | tf_op jit(solution)/shard_map/ppermute | solution.py:20
  16.1 9.7 %collective-permute-start.1 = (bf16[256,256]{1,0:T(8,128)(2,1)}, bf16[256,256]{1,0:T(8,128)(2,1)}, u32[]{:S(2)}, u32[]{:S(2)}) collective-permute-start(bf16[256,256]{1,0:T(8,128)(2,1)} %refs_1_.4), channel_id=1, source_target_pairs={{0,1},{1,0},{2,3},{3,2},{4,5},{5,4},{6,7},{7,6},{8,9},{9,8},{10,11... | collective-permute-start | bytes 393224 | tf_op jit(solution)/shard_map/ppermute | solution.py:20
  20.8 3.7 %copy-start.1 = (s32[1,1024]{1,0:T(1,128)S(1)}, s32[1,1024]{1,0:T(1,128)}, u32[]{:S(2)}) copy-start(s32[1,1024]{1,0:T(1,128)} %constant.63) | copy-start | bytes 12292
  20.9 4.3 %copy-start.3 = (bf16[256,4]{0,1:T(4,128)(2,1)S(1)}, bf16[256,4]{0,1:T(4,128)(2,1)}, u32[]{:S(2)}) copy-start(bf16[256,4]{0,1:T(4,128)(2,1)} %param.36) | copy-start | bytes 6148
  30.8 40.8 %collective-permute-start.5 = (bf16[256,2304]{1,0:T(8,128)(2,1)}, bf16[256,2304]{1,0:T(8,128)(2,1)}, u32[]{:S(2)}, u32[]{:S(2)}) collective-permute-start(bf16[256,2304]{1,0:T(8,128)(2,1)} %get-tuple-element.149), channel_id=1, source_target_pairs={{0,2},{2,0},{1,3},{3,1},{4,6},{6,4},{5,7},{7,5},{8,10},{10,8},{9,1... | collective-permute-start | bytes 3538952 | tf_op jit(solution)/shard_map/ppermute | solution.py:20
  50.4 15.3 %collective-permute-start.4 = (bf16[128,2048]{1,0:T(8,128)(2,1)}, bf16[128,2048]{1,0:T(8,128)(2,1)}, u32[]{:S(2)}, u32[]{:S(2)}) collective-permute-start(bf16[128,2048]{1,0:T(8,128)(2,1)} %get-tuple-element.143.refs_7_), channel_id=1, source_target_pairs={{0,8},{4,12},{8,0},{12,4},{16,24},{20,28},{24,16},{28,20},{1,9},{5... | collective-permute-start | bytes 1572872 | tf_op jit(solution)/shard_map/ppermute | solution.py:20
  52.5 15.2 %collective-permute-start.3 = (bf16[2048,128]{1,0:T(8,128)(2,1)}, bf16[2048,128]{1,0:T(8,128)(2,1)}, u32[]{:S(2)}, u32[]{:S(2)}) collective-permute-start(bf16[2048,128]{1,0:T(8,128)(2,1)} %get-tuple-element.142.refs_3_.refs_9_), channel_id=1, source_target_pairs={{0,4},{4,0},{8,12},{12,8},{16,20},{20,16},{24,28},{28,24},{1,5},{5... | collective-permute-start | bytes 1572872 | tf_op jit(solution)/shard_map/ppermute | solution.py:20
  54.0 2.1 collective-permute-start.2
  54.0 24.9 %collective-permute-start.8 = (bf16[128,2048]{1,0:T(8,128)(2,1)}, bf16[128,2048]{1,0:T(8,128)(2,1)}, u32[]{:S(2)}, u32[]{:S(2)}) collective-permute-start(bf16[128,2048]{1,0:T(8,128)(2,1)} %get-tuple-element.143.refs_7_), channel_id=1, source_target_pairs={{0,4},{4,0},{8,12},{12,8},{16,20},{20,16},{24,28},{28,24},{1,5},{5... | collective-permute-start | bytes 1572872 | tf_op jit(solution)/shard_map/ppermute | solution.py:20
  56.1 22.9 %collective-permute-start.6 = (bf16[2048,128]{1,0:T(8,128)(2,1)}, bf16[2048,128]{1,0:T(8,128)(2,1)}, u32[]{:S(2)}, u32[]{:S(2)}) collective-permute-start(bf16[2048,128]{1,0:T(8,128)(2,1)} %get-tuple-element.142.refs_3_.refs_9_), channel_id=1, source_target_pairs={{0,8},{4,12},{8,0},{12,4},{16,24},{20,28},{24,16},{28,20},{1,9},{5... | collective-permute-start | bytes 1572872 | tf_op jit(solution)/shard_map/ppermute | solution.py:20
  65.7 21.0 %collective-permute-start.9 = (bf16[128,2048]{1,0:T(8,128)(2,1)}, bf16[128,2048]{1,0:T(8,128)(2,1)}, u32[]{:S(2)}, u32[]{:S(2)}) collective-permute-start(bf16[128,2048]{1,0:T(8,128)(2,1)} %collective-permute-done.4.refs_8_.refs_9_), channel_id=1, source_target_pairs={{0,4},{4,0},{8,12},{12,8},{16,20},{20,16},{24,28},{28,24},{1,5},{5... | collective-permute-start | bytes 1572872 | tf_op jit(solution)/shard_map/ppermute | solution.py:20
  67.7 19.0 %collective-permute-start.7 = (bf16[2048,128]{1,0:T(8,128)(2,1)}, bf16[2048,128]{1,0:T(8,128)(2,1)}, u32[]{:S(2)}, u32[]{:S(2)}) collective-permute-start(bf16[2048,128]{1,0:T(8,128)(2,1)} %collective-permute-done.3.refs_7_.refs_4_.refs_10_), channel_id=1, source_target_pairs={{0,8},{4,12},{8,0},{12,4},{16,24},{20,28},{24,16},{28,20},{1,9},{5... | collective-permute-start | bytes 1572872 | tf_op jit(solution)/shard_map/ppermute | solution.py:20
  90.3 3.7 %collective-permute-start.10 = (f32[256,1024]{1,0:T(8,128)}, f32[256,1024]{1,0:T(8,128)}, u32[]{:S(2)}, u32[]{:S(2)}) collective-permute-start(f32[256,1024]{1,0:T(8,128)} %get-tuple-element.155.refs_3_), channel_id=1, source_target_pairs={{0,1},{1,0},{2,3},{3,2},{4,5},{5,4},{6,7},{7,6},{8,9},{9,8},{10,11... | collective-permute-start | bytes 3145736 | tf_op jit(solution)/shard_map/ppermute | solution.py:20
  101.8 8.0 %collective-permute-start.11 = (f32[256,1024]{1,0:T(8,128)}, f32[256,1024]{1,0:T(8,128)}, u32[]{:S(2)}, u32[]{:S(2)}) collective-permute-start(f32[256,1024]{1,0:T(8,128)} %get-tuple-element.161.refs_4_), channel_id=1, source_target_pairs={{0,1},{1,0},{2,3},{3,2},{4,5},{5,4},{6,7},{7,6},{8,9},{9,8},{10,11... | collective-permute-start | bytes 3145736 | tf_op jit(solution)/shard_map/ppermute | solution.py:20
  106.5 26.3 %collective-permute-start.14 = (bf16[256,2048]{1,0:T(8,128)(2,1)}, bf16[256,2048]{1,0:T(8,128)(2,1)}, u32[]{:S(2)}, u32[]{:S(2)}) collective-permute-start(bf16[256,2048]{1,0:T(8,128)(2,1)} %get-tuple-element.182), channel_id=1, source_target_pairs={{0,4},{4,0},{8,12},{12,8},{16,20},{20,16},{24,28},{28,24},{1,5},{5... | collective-permute-start | bytes 3145736 | tf_op jit(solution)/shard_map/ppermute | solution.py:20
  107.9 1.9 collective-permute-start.12
  107.9 34.1 %collective-permute-start.18 = (bf16[256,1024]{1,0:T(8,128)(2,1)}, bf16[256,1024]{1,0:T(8,128)(2,1)}, u32[]{:S(2)}, u32[]{:S(2)}) collective-permute-start(bf16[256,1024]{1,0:T(8,128)(2,1)} %get-tuple-element.191), channel_id=1, source_target_pairs={{0,8},{4,12},{8,0},{12,4},{16,24},{20,28},{24,16},{28,20},{1,9},{5... | collective-permute-start | bytes 1572872 | tf_op jit(solution)/shard_map/ppermute | solution.py:20
  119.0 27.8 %collective-permute-start.17 = (bf16[256,1152]{1,0:T(8,128)(2,1)}, bf16[256,1152]{1,0:T(8,128)(2,1)}, u32[]{:S(2)}, u32[]{:S(2)}) collective-permute-start(bf16[256,1152]{1,0:T(8,128)(2,1)} %get-tuple-element.189), channel_id=1, source_target_pairs={{0,4},{4,0},{8,12},{12,8},{16,20},{20,16},{24,28},{28,24},{1,5},{5... | collective-permute-start | bytes 1769480 | tf_op jit(solution)/shard_map/ppermute | solution.py:20
  128.6 7.9 %collective-permute-start.13 = (f32[264,256]{1,0:T(8,128)}, f32[264,256]{1,0:T(8,128)}, u32[]{:S(2)}, u32[]{:S(2)}) collective-permute-start(f32[264,256]{1,0:T(8,128)} %get-tuple-element.180.refs_3_.refs_5_), channel_id=1, source_target_pairs={{0,1},{1,0},{2,3},{3,2},{4,5},{5,4},{6,7},{7,6},{8,9},{9,8},{10,11... | collective-permute-start | bytes 811016 | tf_op jit(solution)/shard_map/ppermute | solution.py:20
  128.6 15.0 %collective-permute-start.19 = (bf16[256,1024]{1,0:T(8,128)(2,1)}, bf16[256,1024]{1,0:T(8,128)(2,1)}, u32[]{:S(2)}, u32[]{:S(2)}) collective-permute-start(bf16[256,1024]{1,0:T(8,128)(2,1)} %get-tuple-element.194), channel_id=1, source_target_pairs={{0,8},{4,12},{8,0},{12,4},{16,24},{20,28},{24,16},{28,20},{1,9},{5... | collective-permute-start | bytes 1572872 | tf_op jit(solution)/shard_map/ppermute | solution.py:20
  136.0 18.9 %collective-permute-start.16 = (bf16[128,2048]{1,0:T(8,128)(2,1)}, bf16[128,2048]{1,0:T(8,128)(2,1)}, u32[]{:S(2)}, u32[]{:S(2)}) collective-permute-start(bf16[128,2048]{1,0:T(8,128)(2,1)} %get-tuple-element.188), channel_id=1, source_target_pairs={{0,8},{4,12},{8,0},{12,4},{16,24},{20,28},{24,16},{28,20},{1,9},{5... | collective-permute-start | bytes 1572872 | tf_op jit(solution)/shard_map/ppermute | solution.py:20
  140.6 32.9 %collective-permute-start.22 = (bf16[256,1152]{1,0:T(8,128)(2,1)}, bf16[256,1152]{1,0:T(8,128)(2,1)}, u32[]{:S(2)}, u32[]{:S(2)}) collective-permute-start(bf16[256,1152]{1,0:T(8,128)(2,1)} %get-tuple-element.209), channel_id=1, source_target_pairs={{0,4},{4,0},{8,12},{12,8},{16,20},{20,16},{24,28},{28,24},{1,5},{5... | collective-permute-start | bytes 1769480 | tf_op jit(solution)/shard_map/ppermute | solution.py:20
  142.0 17.7 %collective-permute-start.15 = (f32[256,512]{1,0:T(8,128)}, f32[256,512]{1,0:T(8,128)}, u32[]{:S(2)}, u32[]{:S(2)}) collective-permute-start(f32[256,512]{1,0:T(8,128)} %get-tuple-element.185.refs_1_), channel_id=1, source_target_pairs={{0,1},{1,0},{2,3},{3,2},{4,5},{5,4},{6,7},{7,6},{8,9},{9,8},{10,11... | collective-permute-start | bytes 1572872 | tf_op jit(solution)/shard_map/ppermute | solution.py:20
  149.5 14.6 %collective-permute-start.21 = (bf16[128,1152]{1,0:T(8,128)(2,1)}, bf16[128,1152]{1,0:T(8,128)(2,1)}, u32[]{:S(2)}, u32[]{:S(2)}) collective-permute-start(bf16[128,1152]{1,0:T(8,128)(2,1)} %get-tuple-element.204), channel_id=1, source_target_pairs={{0,8},{4,12},{8,0},{12,4},{16,24},{20,28},{24,16},{28,20},{1,9},{5... | collective-permute-start | bytes 884744 | tf_op jit(solution)/shard_map/ppermute | solution.py:20
  150.0 29.2 %collective-permute-start.27 = (bf16[128,2048]{1,0:T(8,128)(2,1)}, bf16[128,2048]{1,0:T(8,128)(2,1)}, u32[]{:S(2)}, u32[]{:S(2)}) collective-permute-start(bf16[128,2048]{1,0:T(8,128)(2,1)} %get-tuple-element.221), channel_id=1, source_target_pairs={{0,4},{4,0},{8,12},{12,8},{16,20},{20,16},{24,28},{28,24},{1,5},{5... | collective-permute-start | bytes 1572872 | tf_op jit(solution)/shard_map/ppermute | solution.py:20
  157.1 14.4 %collective-permute-start.24 = (bf16[64,2048]{1,0:T(8,128)(2,1)}, bf16[64,2048]{1,0:T(8,128)(2,1)}, u32[]{:S(2)}, u32[]{:S(2)}) collective-permute-start(bf16[64,2048]{1,0:T(8,128)(2,1)} %get-tuple-element.212), channel_id=1, source_target_pairs={{0,16},{4,20},{8,24},{12,28},{16,0},{20,4},{24,8},{28,12},{1,17},{... | collective-permute-start | bytes 786440 | tf_op jit(solution)/shard_map/ppermute | solution.py:20
  162.5 4.1 %collective-permute-start.20 = (f32[16,256]{1,0:T(8,128)}, f32[16,256]{1,0:T(8,128)}, u32[]{:S(2)}, u32[]{:S(2)}) collective-permute-start(f32[16,256]{1,0:T(8,128)} %get-tuple-element.200.refs_6_), channel_id=1, source_target_pairs={{0,2},{2,0},{1,3},{3,1},{4,6},{6,4},{5,7},{7,5},{8,10},{10,8},{9,1... | collective-permute-start | bytes 49160 | tf_op jit(solution)/shard_map/ppermute | solution.py:20
  169.1 4.4 %collective-permute-start.23 = (f32[8,1152]{1,0:T(8,128)}, f32[8,1152]{1,0:T(8,128)}, u32[]{:S(2)}, u32[]{:S(2)}) collective-permute-start(f32[8,1152]{1,0:T(8,128)} %get-tuple-element.210.refs_5_), channel_id=1, source_target_pairs={{0,4},{4,0},{8,12},{12,8},{16,20},{20,16},{24,28},{28,24},{1,5},{5... | collective-permute-start | bytes 110600 | tf_op jit(solution)/shard_map/ppermute | solution.py:20
  176.2 13.9 %collective-permute-start.25 = (bf16[144,1152]{1,0:T(8,128)(2,1)}, bf16[144,1152]{1,0:T(8,128)(2,1)}, u32[]{:S(2)}, u32[]{:S(2)}) collective-permute-start(bf16[144,1152]{1,0:T(8,128)(2,1)} %get-tuple-element.216), channel_id=1, source_target_pairs={{0,8},{4,12},{8,0},{12,4},{16,24},{20,28},{24,16},{28,20},{1,9},{5... | collective-permute-start | bytes 995336 | tf_op jit(solution)/shard_map/ppermute | solution.py:20
  176.5 11.8 %collective-permute-start.26 = (bf16[64,1152]{1,0:T(8,128)(2,1)}, bf16[64,1152]{1,0:T(8,128)(2,1)}, u32[]{:S(2)}, u32[]{:S(2)}) collective-permute-start(bf16[64,1152]{1,0:T(8,128)(2,1)} %get-tuple-element.219), channel_id=1, source_target_pairs={{0,16},{4,20},{8,24},{12,28},{16,0},{20,4},{24,8},{28,12},{1,17},{... | collective-permute-start | bytes 442376 | tf_op jit(solution)/shard_map/ppermute | solution.py:20
  181.5 22.1 %collective-permute-start.29 = (bf16[64,2048]{1,0:T(8,128)(2,1)}, bf16[64,2048]{1,0:T(8,128)(2,1)}, u32[]{:S(2)}, u32[]{:S(2)}) collective-permute-start(bf16[64,2048]{1,0:T(8,128)(2,1)} %get-tuple-element.229), channel_id=1, source_target_pairs={{0,16},{4,20},{8,24},{12,28},{16,0},{20,4},{24,8},{28,12},{1,17},{... | collective-permute-start | bytes 786440 | tf_op jit(solution)/shard_map/ppermute | solution.py:20
  192.1 14.0 %collective-permute-start.28 = (bf16[80,1152]{1,0:T(8,128)(2,1)}, bf16[80,1152]{1,0:T(8,128)(2,1)}, u32[]{:S(2)}, u32[]{:S(2)}) collective-permute-start(bf16[80,1152]{1,0:T(8,128)(2,1)} %get-tuple-element.226), channel_id=1, source_target_pairs={{0,16},{4,20},{8,24},{12,28},{16,0},{20,4},{24,8},{28,12},{1,17},{... | collective-permute-start | bytes 552968 | tf_op jit(solution)/shard_map/ppermute | solution.py:20
  (2 other events, 7.3 us)

commit v6 on v5

--- a/solution.py
+++ b/solution.py
@@ -844,11 +844,6 @@
         smem=(0,),
     )
     part_came = swap(part_low, "row")
-    bc_par = jnp.concatenate(
-        [convbc_weight.T, convbc_bias[None], jnp.zeros((3, nbc), BF16)], 0
-    ).astype(F32)
-    seg_row = segment_ids.astype(F32)
-    seg_col = jnp.broadcast_to(segment_ids[0].astype(F32)[:, None], (tokens, LANES))
     t_first, g_first, in_pair, x_par, head_par, gain_two = run(
         lambda *refs: split_kernel(heads, *refs),
         [
@@ -860,7 +855,7 @@
             ((1, full_width), F32),
         ],
         place, got, cotangent, small,
-        smem=(0,), after=(gu, seg_row, seg_col, bc_par, order_near, order_down, order_mix),
+        smem=(0,), after=(gu,),
     )
     t_second = swap(t_first, "dp", 1)
     g_second = swap(g_first, "dp", 2)
@@ -883,6 +878,12 @@
     t_fourth = swap(t_second, "dp", 2)
     g_fourth = swap(g_second, "dp", 1)
     tall_fetch = (t_first, t_second, t_third, t_fourth)
+
+    bc_par = jnp.concatenate(
+        [convbc_weight.T, convbc_bias[None], jnp.zeros((3, nbc), BF16)], 0
+    ).astype(F32)
+    seg_row = segment_ids.astype(F32)
+    seg_col = jnp.broadcast_to(segment_ids[0].astype(F32)[:, None], (tokens, LANES))
 
     mixed, raw, pre, ys = run(
         lambda *refs: mix_kernel(ch, nq, *refs),

time: 210 us -> 209 us (level)
  local copies, waits for them, and re-layouts: 18.2 us -> 14.4 us
  starting transfers between devices: 30.7 us -> 33.4 us
  waiting for transfers between devices: 57.4 us -> 54.7 us
  other arithmetic: 6.98 us -> 9.6 us
    ppermute x30, waiting for transfers between devices: 57.4 us -> 54.7 us  [swap(): return lax.ppermute(values, axis, [(i, i ^ step) for i in range(count)])]
    ppermute x30, starting transfers between devices: 30.7 us -> 33.4 us  [swap(): return lax.ppermute(values, axis, [(i, i ^ step) for i in range(count)])]
    unnamed x16 -> x20, local copies, waits for them, and re-layouts: 7.64 us -> 6.43 us
  transfers between devices with their start and end apart: 30 -> 30, of which waited for: 16 -> 13; matrix products, arithmetic and copies ran while one was open for 7% -> 8% of each run, Pallas kernels for 38% -> 38%
where the time goes in v6:
time: 209 us; the launch traced here: 208 us
  Pallas kernels  95.3 us (46%)
  waiting for transfers between devices  54.7 us (26%)
  starting transfers between devices  33.4 us (16%)
  local copies, waits for them, and re-layouts  14.4 us (7%)
  other arithmetic  9.6 us (5%)
    pallas_call x26, Pallas kernels, __call__(): pl.pallas_call(body, out_shape=[jax.ShapeDtypeStruct((8, LANES), F32)] +...  95.3 us
    ppermute x30, waiting for transfers between devices, swap(): return lax.ppermute(values, axis, [(i, i ^ step) for i in range(count)])  54.7 us
    ppermute x30, starting transfers between devices, swap(): return lax.ppermute(values, axis, [(i, i ^ step) for i in range(count)])  33.4 us
    unnamed x20, local copies, waits for them, and re-layouts  6.43 us
  transfers between devices with their start and end apart: 30, of which 13 were waited for; matrix products, arithmetic and copies ran while one was open for 8% of the time, Pallas kernels for 38%

profile of v6, /device:TPU:0, one launch (start us, length us, event | category | flops | bytes accessed | tf_op | source)
XLA Modules:
  0.0 208.3 jit_solution(5005386599426986664)
XLA Ops:
  6.2 3.0 %shard_map.400 = (f32[8,128]{1,0:T(8,128)}, bf16[5152,128]{1,0:T(8,128)(2,1)}) custom-call(s32[3]{0:T(128)} %pad_add_fusion.1.refs_0_, bf16[768,512]{1,0:T(8,128)(2,1)} %refs_7_.3, bf16[256,512]{1,0:T(8,128)(2,1)} %refs_8_.4, bf16[1024,512]{1,0:T(8,128)(2,1)} %refs_12_.1, bf16[128,2048]{1,0:T(8,128)(2,1)} %bitcast.31, bf16[256,256]{1,0:T(8,128)(2,1)} %refs_2_.5, ...), custom_call_target="tpu_custom_call" | custom-call | tf_op jit(solution)/shard_map/pallas_call | solution.py:59
  9.3 3.0 %collective-permute-start = (bf16[5152,128]{1,0:T(8,128)(2,1)}, bf16[5152,128]{1,0:T(8,128)(2,1)}, u32[]{:S(2)}, u32[]{:S(2)}) collective-permute-start(bf16[5152,128]{1,0:T(8,128)(2,1)} %get-tuple-element.136), channel_id=1, source_target_pairs={{0,2},{2,0},{1,3},{3,1},{4,6},{6,4},{5,7},{7,5},{8,10},{10,8},{9,1... | collective-permute-start | bytes 3956744 | tf_op jit(solution)/shard_map/ppermute | solution.py:20
  15.1 5.1 %shard_map.401 = (f32[8,128]{1,0:T(8,128)}, bf16[256,512]{1,0:T(8,128)(2,1)}, f32[256,2304]{1,0:T(8,128)}, bf16[256,2304]{1,0:T(8,128)(2,1)}) custom-call(s32[3]{0:T(128)} %pad_add_fusion.1.refs_0_, bf16[256,256]{1,0:T(8,128)(2,1)} %refs_1_.4, bf16[256,256]{1,0:T(8,128)(2,1)} %collective-permute-done.1.refs_2_, f32[1,512]{1,0:T(1,128)} %bitcast.35, ...), custom_call_target="tpu_custom_call" | custom-call | tf_op jit(solution)/shard_map/pallas_call | solution.py:59
  20.2 3.5 %copy.49 = bf16[64,8,2,1024]{3,1,2,0:T(8,128)(2,1)} copy(bf16[64,8,2,1024]{3,2,1,0:T(2,128)(2,1)} %bitcast.30) | data formatting | bytes 4194304
  23.7 18.6 %collective-permute-done.refs_1_ = bf16[5152,128]{1,0:T(8,128)(2,1)} collective-permute-done((bf16[5152,128]{1,0:T(8,128)(2,1)}, bf16[5152,128]{1,0:T(8,128)(2,1)}, u32[]{:S(2)}, u32[]{:S(2)}) %collective-permute-start) | collective-permute-done | bytes 1318944 | tf_op jit(solution)/shard_map/ppermute | solution.py:20
  42.3 2.7 %shard_map.402 = (f32[8,128]{1,0:T(8,128)}, bf16[2048,128]{1,0:T(8,128)(2,1)}, bf16[128,2048]{1,0:T(8,128)(2,1)}, bf16[768,256]{1,0:T(8,128)(2,1)}, f32[8,768]{1...) custom-call(s32[3]{0:T(128)} %pad_add_fusion.1.refs_0_, bf16[5152,128]{1,0:T(8,128)(2,1)} %collective-permute-done.refs_1_, ...), custom_call_target="tpu_custom_call" | custom-call | tf_op jit(solution)/shard_map/pallas_call | solution.py:59
  51.2 9.0 %collective-permute-done.3.refs_7_.refs_4_.refs_10_ = bf16[2048,128]{1,0:T(8,128)(2,1)} collective-permute-done((bf16[2048,128]{1,0:T(8,128)(2,1)}, bf16[2048,128]{1,0:T(8,128)(2,1)}, u32[]{:S(2)}, u32[]{:S(2)}) %collective-permute-start.3) | collective-permute-done | bytes 524320 | tf_op jit(solution)/shard_map/ppermute | solution.py:20
  68.4 2.5 %shard_map.403 = (f32[8,128]{1,0:T(8,128)}, bf16[256,512]{1,0:T(8,128)(2,1)}, bf16[256,512]{1,0:T(8,128)(2,1)}, bf16[256,512]{1,0:T(8,128)(2,1)}, f32[256,128]{1...) custom-call(s32[3]{0:T(128)} %pad_add_fusion.1.refs_0_, bf16[768,256]{1,0:T(8,128)(2,1)} %get-tuple-element.139.refs_1_, ...), custom_call_target="tpu_custom_call" | custom-call | tf_op jit(solution)/shard_map/pallas_call | solution.py:59
  72.4 7.1 %shard_map.404 = (f32[8,128]{1,0:T(8,128)}, bf16[256,1024]{1,0:T(8,128)(2,1)}, f32[256,2304]{1,0:T(8,128)}, f32[256,1024]{1,0:T(8,128)}, f32[256,768]{1,0:T(8,128)}) custom-call(f32[1,256]{1,0:T(1,128)} %convert_element_type.23.refs_0_.refs_17_, f32[256,128]{1,0:T(8,128)} %broadcast_in_dim.29.refs_1_.refs_18_, f32[256,128]{1,0:T(8,128)} %get-tuple-element.147.refs_2_, ...), custom_call_target="tpu_custom_call" | custom-call | tf_op jit(solution)/shard_map/pallas_call | solution.py:59
  81.2 3.7 %shard_map.405 = (f32[8,128]{1,0:T(8,128)}, f32[256,1024]{1,0:T(8,128)}) custom-call(bf16[256,1024]{1,0:T(8,128)(2,1)} %get-tuple-element.153.refs_0_.refs_15_, bf16[768,512]{1,0:T(8,128)(2,1)} %refs_7_.3, bf16[256,512]{1,0:T(8,128)(2,1)} %refs_8_.4, bf16[2048,128]{1,0:T(8,128)(2,1)} %get-tuple-element.142.refs_3_.refs_9_, ...), custom_call_target="tpu_custom_call" | custom-call | tf_op jit(solution)/shard_map/pallas_call | solution.py:59
  86.2 3.7 %shard_map.406 = (f32[8,128]{1,0:T(8,128)}, f32[256,1024]{1,0:T(8,128)}) custom-call(bf16[256,512]{1,0:T(8,128)(2,1)} %get-tuple-element.144.refs_0_.refs_3_.refs_1_, bf16[256,512]{1,0:T(8,128)(2,1)} %get-tuple-element.145.refs_1_.refs_2_, bf16[1024,512]{1,0:T(8,128)(2,1)} %refs_12_.1, bf16[2048,128]{1,0:T(8,128)(2,1)} %get-tuple-element.142.refs_3_.refs_9_, ...), custom_call_target="tpu_custom_call" | custom-call | tf_op jit(solution)/shard_map/pallas_call | solution.py:59
  89.9 7.8 %shard_map.407 = (f32[8,128]{1,0:T(8,128)}, f32[256,1024]{1,0:T(8,128)}, bf16[256,512]{1,0:T(8,128)(2,1)}, bf16[256,1024]{1,0:T(8,128)(2,1)}, bf16[256,2048]{1,0...) custom-call(s32[3]{0:T(128)} %pad_add_fusion.1.refs_0_, ...), custom_call_target="tpu_custom_call" | custom-call | tf_op jit(solution)/shard_map/pallas_call | solution.py:59
  99.6 4.1 %shard_map.408 = (f32[8,128]{1,0:T(8,128)}, bf16[256,2048]{1,0:T(8,128)(2,1)}, bf16[256,1024]{1,0:T(8,128)(2,1)}, bf16[256,256]{1,0:T(8,128)(2,1)}, bf16[256,512]{1,0:T(8,128)(2,1)}) custom-call(bf16[256,512]{1,0:T(8,128)(2,1)} %get-tuple-element.168.refs_0_, bf16[256,1024]{1,0:T(8,128)(2,1)} %get-tuple-element.169.refs_1_, ...), custom_call_target="tpu_custom_call" | custom-call | tf_op jit(solution)/shard_map/pallas_call | solution.py:59
  106.2 9.2 %shard_map.409 = (f32[8,128]{1,0:T(8,128)}, f32[256,1024]{1,0:T(8,128)}, f32[256,512]{1,0:T(8,128)}, bf16[256,512]{1,0:T(8,128)(2,1)}, f32[8,512]{1,0:T(8,128)},...) custom-call(s32[3]{0:T(128)} %pad_add_fusion.1.refs_0_, ...), custom_call_target="tpu_custom_call" | custom-call | tf_op jit(solution)/shard_map/pallas_call | solution.py:59
  116.9 9.0 %shard_map.410 = (f32[8,128]{1,0:T(8,128)}, bf16[256,768]{1,0:T(8,128)(2,1)}, bf16[256,128]{1,0:T(8,128)(2,1)}, f32[264,256]{1,0:T(8,128)}, f32[16,768]{1,0:T(8,128)}) custom-call(f32[1,256]{1,0:T(1,128)} %convert_element_type.23.refs_0_.refs_17_, f32[256,128]{1,0:T(8,128)} %broadcast_in_dim.29.refs_1_.refs_18_, ...), custom_call_target="tpu_custom_call" | custom-call | tf_op jit(solution)/shard_map/pallas_call | solution.py:59
  127.4 2.6 %collective-permute-done.14.refs_2_ = bf16[256,2048]{1,0:T(8,128)(2,1)} collective-permute-done((bf16[256,2048]{1,0:T(8,128)(2,1)}, bf16[256,2048]{1,0:T(8,128)(2,1)}, u32[]{:S(2)}, u32[]{:S(2)}) %collective-permute-start.14) | collective-permute-done | bytes 1048608 | tf_op jit(solution)/shard_map/ppermute | solution.py:20
  130.1 3.2 %shard_map.411 = (f32[8,128]{1,0:T(8,128)}, bf16[128,2048]{1,0:T(8,128)(2,1)}, f32[128,2048]{1,0:T(8,128)}) custom-call(bf16[256,256]{1,0:T(8,128)(2,1)} %get-tuple-element.181.refs_0_, bf16[256,2048]{1,0:T(8,128)(2,1)} %get-tuple-element.170.refs_2_.refs_1_, bf16[256,2048]{1,0:T(8,128)(2,1)} %collective-permute-done.14.refs_2_, ...), custom_call_target="tpu_custom_call" | custom-call | tf_op jit(solution)/shard_map/pallas_call | solution.py:59
  134.8 4.1 %shard_map.412 = (f32[8,128]{1,0:T(8,128)}, f32[256,512]{1,0:T(8,128)}, f32[256,512]{1,0:T(8,128)}, bf16[256,256]{1,0:T(8,128)(2,1)}, bf16[256,1152]{1,0:T(8,128)(2,1)}) custom-call(bf16[256,1152]{1,0:T(8,128)(2,1)} %get-tuple-element.175.refs_0_.refs_1_, bf16[256,768]{1,0:T(8,128)(2,1)} %get-tuple-element.178.refs_1_, ...), custom_call_target="tpu_custom_call" | custom-call | tf_op jit(solution)/shard_map/pallas_call | solution.py:59
  140.9 3.4 %shard_map.413 = (f32[8,128]{1,0:T(8,128)}, bf16[128,2048]{1,0:T(8,128)(2,1)}, f32[128,2048]{1,0:T(8,128)}) custom-call(bf16[256,512]{1,0:T(8,128)(2,1)} %get-tuple-element.190.refs_0_, bf16[256,512]{1,0:T(8,128)(2,1)} %get-tuple-element.144.refs_0_.refs_3_.refs_1_, bf16[256,1024]{1,0:T(8,128)(2,1)} %collective-permute-done.18.refs_2_, ...), custom_call_target="tpu_custom_call" | custom-call | tf_op jit(solution)/shard_map/pallas_call | solution.py:59
  144.3 2.7 %shard_map.414 = (f32[8,128]{1,0:T(8,128)}, bf16[128,1152]{1,0:T(8,128)(2,1)}, f32[128,1152]{1,0:T(8,128)}) custom-call(bf16[256,512]{1,0:T(8,128)(2,1)} %get-tuple-element.167.refs_23_.refs_11_.refs_0_, bf16[256,1152]{1,0:T(8,128)(2,1)} %get-tuple-element.175.refs_0_.refs_1_, bf16[256,1152]{1,0:T(8,128)(2,1)} %collective-permute-done.17.refs_2_, ...), custom_call_target="tpu_custom_call" | custom-call | tf_op jit(solution)/shard_map/pallas_call | solution.py:59
  149.0 3.1 %collective-permute-done.16.refs_1_ = bf16[128,2048]{1,0:T(8,128)(2,1)} collective-permute-done((bf16[128,2048]{1,0:T(8,128)(2,1)}, bf16[128,2048]{1,0:T(8,128)(2,1)}, u32[]{:S(2)}, u32[]{:S(2)}) %collective-permute-start.16) | collective-permute-done | bytes 524320 | tf_op jit(solution)/shard_map/ppermute | solution.py:20
  152.2 2.3 %shard_map.415 = (f32[8,128]{1,0:T(8,128)}, bf16[64,2048]{1,0:T(8,128)(2,1)}, f32[64,2048]{1,0:T(8,128)}) custom-call(f32[128,2048]{1,0:T(8,128)} %get-tuple-element.187.refs_0_, bf16[128,2048]{1,0:T(8,128)(2,1)} %collective-permute-done.16.refs_1_, f32[8,128]{1,0:T(8,128)} %get-tuple-element.197.refs_2_), custom_call_target="tpu_custom_call" | custom-call | tf_op jit(solution)/shard_map/pallas_call | solution.py:59
  154.4 2.6 %collective-permute-start.24 = (bf16[64,2048]{1,0:T(8,128)(2,1)}, bf16[64,2048]{1,0:T(8,128)(2,1)}, u32[]{:S(2)}, u32[]{:S(2)}) collective-permute-start(bf16[64,2048]{1,0:T(8,128)(2,1)} %get-tuple-element.212), channel_id=1, source_target_pairs={{0,16},{4,20},{8,24},{12,28},{16,0},{20,4},{24,8},{28,12},{1,17},{... | collective-permute-start | bytes 786440 | tf_op jit(solution)/shard_map/ppermute | solution.py:20
  157.0 2.8 %shard_map.416 = (f32[8,128]{1,0:T(8,128)}, f32[256,512]{1,0:T(8,128)}, f32[16,256]{1,0:T(8,128)}) custom-call(bf16[256,512]{1,0:T(8,128)(2,1)} %get-tuple-element.140.refs_3_.refs_1_.refs_0_, f32[256,512]{1,0:T(8,128)} %get-tuple-element.185.refs_1_, f32[256,512]{1,0:T(8,128)} %collective-permute-done.15.refs_2_, f32[256,512]{1,0:T(8,128)} %get-tuple-element.186.refs_3_, ...), custom_call_target="tpu_custom_call" | custom-call | tf_op jit(solution)/shard_map/pallas_call | solution.py:59
  163.9 2.5 %shard_map.418 = (f32[8,128]{1,0:T(8,128)}, f32[256,256]{1,0:T(8,128)}, f32[8,1152]{1,0:T(8,128)}) custom-call(s32[3]{0:T(128)} %pad_add_fusion.1.refs_0_, bf16[256,512]{1,0:T(8,128)(2,1)} %get-tuple-element.140.refs_3_.refs_1_.refs_0_, f32[256,128]{1,0:T(8,128)} %get-tuple-element.147.refs_2_, f32[256,512]{1,0:T(8,128)} %get-tuple-element.174.refs_3_, ...), custom_call_target="tpu_custom_call" | custom-call | tf_op jit(solution)/shard_map/pallas_call | solution.py:59
  170.9 2.7 %shard_map.420 = (f32[8,128]{1,0:T(8,128)}, bf16[144,1152]{1,0:T(8,128)(2,1)}, f32[128,1152]{1,0:T(8,128)}, f32[8,1152]{1,0:T(8,128)}) custom-call(bf16[256,512]{1,0:T(8,128)(2,1)} %get-tuple-element.167.refs_23_.refs_11_.refs_0_, bf16[256,768]{1,0:T(8,128)(2,1)} %get-tuple-element.178.refs_1_, bf16[256,256]{1,0:T(8,128)(2,1)} %get-tuple-element.208.refs_2_, ...), custom_call_target="tpu_custom_call" | custom-call | tf_op jit(solution)/shard_map/pallas_call | solution.py:59
  174.9 2.7 %collective-permute-start.26 = (bf16[64,1152]{1,0:T(8,128)(2,1)}, bf16[64,1152]{1,0:T(8,128)(2,1)}, u32[]{:S(2)}, u32[]{:S(2)}) collective-permute-start(bf16[64,1152]{1,0:T(8,128)(2,1)} %get-tuple-element.219), channel_id=1, source_target_pairs={{0,16},{4,20},{8,24},{12,28},{16,0},{20,4},{24,8},{28,12},{1,17},{... | collective-permute-start | bytes 442376 | tf_op jit(solution)/shard_map/ppermute | solution.py:20
  177.6 2.3 %shard_map.421 = (f32[8,128]{1,0:T(8,128)}, bf16[64,2048]{1,0:T(8,128)(2,1)}, f32[64,2048]{1,0:T(8,128)}) custom-call(f32[128,2048]{1,0:T(8,128)} %get-tuple-element.220.refs_0_, bf16[128,2048]{1,0:T(8,128)(2,1)} %collective-permute-done.27.refs_1_, f32[8,128]{1,0:T(8,128)} %get-tuple-element.222.refs_2_), custom_call_target="tpu_custom_call" | custom-call | tf_op jit(solution)/shard_map/pallas_call | solution.py:59
  180.2 6.6 %collective-permute-done.26.refs_1_ = bf16[64,1152]{1,0:T(8,128)(2,1)} collective-permute-done((bf16[64,1152]{1,0:T(8,128)(2,1)}, bf16[64,1152]{1,0:T(8,128)(2,1)}, u32[]{:S(2)}, u32[]{:S(2)}) %collective-permute-start.26) | collective-permute-done | bytes 147488 | tf_op jit(solution)/shard_map/ppermute | solution.py:20
  190.4 3.4 %collective-permute-start.28 = (bf16[80,1152]{1,0:T(8,128)(2,1)}, bf16[80,1152]{1,0:T(8,128)(2,1)}, u32[]{:S(2)}, u32[]{:S(2)}) collective-permute-start(bf16[80,1152]{1,0:T(8,128)(2,1)} %get-tuple-element.226), channel_id=1, source_target_pairs={{0,16},{4,20},{8,24},{12,28},{16,0},{20,4},{24,8},{28,12},{1,17},{... | collective-permute-start | bytes 552968 | tf_op jit(solution)/shard_map/ppermute | solution.py:20
  193.9 2.3 %reshape.281 = f32[64,2,1024]{2,1,0:T(2,128)} reshape(f32[64,2048]{1,0:T(8,128)} %get-tuple-element.249) | data formatting | bytes 1048576 | tf_op jit(solution)/shard_map/reshape | solution.py:1082
  196.2 6.6 %collective-permute-done.29.refs_1_ = bf16[64,2048]{1,0:T(8,128)(2,1)} collective-permute-done((bf16[64,2048]{1,0:T(8,128)(2,1)}, bf16[64,2048]{1,0:T(8,128)(2,1)}, u32[]{:S(2)}, u32[]{:S(2)}) %collective-permute-start.29) | collective-permute-done | bytes 262176 | tf_op jit(solution)/shard_map/ppermute | solution.py:20
  (97 shorter events, 59.6 us)
Async XLA Ops:
  0.7 2.7 %copy-start.1 = (bf16[384]{0:T(512)(128)(2,1)S(1)}, bf16[384]{0:T(512)(128)(2,1)}, u32[]{:S(2)}) copy-start(bf16[384]{0:T(512)(128)(2,1)} %param.35) | copy-start | bytes 2308
  0.7 3.0 %copy-start.2 = (bf16[512]{0:T(512)(128)(2,1)S(1)}, bf16[512]{0:T(512)(128)(2,1)}, u32[]{:S(2)}) copy-start(bf16[512]{0:T(512)(128)(2,1)} %param.43) | copy-start | bytes 3076
  9.3 33.1 %collective-permute-start = (bf16[5152,128]{1,0:T(8,128)(2,1)}, bf16[5152,128]{1,0:T(8,128)(2,1)}, u32[]{:S(2)}, u32[]{:S(2)}) collective-permute-start(bf16[5152,128]{1,0:T(8,128)(2,1)} %get-tuple-element.136), channel_id=1, source_target_pairs={{0,2},{2,0},{1,3},{3,1},{4,6},{6,4},{5,7},{7,5},{8,10},{10,8},{9,1... | collective-permute-start | bytes 3956744 | tf_op jit(solution)/shard_map/ppermute | solution.py:20
  12.2 2.8 %collective-permute-start.1 = (bf16[256,256]{1,0:T(8,128)(2,1)}, bf16[256,256]{1,0:T(8,128)(2,1)}, u32[]{:S(2)}, u32[]{:S(2)}) collective-permute-start(bf16[256,256]{1,0:T(8,128)(2,1)} %refs_1_.4), channel_id=1, source_target_pairs={{0,1},{1,0},{2,3},{3,2},{4,5},{5,4},{6,7},{7,6},{8,9},{9,8},{10,11... | collective-permute-start | bytes 393224 | tf_op jit(solution)/shard_map/ppermute | solution.py:20
  20.2 50.8 %collective-permute-start.5 = (bf16[256,2304]{1,0:T(8,128)(2,1)}, bf16[256,2304]{1,0:T(8,128)(2,1)}, u32[]{:S(2)}, u32[]{:S(2)}) collective-permute-start(bf16[256,2304]{1,0:T(8,128)(2,1)} %get-tuple-element.149), channel_id=1, source_target_pairs={{0,2},{2,0},{1,3},{3,1},{4,6},{6,4},{5,7},{7,5},{8,10},{10,8},{9,1... | collective-permute-start | bytes 3538952 | tf_op jit(solution)/shard_map/ppermute | solution.py:20
  45.0 15.2 %collective-permute-start.3 = (bf16[2048,128]{1,0:T(8,128)(2,1)}, bf16[2048,128]{1,0:T(8,128)(2,1)}, u32[]{:S(2)}, u32[]{:S(2)}) collective-permute-start(bf16[2048,128]{1,0:T(8,128)(2,1)} %get-tuple-element.142.refs_3_.refs_9_), channel_id=1, source_target_pairs={{0,4},{4,0},{8,12},{12,8},{16,20},{20,16},{24,28},{28,24},{1,5},{5... | collective-permute-start | bytes 1572872 | tf_op jit(solution)/shard_map/ppermute | solution.py:20
  47.1 15.3 %collective-permute-start.4 = (bf16[128,2048]{1,0:T(8,128)(2,1)}, bf16[128,2048]{1,0:T(8,128)(2,1)}, u32[]{:S(2)}, u32[]{:S(2)}) collective-permute-start(bf16[128,2048]{1,0:T(8,128)(2,1)} %get-tuple-element.143.refs_7_), channel_id=1, source_target_pairs={{0,8},{4,12},{8,0},{12,4},{16,24},{20,28},{24,16},{28,20},{1,9},{5... | collective-permute-start | bytes 1572872 | tf_op jit(solution)/shard_map/ppermute | solution.py:20
  48.6 2.1 collective-permute-start.2
  48.6 30.9 %collective-permute-start.6 = (bf16[2048,128]{1,0:T(8,128)(2,1)}, bf16[2048,128]{1,0:T(8,128)(2,1)}, u32[]{:S(2)}, u32[]{:S(2)}) collective-permute-start(bf16[2048,128]{1,0:T(8,128)(2,1)} %get-tuple-element.142.refs_3_.refs_9_), channel_id=1, source_target_pairs={{0,8},{4,12},{8,0},{12,4},{16,24},{20,28},{24,16},{28,20},{1,9},{5... | collective-permute-start | bytes 1572872 | tf_op jit(solution)/shard_map/ppermute | solution.py:20
  50.7 28.8 %collective-permute-start.8 = (bf16[128,2048]{1,0:T(8,128)(2,1)}, bf16[128,2048]{1,0:T(8,128)(2,1)}, u32[]{:S(2)}, u32[]{:S(2)}) collective-permute-start(bf16[128,2048]{1,0:T(8,128)(2,1)} %get-tuple-element.143.refs_7_), channel_id=1, source_target_pairs={{0,4},{4,0},{8,12},{12,8},{16,20},{20,16},{24,28},{28,24},{1,5},{5... | collective-permute-start | bytes 1572872 | tf_op jit(solution)/shard_map/ppermute | solution.py:20
  60.2 21.0 %collective-permute-start.7 = (bf16[2048,128]{1,0:T(8,128)(2,1)}, bf16[2048,128]{1,0:T(8,128)(2,1)}, u32[]{:S(2)}, u32[]{:S(2)}) collective-permute-start(bf16[2048,128]{1,0:T(8,128)(2,1)} %collective-permute-done.3.refs_7_.refs_4_.refs_10_), channel_id=1, source_target_pairs={{0,8},{4,12},{8,0},{12,4},{16,24},{20,28},{24,16},{28,20},{1,9},{5... | collective-permute-start | bytes 1572872 | tf_op jit(solution)/shard_map/ppermute | solution.py:20
  62.3 18.9 %collective-permute-start.9 = (bf16[128,2048]{1,0:T(8,128)(2,1)}, bf16[128,2048]{1,0:T(8,128)(2,1)}, u32[]{:S(2)}, u32[]{:S(2)}) collective-permute-start(bf16[128,2048]{1,0:T(8,128)(2,1)} %collective-permute-done.4.refs_8_.refs_9_), channel_id=1, source_target_pairs={{0,4},{4,0},{8,12},{12,8},{16,20},{20,16},{24,28},{28,24},{1,5},{5... | collective-permute-start | bytes 1572872 | tf_op jit(solution)/shard_map/ppermute | solution.py:20
  84.9 5.0 %collective-permute-start.10 = (f32[256,1024]{1,0:T(8,128)}, f32[256,1024]{1,0:T(8,128)}, u32[]{:S(2)}, u32[]{:S(2)}) collective-permute-start(f32[256,1024]{1,0:T(8,128)} %get-tuple-element.155.refs_3_), channel_id=1, source_target_pairs={{0,1},{1,0},{2,3},{3,2},{4,5},{5,4},{6,7},{7,6},{8,9},{9,8},{10,11... | collective-permute-start | bytes 3145736 | tf_op jit(solution)/shard_map/ppermute | solution.py:20
  97.7 8.5 %collective-permute-start.11 = (f32[256,1024]{1,0:T(8,128)}, f32[256,1024]{1,0:T(8,128)}, u32[]{:S(2)}, u32[]{:S(2)}) collective-permute-start(f32[256,1024]{1,0:T(8,128)} %get-tuple-element.161.refs_4_), channel_id=1, source_target_pairs={{0,1},{1,0},{2,3},{3,2},{4,5},{5,4},{6,7},{7,6},{8,9},{9,8},{10,11... | collective-permute-start | bytes 3145736 | tf_op jit(solution)/shard_map/ppermute | solution.py:20
  103.7 26.3 %collective-permute-start.14 = (bf16[256,2048]{1,0:T(8,128)(2,1)}, bf16[256,2048]{1,0:T(8,128)(2,1)}, u32[]{:S(2)}, u32[]{:S(2)}) collective-permute-start(bf16[256,2048]{1,0:T(8,128)(2,1)} %get-tuple-element.182), channel_id=1, source_target_pairs={{0,4},{4,0},{8,12},{12,8},{16,20},{20,16},{24,28},{28,24},{1,5},{5... | collective-permute-start | bytes 3145736 | tf_op jit(solution)/shard_map/ppermute | solution.py:20
  104.3 1.9 collective-permute-start.12
  104.3 35.2 %collective-permute-start.18 = (bf16[256,1024]{1,0:T(8,128)(2,1)}, bf16[256,1024]{1,0:T(8,128)(2,1)}, u32[]{:S(2)}, u32[]{:S(2)}) collective-permute-start(bf16[256,1024]{1,0:T(8,128)(2,1)} %get-tuple-element.191), channel_id=1, source_target_pairs={{0,8},{4,12},{8,0},{12,4},{16,24},{20,28},{24,16},{28,20},{1,9},{5... | collective-permute-start | bytes 1572872 | tf_op jit(solution)/shard_map/ppermute | solution.py:20
  115.4 28.9 %collective-permute-start.17 = (bf16[256,1152]{1,0:T(8,128)(2,1)}, bf16[256,1152]{1,0:T(8,128)(2,1)}, u32[]{:S(2)}, u32[]{:S(2)}) collective-permute-start(bf16[256,1152]{1,0:T(8,128)(2,1)} %get-tuple-element.189), channel_id=1, source_target_pairs={{0,4},{4,0},{8,12},{12,8},{16,20},{20,16},{24,28},{28,24},{1,5},{5... | collective-permute-start | bytes 1769480 | tf_op jit(solution)/shard_map/ppermute | solution.py:20
  125.9 9.0 %collective-permute-start.13 = (f32[264,256]{1,0:T(8,128)}, f32[264,256]{1,0:T(8,128)}, u32[]{:S(2)}, u32[]{:S(2)}) collective-permute-start(f32[264,256]{1,0:T(8,128)} %get-tuple-element.180.refs_3_.refs_5_), channel_id=1, source_target_pairs={{0,1},{1,0},{2,3},{3,2},{4,5},{5,4},{6,7},{7,6},{8,9},{9,8},{10,11... | collective-permute-start | bytes 811016 | tf_op jit(solution)/shard_map/ppermute | solution.py:20
  125.9 15.0 %collective-permute-start.19 = (bf16[256,1024]{1,0:T(8,128)(2,1)}, bf16[256,1024]{1,0:T(8,128)(2,1)}, u32[]{:S(2)}, u32[]{:S(2)}) collective-permute-start(bf16[256,1024]{1,0:T(8,128)(2,1)} %get-tuple-element.194), channel_id=1, source_target_pairs={{0,8},{4,12},{8,0},{12,4},{16,24},{20,28},{24,16},{28,20},{1,9},{5... | collective-permute-start | bytes 1572872 | tf_op jit(solution)/shard_map/ppermute | solution.py:20
  133.3 18.9 %collective-permute-start.16 = (bf16[128,2048]{1,0:T(8,128)(2,1)}, bf16[128,2048]{1,0:T(8,128)(2,1)}, u32[]{:S(2)}, u32[]{:S(2)}) collective-permute-start(bf16[128,2048]{1,0:T(8,128)(2,1)} %get-tuple-element.188), channel_id=1, source_target_pairs={{0,8},{4,12},{8,0},{12,4},{16,24},{20,28},{24,16},{28,20},{1,9},{5... | collective-permute-start | bytes 1572872 | tf_op jit(solution)/shard_map/ppermute | solution.py:20
  139.0 31.9 %collective-permute-start.22 = (bf16[256,1152]{1,0:T(8,128)(2,1)}, bf16[256,1152]{1,0:T(8,128)(2,1)}, u32[]{:S(2)}, u32[]{:S(2)}) collective-permute-start(bf16[256,1152]{1,0:T(8,128)(2,1)} %get-tuple-element.209), channel_id=1, source_target_pairs={{0,4},{4,0},{8,12},{12,8},{16,20},{20,16},{24,28},{28,24},{1,5},{5... | collective-permute-start | bytes 1769480 | tf_op jit(solution)/shard_map/ppermute | solution.py:20
  139.5 17.5 %collective-permute-start.15 = (f32[256,512]{1,0:T(8,128)}, f32[256,512]{1,0:T(8,128)}, u32[]{:S(2)}, u32[]{:S(2)}) collective-permute-start(f32[256,512]{1,0:T(8,128)} %get-tuple-element.185.refs_1_), channel_id=1, source_target_pairs={{0,1},{1,0},{2,3},{3,2},{4,5},{5,4},{6,7},{7,6},{8,9},{9,8},{10,11... | collective-permute-start | bytes 1572872 | tf_op jit(solution)/shard_map/ppermute | solution.py:20
  146.9 14.4 %collective-permute-start.21 = (bf16[128,1152]{1,0:T(8,128)(2,1)}, bf16[128,1152]{1,0:T(8,128)(2,1)}, u32[]{:S(2)}, u32[]{:S(2)}) collective-permute-start(bf16[128,1152]{1,0:T(8,128)(2,1)} %get-tuple-element.204), channel_id=1, source_target_pairs={{0,8},{4,12},{8,0},{12,4},{16,24},{20,28},{24,16},{28,20},{1,9},{5... | collective-permute-start | bytes 884744 | tf_op jit(solution)/shard_map/ppermute | solution.py:20
  148.5 29.1 %collective-permute-start.27 = (bf16[128,2048]{1,0:T(8,128)(2,1)}, bf16[128,2048]{1,0:T(8,128)(2,1)}, u32[]{:S(2)}, u32[]{:S(2)}) collective-permute-start(bf16[128,2048]{1,0:T(8,128)(2,1)} %get-tuple-element.221), channel_id=1, source_target_pairs={{0,4},{4,0},{8,12},{12,8},{16,20},{20,16},{24,28},{28,24},{1,5},{5... | collective-permute-start | bytes 1572872 | tf_op jit(solution)/shard_map/ppermute | solution.py:20
  154.4 14.4 %collective-permute-start.24 = (bf16[64,2048]{1,0:T(8,128)(2,1)}, bf16[64,2048]{1,0:T(8,128)(2,1)}, u32[]{:S(2)}, u32[]{:S(2)}) collective-permute-start(bf16[64,2048]{1,0:T(8,128)(2,1)} %get-tuple-element.212), channel_id=1, source_target_pairs={{0,16},{4,20},{8,24},{12,28},{16,0},{20,4},{24,8},{28,12},{1,17},{... | collective-permute-start | bytes 786440 | tf_op jit(solution)/shard_map/ppermute | solution.py:20
  159.8 4.1 %collective-permute-start.20 = (f32[16,256]{1,0:T(8,128)}, f32[16,256]{1,0:T(8,128)}, u32[]{:S(2)}, u32[]{:S(2)}) collective-permute-start(f32[16,256]{1,0:T(8,128)} %get-tuple-element.200.refs_6_), channel_id=1, source_target_pairs={{0,2},{2,0},{1,3},{3,1},{4,6},{6,4},{5,7},{7,5},{8,10},{10,8},{9,1... | collective-permute-start | bytes 49160 | tf_op jit(solution)/shard_map/ppermute | solution.py:20
  166.4 4.4 %collective-permute-start.23 = (f32[8,1152]{1,0:T(8,128)}, f32[8,1152]{1,0:T(8,128)}, u32[]{:S(2)}, u32[]{:S(2)}) collective-permute-start(f32[8,1152]{1,0:T(8,128)} %get-tuple-element.210.refs_5_), channel_id=1, source_target_pairs={{0,4},{4,0},{8,12},{12,8},{16,20},{20,16},{24,28},{28,24},{1,5},{5... | collective-permute-start | bytes 110600 | tf_op jit(solution)/shard_map/ppermute | solution.py:20
  173.5 14.9 %collective-permute-start.25 = (bf16[144,1152]{1,0:T(8,128)(2,1)}, bf16[144,1152]{1,0:T(8,128)(2,1)}, u32[]{:S(2)}, u32[]{:S(2)}) collective-permute-start(bf16[144,1152]{1,0:T(8,128)(2,1)} %get-tuple-element.216), channel_id=1, source_target_pairs={{0,8},{4,12},{8,0},{12,4},{16,24},{20,28},{24,16},{28,20},{1,9},{5... | collective-permute-start | bytes 995336 | tf_op jit(solution)/shard_map/ppermute | solution.py:20
  174.9 11.8 %collective-permute-start.26 = (bf16[64,1152]{1,0:T(8,128)(2,1)}, bf16[64,1152]{1,0:T(8,128)(2,1)}, u32[]{:S(2)}, u32[]{:S(2)}) collective-permute-start(bf16[64,1152]{1,0:T(8,128)(2,1)} %get-tuple-element.219), channel_id=1, source_target_pairs={{0,16},{4,20},{8,24},{12,28},{16,0},{20,4},{24,8},{28,12},{1,17},{... | collective-permute-start | bytes 442376 | tf_op jit(solution)/shard_map/ppermute | solution.py:20
  179.9 22.8 %collective-permute-start.29 = (bf16[64,2048]{1,0:T(8,128)(2,1)}, bf16[64,2048]{1,0:T(8,128)(2,1)}, u32[]{:S(2)}, u32[]{:S(2)}) collective-permute-start(bf16[64,2048]{1,0:T(8,128)(2,1)} %get-tuple-element.229), channel_id=1, source_target_pairs={{0,16},{4,20},{8,24},{12,28},{16,0},{20,4},{24,8},{28,12},{1,17},{... | collective-permute-start | bytes 786440 | tf_op jit(solution)/shard_map/ppermute | solution.py:20
  190.4 14.7 %collective-permute-start.28 = (bf16[80,1152]{1,0:T(8,128)(2,1)}, bf16[80,1152]{1,0:T(8,128)(2,1)}, u32[]{:S(2)}, u32[]{:S(2)}) collective-permute-start(bf16[80,1152]{1,0:T(8,128)(2,1)} %get-tuple-element.226), channel_id=1, source_target_pairs={{0,16},{4,20},{8,24},{12,28},{16,0},{20,4},{24,8},{28,12},{1,17},{... | collective-permute-start | bytes 552968 | tf_op jit(solution)/shard_map/ppermute | solution.py:20
  (4 other events, 9.7 us)
